TPU v7x, 32 devices: a whole 2x2x4 slice. The times are simulated.
32 devices in a mesh: band: 8 (over z, x), rep: 4 (over y, core).
Axes of the slice: x: 2, y: 2, z: 4, core: 2. Of those that a mesh axis runs over, the one named last changes fastest.
Arguments:
- patches: bfloat16 [8, 4, 80, 8, 768], P('rep', None, None, 'band'), may hold values from -6 to 6
- variable_group_index: int32 [5], replicated, may hold values from 0 to 2, as said below
- frozen_patch_weight: bfloat16 [3, 16, 512], replicated, may hold values from -0.625 to 0.625
- adapter_down: bfloat16 [80, 16], P('rep'), may hold values from -0.625 to 0.625
- adapter_up: bfloat16 [16, 512], P(None, 'rep'), may hold values from -1.5 to 1.5
- level_merge_weight: bfloat16 [4, 512, 512], replicated, may hold values from -0.125 to 0.125
- window_patch_mixer: bfloat16 [96, 96], replicated, may hold values from -0.625 to 0.625
- column_block_owner: int32 [8], replicated, may hold values from 0 to 7, each once
- mixed_token_gradient: bfloat16 [8, 8, 8, 96, 512], P('rep', 'band'), may hold values from -0.03125 to 0.03125
Outputs:
- mixed: bfloat16 [8, 8, 8, 96, 512], P('rep', 'band')
- first_factor_gradient: float32 [80, 16], P('rep')
- second_factor_gradient: float32 [16, 512], P(None, 'rep')
Inputs may be any that keep to these rules, and one draw needn't show every extreme that they name: Column block j goes to the band device column_block_owner[j]; each device owns one block. `variable_group_index`: every one of the 3 groups holds at least one variable.
All inputs are finite; a program needn't handle non-finite values.
Results may differ from a plain program's by a relative error of at most 0.01.
Values may be sent and summed in bfloat16 or wider, within the bound.
No kernel may reach another device: no remote copies, remote signals or barrier semaphores. Data moves between devices by JAX's collectives and lax.ppermute only.
A program may use at most 128 MiB of HBM per device.

v0:
```python
import jax
import jax.numpy as jnp
from jax import lax
from jax.sharding import PartitionSpec as P

WLAT = 8
WLON = 12


def gelu_exact(values):
    return jax.nn.gelu(values, approximate=False)


def embed_tokens(pixels, merged, level_merge_weight):
    embedded = jnp.einsum(
        "nlkt,kd->nltd", pixels, merged, preferred_element_type=jnp.float32
    ).astype(jnp.bfloat16)
    return jnp.einsum(
        "nltd,lde->nte", embedded, level_merge_weight, preferred_element_type=jnp.float32
    ).astype(jnp.bfloat16)


def window_forward(tokens, mix_table):
    item_count, lat_rows, block_width, feature_dim = tokens.shape
    window_tiles = tokens.reshape(
        item_count, lat_rows // WLAT, WLAT, block_width // WLON, WLON, feature_dim
    )
    pre_act = jnp.einsum(
        "iwjv,najbvd->naibwd", mix_table, window_tiles, preferred_element_type=jnp.float32
    )
    pre_act = pre_act.reshape(item_count, lat_rows, block_width, feature_dim)
    mixed_out = (tokens.astype(jnp.float32) + gelu_exact(pre_act)).astype(jnp.bfloat16)
    return (mixed_out, pre_act)


def window_backward(grad_out, pre_act, mix_table):
    item_count, lat_rows, block_width, feature_dim = grad_out.shape
    grad_float = grad_out.astype(jnp.float32)
    grad_pre = jax.vjp(gelu_exact, pre_act)[1](grad_float)[0].astype(jnp.bfloat16)
    grad_tiles = grad_pre.reshape(
        item_count, lat_rows // WLAT, WLAT, block_width // WLON, WLON, feature_dim
    )
    spread = jnp.einsum(
        "iwjv,naibwd->najbvd", mix_table, grad_tiles, preferred_element_type=jnp.float32
    )
    spread = spread.reshape(item_count, lat_rows, block_width, feature_dim)
    return (grad_float + spread).astype(jnp.bfloat16)


def weight_gradient(pixels, grad_tokens, level_merge_weight):
    grad_embed = jnp.einsum(
        "nte,lde->nltd", grad_tokens, level_merge_weight, preferred_element_type=jnp.float32
    ).astype(jnp.bfloat16)
    return jnp.einsum("nlkt,nltd->kd", pixels, grad_embed, preferred_element_type=jnp.float32)


def on_device(
    patches,
    variable_group_index,
    frozen_patch_weight,
    adapter_down,
    adapter_up,
    level_merge_weight,
    window_patch_mixer,
    column_block_owner,
    mixed_token_gradient,
):
    full_a, full_b = (
        lax.all_gather(adapter_down, "rep", axis=0, tiled=True),
        lax.all_gather(adapter_up, "rep", axis=1, tiled=True),
    )
    groups = frozen_patch_weight.shape[0]
    feature_dim = frozen_patch_weight.shape[2]
    selector = (
        variable_group_index[:, None] == jnp.arange(groups, dtype=jnp.int32)[None, :]
    ).astype(jnp.float32)
    base_rows = jnp.einsum(
        "vg,gad->vad", selector, frozen_patch_weight.astype(jnp.float32)
    ).reshape(-1, feature_dim)
    merged = (base_rows + jnp.dot(full_a, full_b, preferred_element_type=jnp.float32)).astype(
        jnp.bfloat16
    )
    band_count = lax.axis_size("band")
    samples, level_stack, channels, row_count, col_count = patches.shape
    block_width = col_count // band_count
    lat_rows = band_count * row_count
    block_ids = jnp.arange(band_count, dtype=jnp.int32)
    inverse = jnp.sum(
        jnp.where(column_block_owner[None, :] == block_ids[:, None], block_ids[None, :], 0), axis=1
    )
    mix_table = window_patch_mixer.reshape(WLAT, WLON, WLAT, WLON)
    grad_window = mixed_token_gradient.reshape(samples, lat_rows, block_width, feature_dim)
    pixels = patches.reshape(samples, level_stack, channels, row_count * col_count)
    tokens = embed_tokens(pixels, merged, level_merge_weight)
    blocks = tokens.reshape(samples, row_count, band_count, block_width, feature_dim)
    outgoing = jnp.take(blocks, inverse, axis=2)
    arrived = lax.all_to_all(outgoing, "band", split_axis=2, concat_axis=1, tiled=True)
    item_count = arrived.shape[0]
    flat_tokens = arrived.reshape(item_count, arrived.shape[1], block_width, feature_dim)
    mixed_out, pre_act = window_forward(flat_tokens, mix_table)
    mixed_out, pre_act = (
        mixed_out.reshape(item_count, 1, arrived.shape[1], block_width, feature_dim),
        pre_act,
    )
    grad_tokens = window_backward(grad_window, pre_act, mix_table)
    returned = lax.all_to_all(
        grad_tokens.reshape(samples, lat_rows, 1, block_width, feature_dim),
        "band",
        split_axis=1,
        concat_axis=2,
        tiled=True,
    )
    ordered = jnp.take(returned, column_block_owner, axis=2).reshape(
        samples, row_count * col_count, feature_dim
    )
    local_grad = weight_gradient(pixels, ordered, level_merge_weight)
    factor_b = full_b.astype(jnp.float32)
    factor_a = full_a.astype(jnp.float32)
    summed = lax.psum(local_grad, ("band", "rep"))
    rep_index = lax.axis_index("rep")
    row_share = summed.shape[0] // lax.axis_size("rep")
    col_share = summed.shape[1] // lax.axis_size("rep")
    rows_part = lax.dynamic_slice_in_dim(summed, rep_index * row_share, row_share, 0)
    cols_part = lax.dynamic_slice_in_dim(summed, rep_index * col_share, col_share, 1)
    first_factor_gradient = jnp.dot(rows_part, factor_b.T, precision=lax.Precision.HIGHEST)
    second_factor_gradient = jnp.dot(factor_a.T, cols_part, precision=lax.Precision.HIGHEST)
    return (mixed_out, first_factor_gradient, second_factor_gradient)


def solution(mesh):
    in_specs = (
        P("rep", None, None, "band", None),
        P(),
        P(),
        P("rep", None),
        P(None, "rep"),
        P(),
        P(),
        P(),
        P("rep", "band", None, None, None),
    )
    out_specs = (P("rep", "band", None, None, None), P("rep", None), P(None, "rep"))
    return jax.shard_map(
        on_device, mesh=mesh, in_specs=in_specs, out_specs=out_specs, check_vma=False
    )
```

profile of v0, /device:TPU:10, one launch (start us, length us, event | category | flops | bytes accessed | tf_op | source)
XLA Modules:
  0.0 289.2 jit_solution(16681322762308296985)
XLA Ops:
  7.2 0.0 copy-start
  7.2 0.9 select_reduce_fusion
  8.1 5.4 %all_gather.7 = bf16[16,512]{1,0:T(8,128)(2,1)S(1)} all-gather(bf16[16,128]{1,0:T(8,128)(2,1)} %param.15), channel_id=1, replica_groups=mesh['band'=8,'rep'=4] {'rep'}, dimensions={1}, use_global_device_ids=true | all-gather | bytes 20480 | tf_op jit(solution)/shard_map/all_gather | solution.py:70
  13.5 5.3 %all-gather = bf16[4,20,16]{1,2,0:T(8,128)(2,1)S(1)} all-gather(bf16[1,20,16]{1,2,0:T(8,128)(2,1)} %bitcast.149), channel_id=1, replica_groups=mesh['band'=8,'rep'=4] {'rep'}, dimensions={0}, use_global_device_ids=true | all-gather | bytes 3200 | tf_op jit(solution)/shard_map/all_gather | solution.py:69
  18.8 0.1 reshape.357
  18.9 1.0 fusion.56
  20.0 0.1 copy.83
  20.1 0.2 fusion.53
  20.3 0.0 copy-done
  20.3 7.5 %bitcast_convert_fusion = bf16[2,768,512]{2,1,0:T(8,128)(2,1)} fusion(bf16[4,512,512]{2,1,0:T(8,128)(2,1)S(1)} %copy-done, bf16[80,512,1,1]{1,0,3,2:T(8,128)(2,1)S(1)} %fusion.53, bf16[2,4,80,1,768]{4,2,3,1,0:T(8,128)(2,1)} %param.11), kind=kOutput, calls=%fused_computation.44 | convolution fusion | flops 3728474112 | bytes 4734976 | tf_op jit(solution)/shard_map/nltd,lde->nte/dot_general | solution.py:18
  27.7 3.2 %gather_fusion = bf16[8,2,96,512]{3,2,1,0:T(8,128)(2,1)} fusion(bf16[2,8,96,512]{3,2,1,0:T(8,128)(2,1)} %bitcast.145, s32[1024]{0:T(1024)S(1)} %pad_clamp_fusion.1), kind=kCustom, calls=%fused_computation.clone | custom fusion | bytes 3145760 | tf_op jit(solution)/shard_map/jit(_take)/gather | solution.py:96
  30.9 0.0 copy-start.4
  30.9 2.8 fusion.46
  33.7 6.7 %all-to-all-start = ((bf16[2,1,8,96,512]{4,3,0,1,2:T(8,128)(2,1)}), bf16[2,1,8,96,512]{4,3,0,1,2:T(8,128)(2,1)}, u32[]{:S(2)}, u32[]{:S(2)}) async-start(bf16[2,1,8,96,512]{4,3,0,1,2:T(8,128)(2,1)} %fusion.46), calls=%async_computation | async-start | bytes 3145728 | tf_op jit(solution)/shard_map/all_to_all | solution.py:97
  40.4 0.0 copy-done.4
  40.4 0.2 reshape.328
  40.6 0.5 copy.106
  41.1 4.1 %copy_convert_fusion = f32[2,1,8,96,512]{4,2,3,0,1:T(8,128)} fusion(bf16[2,1,8,96,512]{4,3,2,1,0:T(8,128)(2,1)} %param.19), kind=kLoop, calls=%fused_computation.67 | loop fusion | flops 786432 | bytes 4718592 | tf_op jit(solution)/shard_map/convert_element_type | solution.py:38
  45.2 28.9 %all-to-all-done = bf16[2,1,8,96,512]{4,3,0,1,2:T(8,128)(2,1)} async-done(((bf16[2,1,8,96,512]{4,3,0,1,2:T(8,128)(2,1)}), bf16[2,1,8,96,512]{4,3,0,1,2:T(8,128)(2,1)}, u32[]{:S(2)}, u32[]{:S(2)}) %all-to-all-start) | async-done | bytes 1572896 | tf_op jit(solution)/shard_map/all_to_all | solution.py:97
  74.1 2.3 copy.87
  76.4 0.0 copy-start.3
  76.4 0.8 fusion.101
  77.2 0.0 copy-start.1
  77.2 2.0 copy-done.1
  79.2 0.0 copy-done.3
  79.2 10.8 %convolution_bitcast_fusion = f32[2,1,8,8,12,512]{5,4,2,3,0,1:T(8,128)S(1)} fusion(f32[2,1,8,8,12,512]{5,2,4,3,0,1:T(8,128)S(1)} %bitcast.143, bf16[8,12,8,12,1,1]{3,2,1,0,5,4:T(8,128)(2,1)S(1)} %bitcast.147, f32[2,8,512,8,12,1]{2,4,5,3,1,0:T(8,128)S(1)} %fusion.101), kind=kOutput, calls=%fused_computation.59 | convolution fusion | flops 207618048 | bytes 9455616 | tf_op jit(solution)/shard_map/iwjv,naibwd->najbvd/dot_general | solution.py:43
  90.0 0.0 copy-start.2
  90.1 2.6 copy.96
  92.6 0.0 copy-done.2
  92.7 1.3 fusion.28
  93.9 0.0 copy-start.6
  93.9 1.6 copy.97
  95.6 7.6 %all-to-all-start.1 = ((bf16[2,8,1,96,512]{4,3,0,2,1:T(8,128)(2,1)}), bf16[2,8,1,96,512]{4,3,0,2,1:T(8,128)(2,1)}, u32[]{:S(2)}, u32[]{:S(2)}) async-start(bf16[2,8,1,96,512]{4,3,0,2,1:T(8,128)(2,1)} %copy.97), calls=%async_computation.1 | async-start | bytes 3145728 | tf_op jit(solution)/shard_map/all_to_all | solution.py:106
  103.1 0.2 all-reduce.2.cloned.1.call-start
  103.4 0.0 copy-done.6
  103.4 3.2 %fusion.16 = (f32[2,1,8,8,12,512]{5,4,2,3,0,1:T(8,128)S(1)}, f32[2,1,8,8,12,512]{5,4,2,3,0,1:T(8,128)S(1)}) fusion(f32[2,8,512,8,12,1]{2,4,5,3,1,0:T(8,128)} %copy-done.1), kind=kLoop, calls=%fused_computation.24 | loop fusion | flops 2359296 | bytes 9437184 | tf_op jit(solution)/shard_map/mul | solution.py:11
  106.7 4.1 %copy.91 = f32[2,1,8,8,12,512]{5,2,4,3,0,1:T(8,128)} copy(f32[2,1,8,8,12,512]{5,4,2,3,0,1:T(8,128)S(1)} %get-tuple-element.16) | data formatting | bytes 6291456 | tf_op jit(solution)/shard_map/mul | solution.py:11
  110.8 4.1 %copy.90 = f32[2,1,8,8,12,512]{5,2,4,3,0,1:T(8,128)} copy(f32[2,1,8,8,12,512]{5,4,2,3,0,1:T(8,128)S(1)} %get-tuple-element.17) | data formatting | bytes 6291456 | tf_op jit(solution)/shard_map/mul | solution.py:11
  114.9 21.6 %all-to-all-done.1 = bf16[2,8,1,96,512]{4,3,0,2,1:T(8,128)(2,1)} async-done(((bf16[2,8,1,96,512]{4,3,0,2,1:T(8,128)(2,1)}), bf16[2,8,1,96,512]{4,3,0,2,1:T(8,128)(2,1)}, u32[]{:S(2)}, u32[]{:S(2)}) %all-to-all-start.1) | async-done | bytes 1572896 | tf_op jit(solution)/shard_map/all_to_all | solution.py:106
  136.5 2.7 copy.149
  139.2 3.3 %gather_fusion.1 = bf16[8,2,96,512]{3,2,1,0:T(8,128)(2,1)} fusion(bf16[2,8,96,512]{3,2,1,0:T(8,128)(2,1)} %bitcast.141, s32[1024]{0:T(1024)S(1)} %pad_clamp_fusion), kind=kCustom, calls=%fused_computation.1.clone | custom fusion | bytes 3145760 | tf_op jit(solution)/shard_map/jit(_take)/gather | solution.py:113
  142.5 0.0 copy-start.5
  142.5 1.7 bitcast_select_fusion
  144.2 1.2 copy.99
  145.4 0.0 copy-done.5
  145.4 6.6 %fusion.47 = f32[80,512]{1,0:T(8,128)} fusion(bf16[2,768,512,1]{2,1,0,3:T(8,128)(2,1)} %bitcast.144, bf16[4,512,512]{2,1,0:T(8,128)(2,1)S(1)} %copy-done, bf16[2,4,80,1,768]{4,2,3,1,0:T(8,128)(2,1)S(1)} %copy-done.5), kind=kOutput, calls=%fused_computation.68 | convolution fusion | flops 3727687680 | bytes 4816896 | tf_op jit(solution)/shard_map/nlkt,nltd->kd/dot_general | solution.py:54
  152.1 0.0 all-reduce.2.cloned.1.call-update
  152.1 9.3 %fusion.27 = bf16[2,1,8,96,512]{4,2,3,0,1:T(8,128)(2,1)S(1)} fusion(f32[2,1,8,96,512]{4,2,3,0,1:T(8,128)} %bitcast.140, f32[2,1,8,96,512]{4,2,3,0,1:T(8,128)} %bitcast.139, bf16[2,1,8,96,512]{4,3,0,1,2:T(8,128)(2,1)} %all-to-all-done), kind=kLoop, calls=%fused_computation.41 | loop fusion | flops 50331648 | bytes 9437184 | tf_op jit(solution)/shard_map/convert_element_type | solution.py:32
  161.4 1.7 copy.101
  163.1 115.9 %all-reduce.2.cloned.1.call-done = f32[80,512]{1,0:T(8,128)} async-done(((f32[80,512]{1,0:T(8,128)}), f32[80,512]{1,0:T(8,128)}) %all-reduce.2.cloned.1.call-update) | async-done | bytes 163856 | tf_op jit(solution)/shard_map/psum | solution.py:119
  279.0 1.6 fusion.58
  280.6 1.5 convolution_bitcast_fusion.1
  (7 shorter events, 0.0 us)
Async XLA Ops:
  7.2 13.1 %copy-start = (bf16[4,512,512]{2,1,0:T(8,128)(2,1)S(1)}, bf16[4,512,512]{2,1,0:T(8,128)(2,1)}, u32[]{:S(2)}) copy-start(bf16[4,512,512]{2,1,0:T(8,128)(2,1)} %param.16) | copy-start | bytes 6291460
  30.9 9.5 %copy-start.4 = (bf16[96,96]{1,0:T(8,128)(2,1)S(1)}, bf16[96,96]{1,0:T(8,128)(2,1)}, u32[]{:S(2)}) copy-start(bf16[96,96]{1,0:T(8,128)(2,1)} %param.17) | copy-start | bytes 55300
  33.7 40.4 %all-to-all-start = ((bf16[2,1,8,96,512]{4,3,0,1,2:T(8,128)(2,1)}), bf16[2,1,8,96,512]{4,3,0,1,2:T(8,128)(2,1)}, u32[]{:S(2)}, u32[]{:S(2)}) async-start(bf16[2,1,8,96,512]{4,3,0,1,2:T(8,128)(2,1)} %fusion.46), calls=%async_computation | async-start | bytes 3145728 | tf_op jit(solution)/shard_map/all_to_all | solution.py:97
  76.4 2.8 copy-start.3
  77.2 2.0 copy-start.1
  90.0 2.6 copy-start.2
  93.9 9.5 %copy-start.6 = (s32[8]{0:T(128)S(1)}, s32[8]{0:T(128)}, u32[]{:S(2)}) copy-start(s32[8]{0:T(128)} %param.18) | copy-start | bytes 100
  95.6 40.9 %all-to-all-start.1 = ((bf16[2,8,1,96,512]{4,3,0,2,1:T(8,128)(2,1)}), bf16[2,8,1,96,512]{4,3,0,2,1:T(8,128)(2,1)}, u32[]{:S(2)}, u32[]{:S(2)}) async-start(bf16[2,8,1,96,512]{4,3,0,2,1:T(8,128)(2,1)} %copy.97), calls=%async_computation.1 | async-start | bytes 3145728 | tf_op jit(solution)/shard_map/all_to_all | solution.py:106
  103.1 175.9 %all-reduce.2.cloned.1.call-start = ((), (), s32[]{:S(2)}) async-start(), calls=%async_computation.2 | async-start | bytes 327680 | tf_op jit(solution)/shard_map/psum | solution.py:119
  142.5 3.0 %copy-start.5 = (bf16[2,4,80,1,768]{4,2,3,1,0:T(8,128)(2,1)S(1)}, bf16[2,4,80,1,768]{4,2,3,1,0:T(8,128)(2,1)}, u32[]{:S(2)}) copy-start(bf16[2,4,80,1,768]{4,2,3,1,0:T(8,128)(2,1)} %param.11) | copy-start | bytes 2949124
Sparse Core Ops, SparseCore 0:
  152.2 126.7 all-reduce.1
where the time goes:
time: 295 us; the launch traced here: 289 us
  waiting for transfers between devices  166 us (56%)
  matrix products  30.1 us (10%)
  local copies, waits for them, and re-layouts  29.7 us (10%)
  other arithmetic  23.3 us (8%)
  starting transfers between devices  14.5 us (5%)
  between operations  14.5 us (5%)
  blocking collectives  10.7 us (4%)
    psum x1, waiting for transfers between devices, on_device(): summed = lax.psum(local_grad, ('band', 'rep'))  116 us
    all_to_all x1, waiting for transfers between devices, on_device(): lax.all_to_all(outgoing, 'band', split_axis=2, concat_axis=1, tiled=True)  28.9 us
    all_to_all x1, waiting for transfers between devices, on_device(): lax.all_to_all(grad_tokens.reshape(samples, lat_rows, 1, block_width, fea...  21.6 us
    dot_general x1, matrix products, window_backward(): jnp.einsum('iwjv,naibwd->najbvd', mix_table, grad_tiles, preferred_elemen...  10.8 us
    convert_element_type x1, other arithmetic, window_forward(): (tokens.astype(jnp.float32) + gelu_exact(pre_act)).astype(jnp.bfloat16)  9.33 us
    mul x2, local copies, waits for them, and re-layouts, gelu_exact(): return jax.nn.gelu(values, approximate=False)  8.19 us
    all_to_all x1, starting transfers between devices, on_device(): lax.all_to_all(grad_tokens.reshape(samples, lat_rows, 1, block_width, fea...  7.57 us
    dot_general x1, matrix products, embed_tokens(): jnp.einsum('nltd,lde->nte', embedded, level_merge_weight, preferred_eleme...  7.46 us
  transfers between devices with their start and end apart: 3, of which 3 were waited for; matrix products, arithmetic and copies ran while one was open for 9% of the time, Pallas kernels for 0%

commit v1 on v0

v1 whole, which is shorter than its diff:
```python
import functools

import jax
import jax.numpy as jnp
from jax import lax
from jax.experimental import pallas as pl
from jax.experimental.pallas import tpu as pltpu
from jax.sharding import PartitionSpec as P

WLAT = 8
WLON = 12
LANE = 128
SUB = 16
VMEM_LIMIT = 50 * 1024 * 1024
BF16 = jnp.bfloat16
F32 = jnp.float32


def round_up(value, step):
    return -(-value // step) * step


def dot_nn(a, b):
    return lax.dot_general(a, b, (((1,), (0,)), ((), ())), preferred_element_type=F32)


def dot_nt(a, b):
    return lax.dot_general(a, b, (((1,), (1,)), ((), ())), preferred_element_type=F32)


def dot_tn(a, b):
    return lax.dot_general(a, b, (((0,), (0,)), ((), ())), preferred_element_type=F32)


def split_hi_lo(values):
    high = values.astype(BF16)
    low = (values - high.astype(F32)).astype(BF16)
    return high, low


def iota2(shape, axis):
    return lax.broadcasted_iota(jnp.int32, shape, axis)


def params(**extra):
    return pltpu.CompilerParams(vmem_limit_bytes=VMEM_LIMIT, **extra)


def send_kernel(band_count, half_width, owner_ref, x_ref, *out_refs):
    halves = len(out_refs)
    for tile in range(x_ref.shape[1] // LANE):
        rows = x_ref[:, tile * LANE : (tile + 1) * LANE].T
        start = tile * LANE
        while start < (tile + 1) * LANE:
            piece = start // half_width
            end = min((piece + 1) * half_width, (tile + 1) * LANE)
            slot = owner_ref[piece // halves]
            offset = start - piece * half_width
            out_refs[piece % halves][slot, offset : offset + end - start, :] = rows[
                start - tile * LANE : end - tile * LANE, :
            ]
            start = end


def send_blocks(pixels, owner, band_count, halves, half_width):
    features, columns = pixels.shape
    block = jax.ShapeDtypeStruct((band_count, half_width, features), BF16)
    out_spec = pl.BlockSpec((band_count, half_width, LANE), lambda f, owner: (0, 0, f))
    return pl.pallas_call(
        functools.partial(send_kernel, band_count, half_width),
        out_shape=[block] * halves,
        grid_spec=pltpu.PrefetchScalarGridSpec(
            num_scalar_prefetch=1,
            grid=(features // LANE,),
            in_specs=[pl.BlockSpec((LANE, columns), lambda f, owner: (f, 0))],
            out_specs=[out_spec] * halves,
        ),
        compiler_params=params(),
        name="send_blocks",
    )(owner, pixels)


def expand_table(table, rows, half_width_padded, half_width, transpose):
    position = iota2((rows, WLAT * WLON), 0)
    line, col = position // half_width_padded, position % half_width_padded
    target = iota2((rows, WLAT * WLON), 1)
    pick = jnp.where((target == line * WLON + col % WLON) & (col < half_width), 1.0, 0.0).astype(BF16)
    left = (dot_nt if transpose else dot_nn)(pick, table).astype(BF16)
    full = dot_nt(left, pick)
    row_window = (iota2((rows, 1), 0) % half_width_padded) // WLON
    col_window = (iota2((1, rows), 1) % half_width_padded) // WLON
    return jnp.where(row_window == col_window, full, 0.0).astype(BF16)


def prep_kernel(
    row_share,
    half_width,
    half_width_padded,
    group_ref,
    frozen_ref,
    factors_ref,
    level_ref,
    mixer_ref,
    merged_ref,
    up_ref,
    down_ref,
    mix_ref,
    mix_t_ref,
):
    reps, _, rank, share = factors_ref.shape
    levels = level_ref.shape[0]
    variables = group_ref.shape[0]
    channels = variables * frozen_ref.shape[1]
    up = jnp.concatenate([factors_ref[r, 0] for r in range(reps)], axis=1)
    source, target = iota2((share, channels), 0), iota2((share, channels), 1)
    down_t = jnp.zeros((rank, channels), F32)
    for r in range(reps):
        place = jnp.where((target == source + r * row_share) & (source < row_share), 1.0, 0.0)
        down_t = down_t + dot_nn(factors_ref[r, 1], place.astype(BF16))
    down_t = down_t.astype(BF16)
    down_ref[...] = down_t
    base = jnp.concatenate([frozen_ref[group_ref[v]].astype(F32) for v in range(variables)], axis=0)
    merged = (base + dot_tn(down_t, up)).astype(BF16)
    stacked = jnp.concatenate([merged, up], axis=0)
    merged_ref[...] = jnp.zeros_like(merged_ref)
    for level in range(levels):
        through = dot_nn(stacked, level_ref[level])
        weights = through[:channels].astype(BF16)
        for s in range(merged_ref.shape[0]):
            offset = (s * levels * channels) % LANE + level * channels
            merged_ref[s, offset : offset + channels, :] = weights
        up_high, up_low = split_hi_lo(through[channels:])
        up_ref[level, :rank, :] = up_high
        up_ref[level, rank:, :] = up_low
    rows = mix_ref.shape[0]
    mix_ref[...] = expand_table(mixer_ref[...], rows, half_width_padded, half_width, False)
    mix_t_ref[...] = expand_table(mixer_ref[...], rows, half_width_padded, half_width, True)


def prepare(groups, frozen, factors, level_weight, mixer, samples, row_share, half_width, half_width_padded):
    reps, _, rank, _ = factors.shape
    levels, feature_dim, _ = level_weight.shape
    channels = groups.shape[0] * frozen.shape[1]
    reach = round_up(levels * channels + LANE // 2, LANE)
    rows = WLAT * half_width_padded
    vmem = pl.BlockSpec(memory_space=pltpu.VMEM)
    flops = 2 * levels * (channels + rank) * feature_dim * feature_dim + 4 * rows * rows * WLAT * WLON
    return pl.pallas_call(
        functools.partial(prep_kernel, row_share, half_width, half_width_padded),
        out_shape=[
            jax.ShapeDtypeStruct((samples, reach, feature_dim), BF16),
            jax.ShapeDtypeStruct((levels, 2 * rank, feature_dim), BF16),
            jax.ShapeDtypeStruct((rank, channels), BF16),
            jax.ShapeDtypeStruct((rows, rows), BF16),
            jax.ShapeDtypeStruct((rows, rows), BF16),
        ],
        in_specs=[pl.BlockSpec(memory_space=pltpu.SMEM)] + [vmem] * 4,
        out_specs=[vmem] * 5,
        compiler_params=params(),
        cost_estimate=pl.CostEstimate(flops=flops, bytes_accessed=4 * 2**20, transcendentals=0),
        name="prepare",
    )(groups, frozen, factors, level_weight, mixer)


def normal_parts(values):
    cdf = 0.5 + 0.5 * lax.erf(values * 0.7071067811865476)
    pdf = 0.3989422804014327 * jnp.exp(-0.5 * values * values)
    return cdf, pdf


def mix_kernel(chained, last, dims, *refs):
    levels, channels, rank, reps = dims
    refs = list(refs)
    arrived_ref, merged_ref, mix_ref, mix_t_ref, grad_ref = refs[:5]
    del refs[:5]
    before_ref = None
    if chained:
        before_ref = refs[1]
        del refs[:2]
    if last:
        up_ref, down_ref, level_ref = refs[:3]
        del refs[:3]
    mixed_ref, out_ref, total_ref, tokens_ref, pre_ref, grad_pre_ref = refs

    window_row, sample = pl.program_id(0), pl.program_id(1)
    samples = merged_ref.shape[0]
    reach = merged_ref.shape[1]
    width = arrived_ref.shape[1]
    rows = WLAT * width
    depth = levels * channels
    first_lane = pl.multiple_of((sample * depth) // LANE * LANE, LANE)
    pixels = arrived_ref[:, :, pl.ds(first_lane, reach)].reshape(rows, reach)
    tokens_ref[...] = dot_nn(pixels, merged_ref[sample]).astype(BF16)
    pre_ref[...] = dot_nn(mix_ref[...], tokens_ref[...])

    def line(i, carry):
        for start in range(0, width, SUB):
            at = pl.ds(pl.multiple_of(i * width + start, SUB), SUB)
            pre = pre_ref[at, :]
            cdf, pdf = normal_parts(pre)
            mixed_ref[0, i, start : start + SUB, :] = (
                tokens_ref[at, :].astype(F32) + pre * cdf
            ).astype(BF16)
            grad = grad_ref[0, i, start : start + SUB, :].astype(F32)
            grad_pre_ref[at, :] = (grad * (cdf + pre * pdf)).astype(BF16)
        return carry

    lax.fori_loop(0, WLAT, line, 0)
    feature_dim = tokens_ref.shape[1]
    grad_tokens = dot_nn(mix_t_ref[...], grad_pre_ref[...]) + grad_ref[0].reshape(
        rows, feature_dim
    ).astype(F32)
    share = dot_tn(pixels, grad_tokens.astype(BF16))

    @pl.when(window_row == 0)
    def _():
        total_ref[sample] = share

    @pl.when(window_row != 0)
    def _():
        total_ref[sample] = total_ref[sample] + share

    @pl.when((window_row == pl.num_programs(0) - 1) & (sample == samples - 1))
    def _():
        total = before_ref[...] if chained else jnp.zeros((depth, feature_dim), F32)
        for s in range(samples):
            offset = (s * depth) % LANE
            total = total + total_ref[s, offset : offset + depth, :]
        if not last:
            out_ref[...] = total
            return
        high, low = split_hi_lo(total)
        first = jnp.zeros((rank, channels), F32)
        second = jnp.zeros((2 * rank, feature_dim), F32)
        for level in range(levels):
            at = slice(level * channels, (level + 1) * channels)
            both = dot_nt(up_ref[level], high[at])
            first = first + both[:rank] + both[rank:] + dot_nt(up_ref[level, :rank, :], low[at])
            down = down_ref[...]
            through = dot_nn(down, high[at]) + dot_nn(down, low[at])
            through = jnp.concatenate(split_hi_lo(through), axis=0)
            second = second + dot_nt(through, level_ref[level])
        second = second[:rank] + second[rank:]
        col_share = feature_dim // reps
        out_ref[...] = jnp.zeros_like(out_ref)
        for r in range(reps):
            out_ref[r, :, :col_share] = second[:, r * col_share : (r + 1) * col_share]
            out_ref[r, :, col_share : col_share + channels] = first


def mix_half(half, last, arrived, merged, mix, mix_t, grad, chain, tail, reps):
    lat_rows, width, lanes = arrived.shape
    samples, _, block_width, feature_dim = grad.shape
    reach = merged.shape[1]
    rows = WLAT * width
    levels, two_rank, _ = tail[0].shape
    rank = two_rank // 2
    channels = tail[1].shape[1]
    depth = levels * channels
    whole = lambda shape: pl.BlockSpec(shape, lambda w, s: (0,) * len(shape))
    block = pl.BlockSpec((1, WLAT, width, feature_dim), lambda w, s: (s, w, half, 0))
    in_specs = [
        pl.BlockSpec((WLAT, width, lanes), lambda w, s: (w, 0, 0)),
        whole(merged.shape),
        whole(mix.shape),
        whole(mix_t.shape),
        block,
    ]
    operands = [arrived, merged, mix, mix_t, grad]
    aliases = {}
    if chain is not None:
        aliases = {len(operands): 0}
        in_specs += [pl.BlockSpec(memory_space=pl.ANY), whole(chain[1].shape)]
        operands += list(chain)
    if last:
        in_specs += [whole(array.shape) for array in tail]
        operands += list(tail)
        out_tile = (reps, rank, feature_dim // reps + round_up(channels, LANE))
    else:
        out_tile = (depth, feature_dim)
    flops = 2 * samples * lat_rows * width * feature_dim * (2 * reach + 2 * rows)
    return pl.pallas_call(
        functools.partial(mix_kernel, chain is not None, last, (levels, channels, rank, reps)),
        out_shape=[
            jax.ShapeDtypeStruct(grad.shape, BF16),
            jax.ShapeDtypeStruct(out_tile, F32),
        ],
        grid=(lat_rows // WLAT, samples),
        in_specs=in_specs,
        out_specs=[block, whole(out_tile)],
        scratch_shapes=[
            pltpu.VMEM((samples, reach, feature_dim), F32),
            pltpu.VMEM((rows, feature_dim), BF16),
            pltpu.VMEM((rows, feature_dim), F32),
            pltpu.VMEM((rows, feature_dim), BF16),
        ],
        input_output_aliases=aliases,
        compiler_params=params(dimension_semantics=("arbitrary", "arbitrary")),
        cost_estimate=pl.CostEstimate(
            flops=flops, bytes_accessed=8 * 2**20, transcendentals=samples * lat_rows * width * feature_dim
        ),
        name="mix_half",
    )(*operands)


def on_device(
    patches,
    variable_group_index,
    frozen_patch_weight,
    adapter_down,
    adapter_up,
    level_merge_weight,
    window_patch_mixer,
    column_block_owner,
    mixed_token_gradient,
):
    band_count, reps = lax.axis_size("band"), lax.axis_size("rep")
    samples, levels, channels, row_count, col_count = patches.shape
    feature_dim = frozen_patch_weight.shape[2]
    rank, col_share = adapter_up.shape
    row_share = adapter_down.shape[0]
    lat_rows = band_count * row_count
    block_width = col_count // band_count
    halves = 2 if block_width % (2 * SUB * WLON // 4) == 0 else 1
    half_width = block_width // halves
    half_padded = round_up(half_width, SUB)
    features = samples * levels * channels

    pixels = patches.reshape(features, col_count)
    if half_padded == half_width and features % LANE == 0 and col_count % LANE == 0:
        outgoing = send_blocks(pixels, column_block_owner, band_count, halves, half_width)
    else:
        block_ids = jnp.arange(band_count, dtype=jnp.int32)
        inverse = jnp.sum(
            jnp.where(column_block_owner[None, :] == block_ids[:, None], block_ids[None, :], 0), axis=1
        )
        by_block = jnp.take(pixels.T.reshape(band_count, block_width, features), inverse, axis=0)
        outgoing = [
            jnp.pad(
                by_block[:, h * half_width : (h + 1) * half_width],
                ((0, 0), (0, half_padded - half_width), (0, 0)),
            )
            for h in range(halves)
        ]
    arrived = [lax.all_to_all(part, "band", split_axis=0, concat_axis=0, tiled=True) for part in outgoing]

    pack_width = round_up(max(row_share, col_share), LANE)
    pack = jnp.stack(
        [
            jnp.pad(adapter_up, ((0, 0), (0, pack_width - col_share))),
            jnp.pad(adapter_down.T, ((0, 0), (0, pack_width - row_share))),
        ]
    )
    factors = lax.all_gather(pack, "rep", axis=0, tiled=False)
    merged, up_through, down_t, mix, mix_t = prepare(
        variable_group_index,
        frozen_patch_weight,
        factors,
        level_merge_weight,
        window_patch_mixer,
        samples,
        row_share,
        half_width,
        half_padded,
    )
    tail = (up_through, down_t, level_merge_weight)

    grad = mixed_token_gradient.reshape(samples, lat_rows, block_width, feature_dim)
    if half_padded != half_width:
        grad = jnp.pad(grad, ((0, 0), (0, 0), (0, half_padded - half_width), (0, 0)))
    chain = None
    for half in range(halves):
        chain = mix_half(
            half, half == halves - 1, arrived[half], merged, mix, mix_t, grad, chain, tail, reps
        )
    mixed, shares = chain
    if half_padded != half_width:
        mixed = mixed[:, :, :block_width]

    mine = jnp.sum(lax.all_to_all(shares, "rep", split_axis=0, concat_axis=0, tiled=True), axis=0)
    summed = jnp.sum(lax.all_gather(mine, "band", axis=0, tiled=False), axis=0)
    first_t = lax.dynamic_slice_in_dim(summed, col_share + lax.axis_index("rep") * row_share, row_share, 1)
    return (
        mixed.reshape(mixed_token_gradient.shape),
        first_t.T,
        summed[:, :col_share],
    )


def solution(mesh):
    in_specs = (
        P("rep", None, None, "band", None),
        P(),
        P(),
        P("rep", None),
        P(None, "rep"),
        P(),
        P(),
        P(),
        P("rep", "band", None, None, None),
    )
    out_specs = (P("rep", "band", None, None, None), P("rep", None), P(None, "rep"))
    return jax.shard_map(
        on_device, mesh=mesh, in_specs=in_specs, out_specs=out_specs, check_vma=False
    )
```

time: 295 us -> 95.7 us (0.32)
  the two profiles are of different devices: /device:TPU:10 before, /device:TPU:0 now
where the time goes in v1:
time: 95.7 us; the launch traced here: 95.1 us
  blocking collectives  57.4 us (60%)
  Pallas kernels  16.6 us (17%)
  local copies, waits for them, and re-layouts  9.3 us (10%)
  starting transfers between devices  6.87 us (7%)
  waiting for transfers between devices  4.08 us (4%)
    all_gather x1, blocking collectives, on_device(): summed = jnp.sum(lax.all_gather(mine, 'band', axis=0, tiled=False), axis=0)  31.1 us
    all_to_all x1, blocking collectives, on_device(): lax.all_to_all(part, 'band', split_axis=0, concat_axis=0, tiled=True)  21 us
    pallas_call x2, Pallas kernels, mix_half(): pl.pallas_call(functools.partial(mix_kernel, chain is not None, last, (le...  11.9 us
    unnamed x32, local copies, waits for them, and re-layouts  8.03 us
    all_gather x1, blocking collectives, on_device(): factors = lax.all_gather(pack, 'rep', axis=0, tiled=False)  5.33 us
    all_to_all x1, waiting for transfers between devices, on_device(): lax.all_to_all(shares, 'rep', split_axis=0, concat_axis=0, tiled=True)  4.08 us
    all_to_all x1, starting transfers between devices, on_device(): lax.all_to_all(part, 'band', split_axis=0, concat_axis=0, tiled=True)  3.59 us
    all_to_all x1, starting transfers between devices, on_device(): lax.all_to_all(shares, 'rep', split_axis=0, concat_axis=0, tiled=True)  3.28 us
  transfers between devices with their start and end apart: 2, of which 1 were waited for; matrix products, arithmetic and copies ran while one was open for 0% of the time, Pallas kernels for 7%

profile of v1, /device:TPU:0, one launch (start us, length us, event | category | flops | bytes accessed | tf_op | source)
XLA Modules:
  0.0 95.1 jit_solution(6318290402380886949)
XLA Ops:
  0.6 0.0 copy-start
  0.6 0.0 copy-start.2
  0.7 1.3 %copy-done.2 = bf16[2,4,80,1,768]{4,2,3,1,0:T(8,128)(2,1)S(1)} copy-done((bf16[2,4,80,1,768]{4,2,3,1,0:T(8,128)(2,1)S(1)}, bf16[2,4,80,1,768]{4,2,3,1,0:T(8,128)(2,1)}, u32[]{:S(2)}) %copy-start.2) | copy-done | bytes 983064
  2.0 0.0 copy-start.12
  2.0 0.7 copy-done.12
  2.6 0.0 copy-start.14
  2.7 0.0 copy-start.15
  2.7 0.0 copy-start.8
  2.7 2.9 %send_blocks.1 = (bf16[8,48,640]{2,1,0:T(8,128)(2,1)S(1)}, bf16[8,48,640]{2,1,0:T(8,128)(2,1)}) custom-call(s32[8]{0:T(128)S(1)} %copy-done.12, bf16[640,768]{1,0:T(8,128)(2,1)S(1)} %bitcast.15), custom_call_target="tpu_custom_call" | custom-call | tf_op jit(solution)/shard_map/send_blocks/pallas_call | solution.py:69
  5.6 21.0 %all_to_all.15.refs_0_ = bf16[8,48,640]{2,1,0:T(8,128)(2,1)} all-to-all(bf16[8,48,640]{2,1,0:T(8,128)(2,1)S(1)} %get-tuple-element.18), channel_id=1, replica_groups=mesh['band'=8,'rep'=4] {'band'}, dimensions={0} | all-to-all | bytes 983040 | tf_op jit(solution)/shard_map/all_to_all | solution.py:345
  26.6 3.6 %all-to-all-start = ((bf16[8,48,640]{2,1,0:T(8,128)(2,1)}), bf16[8,48,640]{2,1,0:T(8,128)(2,1)S(1)}, u32[]{:S(2)}, u32[]{:S(2)}) async-start(bf16[8,48,640]{2,1,0:T(8,128)(2,1)} %get-tuple-element.14), calls=%async_computation | async-start | bytes 983040 | tf_op jit(solution)/shard_map/all_to_all | solution.py:345
  30.2 0.0 copy-start.1
  30.2 0.0 copy-start.3
  30.2 0.0 copy-done.14
  30.2 0.0 copy-done.15
  30.2 5.3 %all-gather = bf16[8,16,128]{2,1,0:T(8,128)(2,1)S(1)} all-gather(bf16[2,16,128]{2,1,0:T(8,128)(2,1)S(1)} %pad_maximum_fusion), channel_id=2, replica_groups=mesh['band'=8,'rep'=4] {'rep'}, dimensions={0}, use_global_device_ids=true | all-gather | bytes 40960 | tf_op jit(solution)/shard_map/all_gather | solution.py:354
  35.5 0.0 copy-done
  35.5 0.0 copy-done.8
  35.5 0.0 copy-start.9
  35.5 0.7 copy-done.9
  36.3 0.0 copy-start.13
  36.3 0.7 copy-done.13
  36.9 1.8 %prepare.1 = (bf16[2,384,512]{2,1,0:T(8,128)(2,1)S(1)}, bf16[4,32,512]{2,1,0:T(8,128)(2,1)S(1)}, bf16[16,80]{1,0:T(8,128)(2,1)S(1)}, bf16[384,384]{1,0:T(8,128)(2,1)S(1)}, bf16[384,384]{1,0:T(8,128)(2,1)S(1)}) custom-call(s32[5]{0:T(128)S(1)} %copy-done.13, bf16[3,16,512]{2,1,0:T(8,128)(2,1)S(1)} %copy-done.8, bf16[4,2,16,128]{3,2,1,0:T(8,128)(2,1)S(1)} %bitcast.16, ...), custom_call_target="tpu_custom_call" | custom-call | flops 257949696 | bytes 4194304 | tf_op jit(solution)/shard_map/prepare/pallas_call | solution.py:148
  38.8 0.0 copy-start.10
  38.8 0.6 copy-done.10
  39.4 0.0 copy-done.1
  39.4 0.0 copy-done.3
  39.4 4.6 %mix_half.2 = (bf16[2,8,96,512]{3,2,1,0:T(8,128)(2,1)}, f32[320,512]{1,0:T(8,128)S(1)}) custom-call(bf16[8,48,640]{2,1,0:T(8,128)(2,1)S(1)} %copy-done.3, bf16[2,384,512]{2,1,0:T(8,128)(2,1)S(1)} %get-tuple-element.15.refs_1_, bf16[384,384]{1,0:T(8,128)(2,1)S(1)} %get-tuple-element.16.refs_2_, bf16[384,384]{1,0:T(8,128)(2,1)S(1)} %get-tuple-element.17.refs_3_, ...), custom_call_target="tpu_custom_call" | custom-call | flops 1207959552 | bytes 8388608 | tf_op jit(solution)/shard_map/mix_half/pallas_call | solution.py:282
  44.0 0.0 copy-start.4
  44.0 0.7 copy-done.4
  44.7 0.0 copy-start.6
  44.7 0.7 copy-done.6
  45.4 0.0 all-to-all-done.refs_0_
  45.4 0.0 copy-start.5
  45.4 1.0 %copy-done.5 = bf16[384,384]{1,0:T(8,128)(2,1)S(1)} copy-done((bf16[384,384]{1,0:T(8,128)(2,1)S(1)}, bf16[384,384]{1,0:T(8,128)(2,1)}, u32[]{:S(2)}) %copy-start.5) | copy-done | bytes 294936
  46.3 0.0 copy-start.7
  46.3 1.0 %copy-done.7 = bf16[384,384]{1,0:T(8,128)(2,1)S(1)} copy-done((bf16[384,384]{1,0:T(8,128)(2,1)S(1)}, bf16[384,384]{1,0:T(8,128)(2,1)}, u32[]{:S(2)}) %copy-start.7) | copy-done | bytes 294936
  47.3 0.0 copy-start.11
  47.3 0.7 copy-done.11
  48.0 7.3 %mix_half.3 = (bf16[2,8,96,512]{3,2,1,0:T(8,128)(2,1)}, f32[4,16,256]{2,1,0:T(8,128)}) custom-call(bf16[8,48,640]{2,1,0:T(8,128)(2,1)S(1)} %all-to-all-done.refs_0_, bf16[2,384,512]{2,1,0:T(8,128)(2,1)S(1)} %get-tuple-element.15.refs_1_, bf16[384,384]{1,0:T(8,128)(2,1)S(1)} %copy-done.5, ...), custom_call_target="tpu_custom_call", output_to_operand_aliasing={{0}: (5, {})} | custom-call | flops 1207959552 | bytes 8388608 | tf_op jit(solution)/shard_map/mix_half/pallas_call | solution.py:282
  55.3 3.3 %all-to-all-start.2 = ((f32[4,16,256]{2,1,0:T(8,128)}), f32[4,16,256]{2,1,0:T(8,128)S(1)}, u32[]{:S(2)}, u32[]{:S(2)}) async-start(f32[4,16,256]{2,1,0:T(8,128)} %get-tuple-element.24), calls=%async_computation.2 | async-start | bytes 131072 | tf_op jit(solution)/shard_map/all_to_all | solution.py:380
  58.6 4.1 %all-to-all-done.2 = f32[4,16,256]{2,1,0:T(8,128)S(1)} async-done(((f32[4,16,256]{2,1,0:T(8,128)}), f32[4,16,256]{2,1,0:T(8,128)S(1)}, u32[]{:S(2)}, u32[]{:S(2)}) %all-to-all-start.2) | async-done | bytes 65568 | tf_op jit(solution)/shard_map/all_to_all | solution.py:380
  62.7 31.1 %all-gather.1 = f32[128,256]{1,0:T(8,128)S(1)} all-gather(f32[16,256]{1,0:T(8,128)S(1)} %reduce_sum.18), channel_id=3, replica_groups=mesh['band'=8,'rep'=4] {'band'}, dimensions={0}, use_global_device_ids=true | all-gather | bytes 147456 | tf_op jit(solution)/shard_map/all_gather | solution.py:381
  93.8 0.6 slice.4
  94.4 0.7 dynamic-slice_bitcast_fusion
  (4 shorter events, 0.0 us)
Async XLA Ops:
  0.6 34.9 %copy-start = (bf16[4,512,512]{2,1,0:T(8,128)(2,1)S(1)}, bf16[4,512,512]{2,1,0:T(8,128)(2,1)}, u32[]{:S(2)}) copy-start(bf16[4,512,512]{2,1,0:T(8,128)(2,1)} %refs_9_.1) | copy-start | bytes 6291460
  0.6 1.4 %copy-start.2 = (bf16[2,4,80,1,768]{4,2,3,1,0:T(8,128)(2,1)S(1)}, bf16[2,4,80,1,768]{4,2,3,1,0:T(8,128)(2,1)}, u32[]{:S(2)}) copy-start(bf16[2,4,80,1,768]{4,2,3,1,0:T(8,128)(2,1)} %param.9) | copy-start | bytes 2949124
  2.0 0.7 copy-start.12
  2.6 27.5 %copy-start.14 = (bf16[20,16]{0,1:T(8,128)(2,1)S(1)}, bf16[20,16]{0,1:T(8,128)(2,1)}, u32[]{:S(2)}) copy-start(bf16[20,16]{0,1:T(8,128)(2,1)} %param.12) | copy-start | bytes 1924
  2.7 27.5 %copy-start.15 = (bf16[16,128]{1,0:T(8,128)(2,1)S(1)}, bf16[16,128]{1,0:T(8,128)(2,1)}, u32[]{:S(2)}) copy-start(bf16[16,128]{1,0:T(8,128)(2,1)} %param.13) | copy-start | bytes 12292
  2.7 32.9 %copy-start.8 = (bf16[3,16,512]{2,1,0:T(8,128)(2,1)S(1)}, bf16[3,16,512]{2,1,0:T(8,128)(2,1)}, u32[]{:S(2)}) copy-start(bf16[3,16,512]{2,1,0:T(8,128)(2,1)} %frozen_ref.1) | copy-start | bytes 147460
  26.6 18.8 %all-to-all-start = ((bf16[8,48,640]{2,1,0:T(8,128)(2,1)}), bf16[8,48,640]{2,1,0:T(8,128)(2,1)S(1)}, u32[]{:S(2)}, u32[]{:S(2)}) async-start(bf16[8,48,640]{2,1,0:T(8,128)(2,1)} %get-tuple-element.14), calls=%async_computation | async-start | bytes 983040 | tf_op jit(solution)/shard_map/all_to_all | solution.py:345
  30.2 9.2 %copy-start.1 = (bf16[2,1,8,96,512]{4,3,2,1,0:T(8,128)(2,1)S(1)}, bf16[2,1,8,96,512]{4,3,2,1,0:T(8,128)(2,1)}, u32[]{:S(2)}) copy-start(bf16[2,1,8,96,512]{4,3,2,1,0:T(8,128)(2,1)} %param.17) | copy-start | bytes 4718596
  30.2 9.2 %copy-start.3 = (bf16[8,48,640]{2,1,0:T(8,128)(2,1)S(1)}, bf16[8,48,640]{2,1,0:T(8,128)(2,1)}, u32[]{:S(2)}) copy-start(bf16[8,48,640]{2,1,0:T(8,128)(2,1)} %all_to_all.15.refs_0_) | copy-start | bytes 1474564
  35.5 0.7 copy-start.9
  36.3 0.7 copy-start.13
  38.8 0.6 copy-start.10
  44.0 0.7 copy-start.4
  44.7 0.7 copy-start.6
  45.4 1.0 %copy-start.5 = (bf16[384,384]{1,0:T(8,128)(2,1)S(1)}, bf16[384,384]{1,0:T(8,128)(2,1)}, u32[]{:S(2)}) copy-start(bf16[384,384]{1,0:T(8,128)(2,1)} %copy-done.4) | copy-start | bytes 884740
  46.3 1.0 %copy-start.7 = (bf16[384,384]{1,0:T(8,128)(2,1)S(1)}, bf16[384,384]{1,0:T(8,128)(2,1)}, u32[]{:S(2)}) copy-start(bf16[384,384]{1,0:T(8,128)(2,1)} %copy-done.6) | copy-start | bytes 884740
  47.3 0.7 copy-start.11
  55.3 7.4 %all-to-all-start.2 = ((f32[4,16,256]{2,1,0:T(8,128)}), f32[4,16,256]{2,1,0:T(8,128)S(1)}, u32[]{:S(2)}, u32[]{:S(2)}) async-start(f32[4,16,256]{2,1,0:T(8,128)} %get-tuple-element.24), calls=%async_computation.2 | async-start | bytes 131072 | tf_op jit(solution)/shard_map/all_to_all | solution.py:380

commit v2 on v1

--- a/solution.py
+++ b/solution.py
@@ -11,7 +11,8 @@
 WLON = 12
 LANE = 128
 SUB = 16
-VMEM_LIMIT = 50 * 1024 * 1024
+VMEM_LIMIT = 24 * 1024 * 1024
+MAX_PERMUTES = 8
 BF16 = jnp.bfloat16
 F32 = jnp.float32
 
@@ -46,38 +47,49 @@
     return pltpu.CompilerParams(vmem_limit_bytes=VMEM_LIMIT, **extra)
 
 
-def send_kernel(band_count, half_width, owner_ref, x_ref, *out_refs):
-    halves = len(out_refs)
+def send_kernel(band_count, halves, half_width, owner_ref, x_ref, *refs):
+    out_refs, turned_ref = refs[:-1], refs[-1]
+    me = lax.axis_index("band")
     for tile in range(x_ref.shape[1] // LANE):
-        rows = x_ref[:, tile * LANE : (tile + 1) * LANE].T
-        start = tile * LANE
-        while start < (tile + 1) * LANE:
-            piece = start // half_width
-            end = min((piece + 1) * half_width, (tile + 1) * LANE)
-            slot = owner_ref[piece // halves]
-            offset = start - piece * half_width
-            out_refs[piece % halves][slot, offset : offset + end - start, :] = rows[
-                start - tile * LANE : end - tile * LANE, :
-            ]
-            start = end
+        at = slice(tile * LANE, (tile + 1) * LANE)
+        turned_ref[at, :] = x_ref[:, at].T
+    for k in range(band_count):
+        target = jnp.bitwise_xor(me, k)
+        block = 0
+        for j in range(1, band_count):
+            block = jnp.where(owner_ref[j] == target, j, block)
+        for half in range(halves):
+            start = pl.multiple_of((block * halves + half) * half_width, SUB)
+            out_refs[half * band_count + k][...] = turned_ref[pl.ds(start, half_width), :]
 
 
 def send_blocks(pixels, owner, band_count, halves, half_width):
     features, columns = pixels.shape
-    block = jax.ShapeDtypeStruct((band_count, half_width, features), BF16)
-    out_spec = pl.BlockSpec((band_count, half_width, LANE), lambda f, owner: (0, 0, f))
-    return pl.pallas_call(
-        functools.partial(send_kernel, band_count, half_width),
-        out_shape=[block] * halves,
+    count = band_count * halves
+    block = jax.ShapeDtypeStruct((half_width, features), BF16)
+    out_spec = pl.BlockSpec((half_width, LANE), lambda f, owner: (0, f))
+    pieces = pl.pallas_call(
+        functools.partial(send_kernel, band_count, halves, half_width),
+        out_shape=[block] * count,
         grid_spec=pltpu.PrefetchScalarGridSpec(
             num_scalar_prefetch=1,
             grid=(features // LANE,),
             in_specs=[pl.BlockSpec((LANE, columns), lambda f, owner: (f, 0))],
-            out_specs=[out_spec] * halves,
+            out_specs=[out_spec] * count,
+            scratch_shapes=[pltpu.VMEM((columns, LANE), BF16)],
         ),
         compiler_params=params(),
         name="send_blocks",
     )(owner, pixels)
+    return [pieces[half * band_count : (half + 1) * band_count] for half in range(halves)]
+
+
+def exchange(pieces, band_count):
+    arrived = [pieces[0]]
+    for k in range(1, band_count):
+        pairs = [(source, source ^ k) for source in range(band_count)]
+        arrived.append(lax.ppermute(pieces[k], "band", pairs))
+    return arrived
 
 
 def expand_table(table, rows, half_width_padded, half_width, transpose):
@@ -168,11 +180,13 @@
     return cdf, pdf
 
 
-def mix_kernel(chained, last, dims, *refs):
+def mix_kernel(chained, last, pieces, dims, *refs):
     levels, channels, rank, reps = dims
     refs = list(refs)
-    arrived_ref, merged_ref, mix_ref, mix_t_ref, grad_ref = refs[:5]
-    del refs[:5]
+    piece_refs = refs[:pieces]
+    del refs[:pieces]
+    merged_ref, mix_ref, mix_t_ref, grad_ref = refs[:4]
+    del refs[:4]
     before_ref = None
     if chained:
         before_ref = refs[1]
@@ -180,7 +194,8 @@
     if last:
         up_ref, down_ref, level_ref = refs[:3]
         del refs[:3]
-    mixed_ref, out_ref, total_ref, tokens_ref, pre_ref, grad_pre_ref = refs
+    mixed_ref, out_ref, total_ref, tokens_ref, pre_ref, grad_pre_ref = refs[:6]
+    arrived_ref = piece_refs[0] if pieces == 1 else refs[6]
 
     window_row, sample = pl.program_id(0), pl.program_id(1)
     samples = merged_ref.shape[0]
@@ -188,6 +203,14 @@
     width = arrived_ref.shape[1]
     rows = WLAT * width
     depth = levels * channels
+    if pieces > 1:
+
+        @pl.when(sample == 0)
+        def _():
+            me = lax.axis_index("band")
+            for k in range(pieces):
+                arrived_ref[jnp.bitwise_xor(me, k)] = piece_refs[k][...]
+
     first_lane = pl.multiple_of((sample * depth) // LANE * LANE, LANE)
     pixels = arrived_ref[:, :, pl.ds(first_lane, reach)].reshape(rows, reach)
     tokens_ref[...] = dot_nn(pixels, merged_ref[sample]).astype(BF16)
@@ -244,13 +267,13 @@
         col_share = feature_dim // reps
         out_ref[...] = jnp.zeros_like(out_ref)
         for r in range(reps):
-            out_ref[r, :, :col_share] = second[:, r * col_share : (r + 1) * col_share]
-            out_ref[r, :, col_share : col_share + channels] = first
+            out_ref[r, :, :col_share] = second[:, r * col_share : (r + 1) * col_share].astype(BF16)
+            out_ref[r, :, col_share : col_share + channels] = first.astype(BF16)
 
 
 def mix_half(half, last, arrived, merged, mix, mix_t, grad, chain, tail, reps):
-    lat_rows, width, lanes = arrived.shape
-    samples, _, block_width, feature_dim = grad.shape
+    samples, lat_rows, _, feature_dim = grad.shape
+    width, lanes = arrived[0].shape[-2:]
     reach = merged.shape[1]
     rows = WLAT * width
     levels, two_rank, _ = tail[0].shape
@@ -259,14 +282,24 @@
     depth = levels * channels
     whole = lambda shape: pl.BlockSpec(shape, lambda w, s: (0,) * len(shape))
     block = pl.BlockSpec((1, WLAT, width, feature_dim), lambda w, s: (s, w, half, 0))
-    in_specs = [
-        pl.BlockSpec((WLAT, width, lanes), lambda w, s: (w, 0, 0)),
+    scratch = [
+        pltpu.VMEM((samples, reach, feature_dim), F32),
+        pltpu.VMEM((rows, feature_dim), BF16),
+        pltpu.VMEM((rows, feature_dim), F32),
+        pltpu.VMEM((rows, feature_dim), BF16),
+    ]
+    if len(arrived) > 1:
+        arrived_specs = [whole(piece.shape) for piece in arrived]
+        scratch.append(pltpu.VMEM((WLAT, width, lanes), BF16))
+    else:
+        arrived_specs = [pl.BlockSpec((WLAT, width, lanes), lambda w, s: (w, 0, 0))]
+    in_specs = arrived_specs + [
         whole(merged.shape),
         whole(mix.shape),
         whole(mix_t.shape),
         block,
     ]
-    operands = [arrived, merged, mix, mix_t, grad]
+    operands = list(arrived) + [merged, mix, mix_t, grad]
     aliases = {}
     if chain is not None:
         aliases = {len(operands): 0}
@@ -275,25 +308,20 @@
     if last:
         in_specs += [whole(array.shape) for array in tail]
         operands += list(tail)
-        out_tile = (reps, rank, feature_dim // reps + round_up(channels, LANE))
+        out_tile, out_type = (reps, rank, feature_dim // reps + round_up(channels, LANE)), BF16
     else:
-        out_tile = (depth, feature_dim)
+        out_tile, out_type = (depth, feature_dim), F32
     flops = 2 * samples * lat_rows * width * feature_dim * (2 * reach + 2 * rows)
     return pl.pallas_call(
-        functools.partial(mix_kernel, chain is not None, last, (levels, channels, rank, reps)),
+        functools.partial(mix_kernel, chain is not None, last, len(arrived), (levels, channels, rank, reps)),
         out_shape=[
             jax.ShapeDtypeStruct(grad.shape, BF16),
-            jax.ShapeDtypeStruct(out_tile, F32),
+            jax.ShapeDtypeStruct(out_tile, out_type),
         ],
         grid=(lat_rows // WLAT, samples),
         in_specs=in_specs,
         out_specs=[block, whole(out_tile)],
-        scratch_shapes=[
-            pltpu.VMEM((samples, reach, feature_dim), F32),
-            pltpu.VMEM((rows, feature_dim), BF16),
-            pltpu.VMEM((rows, feature_dim), F32),
-            pltpu.VMEM((rows, feature_dim), BF16),
-        ],
+        scratch_shapes=scratch,
         input_output_aliases=aliases,
         compiler_params=params(dimension_semantics=("arbitrary", "arbitrary")),
         cost_estimate=pl.CostEstimate(
@@ -327,8 +355,10 @@
     features = samples * levels * channels
 
     pixels = patches.reshape(features, col_count)
-    if half_padded == half_width and features % LANE == 0 and col_count % LANE == 0:
+    direct = band_count <= MAX_PERMUTES and lat_rows == WLAT and half_padded == half_width
+    if direct and features % LANE == 0 and col_count % LANE == 0:
         outgoing = send_blocks(pixels, column_block_owner, band_count, halves, half_width)
+        arrived = [exchange(pieces, band_count) for pieces in outgoing]
     else:
         block_ids = jnp.arange(band_count, dtype=jnp.int32)
         inverse = jnp.sum(
@@ -342,7 +372,9 @@
             )
             for h in range(halves)
         ]
-    arrived = [lax.all_to_all(part, "band", split_axis=0, concat_axis=0, tiled=True) for part in outgoing]
+        arrived = [
+            [lax.all_to_all(part, "band", split_axis=0, concat_axis=0, tiled=True)] for part in outgoing
+        ]
 
     pack_width = round_up(max(row_share, col_share), LANE)
     pack = jnp.stack(
@@ -377,8 +409,9 @@
     if half_padded != half_width:
         mixed = mixed[:, :, :block_width]
 
-    mine = jnp.sum(lax.all_to_all(shares, "rep", split_axis=0, concat_axis=0, tiled=True), axis=0)
-    summed = jnp.sum(lax.all_gather(mine, "band", axis=0, tiled=False), axis=0)
+    shares = jnp.broadcast_to(shares[None], (band_count,) + shares.shape).reshape((-1,) + shares.shape[1:])
+    parts = lax.all_to_all(shares, ("band", "rep"), split_axis=0, concat_axis=0, tiled=True)
+    summed = jnp.sum(parts.astype(F32), axis=0)
     first_t = lax.dynamic_slice_in_dim(summed, col_share + lax.axis_index("rep") * row_share, row_share, 1)
     return (
         mixed.reshape(mixed_token_gradient.shape),

time: 95.7 us -> 71.3 us (0.75)
  blocking collectives: 57.4 us -> 5.18 us
  starting transfers between devices: 6.87 us -> 28.1 us
  waiting for transfers between devices: 4.08 us -> 13.9 us
  Pallas kernels: 16.6 us -> 13.9 us
  local copies, waits for them, and re-layouts: 9.3 us -> 8.32 us
    all_gather x1 -> x0, blocking collectives: 31.1 us -> none  [on_device(): summed = jnp.sum(lax.all_gather(mine, 'band', axis=0, tiled=False), axis=0)]
    ppermute x0 -> x14, starting transfers between devices: none -> 23.2 us  [exchange(): arrived.append(lax.ppermute(pieces[k], 'band', pairs))]
    all_to_all x1 -> x0, blocking collectives: 21 us -> none  [on_device(): lax.all_to_all(part, 'band', split_axis=0, concat_axis=0, tiled=True)]
    all_to_all x2 -> x1, waiting for transfers between devices: 4.08 us -> 10.6 us  [on_device(): lax.all_to_all(shares, ('band', 'rep'), split_axis=0, concat_axis=0, tile...]
    ppermute x0 -> x14, waiting for transfers between devices: none -> 3.26 us  [exchange(): arrived.append(lax.ppermute(pieces[k], 'band', pairs))]
    pallas_call x3, Pallas kernels: 14.8 us -> 12.1 us  [the longest x2 10.4 us: mix_half(): pl.pallas_call(functools.partial(mix_kernel, chain is not None, last, len...]
    unnamed x32 -> x16, local copies, waits for them, and re-layouts: 8.03 us -> 5.64 us
    all_to_all x2 -> x1, starting transfers between devices: 6.87 us -> 4.93 us  [on_device(): lax.all_to_all(shares, ('band', 'rep'), split_axis=0, concat_axis=0, tile...]
  transfers between devices with their start and end apart: 2 -> 15, of which waited for: 1 -> 4; matrix products, arithmetic and copies ran while one was open for 0% -> 2% of each run, Pallas kernels for 7% -> 9%
where the time goes in v2:
time: 71.3 us; the launch traced here: 70.9 us
  starting transfers between devices  28.1 us (39%)
  Pallas kernels  13.9 us (19%)
  waiting for transfers between devices  13.9 us (19%)
  local copies, waits for them, and re-layouts  8.32 us (12%)
  blocking collectives  5.18 us (7%)
  other arithmetic  0.74 us (1%)
  between operations  0.72 us (1%)
    ppermute x14, starting transfers between devices, exchange(): arrived.append(lax.ppermute(pieces[k], 'band', pairs))  23.2 us
    all_to_all x1, waiting for transfers between devices, on_device(): lax.all_to_all(shares, ('band', 'rep'), split_axis=0, concat_axis=0, tile...  10.6 us
    pallas_call x2, Pallas kernels, mix_half(): pl.pallas_call(functools.partial(mix_kernel, chain is not None, last, len...  10.4 us
    unnamed x16, local copies, waits for them, and re-layouts  5.64 us
    all_gather x1, blocking collectives, on_device(): factors = lax.all_gather(pack, 'rep', axis=0, tiled=False)  5.18 us
    all_to_all x1, starting transfers between devices, on_device(): lax.all_to_all(shares, ('band', 'rep'), split_axis=0, concat_axis=0, tile...  4.93 us
    ppermute x14, waiting for transfers between devices, exchange(): arrived.append(lax.ppermute(pieces[k], 'band', pairs))  3.26 us
    pallas_call x1, Pallas kernels, prepare(): pl.pallas_call(functools.partial(prep_kernel, row_share, half_width, half...  1.82 us
  transfers between devices with their start and end apart: 15, of which 4 were waited for; matrix products, arithmetic and copies ran while one was open for 2% of the time, Pallas kernels for 9%

profile of v2, /device:TPU:0, one launch (start us, length us, event | category | flops | bytes accessed | tf_op | source)
XLA Modules:
  0.0 70.9 jit_solution(16612103547175259241)
XLA Ops:
  0.6 0.0 copy-start.3
  0.6 1.2 %copy-done.3 = bf16[2,4,80,1,768]{4,2,3,1,0:T(8,128)(2,1)S(1)} copy-done((bf16[2,4,80,1,768]{4,2,3,1,0:T(8,128)(2,1)S(1)}, bf16[2,4,80,1,768]{4,2,3,1,0:T(8,128)(2,1)}, u32[]{:S(2)}) %copy-start.3) | copy-done | bytes 983064
  1.8 0.0 copy-start.6
  1.8 0.7 copy-done.6
  2.5 1.8 %send_blocks.1 = (bf16[48,640]{1,0:T(8,128)(2,1)S(1)}, bf16[48,640]{1,0:T(8,128)(2,1)S(1)}, bf16[48,640]{1,0:T(8,128)(2,1)S(1)}, bf16[48,640]{1,0:T(8,128)(2,1)S...) custom-call(s32[8]{0:T(128)S(1)} %copy-done.6, ...), custom_call_target="tpu_custom_call" | custom-call | tf_op jit(solution)/shard_map/send_blocks/pallas_call | solution.py:71
  4.2 4.1 %collective-permute-start.10 = (bf16[48,640]{1,0:T(8,128)(2,1)S(1)}, bf16[48,640]{1,0:T(8,128)(2,1)S(1)}, u32[]{:S(2)}, u32[]{:S(2)}) collective-permute-start(bf16[48,640]{1,0:T(8,128)(2,1)S(1)} %get-tuple-element.43), channel_id=1, source_target_pairs={{0,16},{4,20},{8,24},{12,28},{16,0},{20,4},{24,8},{28,12},{1,17},{... | collective-permute-start | bytes 184328 | tf_op jit(solution)/shard_map/ppermute | solution.py:91
  8.4 1.2 %collective-permute-start.11 = (bf16[48,640]{1,0:T(8,128)(2,1)S(1)}, bf16[48,640]{1,0:T(8,128)(2,1)S(1)}, u32[]{:S(2)}, u32[]{:S(2)}) collective-permute-start(bf16[48,640]{1,0:T(8,128)(2,1)S(1)} %get-tuple-element.44), channel_id=1, source_target_pairs={{0,20},{4,16},{8,28},{12,24},{16,4},{20,0},{24,12},{28,8},{1,21},{... | collective-permute-start | bytes 184328 | tf_op jit(solution)/shard_map/ppermute | solution.py:91
  9.6 3.6 %collective-permute-start.12 = (bf16[48,640]{1,0:T(8,128)(2,1)S(1)}, bf16[48,640]{1,0:T(8,128)(2,1)S(1)}, u32[]{:S(2)}, u32[]{:S(2)}) collective-permute-start(bf16[48,640]{1,0:T(8,128)(2,1)S(1)} %get-tuple-element.45), channel_id=1, source_target_pairs={{0,24},{4,28},{8,16},{12,20},{16,8},{20,12},{24,0},{28,4},{1,25},{... | collective-permute-start | bytes 184328 | tf_op jit(solution)/shard_map/ppermute | solution.py:91
  13.2 0.0 collective-permute-start.13
  13.2 1.7 %collective-permute-start.7 = (bf16[48,640]{1,0:T(8,128)(2,1)S(1)}, bf16[48,640]{1,0:T(8,128)(2,1)S(1)}, u32[]{:S(2)}, u32[]{:S(2)}) collective-permute-start(bf16[48,640]{1,0:T(8,128)(2,1)S(1)} %get-tuple-element.40), channel_id=1, source_target_pairs={{0,4},{4,0},{8,12},{12,8},{16,20},{20,16},{24,28},{28,24},{1,5},{5... | collective-permute-start | bytes 184328 | tf_op jit(solution)/shard_map/ppermute | solution.py:91
  14.9 0.7 pad_bitcast_fusion
  15.6 0.0 collective-permute-done.10.refs_4_
  15.6 0.0 collective-permute-start.8
  15.6 1.8 %collective-permute-done.11.refs_5_ = bf16[48,640]{1,0:T(8,128)(2,1)S(1)} collective-permute-done((bf16[48,640]{1,0:T(8,128)(2,1)S(1)}, bf16[48,640]{1,0:T(8,128)(2,1)S(1)}, u32[]{:S(2)}, u32[]{:S(2)}) %collective-permute-start.11) | collective-permute-done | bytes 61472 | tf_op jit(solution)/shard_map/ppermute | solution.py:91
  17.4 1.2 %collective-permute-start.9 = (bf16[48,640]{1,0:T(8,128)(2,1)S(1)}, bf16[48,640]{1,0:T(8,128)(2,1)S(1)}, u32[]{:S(2)}, u32[]{:S(2)}) collective-permute-start(bf16[48,640]{1,0:T(8,128)(2,1)S(1)} %get-tuple-element.42), channel_id=1, source_target_pairs={{0,12},{4,8},{8,4},{12,0},{16,28},{20,24},{24,20},{28,16},{1,13},{... | collective-permute-start | bytes 184328 | tf_op jit(solution)/shard_map/ppermute | solution.py:91
  18.6 0.0 collective-permute-done.12.refs_6_
  18.6 0.9 %collective-permute-start = (bf16[48,640]{1,0:T(8,128)(2,1)S(1)}, bf16[48,640]{1,0:T(8,128)(2,1)S(1)}, u32[]{:S(2)}, u32[]{:S(2)}) collective-permute-start(bf16[48,640]{1,0:T(8,128)(2,1)S(1)} %get-tuple-element.29), channel_id=1, source_target_pairs={{0,4},{4,0},{8,12},{12,8},{16,20},{20,16},{24,28},{28,24},{1,5},{5... | collective-permute-start | bytes 184328 | tf_op jit(solution)/shard_map/ppermute | solution.py:91
  19.6 0.7 collective-permute-done.13.refs_7_
  20.3 1.2 %collective-permute-start.1 = (bf16[48,640]{1,0:T(8,128)(2,1)S(1)}, bf16[48,640]{1,0:T(8,128)(2,1)S(1)}, u32[]{:S(2)}, u32[]{:S(2)}) collective-permute-start(bf16[48,640]{1,0:T(8,128)(2,1)S(1)} %get-tuple-element.30), channel_id=1, source_target_pairs={{0,8},{4,12},{8,0},{12,4},{16,24},{20,28},{24,16},{28,20},{1,9},{5... | collective-permute-start | bytes 184328 | tf_op jit(solution)/shard_map/ppermute | solution.py:91
  21.5 0.7 pad_maximum_fusion
  22.2 5.2 %all-gather = bf16[8,16,128]{2,1,0:T(8,128)(2,1)S(1)} all-gather(bf16[2,16,128]{2,1,0:T(8,128)(2,1)S(1)} %pad_maximum_fusion), channel_id=2, replica_groups=mesh['band'=8,'rep'=4] {'rep'}, dimensions={0}, use_global_device_ids=true | all-gather | bytes 40960 | tf_op jit(solution)/shard_map/all_gather | solution.py:386
  27.3 0.0 copy-start
  27.3 1.6 %copy-done = bf16[4,512,512]{2,1,0:T(8,128)(2,1)S(1)} copy-done((bf16[4,512,512]{2,1,0:T(8,128)(2,1)S(1)}, bf16[4,512,512]{2,1,0:T(8,128)(2,1)}, u32[]{:S(2)}) %copy-start) | copy-done | bytes 2097176
  28.9 0.0 copy-start.4
  28.9 0.8 %copy-done.4 = bf16[3,16,512]{2,1,0:T(8,128)(2,1)S(1)} copy-done((bf16[3,16,512]{2,1,0:T(8,128)(2,1)S(1)}, bf16[3,16,512]{2,1,0:T(8,128)(2,1)}, u32[]{:S(2)}) %copy-start.4) | copy-done | bytes 49176
  29.7 0.0 copy-start.5
  29.7 0.7 %copy-done.5 = bf16[96,96]{1,0:T(8,128)(2,1)S(1)} copy-done((bf16[96,96]{1,0:T(8,128)(2,1)S(1)}, bf16[96,96]{1,0:T(8,128)(2,1)}, u32[]{:S(2)}) %copy-start.5) | copy-done | bytes 18456
  30.5 0.0 copy-start.7
  30.5 0.7 copy-done.7
  31.1 0.0 copy-start.2
  31.1 1.8 %prepare.1 = (bf16[2,384,512]{2,1,0:T(8,128)(2,1)S(1)}, bf16[4,32,512]{2,1,0:T(8,128)(2,1)S(1)}, bf16[16,80]{1,0:T(8,128)(2,1)S(1)}, bf16[384,384]{1,0:T(8,128)(2,1)S(1)}, bf16[384,384]{1,0:T(8,128)(2,1)S(1)}) custom-call(s32[5]{0:T(128)S(1)} %copy-done.7, bf16[3,16,512]{2,1,0:T(8,128)(2,1)S(1)} %copy-done.4, bf16[4,2,16,128]{3,2,1,0:T(8,128)(2,1)S(1)} %bitcast.16, ...), custom_call_target="tpu_custom_call" | custom-call | flops 257949696 | bytes 4194304 | tf_op jit(solution)/shard_map/prepare/pallas_call | solution.py:160
  32.9 0.0 collective-permute-done.7.refs_1_
  33.0 1.4 %collective-permute-start.2 = (bf16[48,640]{1,0:T(8,128)(2,1)S(1)}, bf16[48,640]{1,0:T(8,128)(2,1)S(1)}, u32[]{:S(2)}, u32[]{:S(2)}) collective-permute-start(bf16[48,640]{1,0:T(8,128)(2,1)S(1)} %get-tuple-element.31), channel_id=1, source_target_pairs={{0,12},{4,8},{8,4},{12,0},{16,28},{20,24},{24,20},{28,16},{1,13},{... | collective-permute-start | bytes 184328 | tf_op jit(solution)/shard_map/ppermute | solution.py:91
  34.4 0.0 collective-permute-done.8.refs_2_
  34.4 2.9 %collective-permute-start.3 = (bf16[48,640]{1,0:T(8,128)(2,1)S(1)}, bf16[48,640]{1,0:T(8,128)(2,1)S(1)}, u32[]{:S(2)}, u32[]{:S(2)}) collective-permute-start(bf16[48,640]{1,0:T(8,128)(2,1)S(1)} %get-tuple-element.32), channel_id=1, source_target_pairs={{0,16},{4,20},{8,24},{12,28},{16,0},{20,4},{24,8},{28,12},{1,17},{... | collective-permute-start | bytes 184328 | tf_op jit(solution)/shard_map/ppermute | solution.py:91
  37.3 0.0 collective-permute-done.9.refs_3_
  37.3 0.9 %collective-permute-start.4 = (bf16[48,640]{1,0:T(8,128)(2,1)S(1)}, bf16[48,640]{1,0:T(8,128)(2,1)S(1)}, u32[]{:S(2)}, u32[]{:S(2)}) collective-permute-start(bf16[48,640]{1,0:T(8,128)(2,1)S(1)} %get-tuple-element.33), channel_id=1, source_target_pairs={{0,20},{4,16},{8,28},{12,24},{16,4},{20,0},{24,12},{28,8},{1,21},{... | collective-permute-start | bytes 184328 | tf_op jit(solution)/shard_map/ppermute | solution.py:91
  38.3 0.0 collective-permute-done.refs_1_
  38.3 2.3 %collective-permute-start.5 = (bf16[48,640]{1,0:T(8,128)(2,1)S(1)}, bf16[48,640]{1,0:T(8,128)(2,1)S(1)}, u32[]{:S(2)}, u32[]{:S(2)}) collective-permute-start(bf16[48,640]{1,0:T(8,128)(2,1)S(1)} %get-tuple-element.34), channel_id=1, source_target_pairs={{0,24},{4,28},{8,16},{12,20},{16,8},{20,12},{24,0},{28,4},{1,25},{... | collective-permute-start | bytes 184328 | tf_op jit(solution)/shard_map/ppermute | solution.py:91
  40.6 0.0 collective-permute-done.1.refs_2_
  40.6 1.6 %collective-permute-start.6 = (bf16[48,640]{1,0:T(8,128)(2,1)S(1)}, bf16[48,640]{1,0:T(8,128)(2,1)S(1)}, u32[]{:S(2)}, u32[]{:S(2)}) collective-permute-start(bf16[48,640]{1,0:T(8,128)(2,1)S(1)} %get-tuple-element.35), channel_id=1, source_target_pairs={{0,28},{4,24},{8,20},{12,16},{16,12},{20,8},{24,4},{28,0},{1,29},{... | collective-permute-start | bytes 184328 | tf_op jit(solution)/shard_map/ppermute | solution.py:91
  42.1 0.0 copy-done.2
  42.1 0.0 copy-start.1
  42.1 4.7 %mix_half.2 = (bf16[2,8,96,512]{3,2,1,0:T(8,128)(2,1)}, f32[320,512]{1,0:T(8,128)S(1)}) custom-call(bf16[48,640]{1,0:T(8,128)(2,1)S(1)} %get-tuple-element.39.refs_0_, bf16[48,640]{1,0:T(8,128)(2,1)S(1)} %collective-permute-done.7.refs_1_, bf16[48,640]{1,0:T(8,128)(2,1)S(1)} %collective-permute-done.8.refs_2_, ...), custom_call_target="tpu_custom_call" | custom-call | flops 1207959552 | bytes 8388608 | tf_op jit(solution)/shard_map/mix_half/pallas_call | solution.py:315
  46.8 0.0 collective-permute-done.2.refs_3_
  46.8 0.0 collective-permute-done.3.refs_4_
  46.8 0.0 collective-permute-done.4.refs_5_
  46.8 0.0 collective-permute-done.5.refs_6_
  46.8 0.7 %collective-permute-done.6.refs_7_ = bf16[48,640]{1,0:T(8,128)(2,1)S(1)} collective-permute-done((bf16[48,640]{1,0:T(8,128)(2,1)S(1)}, bf16[48,640]{1,0:T(8,128)(2,1)S(1)}, u32[]{:S(2)}, u32[]{:S(2)}) %collective-permute-start.6) | collective-permute-done | bytes 61472 | tf_op jit(solution)/shard_map/ppermute | solution.py:91
  47.6 0.0 copy-done.1
  47.6 5.7 %mix_half.3 = (bf16[2,8,96,512]{3,2,1,0:T(8,128)(2,1)}, bf16[4,16,256]{2,1,0:T(8,128)(2,1)S(1)}) custom-call(bf16[48,640]{1,0:T(8,128)(2,1)S(1)} %get-tuple-element.28.refs_0_, bf16[48,640]{1,0:T(8,128)(2,1)S(1)} %collective-permute-done.refs_1_, bf16[48,640]{1,0:T(8,128)(2,1)S(1)} %collective-permute-done.1.refs_2_, ...), custom_call_target="tpu_custom_call", output_to_operand_aliasing={{0}: (12, {})} | custom-call | flops 1207959552 | bytes 8388608 | tf_op jit(solution)/shard_map/mix_half/pallas_call | solution.py:315
  53.3 0.7 %broadcast_in_dim.2 = bf16[8,4,16,256]{3,2,1,0:T(8,128)(2,1)} broadcast(bf16[4,16,256]{2,1,0:T(8,128)(2,1)S(1)} %get-tuple-element.52), dimensions={1,2,3} | broadcast | bytes 294912 | tf_op jit(solution)/shard_map/broadcast_in_dim | solution.py:412
  54.0 4.9 %all-to-all-start = ((bf16[32,16,256]{2,1,0:T(8,128)(2,1)}), bf16[32,16,256]{2,1,0:T(8,128)(2,1)S(1)}, u32[]{:S(2)}, u32[]{:S(2)}) async-start(bf16[32,16,256]{2,1,0:T(8,128)(2,1)} %bitcast.8), calls=%async_computation | async-start | bytes 524288 | tf_op jit(solution)/shard_map/all_to_all | solution.py:413
  59.0 10.6 %all-to-all-done = bf16[32,16,256]{2,1,0:T(8,128)(2,1)S(1)} async-done(((bf16[32,16,256]{2,1,0:T(8,128)(2,1)}), bf16[32,16,256]{2,1,0:T(8,128)(2,1)S(1)}, u32[]{:S(2)}, u32[]{:S(2)}) %all-to-all-start) | async-done | bytes 262176 | tf_op jit(solution)/shard_map/all_to_all | solution.py:413
  69.6 0.6 slice.4
  70.2 0.7 dynamic-slice_bitcast_fusion
  (1 shorter events, 0.0 us)
Async XLA Ops:
  0.6 1.2 %copy-start.3 = (bf16[2,4,80,1,768]{4,2,3,1,0:T(8,128)(2,1)S(1)}, bf16[2,4,80,1,768]{4,2,3,1,0:T(8,128)(2,1)}, u32[]{:S(2)}) copy-start(bf16[2,4,80,1,768]{4,2,3,1,0:T(8,128)(2,1)} %param.9) | copy-start | bytes 2949124
  1.8 0.7 copy-start.6
  4.2 11.3 %collective-permute-start.10 = (bf16[48,640]{1,0:T(8,128)(2,1)S(1)}, bf16[48,640]{1,0:T(8,128)(2,1)S(1)}, u32[]{:S(2)}, u32[]{:S(2)}) collective-permute-start(bf16[48,640]{1,0:T(8,128)(2,1)S(1)} %get-tuple-element.43), channel_id=1, source_target_pairs={{0,16},{4,20},{8,24},{12,28},{16,0},{20,4},{24,8},{28,12},{1,17},{... | collective-permute-start | bytes 184328 | tf_op jit(solution)/shard_map/ppermute | solution.py:91
  8.4 9.0 %collective-permute-start.11 = (bf16[48,640]{1,0:T(8,128)(2,1)S(1)}, bf16[48,640]{1,0:T(8,128)(2,1)S(1)}, u32[]{:S(2)}, u32[]{:S(2)}) collective-permute-start(bf16[48,640]{1,0:T(8,128)(2,1)S(1)} %get-tuple-element.44), channel_id=1, source_target_pairs={{0,20},{4,16},{8,28},{12,24},{16,4},{20,0},{24,12},{28,8},{1,21},{... | collective-permute-start | bytes 184328 | tf_op jit(solution)/shard_map/ppermute | solution.py:91
  9.6 9.0 %collective-permute-start.12 = (bf16[48,640]{1,0:T(8,128)(2,1)S(1)}, bf16[48,640]{1,0:T(8,128)(2,1)S(1)}, u32[]{:S(2)}, u32[]{:S(2)}) collective-permute-start(bf16[48,640]{1,0:T(8,128)(2,1)S(1)} %get-tuple-element.45), channel_id=1, source_target_pairs={{0,24},{4,28},{8,16},{12,20},{16,8},{20,12},{24,0},{28,4},{1,25},{... | collective-permute-start | bytes 184328 | tf_op jit(solution)/shard_map/ppermute | solution.py:91
  13.2 7.0 %collective-permute-start.13 = (bf16[48,640]{1,0:T(8,128)(2,1)S(1)}, bf16[48,640]{1,0:T(8,128)(2,1)S(1)}, u32[]{:S(2)}, u32[]{:S(2)}) collective-permute-start(bf16[48,640]{1,0:T(8,128)(2,1)S(1)} %get-tuple-element.46), channel_id=1, source_target_pairs={{0,28},{4,24},{8,20},{12,16},{16,12},{20,8},{24,4},{28,0},{1,29},{... | collective-permute-start | bytes 184328 | tf_op jit(solution)/shard_map/ppermute | solution.py:91
  13.2 19.7 %collective-permute-start.7 = (bf16[48,640]{1,0:T(8,128)(2,1)S(1)}, bf16[48,640]{1,0:T(8,128)(2,1)S(1)}, u32[]{:S(2)}, u32[]{:S(2)}) collective-permute-start(bf16[48,640]{1,0:T(8,128)(2,1)S(1)} %get-tuple-element.40), channel_id=1, source_target_pairs={{0,4},{4,0},{8,12},{12,8},{16,20},{20,16},{24,28},{28,24},{1,5},{5... | collective-permute-start | bytes 184328 | tf_op jit(solution)/shard_map/ppermute | solution.py:91
  15.6 18.8 %collective-permute-start.8 = (bf16[48,640]{1,0:T(8,128)(2,1)S(1)}, bf16[48,640]{1,0:T(8,128)(2,1)S(1)}, u32[]{:S(2)}, u32[]{:S(2)}) collective-permute-start(bf16[48,640]{1,0:T(8,128)(2,1)S(1)} %get-tuple-element.41), channel_id=1, source_target_pairs={{0,8},{4,12},{8,0},{12,4},{16,24},{20,28},{24,16},{28,20},{1,9},{5... | collective-permute-start | bytes 184328 | tf_op jit(solution)/shard_map/ppermute | solution.py:91
  17.4 19.9 %collective-permute-start.9 = (bf16[48,640]{1,0:T(8,128)(2,1)S(1)}, bf16[48,640]{1,0:T(8,128)(2,1)S(1)}, u32[]{:S(2)}, u32[]{:S(2)}) collective-permute-start(bf16[48,640]{1,0:T(8,128)(2,1)S(1)} %get-tuple-element.42), channel_id=1, source_target_pairs={{0,12},{4,8},{8,4},{12,0},{16,28},{20,24},{24,20},{28,16},{1,13},{... | collective-permute-start | bytes 184328 | tf_op jit(solution)/shard_map/ppermute | solution.py:91
  18.6 19.6 %collective-permute-start = (bf16[48,640]{1,0:T(8,128)(2,1)S(1)}, bf16[48,640]{1,0:T(8,128)(2,1)S(1)}, u32[]{:S(2)}, u32[]{:S(2)}) collective-permute-start(bf16[48,640]{1,0:T(8,128)(2,1)S(1)} %get-tuple-element.29), channel_id=1, source_target_pairs={{0,4},{4,0},{8,12},{12,8},{16,20},{20,16},{24,28},{28,24},{1,5},{5... | collective-permute-start | bytes 184328 | tf_op jit(solution)/shard_map/ppermute | solution.py:91
  20.3 20.3 %collective-permute-start.1 = (bf16[48,640]{1,0:T(8,128)(2,1)S(1)}, bf16[48,640]{1,0:T(8,128)(2,1)S(1)}, u32[]{:S(2)}, u32[]{:S(2)}) collective-permute-start(bf16[48,640]{1,0:T(8,128)(2,1)S(1)} %get-tuple-element.30), channel_id=1, source_target_pairs={{0,8},{4,12},{8,0},{12,4},{16,24},{20,28},{24,16},{28,20},{1,9},{5... | collective-permute-start | bytes 184328 | tf_op jit(solution)/shard_map/ppermute | solution.py:91
  27.3 1.6 %copy-start = (bf16[4,512,512]{2,1,0:T(8,128)(2,1)S(1)}, bf16[4,512,512]{2,1,0:T(8,128)(2,1)}, u32[]{:S(2)}) copy-start(bf16[4,512,512]{2,1,0:T(8,128)(2,1)} %refs_16_.1) | copy-start | bytes 6291460
  28.9 0.8 %copy-start.4 = (bf16[3,16,512]{2,1,0:T(8,128)(2,1)S(1)}, bf16[3,16,512]{2,1,0:T(8,128)(2,1)}, u32[]{:S(2)}) copy-start(bf16[3,16,512]{2,1,0:T(8,128)(2,1)} %frozen_ref.1) | copy-start | bytes 147460
  29.7 0.7 %copy-start.5 = (bf16[96,96]{1,0:T(8,128)(2,1)S(1)}, bf16[96,96]{1,0:T(8,128)(2,1)}, u32[]{:S(2)}) copy-start(bf16[96,96]{1,0:T(8,128)(2,1)} %mixer_ref.1) | copy-start | bytes 55300
  30.5 0.7 copy-start.7
  31.1 11.0 %copy-start.2 = (bf16[2,1,8,96,512]{4,3,2,1,0:T(8,128)(2,1)S(1)}, bf16[2,1,8,96,512]{4,3,2,1,0:T(8,128)(2,1)}, u32[]{:S(2)}) copy-start(bf16[2,1,8,96,512]{4,3,2,1,0:T(8,128)(2,1)} %param.17) | copy-start | bytes 4718596
  33.0 13.9 %collective-permute-start.2 = (bf16[48,640]{1,0:T(8,128)(2,1)S(1)}, bf16[48,640]{1,0:T(8,128)(2,1)S(1)}, u32[]{:S(2)}, u32[]{:S(2)}) collective-permute-start(bf16[48,640]{1,0:T(8,128)(2,1)S(1)} %get-tuple-element.31), channel_id=1, source_target_pairs={{0,12},{4,8},{8,4},{12,0},{16,28},{20,24},{24,20},{28,16},{1,13},{... | collective-permute-start | bytes 184328 | tf_op jit(solution)/shard_map/ppermute | solution.py:91
  34.4 12.4 %collective-permute-start.3 = (bf16[48,640]{1,0:T(8,128)(2,1)S(1)}, bf16[48,640]{1,0:T(8,128)(2,1)S(1)}, u32[]{:S(2)}, u32[]{:S(2)}) collective-permute-start(bf16[48,640]{1,0:T(8,128)(2,1)S(1)} %get-tuple-element.32), channel_id=1, source_target_pairs={{0,16},{4,20},{8,24},{12,28},{16,0},{20,4},{24,8},{28,12},{1,17},{... | collective-permute-start | bytes 184328 | tf_op jit(solution)/shard_map/ppermute | solution.py:91
  37.3 9.5 %collective-permute-start.4 = (bf16[48,640]{1,0:T(8,128)(2,1)S(1)}, bf16[48,640]{1,0:T(8,128)(2,1)S(1)}, u32[]{:S(2)}, u32[]{:S(2)}) collective-permute-start(bf16[48,640]{1,0:T(8,128)(2,1)S(1)} %get-tuple-element.33), channel_id=1, source_target_pairs={{0,20},{4,16},{8,28},{12,24},{16,4},{20,0},{24,12},{28,8},{1,21},{... | collective-permute-start | bytes 184328 | tf_op jit(solution)/shard_map/ppermute | solution.py:91
  38.3 8.6 %collective-permute-start.5 = (bf16[48,640]{1,0:T(8,128)(2,1)S(1)}, bf16[48,640]{1,0:T(8,128)(2,1)S(1)}, u32[]{:S(2)}, u32[]{:S(2)}) collective-permute-start(bf16[48,640]{1,0:T(8,128)(2,1)S(1)} %get-tuple-element.34), channel_id=1, source_target_pairs={{0,24},{4,28},{8,16},{12,20},{16,8},{20,12},{24,0},{28,4},{1,25},{... | collective-permute-start | bytes 184328 | tf_op jit(solution)/shard_map/ppermute | solution.py:91
  40.6 7.0 %collective-permute-start.6 = (bf16[48,640]{1,0:T(8,128)(2,1)S(1)}, bf16[48,640]{1,0:T(8,128)(2,1)S(1)}, u32[]{:S(2)}, u32[]{:S(2)}) collective-permute-start(bf16[48,640]{1,0:T(8,128)(2,1)S(1)} %get-tuple-element.35), channel_id=1, source_target_pairs={{0,28},{4,24},{8,20},{12,16},{16,12},{20,8},{24,4},{28,0},{1,29},{... | collective-permute-start | bytes 184328 | tf_op jit(solution)/shard_map/ppermute | solution.py:91
  42.1 5.4 %copy-start.1 = (bf16[4,512,512]{2,1,0:T(8,128)(2,1)S(1)}, bf16[4,512,512]{2,1,0:T(8,128)(2,1)}, u32[]{:S(2)}) copy-start(bf16[4,512,512]{2,1,0:T(8,128)(2,1)} %refs_16_.1) | copy-start | bytes 6291460
  54.0 15.5 %all-to-all-start = ((bf16[32,16,256]{2,1,0:T(8,128)(2,1)}), bf16[32,16,256]{2,1,0:T(8,128)(2,1)S(1)}, u32[]{:S(2)}, u32[]{:S(2)}) async-start(bf16[32,16,256]{2,1,0:T(8,128)(2,1)} %bitcast.8), calls=%async_computation | async-start | bytes 524288 | tf_op jit(solution)/shard_map/all_to_all | solution.py:413

commit v3 on v1

v3 whole, which is shorter than its diff:
```python
import functools

import jax
import jax.numpy as jnp
from jax import lax
from jax.experimental import pallas as pl
from jax.experimental.pallas import tpu as pltpu
from jax.sharding import PartitionSpec as P

WLAT = 8
WLON = 12
LANE = 128
SUB = 16
VMEM_LIMIT = 24 * 1024 * 1024
SEND_VMEM_LIMIT = 60 * 1024 * 1024
BF16 = jnp.bfloat16
F32 = jnp.float32


def round_up(value, step):
    return -(-value // step) * step


def dot_nn(a, b):
    return lax.dot_general(a, b, (((1,), (0,)), ((), ())), preferred_element_type=F32)


def dot_nt(a, b):
    return lax.dot_general(a, b, (((1,), (1,)), ((), ())), preferred_element_type=F32)


def dot_tn(a, b):
    return lax.dot_general(a, b, (((0,), (0,)), ((), ())), preferred_element_type=F32)


def split_hi_lo(values):
    high = values.astype(BF16)
    low = (values - high.astype(F32)).astype(BF16)
    return high, low


def iota2(shape, axis):
    return lax.broadcasted_iota(jnp.int32, shape, axis)


def params(limit=VMEM_LIMIT, **extra):
    return pltpu.CompilerParams(vmem_limit_bytes=limit, **extra)


def send_kernel(owner_ref, x_ref, out_ref):
    band_count, width, _ = out_ref.shape
    for tile in range(x_ref.shape[1] // LANE):
        first, past = tile * LANE, (tile + 1) * LANE
        rows = x_ref[:, first:past].T
        start = first
        while start < past:
            block = start // width
            end = min((block + 1) * width, past)
            inside = slice(start - block * width, end - block * width)
            out_ref[owner_ref[block], inside, :] = rows[start - first : end - first, :]
            start = end


def send_blocks(pixels, owner, band_count, width):
    features, columns = pixels.shape
    return pl.pallas_call(
        send_kernel,
        out_shape=jax.ShapeDtypeStruct((band_count, width, features), BF16),
        grid_spec=pltpu.PrefetchScalarGridSpec(
            num_scalar_prefetch=1,
            grid=(features // LANE,),
            in_specs=[pl.BlockSpec((LANE, columns), lambda f, owner: (f, 0))],
            out_specs=pl.BlockSpec((band_count, width, LANE), lambda f, owner: (0, 0, f)),
        ),
        compiler_params=params(SEND_VMEM_LIMIT),
        name="send_blocks",
    )(owner, pixels)


def expand_table(table, rows, half_width_padded, half_width, transpose):
    position = iota2((rows, WLAT * WLON), 0)
    line, col = position // half_width_padded, position % half_width_padded
    target = iota2((rows, WLAT * WLON), 1)
    pick = jnp.where((target == line * WLON + col % WLON) & (col < half_width), 1.0, 0.0).astype(BF16)
    left = (dot_nt if transpose else dot_nn)(pick, table).astype(BF16)
    full = dot_nt(left, pick)
    row_window = (iota2((rows, 1), 0) % half_width_padded) // WLON
    col_window = (iota2((1, rows), 1) % half_width_padded) // WLON
    return jnp.where(row_window == col_window, full, 0.0).astype(BF16)


def prep_kernel(
    row_share,
    half_width,
    half_width_padded,
    group_ref,
    frozen_ref,
    factors_ref,
    level_ref,
    mixer_ref,
    merged_ref,
    up_ref,
    down_ref,
    mix_ref,
    mix_t_ref,
):
    reps, _, rank, share = factors_ref.shape
    levels = level_ref.shape[0]
    variables = group_ref.shape[0]
    channels = variables * frozen_ref.shape[1]
    up = jnp.concatenate([factors_ref[r, 0] for r in range(reps)], axis=1)
    source, target = iota2((share, channels), 0), iota2((share, channels), 1)
    down_t = jnp.zeros((rank, channels), F32)
    for r in range(reps):
        place = jnp.where((target == source + r * row_share) & (source < row_share), 1.0, 0.0)
        down_t = down_t + dot_nn(factors_ref[r, 1], place.astype(BF16))
    down_t = down_t.astype(BF16)
    down_ref[...] = down_t
    base = jnp.concatenate([frozen_ref[group_ref[v]].astype(F32) for v in range(variables)], axis=0)
    merged = (base + dot_tn(down_t, up)).astype(BF16)
    stacked = jnp.concatenate([merged, up], axis=0)
    merged_ref[...] = jnp.zeros_like(merged_ref)
    for level in range(levels):
        through = dot_nn(stacked, level_ref[level])
        weights = through[:channels].astype(BF16)
        for s in range(merged_ref.shape[0]):
            offset = (s * levels * channels) % LANE + level * channels
            merged_ref[s, offset : offset + channels, :] = weights
        up_high, up_low = split_hi_lo(through[channels:])
        up_ref[level, :rank, :] = up_high
        up_ref[level, rank:, :] = up_low
    rows = mix_ref.shape[0]
    mix_ref[...] = expand_table(mixer_ref[...], rows, half_width_padded, half_width, False)
    mix_t_ref[...] = expand_table(mixer_ref[...], rows, half_width_padded, half_width, True)


def prepare(groups, frozen, factors, level_weight, mixer, samples, row_share, half_width, half_width_padded):
    reps, _, rank, _ = factors.shape
    levels, feature_dim, _ = level_weight.shape
    channels = groups.shape[0] * frozen.shape[1]
    reach = round_up(levels * channels + LANE // 2, LANE)
    rows = WLAT * half_width_padded
    vmem = pl.BlockSpec(memory_space=pltpu.VMEM)
    flops = 2 * levels * (channels + rank) * feature_dim * feature_dim + 4 * rows * rows * WLAT * WLON
    return pl.pallas_call(
        functools.partial(prep_kernel, row_share, half_width, half_width_padded),
        out_shape=[
            jax.ShapeDtypeStruct((samples, reach, feature_dim), BF16),
            jax.ShapeDtypeStruct((levels, 2 * rank, feature_dim), BF16),
            jax.ShapeDtypeStruct((rank, channels), BF16),
            jax.ShapeDtypeStruct((rows, rows), BF16),
            jax.ShapeDtypeStruct((rows, rows), BF16),
        ],
        in_specs=[pl.BlockSpec(memory_space=pltpu.SMEM)] + [vmem] * 4,
        out_specs=[vmem] * 5,
        compiler_params=params(),
        cost_estimate=pl.CostEstimate(flops=flops, bytes_accessed=4 * 2**20, transcendentals=0),
        name="prepare",
    )(groups, frozen, factors, level_weight, mixer)


def normal_parts(values):
    bell = jnp.exp(-0.5 * values * values)
    t = 1.0 / (1.0 + 0.23164189 * jnp.abs(values))
    tail = t * (
        0.127414796 + t * (-0.142248368 + t * (0.7107068705 + t * (-0.7265760135 + t * 0.5307027145)))
    )
    tail = tail * bell
    return jnp.where(values < 0.0, tail, 1.0 - tail), 0.3989422804014327 * bell


def factor_shares(total, up_ref, down_ref, level_ref):
    levels, two_rank, feature_dim = up_ref.shape
    rank, channels = down_ref.shape
    high, low = split_hi_lo(total)
    down = down_ref[...]
    first = jnp.zeros((rank, channels), F32)
    second = jnp.zeros((two_rank, feature_dim), F32)
    for level in range(levels):
        at = slice(level * channels, (level + 1) * channels)
        both = dot_nt(up_ref[level], high[at])
        first = first + both[:rank] + both[rank:] + dot_nt(up_ref[level, :rank, :], low[at])
        through = dot_nn(down, high[at]) + dot_nn(down, low[at])
        through = jnp.concatenate(split_hi_lo(through), axis=0)
        second = second + dot_nt(through, level_ref[level])
    return first, second[:rank] + second[rank:]


def mix_kernel(
    arrived_ref,
    merged_ref,
    mix_ref,
    mix_t_ref,
    grad_ref,
    up_ref,
    down_ref,
    level_ref,
    mixed_ref,
    share_ref,
    total_ref,
    pre_ref,
    tokens_ref,
    grad_pre_ref,
    second_ref,
):
    samples, reach, feature_dim = merged_ref.shape
    _, width, features = arrived_ref.shape
    depth = features // samples
    rows = WLAT * width
    step = pl.program_id(0) * pl.num_programs(1) + pl.program_id(1)

    def forward(s):
        lane = s * depth // LANE * LANE
        pixels = arrived_ref[:, :, lane : lane + reach].reshape(rows, reach)
        tokens = dot_nn(pixels, merged_ref[s]).astype(BF16)
        tokens_ref[s] = tokens
        pre_ref[s] = dot_nn(mix_ref[...], tokens)
        return pixels

    def pointwise(s):
        for line in range(WLAT):
            for start in range(0, width, SUB):
                at, within = pl.ds(line * width + start, SUB), pl.ds(start, SUB)
                pre = pre_ref[s, at, :]
                cdf, pdf = normal_parts(pre)
                tokens = tokens_ref[s, at, :].astype(F32)
                mixed_ref[s, line, within, :] = (tokens + pre * cdf).astype(BF16)
                grad = grad_ref[s, line, within, :].astype(F32)
                grad_pre_ref[s, at, :] = (grad * (cdf + pre * pdf)).astype(BF16)

    def backward(s, pixels):
        direct = grad_ref[s].reshape(rows, feature_dim).astype(F32)
        grad_tokens = dot_nn(mix_t_ref[...], grad_pre_ref[s]) + direct
        offset = s * depth % LANE
        return dot_tn(pixels, grad_tokens.astype(BF16))[offset : offset + depth]

    pixels = [forward(s) for s in range(samples)]
    share = jnp.zeros((depth, feature_dim), F32)
    for s in range(samples):
        pointwise(s)
        share = share + backward(s, pixels[s])

    @pl.when(step == 0)
    def _():
        total_ref[...] = share

    @pl.when(step != 0)
    def _():
        total_ref[...] = total_ref[...] + share

    @pl.when(step == pl.num_programs(0) * pl.num_programs(1) - 1)
    def _():
        first, second = factor_shares(total_ref[...], up_ref, down_ref, level_ref)
        second_ref[...] = second
        reps, channels = share_ref.shape[0], down_ref.shape[1]
        columns = feature_dim // reps
        me = lax.axis_index("rep")
        share_ref[...] = jnp.zeros_like(share_ref)
        for k in range(reps):
            lane = pl.multiple_of(jnp.bitwise_xor(me, k) * columns, LANE)
            share_ref[k, :, :columns] = second_ref[:, pl.ds(lane, columns)]
            share_ref[k, :, columns : columns + channels] = first


def mix_blocks(halves, arrived, merged, mix, mix_t, grad, up_through, down_t, level_weight, reps):
    samples, lat_rows, block_width, feature_dim = grad.shape
    width = block_width // halves
    lanes = arrived.shape[2]
    reach = merged.shape[1]
    rows = WLAT * width
    rank, channels = down_t.shape

    def whole(shape):
        return pl.BlockSpec(shape, lambda w, h: (0,) * len(shape))

    block = pl.BlockSpec((samples, WLAT, width, feature_dim), lambda w, h: (0, w, h, 0))
    share_shape = (reps, rank, feature_dim // reps + round_up(channels, LANE))
    flops = 2 * samples * lat_rows * block_width * feature_dim * (2 * reach + 2 * rows)
    constants = [up_through, down_t, level_weight]
    return pl.pallas_call(
        mix_kernel,
        out_shape=[
            jax.ShapeDtypeStruct(grad.shape, BF16),
            jax.ShapeDtypeStruct(share_shape, F32),
        ],
        grid=(lat_rows // WLAT, halves),
        in_specs=[
            pl.BlockSpec((WLAT, width, lanes), lambda w, h: (w, h, 0)),
            whole(merged.shape),
            whole(mix.shape),
            whole(mix_t.shape),
            block,
        ]
        + [whole(array.shape) for array in constants],
        out_specs=[block, whole(share_shape)],
        scratch_shapes=[
            pltpu.VMEM((lanes // samples, feature_dim), F32),
            pltpu.VMEM((samples, rows, feature_dim), F32),
            pltpu.VMEM((samples, rows, feature_dim), BF16),
            pltpu.VMEM((samples, rows, feature_dim), BF16),
            pltpu.VMEM((rank, feature_dim), F32),
        ],
        compiler_params=params(dimension_semantics=("arbitrary", "arbitrary")),
        cost_estimate=pl.CostEstimate(
            flops=flops,
            bytes_accessed=12 * 2**20,
            transcendentals=samples * lat_rows * block_width * feature_dim,
        ),
        name="mix_blocks",
    )(arrived, merged, mix, mix_t, grad, *constants)


def swap(values, axis, distance):
    count = lax.axis_size(axis)
    return lax.ppermute(values, axis, [(source, source ^ distance) for source in range(count)])


def sum_shares(shares):
    half = shares.shape[0] // 2
    while half >= 1:
        shares = shares[:half] + swap(shares[half:], "rep", half)
        half //= 2
    total = shares[0]
    distance = 1
    while distance < lax.axis_size("band"):
        total = total + swap(total, "band", distance)
        distance *= 2
    return total


def on_device(
    patches,
    variable_group_index,
    frozen_patch_weight,
    adapter_down,
    adapter_up,
    level_merge_weight,
    window_patch_mixer,
    column_block_owner,
    mixed_token_gradient,
):
    band_count, reps = lax.axis_size("band"), lax.axis_size("rep")
    samples, levels, channels, row_count, col_count = patches.shape
    feature_dim = frozen_patch_weight.shape[2]
    rank, col_share = adapter_up.shape
    row_share = adapter_down.shape[0]
    lat_rows = band_count * row_count
    block_width = col_count // band_count
    halves = 2 if block_width % (2 * SUB * WLON // 4) == 0 else 1
    half_width = block_width // halves
    half_padded = round_up(half_width, SUB)
    padded_width = halves * half_padded
    features = samples * levels * channels

    pixels = patches.reshape(features, col_count)
    if half_padded == half_width and features % LANE == 0 and col_count % LANE == 0:
        outgoing = send_blocks(pixels, column_block_owner, band_count, block_width)
    else:
        block_ids = jnp.arange(band_count, dtype=jnp.int32)
        inverse = jnp.sum(
            jnp.where(column_block_owner[None, :] == block_ids[:, None], block_ids[None, :], 0), axis=1
        )
        outgoing = jnp.take(pixels.T.reshape(band_count, block_width, features), inverse, axis=0)
        outgoing = jnp.pad(outgoing, ((0, 0), (0, padded_width - block_width), (0, 0)))
    arrived = lax.all_to_all(outgoing, "band", split_axis=0, concat_axis=0, tiled=True)

    pack_width = round_up(max(row_share, col_share), LANE)
    pack = jnp.stack(
        [
            jnp.pad(adapter_up, ((0, 0), (0, pack_width - col_share))),
            jnp.pad(adapter_down.T, ((0, 0), (0, pack_width - row_share))),
        ]
    )
    factors = lax.all_gather(pack, "rep", axis=0, tiled=False)
    merged, up_through, down_t, mix, mix_t = prepare(
        variable_group_index,
        frozen_patch_weight,
        factors,
        level_merge_weight,
        window_patch_mixer,
        samples,
        row_share,
        half_width,
        half_padded,
    )
    grad = mixed_token_gradient.reshape(samples, lat_rows, block_width, feature_dim)
    if padded_width != block_width:
        grad = jnp.pad(grad, ((0, 0), (0, 0), (0, padded_width - block_width), (0, 0)))
    mixed, shares = mix_blocks(
        halves, arrived, merged, mix, mix_t, grad, up_through, down_t, level_merge_weight, reps
    )
    if padded_width != block_width:
        mixed = mixed[:, :, :block_width]

    summed = sum_shares(shares)
    first_t = lax.dynamic_slice_in_dim(summed, col_share + lax.axis_index("rep") * row_share, row_share, 1)
    return (
        mixed.reshape(mixed_token_gradient.shape),
        first_t.T,
        summed[:, :col_share],
    )


def solution(mesh):
    in_specs = (
        P("rep", None, None, "band", None),
        P(),
        P(),
        P("rep", None),
        P(None, "rep"),
        P(),
        P(),
        P(),
        P("rep", "band", None, None, None),
    )
    out_specs = (P("rep", "band", None, None, None), P("rep", None), P(None, "rep"))
    return jax.shard_map(
        on_device, mesh=mesh, in_specs=in_specs, out_specs=out_specs, check_vma=False
    )
```

time: 95.7 us -> 68.9 us (0.72)
  blocking collectives: 57.4 us -> 5.19 us
  waiting for transfers between devices: 4.08 us -> 29.4 us
  starting transfers between devices: 6.87 us -> 10.2 us
  Pallas kernels: 16.6 us -> 15 us
  local copies, waits for them, and re-layouts: 9.3 us -> 7.95 us
    all_gather x1 -> x0, blocking collectives: 31.1 us -> none  [on_device(): summed = jnp.sum(lax.all_gather(mine, 'band', axis=0, tiled=False), axis=0)]
    all_to_all x1 -> x0, blocking collectives: 21 us -> none  [on_device(): lax.all_to_all(part, 'band', split_axis=0, concat_axis=0, tiled=True)]
    ppermute x0 -> x5, waiting for transfers between devices: none -> 14.3 us  [swap(): lax.ppermute(values, axis, [(source, source ^ distance) for source in ran...]
    all_to_all x2 -> x1, waiting for transfers between devices: 4.08 us -> 15.1 us  [on_device(): lax.all_to_all(outgoing, 'band', split_axis=0, concat_axis=0, tiled=True)]
    ppermute x0 -> x5, starting transfers between devices: none -> 2.98 us  [swap(): lax.ppermute(values, axis, [(source, source ^ distance) for source in ran...]
    pallas_call x3 -> x2, Pallas kernels: 14.8 us -> 13.1 us  [the longest x1 8.3 us: mix_blocks(): pl.pallas_call(mix_kernel, out_shape=[jax.ShapeDtypeStruct(grad.shape, BF...]
    unnamed x32 -> x26, local copies, waits for them, and re-layouts: 8.03 us -> 6.66 us
    all_to_all x2 -> x1, starting transfers between devices: 6.87 us -> 7.25 us  [on_device(): lax.all_to_all(outgoing, 'band', split_axis=0, concat_axis=0, tiled=True)]
  transfers between devices with their start and end apart: 2 -> 6, of which waited for: 1 -> 6; matrix products, arithmetic and copies ran while one was open for 0% -> 0% of each run, Pallas kernels for 7% -> 3%
where the time goes in v3:
time: 68.9 us; the launch traced here: 68.5 us
  waiting for transfers between devices  29.4 us (43%)
  Pallas kernels  15 us (22%)
  starting transfers between devices  10.2 us (15%)
  local copies, waits for them, and re-layouts  7.95 us (12%)
  blocking collectives  5.19 us (8%)
  between operations  0.76 us (1%)
    all_to_all x1, waiting for transfers between devices, on_device(): lax.all_to_all(outgoing, 'band', split_axis=0, concat_axis=0, tiled=True)  15.1 us
    ppermute x5, waiting for transfers between devices, swap(): lax.ppermute(values, axis, [(source, source ^ distance) for source in ran...  14.3 us
    pallas_call x1, Pallas kernels, mix_blocks(): pl.pallas_call(mix_kernel, out_shape=[jax.ShapeDtypeStruct(grad.shape, BF...  8.3 us
    all_to_all x1, starting transfers between devices, on_device(): lax.all_to_all(outgoing, 'band', split_axis=0, concat_axis=0, tiled=True)  7.25 us
    unnamed x26, local copies, waits for them, and re-layouts  6.66 us
    all_gather x1, blocking collectives, on_device(): factors = lax.all_gather(pack, 'rep', axis=0, tiled=False)  5.19 us
    pallas_call x1, Pallas kernels, send_blocks(): pl.pallas_call(send_kernel, out_shape=jax.ShapeDtypeStruct((band_count, w...  4.83 us
    ppermute x5, starting transfers between devices, swap(): lax.ppermute(values, axis, [(source, source ^ distance) for source in ran...  2.98 us
  transfers between devices with their start and end apart: 6, of which 6 were waited for; matrix products, arithmetic and copies ran while one was open for 0% of the time, Pallas kernels for 3%

profile of v3, /device:TPU:0, one launch (start us, length us, event | category | flops | bytes accessed | tf_op | source)
XLA Modules:
  0.0 68.5 jit_solution(14663429062422125453)
XLA Ops:
  0.6 0.0 copy-start.11
  0.6 0.0 copy-start.12
  0.7 0.0 copy-start
  0.7 0.0 copy-start.1
  0.7 0.0 copy-start.2
  0.7 0.0 copy-start.3
  0.7 4.8 %send_blocks.1 = bf16[8,96,640]{2,1,0:T(8,128)(2,1)} custom-call(s32[8]{0:T(128)} %owner_ref.1, bf16[640,768]{1,0:T(8,128)(2,1)} %bitcast.16), custom_call_target="tpu_custom_call" | custom-call | tf_op jit(solution)/shard_map/send_blocks/pallas_call | solution.py:66
  5.5 7.3 %all-to-all-start = ((bf16[8,96,640]{2,1,0:T(8,128)(2,1)}), bf16[8,96,640]{2,1,0:T(8,128)(2,1)S(1)}, u32[]{:S(2)}, u32[]{:S(2)}) async-start(bf16[8,96,640]{2,1,0:T(8,128)(2,1)} %send_blocks.1), calls=%async_computation | async-start | bytes 1966080 | tf_op jit(solution)/shard_map/all_to_all | solution.py:365
  12.8 0.0 copy-done.11
  12.8 0.0 copy-done.12
  12.8 5.2 %all-gather = bf16[8,16,128]{2,1,0:T(8,128)(2,1)S(1)} all-gather(bf16[2,16,128]{2,1,0:T(8,128)(2,1)S(1)} %pad_maximum_fusion), channel_id=2, replica_groups=mesh['band'=8,'rep'=4] {'rep'}, dimensions={0}, use_global_device_ids=true | all-gather | bytes 40960 | tf_op jit(solution)/shard_map/all_gather | solution.py:374
  18.0 0.0 copy-done
  18.0 0.0 copy-done.1
  18.0 0.0 copy-done.2
  18.0 0.0 copy-done.3
  18.0 1.8 %prepare.1 = (bf16[2,384,512]{2,1,0:T(8,128)(2,1)S(1)}, bf16[4,32,512]{2,1,0:T(8,128)(2,1)S(1)}, bf16[16,80]{1,0:T(8,128)(2,1)S(1)}, bf16[384,384]{1,0:T(8,128)(2,1)S(1)}, bf16[384,384]{1,0:T(8,128)(2,1)S(1)}) custom-call(s32[5]{0:T(128)S(1)} %copy-done.3, bf16[3,16,512]{2,1,0:T(8,128)(2,1)S(1)} %copy-done.1, bf16[4,2,16,128]{3,2,1,0:T(8,128)(2,1)S(1)} %bitcast.14, ...), custom_call_target="tpu_custom_call" | custom-call | flops 257949696 | bytes 4194304 | tf_op jit(solution)/shard_map/prepare/pallas_call | solution.py:145
  19.9 0.0 copy-start.5
  19.9 0.9 %copy-done.5 = bf16[2,384,512]{2,1,0:T(8,128)(2,1)} copy-done((bf16[2,384,512]{2,1,0:T(8,128)(2,1)}, bf16[2,384,512]{2,1,0:T(8,128)(2,1)S(1)}, u32[]{:S(2)}) %copy-start.5) | copy-done | bytes 786456
  20.7 0.0 copy-start.7
  20.7 0.7 %copy-done.7 = bf16[384,384]{1,0:T(8,128)(2,1)} copy-done((bf16[384,384]{1,0:T(8,128)(2,1)}, bf16[384,384]{1,0:T(8,128)(2,1)S(1)}, u32[]{:S(2)}) %copy-start.7) | copy-done | bytes 294936
  21.4 0.0 copy-start.9
  21.4 0.7 copy-done.9
  22.1 15.1 %all-to-all-done.arrived_ref = bf16[8,96,640]{2,1,0:T(8,128)(2,1)S(1)} async-done(((bf16[8,96,640]{2,1,0:T(8,128)(2,1)}), bf16[8,96,640]{2,1,0:T(8,128)(2,1)S(1)}, u32[]{:S(2)}, u32[]{:S(2)}) %all-to-all-start) | async-done | bytes 983072 | tf_op jit(solution)/shard_map/all_to_all | solution.py:365
  37.2 0.0 copy-start.4
  37.2 1.4 %copy-done.4 = bf16[2,1,8,96,512]{4,3,2,1,0:T(8,128)(2,1)S(1)} copy-done((bf16[2,1,8,96,512]{4,3,2,1,0:T(8,128)(2,1)S(1)}, bf16[2,1,8,96,512]{4,3,2,1,0:T(8,128)(2,1)}, u32[]{:S(2)}) %copy-start.4) | copy-done | bytes 1572888
  38.6 0.0 copy-start.6
  38.6 1.1 %copy-done.6 = bf16[2,384,512]{2,1,0:T(8,128)(2,1)S(1)} copy-done((bf16[2,384,512]{2,1,0:T(8,128)(2,1)S(1)}, bf16[2,384,512]{2,1,0:T(8,128)(2,1)}, u32[]{:S(2)}) %copy-start.6) | copy-done | bytes 786456
  39.7 0.0 copy-start.8
  39.7 1.0 %copy-done.8 = bf16[384,384]{1,0:T(8,128)(2,1)S(1)} copy-done((bf16[384,384]{1,0:T(8,128)(2,1)S(1)}, bf16[384,384]{1,0:T(8,128)(2,1)}, u32[]{:S(2)}) %copy-start.8) | copy-done | bytes 294936
  40.7 0.0 copy-start.10
  40.7 0.9 %copy-done.10 = bf16[4,32,512]{2,1,0:T(8,128)(2,1)S(1)} copy-done((bf16[4,32,512]{2,1,0:T(8,128)(2,1)S(1)}, bf16[4,32,512]{2,1,0:T(8,128)(2,1)}, u32[]{:S(2)}) %copy-start.10) | copy-done | bytes 131096
  41.6 8.3 %mix_blocks.1 = (bf16[2,8,96,512]{3,2,1,0:T(8,128)(2,1)}, f32[4,16,256]{2,1,0:T(8,128)S(1)}) custom-call(bf16[8,96,640]{2,1,0:T(8,128)(2,1)S(1)} %all-to-all-done.arrived_ref, bf16[2,384,512]{2,1,0:T(8,128)(2,1)S(1)} %copy-done.6, bf16[384,384]{1,0:T(8,128)(2,1)S(1)} %get-tuple-element.11.mix_ref, bf16[384,384]{1,0:T(8,128)(2,1)S(1)} %copy-done.8, ...), custom_call_target="tpu_custom_call" | custom-call | flops 2415919104 | bytes 12582912 | tf_op jit(solution)/shard_map/mix_blocks/pallas_call | solution.py:280
  49.9 1.5 %collective-permute-start = (f32[2,16,256]{2,1,0:T(8,128)S(1)}, f32[2,16,256]{2,1,0:T(8,128)S(1)}, u32[]{:S(2)}, u32[]{:S(2)}) collective-permute-start(f32[2,16,256]{2,1,0:T(8,128)S(1)} %slice.16), channel_id=1, source_target_pairs={{0,2},{1,3},{2,0},{3,1},{4,6},{5,7},{6,4},{7,5},{8,10},{9,11},{10,... | collective-permute-start | bytes 98312 | tf_op jit(solution)/shard_map/ppermute | solution.py:315
  51.4 2.4 %collective-permute-done = f32[2,16,256]{2,1,0:T(8,128)S(1)} collective-permute-done((f32[2,16,256]{2,1,0:T(8,128)S(1)}, f32[2,16,256]{2,1,0:T(8,128)S(1)}, u32[]{:S(2)}, u32[]{:S(2)}) %collective-permute-start) | collective-permute-done | bytes 32800 | tf_op jit(solution)/shard_map/ppermute | solution.py:315
  53.8 0.1 collective-permute-start.1
  53.9 1.2 %collective-permute-done.1 = f32[1,16,256]{2,1,0:T(8,128)S(1)} collective-permute-done((f32[1,16,256]{2,1,0:T(8,128)S(1)}, f32[1,16,256]{2,1,0:T(8,128)S(1)}, u32[]{:S(2)}, u32[]{:S(2)}) %collective-permute-start.1) | collective-permute-done | bytes 16416 | tf_op jit(solution)/shard_map/ppermute | solution.py:315
  55.1 1.4 %collective-permute-start.2 = (f32[16,256]{1,0:T(8,128)S(1)}, f32[16,256]{1,0:T(8,128)S(1)}, u32[]{:S(2)}, u32[]{:S(2)}) collective-permute-start(f32[16,256]{1,0:T(8,128)S(1)} %fusion), channel_id=1, source_target_pairs={{0,4},{4,0},{8,12},{12,8},{16,20},{20,16},{24,28},{28,24},{1,5},{5... | collective-permute-start | bytes 49160 | tf_op jit(solution)/shard_map/ppermute | solution.py:315
  56.4 2.4 %collective-permute-done.2 = f32[16,256]{1,0:T(8,128)S(1)} collective-permute-done((f32[16,256]{1,0:T(8,128)S(1)}, f32[16,256]{1,0:T(8,128)S(1)}, u32[]{:S(2)}, u32[]{:S(2)}) %collective-permute-start.2) | collective-permute-done | bytes 16416 | tf_op jit(solution)/shard_map/ppermute | solution.py:315
  58.8 0.0 collective-permute-start.3
  58.8 3.7 %collective-permute-done.3 = f32[16,256]{1,0:T(8,128)S(1)} collective-permute-done((f32[16,256]{1,0:T(8,128)S(1)}, f32[16,256]{1,0:T(8,128)S(1)}, u32[]{:S(2)}, u32[]{:S(2)}) %collective-permute-start.3) | collective-permute-done | bytes 16416 | tf_op jit(solution)/shard_map/ppermute | solution.py:315
  62.6 0.0 collective-permute-start.4
  62.6 4.6 %collective-permute-done.4 = f32[16,256]{1,0:T(8,128)S(1)} collective-permute-done((f32[16,256]{1,0:T(8,128)S(1)}, f32[16,256]{1,0:T(8,128)S(1)}, u32[]{:S(2)}, u32[]{:S(2)}) %collective-permute-start.4) | collective-permute-done | bytes 16416 | tf_op jit(solution)/shard_map/ppermute | solution.py:315
  67.2 0.6 slice.22
  67.8 0.7 dynamic-slice_bitcast_fusion
  (9 shorter events, 0.0 us)
Async XLA Ops:
  0.6 12.1 %copy-start.11 = (bf16[20,16]{0,1:T(8,128)(2,1)S(1)}, bf16[20,16]{0,1:T(8,128)(2,1)}, u32[]{:S(2)}) copy-start(bf16[20,16]{0,1:T(8,128)(2,1)} %param.12) | copy-start | bytes 1924
  0.6 12.2 %copy-start.12 = (bf16[16,128]{1,0:T(8,128)(2,1)S(1)}, bf16[16,128]{1,0:T(8,128)(2,1)}, u32[]{:S(2)}) copy-start(bf16[16,128]{1,0:T(8,128)(2,1)} %param.13) | copy-start | bytes 12292
  0.7 17.4 %copy-start = (bf16[4,512,512]{2,1,0:T(8,128)(2,1)S(1)}, bf16[4,512,512]{2,1,0:T(8,128)(2,1)}, u32[]{:S(2)}) copy-start(bf16[4,512,512]{2,1,0:T(8,128)(2,1)} %level_ref.3) | copy-start | bytes 6291460
  0.7 17.4 %copy-start.1 = (bf16[3,16,512]{2,1,0:T(8,128)(2,1)S(1)}, bf16[3,16,512]{2,1,0:T(8,128)(2,1)}, u32[]{:S(2)}) copy-start(bf16[3,16,512]{2,1,0:T(8,128)(2,1)} %frozen_ref.1) | copy-start | bytes 147460
  0.7 17.3 %copy-start.2 = (bf16[96,96]{1,0:T(8,128)(2,1)S(1)}, bf16[96,96]{1,0:T(8,128)(2,1)}, u32[]{:S(2)}) copy-start(bf16[96,96]{1,0:T(8,128)(2,1)} %mixer_ref.1) | copy-start | bytes 55300
  0.7 17.3 %copy-start.3 = (s32[5]{0:T(128)S(1)}, s32[5]{0:T(128)}, u32[]{:S(2)}) copy-start(s32[5]{0:T(128)} %group_ref.1) | copy-start | bytes 64
  5.5 31.6 %all-to-all-start = ((bf16[8,96,640]{2,1,0:T(8,128)(2,1)}), bf16[8,96,640]{2,1,0:T(8,128)(2,1)S(1)}, u32[]{:S(2)}, u32[]{:S(2)}) async-start(bf16[8,96,640]{2,1,0:T(8,128)(2,1)} %send_blocks.1), calls=%async_computation | async-start | bytes 1966080 | tf_op jit(solution)/shard_map/all_to_all | solution.py:365
  19.9 0.9 %copy-start.5 = (bf16[2,384,512]{2,1,0:T(8,128)(2,1)}, bf16[2,384,512]{2,1,0:T(8,128)(2,1)S(1)}, u32[]{:S(2)}) copy-start(bf16[2,384,512]{2,1,0:T(8,128)(2,1)S(1)} %get-tuple-element.10.merged_ref) | copy-start | bytes 2359300
  20.7 0.7 %copy-start.7 = (bf16[384,384]{1,0:T(8,128)(2,1)}, bf16[384,384]{1,0:T(8,128)(2,1)S(1)}, u32[]{:S(2)}) copy-start(bf16[384,384]{1,0:T(8,128)(2,1)S(1)} %get-tuple-element.12.mix_t_ref) | copy-start | bytes 884740
  21.4 0.7 copy-start.9
  37.2 1.4 %copy-start.4 = (bf16[2,1,8,96,512]{4,3,2,1,0:T(8,128)(2,1)S(1)}, bf16[2,1,8,96,512]{4,3,2,1,0:T(8,128)(2,1)}, u32[]{:S(2)}) copy-start(bf16[2,1,8,96,512]{4,3,2,1,0:T(8,128)(2,1)} %param.17) | copy-start | bytes 4718596
  38.6 1.1 %copy-start.6 = (bf16[2,384,512]{2,1,0:T(8,128)(2,1)S(1)}, bf16[2,384,512]{2,1,0:T(8,128)(2,1)}, u32[]{:S(2)}) copy-start(bf16[2,384,512]{2,1,0:T(8,128)(2,1)} %copy-done.5) | copy-start | bytes 2359300
  39.7 1.0 %copy-start.8 = (bf16[384,384]{1,0:T(8,128)(2,1)S(1)}, bf16[384,384]{1,0:T(8,128)(2,1)}, u32[]{:S(2)}) copy-start(bf16[384,384]{1,0:T(8,128)(2,1)} %copy-done.7) | copy-start | bytes 884740
  40.7 0.9 %copy-start.10 = (bf16[4,32,512]{2,1,0:T(8,128)(2,1)S(1)}, bf16[4,32,512]{2,1,0:T(8,128)(2,1)}, u32[]{:S(2)}) copy-start(bf16[4,32,512]{2,1,0:T(8,128)(2,1)} %copy-done.9) | copy-start | bytes 393220
  49.9 3.9 %collective-permute-start = (f32[2,16,256]{2,1,0:T(8,128)S(1)}, f32[2,16,256]{2,1,0:T(8,128)S(1)}, u32[]{:S(2)}, u32[]{:S(2)}) collective-permute-start(f32[2,16,256]{2,1,0:T(8,128)S(1)} %slice.16), channel_id=1, source_target_pairs={{0,2},{1,3},{2,0},{3,1},{4,6},{5,7},{6,4},{7,5},{8,10},{9,11},{10,... | collective-permute-start | bytes 98312 | tf_op jit(solution)/shard_map/ppermute | solution.py:315
  53.8 1.2 %collective-permute-start.1 = (f32[1,16,256]{2,1,0:T(8,128)S(1)}, f32[1,16,256]{2,1,0:T(8,128)S(1)}, u32[]{:S(2)}, u32[]{:S(2)}) collective-permute-start(f32[1,16,256]{2,1,0:T(8,128)S(1)} %slice.21), channel_id=1, source_target_pairs={{0,1},{1,0},{2,3},{3,2},{4,5},{5,4},{6,7},{7,6},{8,9},{9,8},{10,11... | collective-permute-start | bytes 49160 | tf_op jit(solution)/shard_map/ppermute | solution.py:315
  55.1 3.7 %collective-permute-start.2 = (f32[16,256]{1,0:T(8,128)S(1)}, f32[16,256]{1,0:T(8,128)S(1)}, u32[]{:S(2)}, u32[]{:S(2)}) collective-permute-start(f32[16,256]{1,0:T(8,128)S(1)} %fusion), channel_id=1, source_target_pairs={{0,4},{4,0},{8,12},{12,8},{16,20},{20,16},{24,28},{28,24},{1,5},{5... | collective-permute-start | bytes 49160 | tf_op jit(solution)/shard_map/ppermute | solution.py:315
  58.8 3.7 %collective-permute-start.3 = (f32[16,256]{1,0:T(8,128)S(1)}, f32[16,256]{1,0:T(8,128)S(1)}, u32[]{:S(2)}, u32[]{:S(2)}) collective-permute-start(f32[16,256]{1,0:T(8,128)S(1)} %add.24), channel_id=1, source_target_pairs={{0,8},{4,12},{8,0},{12,4},{16,24},{20,28},{24,16},{28,20},{1,9},{5... | collective-permute-start | bytes 49160 | tf_op jit(solution)/shard_map/ppermute | solution.py:315
  62.6 4.6 %collective-permute-start.4 = (f32[16,256]{1,0:T(8,128)S(1)}, f32[16,256]{1,0:T(8,128)S(1)}, u32[]{:S(2)}, u32[]{:S(2)}) collective-permute-start(f32[16,256]{1,0:T(8,128)S(1)} %add.25), channel_id=1, source_target_pairs={{0,16},{4,20},{8,24},{12,28},{16,0},{20,4},{24,8},{28,12},{1,17},{... | collective-permute-start | bytes 49160 | tf_op jit(solution)/shard_map/ppermute | solution.py:315

commit v4 on v3

--- a/solution.py
+++ b/solution.py
@@ -12,7 +12,7 @@
 LANE = 128
 SUB = 16
 VMEM_LIMIT = 24 * 1024 * 1024
-SEND_VMEM_LIMIT = 60 * 1024 * 1024
+MAX_PERMUTES = 8
 BF16 = jnp.bfloat16
 F32 = jnp.float32
 
@@ -43,38 +43,69 @@
     return lax.broadcasted_iota(jnp.int32, shape, axis)
 
 
-def params(limit=VMEM_LIMIT, **extra):
-    return pltpu.CompilerParams(vmem_limit_bytes=limit, **extra)
-
-
-def send_kernel(owner_ref, x_ref, out_ref):
-    band_count, width, _ = out_ref.shape
-    for tile in range(x_ref.shape[1] // LANE):
-        first, past = tile * LANE, (tile + 1) * LANE
-        rows = x_ref[:, first:past].T
-        start = first
-        while start < past:
-            block = start // width
-            end = min((block + 1) * width, past)
-            inside = slice(start - block * width, end - block * width)
-            out_ref[owner_ref[block], inside, :] = rows[start - first : end - first, :]
-            start = end
+def params(**extra):
+    return pltpu.CompilerParams(vmem_limit_bytes=VMEM_LIMIT, **extra)
+
+
+def in_hbm(values):
+    return pltpu.with_memory_space_constraint(values, pltpu.HBM)
+
+
+def swap(values, axis, distance):
+    count = lax.axis_size(axis)
+    return lax.ppermute(values, axis, [(source, source ^ distance) for source in range(count)])
+
+
+def send_kernel(owner_hbm_ref, x_hbm_ref, *refs):
+    out_refs, (owner_ref, x_ref, turned_ref, owner_sem, x_sems) = refs[:-5], refs[-5:]
+    band_count, width = len(out_refs), out_refs[0].shape[0]
+    features, columns = x_ref.shape
+    copies = [pltpu.make_async_copy(owner_hbm_ref, owner_ref, owner_sem)]
+    parts = [slice(start, start + LANE) for start in range(0, features, LANE)]
+    for n, part in enumerate(parts):
+        copies.append(pltpu.make_async_copy(x_hbm_ref.at[part, :], x_ref.at[part, :], x_sems.at[n]))
+    for copy in copies:
+        copy.start()
+    for n, part in enumerate(parts):
+        copies[n + 1].wait()
+        for start in range(0, columns, LANE):
+            at = slice(start, start + LANE)
+            turned_ref[at, part] = x_ref[part, at].T
+    copies[0].wait()
+    me = lax.axis_index("band")
+    for k, out_ref in enumerate(out_refs):
+        target = jnp.bitwise_xor(me, k)
+        block = 0
+        for j in range(1, band_count):
+            block = jnp.where(owner_ref[j] == target, j, block)
+        out_ref[...] = turned_ref[pl.ds(pl.multiple_of(block * width, SUB), width), :]
 
 
 def send_blocks(pixels, owner, band_count, width):
     features, columns = pixels.shape
+    any_space = pl.BlockSpec(memory_space=pl.ANY)
     return pl.pallas_call(
         send_kernel,
-        out_shape=jax.ShapeDtypeStruct((band_count, width, features), BF16),
-        grid_spec=pltpu.PrefetchScalarGridSpec(
-            num_scalar_prefetch=1,
-            grid=(features // LANE,),
-            in_specs=[pl.BlockSpec((LANE, columns), lambda f, owner: (f, 0))],
-            out_specs=pl.BlockSpec((band_count, width, LANE), lambda f, owner: (0, 0, f)),
-        ),
-        compiler_params=params(SEND_VMEM_LIMIT),
+        out_shape=[jax.ShapeDtypeStruct((width, features), BF16)] * band_count,
+        in_specs=[any_space, any_space],
+        out_specs=[pl.BlockSpec(memory_space=pltpu.VMEM)] * band_count,
+        scratch_shapes=[
+            pltpu.SMEM(owner.shape, jnp.int32),
+            pltpu.VMEM((features, columns), BF16),
+            pltpu.VMEM((columns, features), BF16),
+            pltpu.SemaphoreType.DMA,
+            pltpu.SemaphoreType.DMA((features // LANE,)),
+        ],
+        compiler_params=params(),
         name="send_blocks",
-    )(owner, pixels)
+    )(in_hbm(owner), in_hbm(pixels))
+
+
+def exchange(pieces):
+    arrived = list(pieces)
+    for k in reversed(range(1, len(pieces))):
+        arrived[k] = swap(pieces[k], "band", k)
+    return arrived
 
 
 def expand_table(table, rows, half_width_padded, half_width, transpose):
@@ -156,7 +187,7 @@
         compiler_params=params(),
         cost_estimate=pl.CostEstimate(flops=flops, bytes_accessed=4 * 2**20, transcendentals=0),
         name="prepare",
-    )(groups, frozen, factors, level_weight, mixer)
+    )(groups, in_hbm(frozen), factors, in_hbm(level_weight), in_hbm(mixer))
 
 
 def normal_parts(values):
@@ -187,7 +218,7 @@
 
 
 def mix_kernel(
-    arrived_ref,
+    piece_refs,
     merged_ref,
     mix_ref,
     mix_t_ref,
@@ -202,16 +233,29 @@
     tokens_ref,
     grad_pre_ref,
     second_ref,
+    arrived_ref,
 ):
     samples, reach, feature_dim = merged_ref.shape
-    _, width, features = arrived_ref.shape
+    _, _, width, features = arrived_ref.shape
     depth = features // samples
     rows = WLAT * width
-    step = pl.program_id(0) * pl.num_programs(1) + pl.program_id(1)
+    half = pl.program_id(1)
+    step = pl.program_id(0) * pl.num_programs(1) + half
+
+    @pl.when(half == 0)
+    def _():
+        for h in range(arrived_ref.shape[0]):
+            within = slice(h * width, (h + 1) * width)
+            if len(piece_refs) == 1:
+                arrived_ref[h] = piece_refs[0][:, within, :]
+            else:
+                me = lax.axis_index("band")
+                for k, piece_ref in enumerate(piece_refs):
+                    arrived_ref[h, jnp.bitwise_xor(me, k)] = piece_ref[within, :]
 
     def forward(s):
         lane = s * depth // LANE * LANE
-        pixels = arrived_ref[:, :, lane : lane + reach].reshape(rows, reach)
+        pixels = arrived_ref[half, :, :, lane : lane + reach].reshape(rows, reach)
         tokens = dot_nn(pixels, merged_ref[s]).astype(BF16)
         tokens_ref[s] = tokens
         pre_ref[s] = dot_nn(mix_ref[...], tokens)
@@ -265,7 +309,7 @@
 def mix_blocks(halves, arrived, merged, mix, mix_t, grad, up_through, down_t, level_weight, reps):
     samples, lat_rows, block_width, feature_dim = grad.shape
     width = block_width // halves
-    lanes = arrived.shape[2]
+    lanes = arrived[0].shape[-1]
     reach = merged.shape[1]
     rows = WLAT * width
     rank, channels = down_t.shape
@@ -274,18 +318,22 @@
         return pl.BlockSpec(shape, lambda w, h: (0,) * len(shape))
 
     block = pl.BlockSpec((samples, WLAT, width, feature_dim), lambda w, h: (0, w, h, 0))
+    if len(arrived) == 1:
+        arrived_specs = [pl.BlockSpec((WLAT, block_width, lanes), lambda w, h: (w, 0, 0))]
+    else:
+        arrived_specs = [whole(piece.shape) for piece in arrived]
     share_shape = (reps, rank, feature_dim // reps + round_up(channels, LANE))
     flops = 2 * samples * lat_rows * block_width * feature_dim * (2 * reach + 2 * rows)
     constants = [up_through, down_t, level_weight]
     return pl.pallas_call(
-        mix_kernel,
+        lambda *refs: mix_kernel(refs[: len(arrived)], *refs[len(arrived) :]),
         out_shape=[
             jax.ShapeDtypeStruct(grad.shape, BF16),
             jax.ShapeDtypeStruct(share_shape, F32),
         ],
         grid=(lat_rows // WLAT, halves),
-        in_specs=[
-            pl.BlockSpec((WLAT, width, lanes), lambda w, h: (w, h, 0)),
+        in_specs=arrived_specs
+        + [
             whole(merged.shape),
             whole(mix.shape),
             whole(mix_t.shape),
@@ -299,6 +347,7 @@
             pltpu.VMEM((samples, rows, feature_dim), BF16),
             pltpu.VMEM((samples, rows, feature_dim), BF16),
             pltpu.VMEM((rank, feature_dim), F32),
+            pltpu.VMEM((halves, WLAT, width, lanes), BF16),
         ],
         compiler_params=params(dimension_semantics=("arbitrary", "arbitrary")),
         cost_estimate=pl.CostEstimate(
@@ -307,12 +356,7 @@
             transcendentals=samples * lat_rows * block_width * feature_dim,
         ),
         name="mix_blocks",
-    )(arrived, merged, mix, mix_t, grad, *constants)
-
-
-def swap(values, axis, distance):
-    count = lax.axis_size(axis)
-    return lax.ppermute(values, axis, [(source, source ^ distance) for source in range(count)])
+    )(*arrived, merged, mix, mix_t, in_hbm(grad), *constants)
 
 
 def sum_shares(shares):
@@ -320,12 +364,8 @@
     while half >= 1:
         shares = shares[:half] + swap(shares[half:], "rep", half)
         half //= 2
-    total = shares[0]
-    distance = 1
-    while distance < lax.axis_size("band"):
-        total = total + swap(total, "band", distance)
-        distance *= 2
-    return total
+    copies = jnp.broadcast_to(shares, (lax.axis_size("band"),) + shares.shape[1:])
+    return jnp.sum(lax.all_to_all(copies, "band", split_axis=0, concat_axis=0, tiled=True), axis=0)
 
 
 def on_device(
@@ -353,8 +393,9 @@
     features = samples * levels * channels
 
     pixels = patches.reshape(features, col_count)
-    if half_padded == half_width and features % LANE == 0 and col_count % LANE == 0:
-        outgoing = send_blocks(pixels, column_block_owner, band_count, block_width)
+    direct = band_count <= MAX_PERMUTES and lat_rows == WLAT and half_padded == half_width
+    if direct and features % LANE == 0 and col_count % LANE == 0:
+        arrived = exchange(send_blocks(pixels, column_block_owner, band_count, block_width))
     else:
         block_ids = jnp.arange(band_count, dtype=jnp.int32)
         inverse = jnp.sum(
@@ -362,7 +403,7 @@
         )
         outgoing = jnp.take(pixels.T.reshape(band_count, block_width, features), inverse, axis=0)
         outgoing = jnp.pad(outgoing, ((0, 0), (0, padded_width - block_width), (0, 0)))
-    arrived = lax.all_to_all(outgoing, "band", split_axis=0, concat_axis=0, tiled=True)
+        arrived = [lax.all_to_all(outgoing, "band", split_axis=0, concat_axis=0, tiled=True)]
 
     pack_width = round_up(max(row_share, col_share), LANE)
     pack = jnp.stack(

time: 68.9 us -> 60.1 us (0.87)
  waiting for transfers between devices: 29.4 us -> 13.7 us
  starting transfers between devices: 10.2 us -> 22.1 us
  local copies, waits for them, and re-layouts: 7.95 us -> 3.3 us
  Pallas kernels: 15 us -> 14 us
    ppermute x5 -> x9, starting transfers between devices: 2.98 us -> 14.5 us  [swap(): lax.ppermute(values, axis, [(source, source ^ distance) for source in ran...]
    ppermute x5 -> x9, waiting for transfers between devices: 14.3 us -> 6.41 us  [swap(): lax.ppermute(values, axis, [(source, source ^ distance) for source in ran...]
    all_to_all x1, waiting for transfers between devices: 15.1 us -> 7.34 us  [sum_shares(): lax.all_to_all(copies, 'band', split_axis=0, concat_axis=0, tiled=True)]
    unnamed x26 -> x4, local copies, waits for them, and re-layouts: 6.66 us -> 0.66 us
    pallas_call x2, Pallas kernels: 13.1 us -> 11.2 us  [the longest x1 9.4 us: mix_blocks(): pl.pallas_call(lambda *refs: mix_kernel(refs[:len(arrived)], *refs[len(ar...]
    pallas_call x1, Pallas kernels: 1.82 us -> 2.88 us  [prepare(): pl.pallas_call(functools.partial(prep_kernel, row_share, half_width, half...]
  transfers between devices with their start and end apart: 6 -> 10, of which waited for: 6 -> 4; matrix products, arithmetic and copies ran while one was open for 0% -> 2% of each run, Pallas kernels for 3% -> 5%
where the time goes in v4:
time: 60.1 us; the launch traced here: 59.8 us
  starting transfers between devices  22.1 us (37%)
  Pallas kernels  14 us (23%)
  waiting for transfers between devices  13.7 us (23%)
  blocking collectives  5.18 us (9%)
  local copies, waits for them, and re-layouts  3.3 us (5%)
  other arithmetic  0.71 us (1%)
  between operations  0.7 us (1%)
    ppermute x9, starting transfers between devices, swap(): lax.ppermute(values, axis, [(source, source ^ distance) for source in ran...  14.5 us
    pallas_call x1, Pallas kernels, mix_blocks(): pl.pallas_call(lambda *refs: mix_kernel(refs[:len(arrived)], *refs[len(ar...  9.4 us
    all_to_all x1, starting transfers between devices, sum_shares(): lax.all_to_all(copies, 'band', split_axis=0, concat_axis=0, tiled=True)  7.57 us
    all_to_all x1, waiting for transfers between devices, sum_shares(): lax.all_to_all(copies, 'band', split_axis=0, concat_axis=0, tiled=True)  7.34 us
    ppermute x9, waiting for transfers between devices, swap(): lax.ppermute(values, axis, [(source, source ^ distance) for source in ran...  6.41 us
    all_gather x1, blocking collectives, on_device(): factors = lax.all_gather(pack, 'rep', axis=0, tiled=False)  5.18 us
    pallas_call x1, Pallas kernels, prepare(): pl.pallas_call(functools.partial(prep_kernel, row_share, half_width, half...  2.88 us
    pallas_call x1, Pallas kernels, send_blocks(): pl.pallas_call(send_kernel, out_shape=[jax.ShapeDtypeStruct((width, featu...  1.76 us
  transfers between devices with their start and end apart: 10, of which 4 were waited for; matrix products, arithmetic and copies ran while one was open for 2% of the time, Pallas kernels for 5%

profile of v4, /device:TPU:0, one launch (start us, length us, event | category | flops | bytes accessed | tf_op | source)
XLA Modules:
  0.0 59.8 jit_solution(15757487479472185862)
XLA Ops:
  0.6 0.0 copy-start
  0.6 1.8 %send_blocks.1 = (bf16[96,640]{1,0:T(8,128)(2,1)S(1)}, bf16[96,640]{1,0:T(8,128)(2,1)S(1)}, bf16[96,640]{1,0:T(8,128)(2,1)S(1)}, bf16[96,640]{1,0:T(8,128)(2,1)S...) custom-call(s32[8]{0:T(128)} %owner_hbm_ref.1, ...), custom_call_target="tpu_custom_call" | custom-call | tf_op jit(solution)/shard_map/send_blocks/pallas_call | solution.py:87
  2.4 3.0 %collective-permute-start = (bf16[96,640]{1,0:T(8,128)(2,1)S(1)}, bf16[96,640]{1,0:T(8,128)(2,1)S(1)}, u32[]{:S(2)}, u32[]{:S(2)}) collective-permute-start(bf16[96,640]{1,0:T(8,128)(2,1)S(1)} %get-tuple-element.19), channel_id=1, source_target_pairs={{0,4},{4,0},{8,12},{12,8},{16,20},{20,16},{24,28},{28,24},{1,5},{5... | collective-permute-start | bytes 368648 | tf_op jit(solution)/shard_map/ppermute | solution.py:56
  5.4 1.6 %collective-permute-start.1 = (bf16[96,640]{1,0:T(8,128)(2,1)S(1)}, bf16[96,640]{1,0:T(8,128)(2,1)S(1)}, u32[]{:S(2)}, u32[]{:S(2)}) collective-permute-start(bf16[96,640]{1,0:T(8,128)(2,1)S(1)} %get-tuple-element.20), channel_id=1, source_target_pairs={{0,8},{4,12},{8,0},{12,4},{16,24},{20,28},{24,16},{28,20},{1,9},{5... | collective-permute-start | bytes 368648 | tf_op jit(solution)/shard_map/ppermute | solution.py:56
  7.0 0.0 collective-permute-start.2
  7.0 3.0 %collective-permute-start.3 = (bf16[96,640]{1,0:T(8,128)(2,1)S(1)}, bf16[96,640]{1,0:T(8,128)(2,1)S(1)}, u32[]{:S(2)}, u32[]{:S(2)}) collective-permute-start(bf16[96,640]{1,0:T(8,128)(2,1)S(1)} %get-tuple-element.22), channel_id=1, source_target_pairs={{0,16},{4,20},{8,24},{12,28},{16,0},{20,4},{24,8},{28,12},{1,17},{... | collective-permute-start | bytes 368648 | tf_op jit(solution)/shard_map/ppermute | solution.py:56
  10.0 1.3 %collective-permute-start.4 = (bf16[96,640]{1,0:T(8,128)(2,1)S(1)}, bf16[96,640]{1,0:T(8,128)(2,1)S(1)}, u32[]{:S(2)}, u32[]{:S(2)}) collective-permute-start(bf16[96,640]{1,0:T(8,128)(2,1)S(1)} %get-tuple-element.23), channel_id=1, source_target_pairs={{0,20},{4,16},{8,28},{12,24},{16,4},{20,0},{24,12},{28,8},{1,21},{... | collective-permute-start | bytes 368648 | tf_op jit(solution)/shard_map/ppermute | solution.py:56
  11.3 0.7 %pad_bitcast_fusion = bf16[1,16,128]{2,1,0:T(8,128)(2,1)S(1)} fusion(bf16[16,20]{1,0:T(8,128)(2,1)} %bitcast.16), kind=kLoop, calls=%fused_computation.5 | loop fusion | bytes 4736 | tf_op jit(solution)/shard_map/stack | solution.py:409
  12.0 0.0 collective-permute-done.refs_1_
  12.0 3.6 %collective-permute-start.5 = (bf16[96,640]{1,0:T(8,128)(2,1)S(1)}, bf16[96,640]{1,0:T(8,128)(2,1)S(1)}, u32[]{:S(2)}, u32[]{:S(2)}) collective-permute-start(bf16[96,640]{1,0:T(8,128)(2,1)S(1)} %get-tuple-element.24), channel_id=1, source_target_pairs={{0,24},{4,28},{8,16},{12,20},{16,8},{20,12},{24,0},{28,4},{1,25},{... | collective-permute-start | bytes 368648 | tf_op jit(solution)/shard_map/ppermute | solution.py:56
  15.6 0.0 collective-permute-done.1.refs_2_
  15.6 0.5 collective-permute-start.6
  16.0 0.7 %pad_maximum_fusion = bf16[2,16,128]{2,1,0:T(8,128)(2,1)S(1)} fusion(bf16[1,16,128]{2,1,0:T(8,128)(2,1)S(1)} %pad_bitcast_fusion, bf16[1,16,128]{2,1,0:T(8,128)(2,1)} %bitcast.17), kind=kLoop, calls=%fused_computation.3 | loop fusion | flops 4096 | bytes 16384 | tf_op jit(solution)/shard_map/stack | solution.py:409
  16.7 5.2 %all-gather = bf16[8,16,128]{2,1,0:T(8,128)(2,1)S(1)} all-gather(bf16[2,16,128]{2,1,0:T(8,128)(2,1)S(1)} %pad_maximum_fusion), channel_id=2, replica_groups=mesh['band'=8,'rep'=4] {'rep'}, dimensions={0}, use_global_device_ids=true | all-gather | bytes 40960 | tf_op jit(solution)/shard_map/all_gather | solution.py:415
  21.9 0.0 copy-start.1
  21.9 0.7 %copy-done.1 = s32[5]{0:T(128)S(1)} copy-done((s32[5]{0:T(128)S(1)}, s32[5]{0:T(128)}, u32[]{:S(2)}) %copy-start.1) | copy-done | bytes 44
  22.5 2.9 %prepare.1 = (bf16[2,384,512]{2,1,0:T(8,128)(2,1)S(1)}, bf16[4,32,512]{2,1,0:T(8,128)(2,1)S(1)}, bf16[16,80]{1,0:T(8,128)(2,1)S(1)}, bf16[384,384]{1,0:T(8,128)(2,1)S(1)}, bf16[384,384]{1,0:T(8,128)(2,1)S(1)}) custom-call(s32[5]{0:T(128)S(1)} %copy-done.1, bf16[3,16,512]{2,1,0:T(8,128)(2,1)} %frozen_ref.1, bf16[4,2,16,128]{3,2,1,0:T(8,128)(2,1)S(1)} %bitcast.14, ...), custom_call_target="tpu_custom_call" | custom-call | flops 257949696 | bytes 4194304 | tf_op jit(solution)/shard_map/prepare/pallas_call | solution.py:176
  25.4 0.0 collective-permute-done.2.refs_3_
  25.4 0.0 collective-permute-done.3.refs_4_
  25.5 2.8 %collective-permute-done.4.refs_5_ = bf16[96,640]{1,0:T(8,128)(2,1)S(1)} collective-permute-done((bf16[96,640]{1,0:T(8,128)(2,1)S(1)}, bf16[96,640]{1,0:T(8,128)(2,1)S(1)}, u32[]{:S(2)}, u32[]{:S(2)}) %collective-permute-start.4) | collective-permute-done | bytes 122912 | tf_op jit(solution)/shard_map/ppermute | solution.py:56
  28.3 0.0 collective-permute-done.5.refs_6_
  28.3 0.0 collective-permute-done.6.refs_7_
  28.3 0.0 copy-done
  28.3 9.4 %mix_blocks.1 = (bf16[2,8,96,512]{3,2,1,0:T(8,128)(2,1)}, f32[4,16,256]{2,1,0:T(8,128)S(1)}) custom-call(bf16[96,640]{1,0:T(8,128)(2,1)S(1)} %get-tuple-element.18.refs_0_, bf16[96,640]{1,0:T(8,128)(2,1)S(1)} %collective-permute-done.refs_1_, bf16[96,640]{1,0:T(8,128)(2,1)S(1)} %collective-permute-done.1.refs_2_, ...), custom_call_target="tpu_custom_call" | custom-call | flops 2415919104 | bytes 12582912 | tf_op jit(solution)/shard_map/mix_blocks/pallas_call | solution.py:328
  37.7 1.5 %collective-permute-start.7 = (f32[2,16,256]{2,1,0:T(8,128)S(1)}, f32[2,16,256]{2,1,0:T(8,128)S(1)}, u32[]{:S(2)}, u32[]{:S(2)}) collective-permute-start(f32[2,16,256]{2,1,0:T(8,128)S(1)} %slice.16), channel_id=1, source_target_pairs={{0,2},{1,3},{2,0},{3,1},{4,6},{5,7},{6,4},{7,5},{8,10},{9,11},{10,... | collective-permute-start | bytes 98312 | tf_op jit(solution)/shard_map/ppermute | solution.py:56
  39.3 2.4 %collective-permute-done.7 = f32[2,16,256]{2,1,0:T(8,128)S(1)} collective-permute-done((f32[2,16,256]{2,1,0:T(8,128)S(1)}, f32[2,16,256]{2,1,0:T(8,128)S(1)}, u32[]{:S(2)}, u32[]{:S(2)}) %collective-permute-start.7) | collective-permute-done | bytes 32800 | tf_op jit(solution)/shard_map/ppermute | solution.py:56
  41.6 0.1 collective-permute-start.8
  41.7 1.2 %collective-permute-done.8 = f32[1,16,256]{2,1,0:T(8,128)S(1)} collective-permute-done((f32[1,16,256]{2,1,0:T(8,128)S(1)}, f32[1,16,256]{2,1,0:T(8,128)S(1)}, u32[]{:S(2)}, u32[]{:S(2)}) %collective-permute-start.8) | collective-permute-done | bytes 16416 | tf_op jit(solution)/shard_map/ppermute | solution.py:56
  42.9 0.7 %broadcast_in_dim.8 = f32[8,16,256]{2,1,0:T(8,128)} broadcast(f32[16,256]{1,0:T(8,128)S(1)} %fusion), dimensions={1,2} | broadcast | bytes 147456 | tf_op jit(solution)/shard_map/broadcast_in_dim | solution.py:367
  43.6 7.6 %all-to-all-start = ((f32[8,16,256]{2,1,0:T(8,128)}), f32[8,16,256]{2,1,0:T(8,128)S(1)}, u32[]{:S(2)}, u32[]{:S(2)}) async-start(f32[8,16,256]{2,1,0:T(8,128)} %broadcast_in_dim.8), calls=%async_computation | async-start | bytes 262144 | tf_op jit(solution)/shard_map/all_to_all | solution.py:368
  51.1 7.3 %all-to-all-done = f32[8,16,256]{2,1,0:T(8,128)S(1)} async-done(((f32[8,16,256]{2,1,0:T(8,128)}), f32[8,16,256]{2,1,0:T(8,128)S(1)}, u32[]{:S(2)}, u32[]{:S(2)}) %all-to-all-start) | async-done | bytes 131104 | tf_op jit(solution)/shard_map/all_to_all | solution.py:368
  58.5 0.6 %slice.22 = f32[16,128]{1,0:T(8,128)} slice(f32[16,256]{1,0:T(8,128)S(1)} %reduce_sum.9), slice={[0:16], [0:128]} | slice | bytes 16384 | tf_op jit(solution)/shard_map/slice | solution.py:441
  59.1 0.7 %dynamic-slice_bitcast_fusion = f32[20,16]{0,1:T(8,128)} fusion(f32[16,256]{1,0:T(8,128)S(1)} %reduce_sum.9, s32[]{:T(128)S(6)} %select_n.3), kind=kLoop, calls=%fused_computation.4 | loop fusion | bytes 2564 | tf_op jit(solution)/shard_map/transpose | solution.py:440
  (5 shorter events, 0.0 us)
Async XLA Ops:
  0.6 27.7 %copy-start = (bf16[4,512,512]{2,1,0:T(8,128)(2,1)S(1)}, bf16[4,512,512]{2,1,0:T(8,128)(2,1)}, u32[]{:S(2)}) copy-start(bf16[4,512,512]{2,1,0:T(8,128)(2,1)} %refs_14_.1) | copy-start | bytes 6291460
  2.4 9.6 %collective-permute-start = (bf16[96,640]{1,0:T(8,128)(2,1)S(1)}, bf16[96,640]{1,0:T(8,128)(2,1)S(1)}, u32[]{:S(2)}, u32[]{:S(2)}) collective-permute-start(bf16[96,640]{1,0:T(8,128)(2,1)S(1)} %get-tuple-element.19), channel_id=1, source_target_pairs={{0,4},{4,0},{8,12},{12,8},{16,20},{20,16},{24,28},{28,24},{1,5},{5... | collective-permute-start | bytes 368648 | tf_op jit(solution)/shard_map/ppermute | solution.py:56
  5.4 10.2 %collective-permute-start.1 = (bf16[96,640]{1,0:T(8,128)(2,1)S(1)}, bf16[96,640]{1,0:T(8,128)(2,1)S(1)}, u32[]{:S(2)}, u32[]{:S(2)}) collective-permute-start(bf16[96,640]{1,0:T(8,128)(2,1)S(1)} %get-tuple-element.20), channel_id=1, source_target_pairs={{0,8},{4,12},{8,0},{12,4},{16,24},{20,28},{24,16},{28,20},{1,9},{5... | collective-permute-start | bytes 368648 | tf_op jit(solution)/shard_map/ppermute | solution.py:56
  7.0 18.4 %collective-permute-start.2 = (bf16[96,640]{1,0:T(8,128)(2,1)S(1)}, bf16[96,640]{1,0:T(8,128)(2,1)S(1)}, u32[]{:S(2)}, u32[]{:S(2)}) collective-permute-start(bf16[96,640]{1,0:T(8,128)(2,1)S(1)} %get-tuple-element.21), channel_id=1, source_target_pairs={{0,12},{4,8},{8,4},{12,0},{16,28},{20,24},{24,20},{28,16},{1,13},{... | collective-permute-start | bytes 368648 | tf_op jit(solution)/shard_map/ppermute | solution.py:56
  7.0 18.4 %collective-permute-start.3 = (bf16[96,640]{1,0:T(8,128)(2,1)S(1)}, bf16[96,640]{1,0:T(8,128)(2,1)S(1)}, u32[]{:S(2)}, u32[]{:S(2)}) collective-permute-start(bf16[96,640]{1,0:T(8,128)(2,1)S(1)} %get-tuple-element.22), channel_id=1, source_target_pairs={{0,16},{4,20},{8,24},{12,28},{16,0},{20,4},{24,8},{28,12},{1,17},{... | collective-permute-start | bytes 368648 | tf_op jit(solution)/shard_map/ppermute | solution.py:56
  10.0 18.3 %collective-permute-start.4 = (bf16[96,640]{1,0:T(8,128)(2,1)S(1)}, bf16[96,640]{1,0:T(8,128)(2,1)S(1)}, u32[]{:S(2)}, u32[]{:S(2)}) collective-permute-start(bf16[96,640]{1,0:T(8,128)(2,1)S(1)} %get-tuple-element.23), channel_id=1, source_target_pairs={{0,20},{4,16},{8,28},{12,24},{16,4},{20,0},{24,12},{28,8},{1,21},{... | collective-permute-start | bytes 368648 | tf_op jit(solution)/shard_map/ppermute | solution.py:56
  12.0 16.3 %collective-permute-start.5 = (bf16[96,640]{1,0:T(8,128)(2,1)S(1)}, bf16[96,640]{1,0:T(8,128)(2,1)S(1)}, u32[]{:S(2)}, u32[]{:S(2)}) collective-permute-start(bf16[96,640]{1,0:T(8,128)(2,1)S(1)} %get-tuple-element.24), channel_id=1, source_target_pairs={{0,24},{4,28},{8,16},{12,20},{16,8},{20,12},{24,0},{28,4},{1,25},{... | collective-permute-start | bytes 368648 | tf_op jit(solution)/shard_map/ppermute | solution.py:56
  15.6 12.7 %collective-permute-start.6 = (bf16[96,640]{1,0:T(8,128)(2,1)S(1)}, bf16[96,640]{1,0:T(8,128)(2,1)S(1)}, u32[]{:S(2)}, u32[]{:S(2)}) collective-permute-start(bf16[96,640]{1,0:T(8,128)(2,1)S(1)} %get-tuple-element.25), channel_id=1, source_target_pairs={{0,28},{4,24},{8,20},{12,16},{16,12},{20,8},{24,4},{28,0},{1,29},{... | collective-permute-start | bytes 368648 | tf_op jit(solution)/shard_map/ppermute | solution.py:56
  21.9 0.7 %copy-start.1 = (s32[5]{0:T(128)S(1)}, s32[5]{0:T(128)}, u32[]{:S(2)}) copy-start(s32[5]{0:T(128)} %group_ref.1) | copy-start | bytes 64
  37.7 3.9 %collective-permute-start.7 = (f32[2,16,256]{2,1,0:T(8,128)S(1)}, f32[2,16,256]{2,1,0:T(8,128)S(1)}, u32[]{:S(2)}, u32[]{:S(2)}) collective-permute-start(f32[2,16,256]{2,1,0:T(8,128)S(1)} %slice.16), channel_id=1, source_target_pairs={{0,2},{1,3},{2,0},{3,1},{4,6},{5,7},{6,4},{7,5},{8,10},{9,11},{10,... | collective-permute-start | bytes 98312 | tf_op jit(solution)/shard_map/ppermute | solution.py:56
  41.6 1.2 %collective-permute-start.8 = (f32[1,16,256]{2,1,0:T(8,128)S(1)}, f32[1,16,256]{2,1,0:T(8,128)S(1)}, u32[]{:S(2)}, u32[]{:S(2)}) collective-permute-start(f32[1,16,256]{2,1,0:T(8,128)S(1)} %slice.21), channel_id=1, source_target_pairs={{0,1},{1,0},{2,3},{3,2},{4,5},{5,4},{6,7},{7,6},{8,9},{9,8},{10,11... | collective-permute-start | bytes 49160 | tf_op jit(solution)/shard_map/ppermute | solution.py:56
  43.6 14.9 %all-to-all-start = ((f32[8,16,256]{2,1,0:T(8,128)}), f32[8,16,256]{2,1,0:T(8,128)S(1)}, u32[]{:S(2)}, u32[]{:S(2)}) async-start(f32[8,16,256]{2,1,0:T(8,128)} %broadcast_in_dim.8), calls=%async_computation | async-start | bytes 262144 | tf_op jit(solution)/shard_map/all_to_all | solution.py:368

commit v5 on v4

--- a/solution.py
+++ b/solution.py
@@ -13,6 +13,7 @@
 SUB = 16
 VMEM_LIMIT = 24 * 1024 * 1024
 MAX_PERMUTES = 8
+FOLDS = 2
 BF16 = jnp.bfloat16
 F32 = jnp.float32
 
@@ -54,6 +55,11 @@
 def swap(values, axis, distance):
     count = lax.axis_size(axis)
     return lax.ppermute(values, axis, [(source, source ^ distance) for source in range(count)])
+
+
+def distances(band_count):
+    half = band_count // 2
+    return [0] + [k for pair in zip(range(half, band_count), range(1, half)) for k in pair] + [band_count - 1]
 
 
 def send_kernel(owner_hbm_ref, x_hbm_ref, *refs):
@@ -73,7 +79,7 @@
             turned_ref[at, part] = x_ref[part, at].T
     copies[0].wait()
     me = lax.axis_index("band")
-    for k, out_ref in enumerate(out_refs):
+    for k, out_ref in zip(distances(band_count), out_refs):
         target = jnp.bitwise_xor(me, k)
         block = 0
         for j in range(1, band_count):
@@ -102,10 +108,7 @@
 
 
 def exchange(pieces):
-    arrived = list(pieces)
-    for k in reversed(range(1, len(pieces))):
-        arrived[k] = swap(pieces[k], "band", k)
-    return arrived
+    return [piece if k == 0 else swap(piece, "band", k) for k, piece in zip(distances(len(pieces)), pieces)]
 
 
 def expand_table(table, rows, half_width_padded, half_width, transpose):
@@ -191,8 +194,10 @@
 
 
 def normal_parts(values):
-    bell = jnp.exp(-0.5 * values * values)
-    t = 1.0 / (1.0 + 0.23164189 * jnp.abs(values))
+    bell = jnp.exp2(values * values * -0.7213475204444817)
+    scaled = 1.0 + 0.23164189 * jnp.abs(values)
+    t = pl.reciprocal(scaled, approx=True)
+    t = t * (2.0 - scaled * t)
     tail = t * (
         0.127414796 + t * (-0.142248368 + t * (0.7107068705 + t * (-0.7265760135 + t * 0.5307027145)))
     )
@@ -232,7 +237,6 @@
     pre_ref,
     tokens_ref,
     grad_pre_ref,
-    second_ref,
     arrived_ref,
 ):
     samples, reach, feature_dim = merged_ref.shape
@@ -250,7 +254,7 @@
                 arrived_ref[h] = piece_refs[0][:, within, :]
             else:
                 me = lax.axis_index("band")
-                for k, piece_ref in enumerate(piece_refs):
+                for k, piece_ref in zip(distances(len(piece_refs)), piece_refs):
                     arrived_ref[h, jnp.bitwise_xor(me, k)] = piece_ref[within, :]
 
     def forward(s):
@@ -295,18 +299,28 @@
     @pl.when(step == pl.num_programs(0) * pl.num_programs(1) - 1)
     def _():
         first, second = factor_shares(total_ref[...], up_ref, down_ref, level_ref)
-        second_ref[...] = second
-        reps, channels = share_ref.shape[0], down_ref.shape[1]
-        columns = feature_dim // reps
-        me = lax.axis_index("rep")
-        share_ref[...] = jnp.zeros_like(share_ref)
-        for k in range(reps):
-            lane = pl.multiple_of(jnp.bitwise_xor(me, k) * columns, LANE)
-            share_ref[k, :, :columns] = second_ref[:, pl.ds(lane, columns)]
-            share_ref[k, :, columns : columns + channels] = first
-
-
-def mix_blocks(halves, arrived, merged, mix, mix_t, grad, up_through, down_t, level_weight, reps):
+        rank, channels = down_ref.shape
+        columns = share_ref.shape[2]
+        reps = feature_dim // columns
+        folds = rank // (share_ref.shape[1] - rank)
+        depth_rows, fold_lanes, row_share = rank // folds, columns // folds, channels // reps
+        packed = jnp.zeros((depth_rows, feature_dim), F32)
+        row, lane = iota2((channels, feature_dim), 0), iota2((channels, feature_dim), 1)
+        rep, lane = lane // columns, lane % columns
+        for fold in range(folds):
+            inside = lane - fold * fold_lanes
+            pick = (row == inside + rep * row_share) & (inside >= 0) & (inside < row_share)
+            pick = jnp.where(pick, 1.0, 0.0).astype(BF16)
+            packed = packed + dot_nn(
+                first[fold * depth_rows : (fold + 1) * depth_rows].astype(BF16), pick
+            )
+        payload = jnp.concatenate([second, packed], axis=0).astype(BF16)
+        for slot in range(share_ref.shape[0]):
+            at = slot % reps * columns
+            share_ref[slot] = payload[:, at : at + columns]
+
+
+def mix_blocks(halves, arrived, merged, mix, mix_t, grad, up_through, down_t, level_weight, band_count, reps):
     samples, lat_rows, block_width, feature_dim = grad.shape
     width = block_width // halves
     lanes = arrived[0].shape[-1]
@@ -322,14 +336,14 @@
         arrived_specs = [pl.BlockSpec((WLAT, block_width, lanes), lambda w, h: (w, 0, 0))]
     else:
         arrived_specs = [whole(piece.shape) for piece in arrived]
-    share_shape = (reps, rank, feature_dim // reps + round_up(channels, LANE))
+    share_shape = (band_count * reps, rank + rank // FOLDS, feature_dim // reps)
     flops = 2 * samples * lat_rows * block_width * feature_dim * (2 * reach + 2 * rows)
     constants = [up_through, down_t, level_weight]
     return pl.pallas_call(
         lambda *refs: mix_kernel(refs[: len(arrived)], *refs[len(arrived) :]),
         out_shape=[
             jax.ShapeDtypeStruct(grad.shape, BF16),
-            jax.ShapeDtypeStruct(share_shape, F32),
+            jax.ShapeDtypeStruct(share_shape, BF16),
         ],
         grid=(lat_rows // WLAT, halves),
         in_specs=arrived_specs
@@ -346,7 +360,6 @@
             pltpu.VMEM((samples, rows, feature_dim), F32),
             pltpu.VMEM((samples, rows, feature_dim), BF16),
             pltpu.VMEM((samples, rows, feature_dim), BF16),
-            pltpu.VMEM((rank, feature_dim), F32),
             pltpu.VMEM((halves, WLAT, width, lanes), BF16),
         ],
         compiler_params=params(dimension_semantics=("arbitrary", "arbitrary")),
@@ -359,13 +372,29 @@
     )(*arrived, merged, mix, mix_t, in_hbm(grad), *constants)
 
 
-def sum_shares(shares):
-    half = shares.shape[0] // 2
-    while half >= 1:
-        shares = shares[:half] + swap(shares[half:], "rep", half)
-        half //= 2
-    copies = jnp.broadcast_to(shares, (lax.axis_size("band"),) + shares.shape[1:])
-    return jnp.sum(lax.all_to_all(copies, "band", split_axis=0, concat_axis=0, tiled=True), axis=0)
+def sum_kernel(parts_ref, first_ref, second_ref):
+    rank, row_share = first_ref.shape
+    total = parts_ref[0].astype(F32)
+    for n in range(1, parts_ref.shape[0]):
+        total = total + parts_ref[n].astype(F32)
+    second_ref[...] = total[:rank]
+    depth_rows = total.shape[0] - rank
+    for fold in range(rank // depth_rows):
+        lane = fold * depth_rows * total.shape[1] // rank
+        first_ref[fold * depth_rows : (fold + 1) * depth_rows, :] = total[rank:, lane : lane + row_share]
+
+
+def sum_shares(shares, rank, row_share):
+    parts = lax.all_to_all(shares, ("band", "rep"), split_axis=0, concat_axis=0, tiled=True)
+    return pl.pallas_call(
+        sum_kernel,
+        out_shape=[
+            jax.ShapeDtypeStruct((rank, row_share), F32),
+            jax.ShapeDtypeStruct((rank, shares.shape[2]), F32),
+        ],
+        compiler_params=params(),
+        name="sum_shares",
+    )(parts)
 
 
 def on_device(
@@ -428,18 +457,12 @@
     if padded_width != block_width:
         grad = jnp.pad(grad, ((0, 0), (0, 0), (0, padded_width - block_width), (0, 0)))
     mixed, shares = mix_blocks(
-        halves, arrived, merged, mix, mix_t, grad, up_through, down_t, level_merge_weight, reps
+        halves, arrived, merged, mix, mix_t, grad, up_through, down_t, level_merge_weight, band_count, reps
     )
     if padded_width != block_width:
         mixed = mixed[:, :, :block_width]
-
-    summed = sum_shares(shares)
-    first_t = lax.dynamic_slice_in_dim(summed, col_share + lax.axis_index("rep") * row_share, row_share, 1)
-    return (
-        mixed.reshape(mixed_token_gradient.shape),
-        first_t.T,
-        summed[:, :col_share],
-    )
+    first_t, second = sum_shares(shares, rank, row_share)
+    return mixed.reshape(mixed_token_gradient.shape), first_t.T, second
 
 
 def solution(mesh):

time: 60.1 us -> 54.4 us (0.905)
  blocking collectives: 5.18 us -> 17.2 us
  waiting for transfers between devices: 13.7 us -> 3.46 us
  starting transfers between devices: 22.1 us -> 15.5 us
  local copies, waits for them, and re-layouts: 3.3 us -> 1.35 us
  Pallas kernels: 14 us -> 15 us
    all_to_all x0 -> x1, blocking collectives: none -> 12 us  [sum_shares(): lax.all_to_all(shares, ('band', 'rep'), split_axis=0, concat_axis=0, tile...]
    all_to_all x1 -> x0, starting transfers between devices: 7.57 us -> none  [sum_shares(): lax.all_to_all(copies, 'band', split_axis=0, concat_axis=0, tiled=True)]
    all_to_all x1 -> x0, waiting for transfers between devices: 7.34 us -> none  [sum_shares(): lax.all_to_all(copies, 'band', split_axis=0, concat_axis=0, tiled=True)]
    ppermute x9 -> x7, waiting for transfers between devices: 6.41 us -> 3.46 us  [swap(): lax.ppermute(values, axis, [(source, source ^ distance) for source in ran...]
    ppermute x9 -> x7, starting transfers between devices: 14.5 us -> 15.5 us  [swap(): lax.ppermute(values, axis, [(source, source ^ distance) for source in ran...]
    pallas_call x0 -> x1, Pallas kernels: none -> 0.7 us  [sum_shares(): pl.pallas_call(sum_kernel, out_shape=[jax.ShapeDtypeStruct((rank, row_sha...]
    transpose x1 -> x0, local copies, waits for them, and re-layouts: 0.67 us -> none  [on_device(): return (mixed.reshape(mixed_token_gradient.shape), first_t.T, summed[:, :...]
    broadcast_in_dim x1 -> x0, local copies, waits for them, and re-layouts: 0.66 us -> none  [sum_shares(): jnp.broadcast_to(shares, (lax.axis_size('band'),) + shares.shape[1:])]
  transfers between devices with their start and end apart: 10 -> 7, of which waited for: 4 -> 1; matrix products, arithmetic and copies ran while one was open for 2% -> 3% of each run, Pallas kernels for 5% -> 5%
where the time goes in v5:
time: 54.4 us; the launch traced here: 53.9 us
  blocking collectives  17.2 us (32%)
  starting transfers between devices  15.5 us (28%)
  Pallas kernels  15 us (28%)
  waiting for transfers between devices  3.46 us (6%)
  local copies, waits for them, and re-layouts  1.35 us (2%)
  between operations  0.71 us (1%)
  other arithmetic  0.69 us (1%)
    ppermute x7, starting transfers between devices, swap(): lax.ppermute(values, axis, [(source, source ^ distance) for source in ran...  15.5 us
    all_to_all x1, blocking collectives, sum_shares(): lax.all_to_all(shares, ('band', 'rep'), split_axis=0, concat_axis=0, tile...  12 us
    pallas_call x1, Pallas kernels, mix_blocks(): pl.pallas_call(lambda *refs: mix_kernel(refs[:len(arrived)], *refs[len(ar...  9.66 us
    all_gather x1, blocking collectives, on_device(): factors = lax.all_gather(pack, 'rep', axis=0, tiled=False)  5.18 us
    ppermute x7, waiting for transfers between devices, swap(): lax.ppermute(values, axis, [(source, source ^ distance) for source in ran...  3.46 us
    pallas_call x1, Pallas kernels, prepare(): pl.pallas_call(functools.partial(prep_kernel, row_share, half_width, half...  2.88 us
    pallas_call x1, Pallas kernels, send_blocks(): pl.pallas_call(send_kernel, out_shape=[jax.ShapeDtypeStruct((width, featu...  1.76 us
  transfers between devices with their start and end apart: 7, of which 1 were waited for; matrix products, arithmetic and copies ran while one was open for 3% of the time, Pallas kernels for 5%

profile of v5, /device:TPU:0, one launch (start us, length us, event | category | flops | bytes accessed | tf_op | source)
XLA Modules:
  0.0 53.9 jit_solution(15710553601975321092)
XLA Ops:
  0.6 0.0 copy-start
  0.6 1.8 %send_blocks.1 = (bf16[96,640]{1,0:T(8,128)(2,1)S(1)}, bf16[96,640]{1,0:T(8,128)(2,1)S(1)}, bf16[96,640]{1,0:T(8,128)(2,1)S(1)}, bf16[96,640]{1,0:T(8,128)(2,1)S...) custom-call(s32[8]{0:T(128)} %owner_hbm_ref.1, ...), custom_call_target="tpu_custom_call" | custom-call | tf_op jit(solution)/shard_map/send_blocks/pallas_call | solution.py:93
  2.4 4.1 %collective-permute-start = (bf16[96,640]{1,0:T(8,128)(2,1)S(1)}, bf16[96,640]{1,0:T(8,128)(2,1)S(1)}, u32[]{:S(2)}, u32[]{:S(2)}) collective-permute-start(bf16[96,640]{1,0:T(8,128)(2,1)S(1)} %get-tuple-element.21), channel_id=1, source_target_pairs={{0,16},{4,20},{8,24},{12,28},{16,0},{20,4},{24,8},{28,12},{1,17},{... | collective-permute-start | bytes 368648 | tf_op jit(solution)/shard_map/ppermute | solution.py:57
  6.5 1.5 %collective-permute-start.1 = (bf16[96,640]{1,0:T(8,128)(2,1)S(1)}, bf16[96,640]{1,0:T(8,128)(2,1)S(1)}, u32[]{:S(2)}, u32[]{:S(2)}) collective-permute-start(bf16[96,640]{1,0:T(8,128)(2,1)S(1)} %get-tuple-element.22), channel_id=1, source_target_pairs={{0,4},{4,0},{8,12},{12,8},{16,20},{20,16},{24,28},{28,24},{1,5},{5... | collective-permute-start | bytes 368648 | tf_op jit(solution)/shard_map/ppermute | solution.py:57
  8.0 0.0 collective-permute-start.2
  8.1 1.8 %collective-permute-start.3 = (bf16[96,640]{1,0:T(8,128)(2,1)S(1)}, bf16[96,640]{1,0:T(8,128)(2,1)S(1)}, u32[]{:S(2)}, u32[]{:S(2)}) collective-permute-start(bf16[96,640]{1,0:T(8,128)(2,1)S(1)} %get-tuple-element.24), channel_id=1, source_target_pairs={{0,8},{4,12},{8,0},{12,4},{16,24},{20,28},{24,16},{28,20},{1,9},{5... | collective-permute-start | bytes 368648 | tf_op jit(solution)/shard_map/ppermute | solution.py:57
  9.9 2.5 %collective-permute-start.4 = (bf16[96,640]{1,0:T(8,128)(2,1)S(1)}, bf16[96,640]{1,0:T(8,128)(2,1)S(1)}, u32[]{:S(2)}, u32[]{:S(2)}) collective-permute-start(bf16[96,640]{1,0:T(8,128)(2,1)S(1)} %get-tuple-element.25), channel_id=1, source_target_pairs={{0,24},{4,28},{8,16},{12,20},{16,8},{20,12},{24,0},{28,4},{1,25},{... | collective-permute-start | bytes 368648 | tf_op jit(solution)/shard_map/ppermute | solution.py:57
  12.4 0.7 %pad_bitcast_fusion = bf16[1,16,128]{2,1,0:T(8,128)(2,1)S(1)} fusion(bf16[16,20]{1,0:T(8,128)(2,1)} %bitcast.13), kind=kLoop, calls=%fused_computation.1 | loop fusion | bytes 4736 | tf_op jit(solution)/shard_map/stack | solution.py:438
  13.1 3.4 %collective-permute-done.refs_1_ = bf16[96,640]{1,0:T(8,128)(2,1)S(1)} collective-permute-done((bf16[96,640]{1,0:T(8,128)(2,1)S(1)}, bf16[96,640]{1,0:T(8,128)(2,1)S(1)}, u32[]{:S(2)}, u32[]{:S(2)}) %collective-permute-start) | collective-permute-done | bytes 122912 | tf_op jit(solution)/shard_map/ppermute | solution.py:57
  16.5 1.3 %collective-permute-start.5 = (bf16[96,640]{1,0:T(8,128)(2,1)S(1)}, bf16[96,640]{1,0:T(8,128)(2,1)S(1)}, u32[]{:S(2)}, u32[]{:S(2)}) collective-permute-start(bf16[96,640]{1,0:T(8,128)(2,1)S(1)} %get-tuple-element.26), channel_id=1, source_target_pairs={{0,12},{4,8},{8,4},{12,0},{16,28},{20,24},{24,20},{28,16},{1,13},{... | collective-permute-start | bytes 368648 | tf_op jit(solution)/shard_map/ppermute | solution.py:57
  17.8 0.0 collective-permute-done.1.refs_2_
  17.8 4.2 %collective-permute-start.6 = (bf16[96,640]{1,0:T(8,128)(2,1)S(1)}, bf16[96,640]{1,0:T(8,128)(2,1)S(1)}, u32[]{:S(2)}, u32[]{:S(2)}) collective-permute-start(bf16[96,640]{1,0:T(8,128)(2,1)S(1)} %get-tuple-element.27), channel_id=1, source_target_pairs={{0,28},{4,24},{8,20},{12,16},{16,12},{20,8},{24,4},{28,0},{1,29},{... | collective-permute-start | bytes 368648 | tf_op jit(solution)/shard_map/ppermute | solution.py:57
  22.0 0.7 %pad_maximum_fusion = bf16[2,16,128]{2,1,0:T(8,128)(2,1)S(1)} fusion(bf16[1,16,128]{2,1,0:T(8,128)(2,1)S(1)} %pad_bitcast_fusion, bf16[1,16,128]{2,1,0:T(8,128)(2,1)} %bitcast.14), kind=kLoop, calls=%fused_computation | loop fusion | flops 4096 | bytes 16384 | tf_op jit(solution)/shard_map/stack | solution.py:438
  22.7 5.2 %all-gather = bf16[8,16,128]{2,1,0:T(8,128)(2,1)S(1)} all-gather(bf16[2,16,128]{2,1,0:T(8,128)(2,1)S(1)} %pad_maximum_fusion), channel_id=2, replica_groups=mesh['band'=8,'rep'=4] {'rep'}, dimensions={0}, use_global_device_ids=true | all-gather | bytes 40960 | tf_op jit(solution)/shard_map/all_gather | solution.py:444
  27.9 0.0 copy-start.1
  27.9 0.7 %copy-done.1 = s32[5]{0:T(128)S(1)} copy-done((s32[5]{0:T(128)S(1)}, s32[5]{0:T(128)}, u32[]{:S(2)}) %copy-start.1) | copy-done | bytes 44
  28.6 2.9 %prepare.1 = (bf16[2,384,512]{2,1,0:T(8,128)(2,1)S(1)}, bf16[4,32,512]{2,1,0:T(8,128)(2,1)S(1)}, bf16[16,80]{1,0:T(8,128)(2,1)S(1)}, bf16[384,384]{1,0:T(8,128)(2,1)S(1)}, bf16[384,384]{1,0:T(8,128)(2,1)S(1)}) custom-call(s32[5]{0:T(128)S(1)} %copy-done.1, bf16[3,16,512]{2,1,0:T(8,128)(2,1)} %frozen_ref.1, bf16[4,2,16,128]{3,2,1,0:T(8,128)(2,1)S(1)} %bitcast.11, ...), custom_call_target="tpu_custom_call" | custom-call | flops 257949696 | bytes 4194304 | tf_op jit(solution)/shard_map/prepare/pallas_call | solution.py:179
  31.5 0.0 collective-permute-done.2.refs_3_
  31.5 0.0 collective-permute-done.3.refs_4_
  31.5 0.0 collective-permute-done.4.refs_5_
  31.5 0.0 collective-permute-done.5.refs_6_
  31.5 0.0 collective-permute-done.6.refs_7_
  31.5 0.0 copy-done
  31.5 9.7 %mix_blocks.1 = (bf16[2,8,96,512]{3,2,1,0:T(8,128)(2,1)}, bf16[32,24,128]{2,1,0:T(8,128)(2,1)S(1)}) custom-call(bf16[96,640]{1,0:T(8,128)(2,1)S(1)} %get-tuple-element.20.refs_0_, bf16[96,640]{1,0:T(8,128)(2,1)S(1)} %collective-permute-done.refs_1_, bf16[96,640]{1,0:T(8,128)(2,1)S(1)} %collective-permute-done.1.refs_2_, ...), custom_call_target="tpu_custom_call" | custom-call | flops 2415919104 | bytes 12582912 | tf_op jit(solution)/shard_map/mix_blocks/pallas_call | solution.py:342
  41.2 12.0 %all_to_all.5.parts_ref = bf16[32,24,128]{2,1,0:T(8,128)(2,1)S(1)} all-to-all(bf16[32,24,128]{2,1,0:T(8,128)(2,1)S(1)} %get-tuple-element.34), channel_id=1, replica_groups=mesh['band'=8,'rep'=4] {'band','rep'}, dimensions={0} | all-to-all | bytes 393216 | tf_op jit(solution)/shard_map/all_to_all | solution.py:388
  53.2 0.7 %sum_shares.1 = (f32[16,20]{1,0:T(8,128)}, f32[16,128]{1,0:T(8,128)}) custom-call(bf16[32,24,128]{2,1,0:T(8,128)(2,1)S(1)} %all_to_all.5.parts_ref), custom_call_target="tpu_custom_call" | custom-call | tf_op jit(solution)/shard_map/sum_shares/pallas_call | solution.py:389
Async XLA Ops:
  0.6 30.9 %copy-start = (bf16[4,512,512]{2,1,0:T(8,128)(2,1)S(1)}, bf16[4,512,512]{2,1,0:T(8,128)(2,1)}, u32[]{:S(2)}) copy-start(bf16[4,512,512]{2,1,0:T(8,128)(2,1)} %refs_14_.1) | copy-start | bytes 6291460
  2.4 14.1 %collective-permute-start = (bf16[96,640]{1,0:T(8,128)(2,1)S(1)}, bf16[96,640]{1,0:T(8,128)(2,1)S(1)}, u32[]{:S(2)}, u32[]{:S(2)}) collective-permute-start(bf16[96,640]{1,0:T(8,128)(2,1)S(1)} %get-tuple-element.21), channel_id=1, source_target_pairs={{0,16},{4,20},{8,24},{12,28},{16,0},{20,4},{24,8},{28,12},{1,17},{... | collective-permute-start | bytes 368648 | tf_op jit(solution)/shard_map/ppermute | solution.py:57
  6.5 11.3 %collective-permute-start.1 = (bf16[96,640]{1,0:T(8,128)(2,1)S(1)}, bf16[96,640]{1,0:T(8,128)(2,1)S(1)}, u32[]{:S(2)}, u32[]{:S(2)}) collective-permute-start(bf16[96,640]{1,0:T(8,128)(2,1)S(1)} %get-tuple-element.22), channel_id=1, source_target_pairs={{0,4},{4,0},{8,12},{12,8},{16,20},{20,16},{24,28},{28,24},{1,5},{5... | collective-permute-start | bytes 368648 | tf_op jit(solution)/shard_map/ppermute | solution.py:57
  8.0 23.4 %collective-permute-start.2 = (bf16[96,640]{1,0:T(8,128)(2,1)S(1)}, bf16[96,640]{1,0:T(8,128)(2,1)S(1)}, u32[]{:S(2)}, u32[]{:S(2)}) collective-permute-start(bf16[96,640]{1,0:T(8,128)(2,1)S(1)} %get-tuple-element.23), channel_id=1, source_target_pairs={{0,20},{4,16},{8,28},{12,24},{16,4},{20,0},{24,12},{28,8},{1,21},{... | collective-permute-start | bytes 368648 | tf_op jit(solution)/shard_map/ppermute | solution.py:57
  8.1 23.4 %collective-permute-start.3 = (bf16[96,640]{1,0:T(8,128)(2,1)S(1)}, bf16[96,640]{1,0:T(8,128)(2,1)S(1)}, u32[]{:S(2)}, u32[]{:S(2)}) collective-permute-start(bf16[96,640]{1,0:T(8,128)(2,1)S(1)} %get-tuple-element.24), channel_id=1, source_target_pairs={{0,8},{4,12},{8,0},{12,4},{16,24},{20,28},{24,16},{28,20},{1,9},{5... | collective-permute-start | bytes 368648 | tf_op jit(solution)/shard_map/ppermute | solution.py:57
  9.9 21.6 %collective-permute-start.4 = (bf16[96,640]{1,0:T(8,128)(2,1)S(1)}, bf16[96,640]{1,0:T(8,128)(2,1)S(1)}, u32[]{:S(2)}, u32[]{:S(2)}) collective-permute-start(bf16[96,640]{1,0:T(8,128)(2,1)S(1)} %get-tuple-element.25), channel_id=1, source_target_pairs={{0,24},{4,28},{8,16},{12,20},{16,8},{20,12},{24,0},{28,4},{1,25},{... | collective-permute-start | bytes 368648 | tf_op jit(solution)/shard_map/ppermute | solution.py:57
  16.5 15.0 %collective-permute-start.5 = (bf16[96,640]{1,0:T(8,128)(2,1)S(1)}, bf16[96,640]{1,0:T(8,128)(2,1)S(1)}, u32[]{:S(2)}, u32[]{:S(2)}) collective-permute-start(bf16[96,640]{1,0:T(8,128)(2,1)S(1)} %get-tuple-element.26), channel_id=1, source_target_pairs={{0,12},{4,8},{8,4},{12,0},{16,28},{20,24},{24,20},{28,16},{1,13},{... | collective-permute-start | bytes 368648 | tf_op jit(solution)/shard_map/ppermute | solution.py:57
  17.8 13.7 %collective-permute-start.6 = (bf16[96,640]{1,0:T(8,128)(2,1)S(1)}, bf16[96,640]{1,0:T(8,128)(2,1)S(1)}, u32[]{:S(2)}, u32[]{:S(2)}) collective-permute-start(bf16[96,640]{1,0:T(8,128)(2,1)S(1)} %get-tuple-element.27), channel_id=1, source_target_pairs={{0,28},{4,24},{8,20},{12,16},{16,12},{20,8},{24,4},{28,0},{1,29},{... | collective-permute-start | bytes 368648 | tf_op jit(solution)/shard_map/ppermute | solution.py:57
  27.9 0.7 %copy-start.1 = (s32[5]{0:T(128)S(1)}, s32[5]{0:T(128)}, u32[]{:S(2)}) copy-start(s32[5]{0:T(128)} %group_ref.1) | copy-start | bytes 64

commit v6 on v5

--- a/solution.py
+++ b/solution.py
@@ -59,7 +59,7 @@
 
 def distances(band_count):
     half = band_count // 2
-    return [0] + [k for pair in zip(range(half, band_count), range(1, half)) for k in pair] + [band_count - 1]
+    return [0] + list(range(half, band_count)) + list(range(2, half)) + [1]
 
 
 def send_kernel(owner_hbm_ref, x_hbm_ref, *refs):
@@ -107,8 +107,13 @@
     )(in_hbm(owner), in_hbm(pixels))
 
 
-def exchange(pieces):
-    return [piece if k == 0 else swap(piece, "band", k) for k, piece in zip(distances(len(pieces)), pieces)]
+def exchange(pieces, factors):
+    far = len(pieces) - 2
+    late = lax.optimization_barrier((factors, *pieces[far:]))
+    factors, pieces = late[0], list(pieces[:far]) + list(late[1:])
+    return factors, [
+        piece if k == 0 else swap(piece, "band", k) for k, piece in zip(distances(len(pieces)), pieces)
+    ]
 
 
 def expand_table(table, rows, half_width_padded, half_width, transpose):
@@ -227,97 +232,118 @@
     merged_ref,
     mix_ref,
     mix_t_ref,
-    grad_ref,
     up_ref,
     down_ref,
+    grad_hbm_ref,
+    level_hbm_ref,
+    mixed_hbm_ref,
+    share_ref,
+    arrived_ref,
+    grad_ref,
+    mixed_ref,
     level_ref,
-    mixed_ref,
-    share_ref,
     total_ref,
     pre_ref,
     tokens_ref,
     grad_pre_ref,
-    arrived_ref,
+    grad_sems,
+    mixed_sems,
+    level_sem,
 ):
     samples, reach, feature_dim = merged_ref.shape
-    _, _, width, features = arrived_ref.shape
-    depth = features // samples
+    chunk_count, _, width, _ = grad_ref.shape
+    halves = piece_refs[0].shape[-2] // width
+    depth = piece_refs[0].shape[-1] // samples
     rows = WLAT * width
-    half = pl.program_id(1)
-    step = pl.program_id(0) * pl.num_programs(1) + half
-
-    @pl.when(half == 0)
-    def _():
-        for h in range(arrived_ref.shape[0]):
-            within = slice(h * width, (h + 1) * width)
-            if len(piece_refs) == 1:
-                arrived_ref[h] = piece_refs[0][:, within, :]
-            else:
-                me = lax.axis_index("band")
-                for k, piece_ref in zip(distances(len(piece_refs)), piece_refs):
-                    arrived_ref[h, jnp.bitwise_xor(me, k)] = piece_ref[within, :]
-
-    def forward(s):
-        lane = s * depth // LANE * LANE
-        pixels = arrived_ref[half, :, :, lane : lane + reach].reshape(rows, reach)
-        tokens = dot_nn(pixels, merged_ref[s]).astype(BF16)
-        tokens_ref[s] = tokens
-        pre_ref[s] = dot_nn(mix_ref[...], tokens)
-        return pixels
-
-    def pointwise(s):
+
+    def place(n):
+        window_row, half, s = n // (halves * samples), n // samples % halves, n % samples
+        lines, columns = pl.ds(window_row * WLAT, WLAT), pl.ds(half * width, width)
+        return window_row, half, s, (s, lines, columns)
+
+    loads = [
+        pltpu.make_async_copy(grad_hbm_ref.at[place(n)[3]], grad_ref.at[n], grad_sems.at[n])
+        for n in range(chunk_count)
+    ]
+    stores = [
+        pltpu.make_async_copy(mixed_ref.at[n], mixed_hbm_ref.at[place(n)[3]], mixed_sems.at[n])
+        for n in range(chunk_count)
+    ]
+    level_load = pltpu.make_async_copy(level_hbm_ref, level_ref, level_sem)
+    for load in loads:
+        load.start()
+    level_load.start()
+    if len(piece_refs) > 1:
+        me = lax.axis_index("band")
+        for k, piece_ref in zip(distances(len(piece_refs)), piece_refs):
+            for half in range(halves):
+                within = slice(half * width, (half + 1) * width)
+                arrived_ref[half, jnp.bitwise_xor(me, k)] = piece_ref[within, :]
+
+    def pixels_of(n):
+        window_row, half, s, _ = place(n)
+        lanes = slice(s * depth // LANE * LANE, s * depth // LANE * LANE + reach)
+        if len(piece_refs) > 1:
+            block = arrived_ref[half, :, :, lanes]
+        else:
+            lines = slice(window_row * WLAT, (window_row + 1) * WLAT)
+            block = piece_refs[0][lines, half * width : (half + 1) * width, lanes]
+        return block.reshape(rows, reach)
+
+    def forward(n):
+        tokens = dot_nn(pixels_of(n), merged_ref[n % samples]).astype(BF16)
+        tokens_ref[n] = tokens
+        pre_ref[n] = dot_nn(mix_ref[...], tokens)
+
+    def pointwise(n):
+        loads[n].wait()
         for line in range(WLAT):
             for start in range(0, width, SUB):
                 at, within = pl.ds(line * width + start, SUB), pl.ds(start, SUB)
-                pre = pre_ref[s, at, :]
+                pre = pre_ref[n, at, :]
                 cdf, pdf = normal_parts(pre)
-                tokens = tokens_ref[s, at, :].astype(F32)
-                mixed_ref[s, line, within, :] = (tokens + pre * cdf).astype(BF16)
-                grad = grad_ref[s, line, within, :].astype(F32)
-                grad_pre_ref[s, at, :] = (grad * (cdf + pre * pdf)).astype(BF16)
-
-    def backward(s, pixels):
-        direct = grad_ref[s].reshape(rows, feature_dim).astype(F32)
-        grad_tokens = dot_nn(mix_t_ref[...], grad_pre_ref[s]) + direct
-        offset = s * depth % LANE
-        return dot_tn(pixels, grad_tokens.astype(BF16))[offset : offset + depth]
-
-    pixels = [forward(s) for s in range(samples)]
-    share = jnp.zeros((depth, feature_dim), F32)
-    for s in range(samples):
-        pointwise(s)
-        share = share + backward(s, pixels[s])
-
-    @pl.when(step == 0)
-    def _():
-        total_ref[...] = share
-
-    @pl.when(step != 0)
-    def _():
-        total_ref[...] = total_ref[...] + share
-
-    @pl.when(step == pl.num_programs(0) * pl.num_programs(1) - 1)
-    def _():
-        first, second = factor_shares(total_ref[...], up_ref, down_ref, level_ref)
-        rank, channels = down_ref.shape
-        columns = share_ref.shape[2]
-        reps = feature_dim // columns
-        folds = rank // (share_ref.shape[1] - rank)
-        depth_rows, fold_lanes, row_share = rank // folds, columns // folds, channels // reps
-        packed = jnp.zeros((depth_rows, feature_dim), F32)
-        row, lane = iota2((channels, feature_dim), 0), iota2((channels, feature_dim), 1)
-        rep, lane = lane // columns, lane % columns
-        for fold in range(folds):
-            inside = lane - fold * fold_lanes
-            pick = (row == inside + rep * row_share) & (inside >= 0) & (inside < row_share)
-            pick = jnp.where(pick, 1.0, 0.0).astype(BF16)
-            packed = packed + dot_nn(
-                first[fold * depth_rows : (fold + 1) * depth_rows].astype(BF16), pick
-            )
-        payload = jnp.concatenate([second, packed], axis=0).astype(BF16)
-        for slot in range(share_ref.shape[0]):
-            at = slot % reps * columns
-            share_ref[slot] = payload[:, at : at + columns]
+                tokens = tokens_ref[n, at, :].astype(F32)
+                mixed_ref[n, line, within, :] = (tokens + pre * cdf).astype(BF16)
+                grad = grad_ref[n, line, within, :].astype(F32)
+                grad_pre_ref[n, at, :] = (grad * (cdf + pre * pdf)).astype(BF16)
+        stores[n].start()
+
+    def backward(n):
+        direct = grad_ref[n].reshape(rows, feature_dim).astype(F32)
+        grad_tokens = dot_nn(mix_t_ref[...], grad_pre_ref[n]) + direct
+        offset = n % samples * depth % LANE
+        share = dot_tn(pixels_of(n), grad_tokens.astype(BF16))[offset : offset + depth]
+        total_ref[...] = share if n == 0 else total_ref[...] + share
+
+    forward(0)
+    for n in range(chunk_count):
+        if n + 1 < chunk_count:
+            forward(n + 1)
+        pointwise(n)
+        backward(n)
+
+    level_load.wait()
+    first, second = factor_shares(total_ref[...], up_ref, down_ref, level_ref)
+    rank, channels = down_ref.shape
+    columns = share_ref.shape[2]
+    reps = feature_dim // columns
+    folds = rank // (share_ref.shape[1] - rank)
+    depth_rows, fold_lanes, row_share = rank // folds, columns // folds, channels // reps
+    packed = jnp.zeros((depth_rows, feature_dim), F32)
+    row, lane = iota2((channels, feature_dim), 0), iota2((channels, feature_dim), 1)
+    rep, lane = lane // columns, lane % columns
+    for fold in range(folds):
+        inside = lane - fold * fold_lanes
+        pick = (row == inside + rep * row_share) & (inside >= 0) & (inside < row_share)
+        pick = jnp.where(pick, 1.0, 0.0).astype(BF16)
+        part = first[fold * depth_rows : (fold + 1) * depth_rows].astype(BF16)
+        packed = packed + dot_nn(part, pick)
+    payload = jnp.concatenate([second, packed], axis=0).astype(BF16)
+    for slot in range(share_ref.shape[0]):
+        at = slot % reps * columns
+        share_ref[slot] = payload[:, at : at + columns]
+    for store in stores:
+        store.wait()
 
 
 def mix_blocks(halves, arrived, merged, mix, mix_t, grad, up_through, down_t, level_weight, band_count, reps):
@@ -326,50 +352,42 @@
     lanes = arrived[0].shape[-1]
     reach = merged.shape[1]
     rows = WLAT * width
-    rank, channels = down_t.shape
-
-    def whole(shape):
-        return pl.BlockSpec(shape, lambda w, h: (0,) * len(shape))
-
-    block = pl.BlockSpec((samples, WLAT, width, feature_dim), lambda w, h: (0, w, h, 0))
-    if len(arrived) == 1:
-        arrived_specs = [pl.BlockSpec((WLAT, block_width, lanes), lambda w, h: (w, 0, 0))]
-    else:
-        arrived_specs = [whole(piece.shape) for piece in arrived]
+    rank = down_t.shape[0]
+    chunks = lat_rows // WLAT * halves * samples
     share_shape = (band_count * reps, rank + rank // FOLDS, feature_dim // reps)
     flops = 2 * samples * lat_rows * block_width * feature_dim * (2 * reach + 2 * rows)
-    constants = [up_through, down_t, level_weight]
+    vmem = pl.BlockSpec(memory_space=pltpu.VMEM)
+    any_space = pl.BlockSpec(memory_space=pl.ANY)
+    local = [*arrived, merged, mix, mix_t, up_through, down_t]
     return pl.pallas_call(
         lambda *refs: mix_kernel(refs[: len(arrived)], *refs[len(arrived) :]),
         out_shape=[
             jax.ShapeDtypeStruct(grad.shape, BF16),
             jax.ShapeDtypeStruct(share_shape, BF16),
         ],
-        grid=(lat_rows // WLAT, halves),
-        in_specs=arrived_specs
-        + [
-            whole(merged.shape),
-            whole(mix.shape),
-            whole(mix_t.shape),
-            block,
-        ]
-        + [whole(array.shape) for array in constants],
-        out_specs=[block, whole(share_shape)],
+        in_specs=[vmem] * len(local) + [any_space, any_space],
+        out_specs=[any_space, vmem],
         scratch_shapes=[
+            pltpu.VMEM((halves, WLAT, width, lanes), BF16),
+            pltpu.VMEM((chunks, WLAT, width, feature_dim), BF16),
+            pltpu.VMEM((chunks, WLAT, width, feature_dim), BF16),
+            pltpu.VMEM(level_weight.shape, BF16),
             pltpu.VMEM((lanes // samples, feature_dim), F32),
-            pltpu.VMEM((samples, rows, feature_dim), F32),
-            pltpu.VMEM((samples, rows, feature_dim), BF16),
-            pltpu.VMEM((samples, rows, feature_dim), BF16),
-            pltpu.VMEM((halves, WLAT, width, lanes), BF16),
+            pltpu.VMEM((chunks, rows, feature_dim), F32),
+            pltpu.VMEM((chunks, rows, feature_dim), BF16),
+            pltpu.VMEM((chunks, rows, feature_dim), BF16),
+            pltpu.SemaphoreType.DMA((chunks,)),
+            pltpu.SemaphoreType.DMA((chunks,)),
+            pltpu.SemaphoreType.DMA,
         ],
-        compiler_params=params(dimension_semantics=("arbitrary", "arbitrary")),
+        compiler_params=params(),
         cost_estimate=pl.CostEstimate(
             flops=flops,
             bytes_accessed=12 * 2**20,
             transcendentals=samples * lat_rows * block_width * feature_dim,
         ),
         name="mix_blocks",
-    )(*arrived, merged, mix, mix_t, in_hbm(grad), *constants)
+    )(*local, in_hbm(grad), in_hbm(level_weight))
 
 
 def sum_kernel(parts_ref, first_ref, second_ref):
@@ -421,10 +439,20 @@
     padded_width = halves * half_padded
     features = samples * levels * channels
 
+    pack_width = round_up(max(row_share, col_share), LANE)
+    pack = jnp.stack(
+        [
+            jnp.pad(adapter_up, ((0, 0), (0, pack_width - col_share))),
+            jnp.pad(adapter_down.T, ((0, 0), (0, pack_width - row_share))),
+        ]
+    )
+    factors = lax.all_gather(pack, "rep", axis=0, tiled=False)
+
     pixels = patches.reshape(features, col_count)
     direct = band_count <= MAX_PERMUTES and lat_rows == WLAT and half_padded == half_width
     if direct and features % LANE == 0 and col_count % LANE == 0:
-        arrived = exchange(send_blocks(pixels, column_block_owner, band_count, block_width))
+        pieces = send_blocks(pixels, column_block_owner, band_count, block_width)
+        factors, arrived = exchange(pieces, factors)
     else:
         block_ids = jnp.arange(band_count, dtype=jnp.int32)
         inverse = jnp.sum(
@@ -434,14 +462,6 @@
         outgoing = jnp.pad(outgoing, ((0, 0), (0, padded_width - block_width), (0, 0)))
         arrived = [lax.all_to_all(outgoing, "band", split_axis=0, concat_axis=0, tiled=True)]
 
-    pack_width = round_up(max(row_share, col_share), LANE)
-    pack = jnp.stack(
-        [
-            jnp.pad(adapter_up, ((0, 0), (0, pack_width - col_share))),
-            jnp.pad(adapter_down.T, ((0, 0), (0, pack_width - row_share))),
-        ]
-    )
-    factors = lax.all_gather(pack, "rep", axis=0, tiled=False)
     merged, up_through, down_t, mix, mix_t = prepare(
         variable_group_index,
         frozen_patch_weight,

time: 54.4 us -> 60.4 us (1.11)
  waiting for transfers between devices: 3.46 us -> 8.69 us
  blocking collectives: 17.2 us -> 21.6 us
  starting transfers between devices: 15.5 us -> 12.8 us
  Pallas kernels: 15 us -> 14.2 us
    ppermute x7, waiting for transfers between devices: 3.46 us -> 8.69 us  [swap(): lax.ppermute(values, axis, [(source, source ^ distance) for source in ran...]
    all_to_all x1, blocking collectives: 12 us -> 15.4 us  [sum_shares(): lax.all_to_all(shares, ('band', 'rep'), split_axis=0, concat_axis=0, tile...]
    ppermute x7, starting transfers between devices: 15.5 us -> 12.8 us  [swap(): lax.ppermute(values, axis, [(source, source ^ distance) for source in ran...]
    all_gather x1, blocking collectives: 5.18 us -> 6.19 us  [on_device(): factors = lax.all_gather(pack, 'rep', axis=0, tiled=False)]
    pallas_call x1, Pallas kernels: 9.66 us -> 8.96 us  [mix_blocks(): pl.pallas_call(lambda *refs: mix_kernel(refs[:len(arrived)], *refs[len(ar...]
  transfers between devices with their start and end apart: 7 -> 7, of which waited for: 1 -> 3; matrix products, arithmetic and copies ran while one was open for 3% -> 0% of each run, Pallas kernels for 5% -> 5%
where the time goes in v6:
time: 60.4 us; the launch traced here: 60 us
  blocking collectives  21.6 us (36%)
  Pallas kernels  14.2 us (24%)
  starting transfers between devices  12.8 us (21%)
  waiting for transfers between devices  8.69 us (14%)
  local copies, waits for them, and re-layouts  1.35 us (2%)
  other arithmetic  0.69 us (1%)
  between operations  0.67 us (1%)
    all_to_all x1, blocking collectives, sum_shares(): lax.all_to_all(shares, ('band', 'rep'), split_axis=0, concat_axis=0, tile...  15.4 us
    ppermute x7, starting transfers between devices, swap(): lax.ppermute(values, axis, [(source, source ^ distance) for source in ran...  12.8 us
    pallas_call x1, Pallas kernels, mix_blocks(): pl.pallas_call(lambda *refs: mix_kernel(refs[:len(arrived)], *refs[len(ar...  8.96 us
    ppermute x7, waiting for transfers between devices, swap(): lax.ppermute(values, axis, [(source, source ^ distance) for source in ran...  8.69 us
    all_gather x1, blocking collectives, on_device(): factors = lax.all_gather(pack, 'rep', axis=0, tiled=False)  6.19 us
    pallas_call x1, Pallas kernels, prepare(): pl.pallas_call(functools.partial(prep_kernel, row_share, half_width, half...  2.88 us
    pallas_call x1, Pallas kernels, send_blocks(): pl.pallas_call(send_kernel, out_shape=[jax.ShapeDtypeStruct((width, featu...  1.61 us
  transfers between devices with their start and end apart: 7, of which 3 were waited for; matrix products, arithmetic and copies ran while one was open for 0% of the time, Pallas kernels for 5%

profile of v6, /device:TPU:0, one launch (start us, length us, event | category | flops | bytes accessed | tf_op | source)
XLA Modules:
  0.0 60.0 jit_solution(8187633087606284060)
XLA Ops:
  0.6 0.7 %pad_bitcast_fusion = bf16[1,16,128]{2,1,0:T(8,128)(2,1)S(1)} fusion(bf16[16,20]{1,0:T(8,128)(2,1)} %bitcast.13), kind=kLoop, calls=%fused_computation.1 | loop fusion | bytes 4736 | tf_op jit(solution)/shard_map/stack | solution.py:443
  1.3 0.7 %pad_maximum_fusion = bf16[2,16,128]{2,1,0:T(8,128)(2,1)S(1)} fusion(bf16[1,16,128]{2,1,0:T(8,128)(2,1)S(1)} %pad_bitcast_fusion, bf16[1,16,128]{2,1,0:T(8,128)(2,1)} %bitcast.14), kind=kLoop, calls=%fused_computation | loop fusion | flops 4096 | bytes 16384 | tf_op jit(solution)/shard_map/stack | solution.py:443
  2.0 6.2 %all-gather = bf16[8,16,128]{2,1,0:T(8,128)(2,1)S(1)} all-gather(bf16[2,16,128]{2,1,0:T(8,128)(2,1)S(1)} %pad_maximum_fusion), channel_id=2, replica_groups=mesh['band'=8,'rep'=4] {'rep'}, dimensions={0}, use_global_device_ids=true | all-gather | bytes 40960 | tf_op jit(solution)/shard_map/all_gather | solution.py:449
  8.2 1.6 %send_blocks.1 = (bf16[96,640]{1,0:T(8,128)(2,1)S(1)}, bf16[96,640]{1,0:T(8,128)(2,1)S(1)}, bf16[96,640]{1,0:T(8,128)(2,1)S(1)}, bf16[96,640]{1,0:T(8,128)(2,1)S...) custom-call(s32[8]{0:T(128)} %owner_hbm_ref.1, ...), custom_call_target="tpu_custom_call" | custom-call | tf_op jit(solution)/shard_map/send_blocks/pallas_call | solution.py:93
  9.8 3.0 %collective-permute-start.5 = (bf16[96,640]{1,0:T(8,128)(2,1)S(1)}, bf16[96,640]{1,0:T(8,128)(2,1)S(1)}, u32[]{:S(2)}, u32[]{:S(2)}) collective-permute-start(bf16[96,640]{1,0:T(8,128)(2,1)S(1)} %get-tuple-element.31), channel_id=1, source_target_pairs={{0,12},{4,8},{8,4},{12,0},{16,28},{20,24},{24,20},{28,16},{1,13},{... | collective-permute-start | bytes 368648 | tf_op jit(solution)/shard_map/ppermute | solution.py:57
  12.8 0.5 collective-permute-start.6
  13.4 2.6 %collective-permute-start = (bf16[96,640]{1,0:T(8,128)(2,1)S(1)}, bf16[96,640]{1,0:T(8,128)(2,1)S(1)}, u32[]{:S(2)}, u32[]{:S(2)}) collective-permute-start(bf16[96,640]{1,0:T(8,128)(2,1)S(1)} %get-tuple-element.24), channel_id=1, source_target_pairs={{0,16},{4,20},{8,24},{12,28},{16,0},{20,4},{24,8},{28,12},{1,17},{... | collective-permute-start | bytes 368648 | tf_op jit(solution)/shard_map/ppermute | solution.py:57
  16.0 1.3 %collective-permute-start.1 = (bf16[96,640]{1,0:T(8,128)(2,1)S(1)}, bf16[96,640]{1,0:T(8,128)(2,1)S(1)}, u32[]{:S(2)}, u32[]{:S(2)}) collective-permute-start(bf16[96,640]{1,0:T(8,128)(2,1)S(1)} %get-tuple-element.25), channel_id=1, source_target_pairs={{0,20},{4,16},{8,28},{12,24},{16,4},{20,0},{24,12},{28,8},{1,21},{... | collective-permute-start | bytes 368648 | tf_op jit(solution)/shard_map/ppermute | solution.py:57
  17.2 2.5 %collective-permute-start.2 = (bf16[96,640]{1,0:T(8,128)(2,1)S(1)}, bf16[96,640]{1,0:T(8,128)(2,1)S(1)}, u32[]{:S(2)}, u32[]{:S(2)}) collective-permute-start(bf16[96,640]{1,0:T(8,128)(2,1)S(1)} %get-tuple-element.26), channel_id=1, source_target_pairs={{0,24},{4,28},{8,16},{12,20},{16,8},{20,12},{24,0},{28,4},{1,25},{... | collective-permute-start | bytes 368648 | tf_op jit(solution)/shard_map/ppermute | solution.py:57
  19.7 0.0 collective-permute-done.5.refs_6_
  19.7 2.9 %collective-permute-start.3 = (bf16[96,640]{1,0:T(8,128)(2,1)S(1)}, bf16[96,640]{1,0:T(8,128)(2,1)S(1)}, u32[]{:S(2)}, u32[]{:S(2)}) collective-permute-start(bf16[96,640]{1,0:T(8,128)(2,1)S(1)} %get-tuple-element.27), channel_id=1, source_target_pairs={{0,28},{4,24},{8,20},{12,16},{16,12},{20,8},{24,4},{28,0},{1,29},{... | collective-permute-start | bytes 368648 | tf_op jit(solution)/shard_map/ppermute | solution.py:57
  22.6 0.0 collective-permute-done.6.refs_7_
  22.6 0.0 collective-permute-start.4
  22.6 0.0 copy-start
  22.6 0.7 %copy-done = s32[5]{0:T(128)S(1)} copy-done((s32[5]{0:T(128)S(1)}, s32[5]{0:T(128)}, u32[]{:S(2)}) %copy-start) | copy-done | bytes 44
  23.3 2.9 %prepare.1 = (bf16[2,384,512]{2,1,0:T(8,128)(2,1)S(1)}, bf16[4,32,512]{2,1,0:T(8,128)(2,1)S(1)}, bf16[16,80]{1,0:T(8,128)(2,1)S(1)}, bf16[384,384]{1,0:T(8,128)(2,1)S(1)}, bf16[384,384]{1,0:T(8,128)(2,1)S(1)}) custom-call(s32[5]{0:T(128)S(1)} %copy-done, bf16[3,16,512]{2,1,0:T(8,128)(2,1)} %frozen_ref.1, bf16[4,2,16,128]{3,2,1,0:T(8,128)(2,1)S(1)} %bitcast.11, ...), custom_call_target="tpu_custom_call" | custom-call | flops 257949696 | bytes 4194304 | tf_op jit(solution)/shard_map/prepare/pallas_call | solution.py:184
  26.2 4.0 %collective-permute-done.refs_1_ = bf16[96,640]{1,0:T(8,128)(2,1)S(1)} collective-permute-done((bf16[96,640]{1,0:T(8,128)(2,1)S(1)}, bf16[96,640]{1,0:T(8,128)(2,1)S(1)}, u32[]{:S(2)}, u32[]{:S(2)}) %collective-permute-start) | collective-permute-done | bytes 122912 | tf_op jit(solution)/shard_map/ppermute | solution.py:57
  30.2 4.1 %collective-permute-done.1.refs_2_ = bf16[96,640]{1,0:T(8,128)(2,1)S(1)} collective-permute-done((bf16[96,640]{1,0:T(8,128)(2,1)S(1)}, bf16[96,640]{1,0:T(8,128)(2,1)S(1)}, u32[]{:S(2)}, u32[]{:S(2)}) %collective-permute-start.1) | collective-permute-done | bytes 122912 | tf_op jit(solution)/shard_map/ppermute | solution.py:57
  34.3 0.0 collective-permute-done.2.refs_3_
  34.3 0.0 collective-permute-done.3.refs_4_
  34.4 0.5 collective-permute-done.4.refs_5_
  34.9 9.0 %mix_blocks.1 = (bf16[2,8,96,512]{3,2,1,0:T(8,128)(2,1)}, bf16[32,24,128]{2,1,0:T(8,128)(2,1)S(1)}) custom-call(bf16[96,640]{1,0:T(8,128)(2,1)S(1)} %get-tuple-element.23.refs_0_, bf16[96,640]{1,0:T(8,128)(2,1)S(1)} %collective-permute-done.refs_1_, bf16[96,640]{1,0:T(8,128)(2,1)S(1)} %collective-permute-done.1.refs_2_, ...), custom_call_target="tpu_custom_call" | custom-call | flops 2415919104 | bytes 12582912 | tf_op jit(solution)/shard_map/mix_blocks/pallas_call | solution.py:362
  43.8 15.4 %all_to_all.5.parts_ref = bf16[32,24,128]{2,1,0:T(8,128)(2,1)S(1)} all-to-all(bf16[32,24,128]{2,1,0:T(8,128)(2,1)S(1)} %get-tuple-element.40), channel_id=1, replica_groups=mesh['band'=8,'rep'=4] {'band','rep'}, dimensions={0} | all-to-all | bytes 393216 | tf_op jit(solution)/shard_map/all_to_all | solution.py:406
  59.3 0.7 %sum_shares.1 = (f32[16,20]{1,0:T(8,128)}, f32[16,128]{1,0:T(8,128)}) custom-call(bf16[32,24,128]{2,1,0:T(8,128)(2,1)S(1)} %all_to_all.5.parts_ref), custom_call_target="tpu_custom_call" | custom-call | tf_op jit(solution)/shard_map/sum_shares/pallas_call | solution.py:407
Async XLA Ops:
  9.8 9.9 %collective-permute-start.5 = (bf16[96,640]{1,0:T(8,128)(2,1)S(1)}, bf16[96,640]{1,0:T(8,128)(2,1)S(1)}, u32[]{:S(2)}, u32[]{:S(2)}) collective-permute-start(bf16[96,640]{1,0:T(8,128)(2,1)S(1)} %get-tuple-element.31), channel_id=1, source_target_pairs={{0,12},{4,8},{8,4},{12,0},{16,28},{20,24},{24,20},{28,16},{1,13},{... | collective-permute-start | bytes 368648 | tf_op jit(solution)/shard_map/ppermute | solution.py:57
  12.8 9.8 %collective-permute-start.6 = (bf16[96,640]{1,0:T(8,128)(2,1)S(1)}, bf16[96,640]{1,0:T(8,128)(2,1)S(1)}, u32[]{:S(2)}, u32[]{:S(2)}) collective-permute-start(bf16[96,640]{1,0:T(8,128)(2,1)S(1)} %get-tuple-element.32), channel_id=1, source_target_pairs={{0,4},{4,0},{8,12},{12,8},{16,20},{20,16},{24,28},{28,24},{1,5},{5... | collective-permute-start | bytes 368648 | tf_op jit(solution)/shard_map/ppermute | solution.py:57
  13.4 16.9 %collective-permute-start = (bf16[96,640]{1,0:T(8,128)(2,1)S(1)}, bf16[96,640]{1,0:T(8,128)(2,1)S(1)}, u32[]{:S(2)}, u32[]{:S(2)}) collective-permute-start(bf16[96,640]{1,0:T(8,128)(2,1)S(1)} %get-tuple-element.24), channel_id=1, source_target_pairs={{0,16},{4,20},{8,24},{12,28},{16,0},{20,4},{24,8},{28,12},{1,17},{... | collective-permute-start | bytes 368648 | tf_op jit(solution)/shard_map/ppermute | solution.py:57
  16.0 18.4 %collective-permute-start.1 = (bf16[96,640]{1,0:T(8,128)(2,1)S(1)}, bf16[96,640]{1,0:T(8,128)(2,1)S(1)}, u32[]{:S(2)}, u32[]{:S(2)}) collective-permute-start(bf16[96,640]{1,0:T(8,128)(2,1)S(1)} %get-tuple-element.25), channel_id=1, source_target_pairs={{0,20},{4,16},{8,28},{12,24},{16,4},{20,0},{24,12},{28,8},{1,21},{... | collective-permute-start | bytes 368648 | tf_op jit(solution)/shard_map/ppermute | solution.py:57
  17.2 17.1 %collective-permute-start.2 = (bf16[96,640]{1,0:T(8,128)(2,1)S(1)}, bf16[96,640]{1,0:T(8,128)(2,1)S(1)}, u32[]{:S(2)}, u32[]{:S(2)}) collective-permute-start(bf16[96,640]{1,0:T(8,128)(2,1)S(1)} %get-tuple-element.26), channel_id=1, source_target_pairs={{0,24},{4,28},{8,16},{12,20},{16,8},{20,12},{24,0},{28,4},{1,25},{... | collective-permute-start | bytes 368648 | tf_op jit(solution)/shard_map/ppermute | solution.py:57
  19.7 14.7 %collective-permute-start.3 = (bf16[96,640]{1,0:T(8,128)(2,1)S(1)}, bf16[96,640]{1,0:T(8,128)(2,1)S(1)}, u32[]{:S(2)}, u32[]{:S(2)}) collective-permute-start(bf16[96,640]{1,0:T(8,128)(2,1)S(1)} %get-tuple-element.27), channel_id=1, source_target_pairs={{0,28},{4,24},{8,20},{12,16},{16,12},{20,8},{24,4},{28,0},{1,29},{... | collective-permute-start | bytes 368648 | tf_op jit(solution)/shard_map/ppermute | solution.py:57
  22.6 12.2 %collective-permute-start.4 = (bf16[96,640]{1,0:T(8,128)(2,1)S(1)}, bf16[96,640]{1,0:T(8,128)(2,1)S(1)}, u32[]{:S(2)}, u32[]{:S(2)}) collective-permute-start(bf16[96,640]{1,0:T(8,128)(2,1)S(1)} %get-tuple-element.28), channel_id=1, source_target_pairs={{0,8},{4,12},{8,0},{12,4},{16,24},{20,28},{24,16},{28,20},{1,9},{5... | collective-permute-start | bytes 368648 | tf_op jit(solution)/shard_map/ppermute | solution.py:57
  22.6 0.7 %copy-start = (s32[5]{0:T(128)S(1)}, s32[5]{0:T(128)}, u32[]{:S(2)}) copy-start(s32[5]{0:T(128)} %group_ref.1) | copy-start | bytes 64

commit v7 on v6

--- a/solution.py
+++ b/solution.py
@@ -14,6 +14,7 @@
 VMEM_LIMIT = 24 * 1024 * 1024
 MAX_PERMUTES = 8
 FOLDS = 2
+COLUMNS = 256
 BF16 = jnp.bfloat16
 F32 = jnp.float32
 
@@ -59,7 +60,7 @@
 
 def distances(band_count):
     half = band_count // 2
-    return [0] + list(range(half, band_count)) + list(range(2, half)) + [1]
+    return [0, 1] + list(range(half, band_count)) + list(range(2, half))
 
 
 def send_kernel(owner_hbm_ref, x_hbm_ref, *refs):
@@ -107,13 +108,16 @@
     )(in_hbm(owner), in_hbm(pixels))
 
 
-def exchange(pieces, factors):
-    far = len(pieces) - 2
-    late = lax.optimization_barrier((factors, *pieces[far:]))
-    factors, pieces = late[0], list(pieces[:far]) + list(late[1:])
-    return factors, [
-        piece if k == 0 else swap(piece, "band", k) for k, piece in zip(distances(len(pieces)), pieces)
-    ]
+def exchange(pieces, pack):
+    order = distances(len(pieces))
+    near = swap(pieces[1], "band", order[1])
+    near, pack = lax.optimization_barrier((near, pack))
+    factors = lax.all_gather(pack, "rep", axis=0, tiled=False)
+    first_late = 2 + len(pieces) // 2
+    far = [swap(piece, "band", k) for k, piece in zip(order[2:first_late], pieces[2:first_late])]
+    factors, *late = lax.optimization_barrier((factors, *pieces[first_late:]))
+    late = [swap(piece, "band", k) for k, piece in zip(order[first_late:], late)]
+    return [pieces[0], near, *far, *late], factors
 
 
 def expand_table(table, rows, half_width_padded, half_width, transpose):
@@ -246,6 +250,8 @@
     pre_ref,
     tokens_ref,
     grad_pre_ref,
+    grad_tokens_ref,
+    turned_ref,
     grad_sems,
     mixed_sems,
     level_sem,
@@ -280,47 +286,89 @@
                 within = slice(half * width, (half + 1) * width)
                 arrived_ref[half, jnp.bitwise_xor(me, k)] = piece_ref[within, :]
 
-    def pixels_of(n):
-        window_row, half, s, _ = place(n)
-        lanes = slice(s * depth // LANE * LANE, s * depth // LANE * LANE + reach)
+    def pixels_of(n, lanes):
+        window_row, half, _, _ = place(n)
         if len(piece_refs) > 1:
             block = arrived_ref[half, :, :, lanes]
         else:
             lines = slice(window_row * WLAT, (window_row + 1) * WLAT)
             block = piece_refs[0][lines, half * width : (half + 1) * width, lanes]
-        return block.reshape(rows, reach)
-
-    def forward(n):
-        tokens = dot_nn(pixels_of(n), merged_ref[n % samples]).astype(BF16)
-        tokens_ref[n] = tokens
-        pre_ref[n] = dot_nn(mix_ref[...], tokens)
-
-    def pointwise(n):
-        loads[n].wait()
-        for line in range(WLAT):
+        return block.reshape(rows, lanes.stop - lanes.start)
+
+    def turn(n):
+        def part(lanes):
+            turned_ref[n // samples, lanes, :] = pixels_of(n, lanes).T
+
+        starts = range(0, samples * depth, LANE)
+        return [functools.partial(part, slice(start, start + LANE)) for start in starts]
+
+    def forward(n, columns):
+        s = n % samples
+        lane = s * depth // LANE * LANE
+
+        def embed():
+            pixels = pixels_of(n, slice(lane, lane + reach))
+            tokens_ref[n, :, columns] = dot_nn(pixels, merged_ref[s, :, columns]).astype(BF16)
+
+        def mixing():
+            pre_ref[n, :, columns] = dot_nn(mix_ref[...], tokens_ref[n, :, columns])
+
+        return [embed, mixing]
+
+    def pointwise(n, columns):
+        def part(line):
             for start in range(0, width, SUB):
                 at, within = pl.ds(line * width + start, SUB), pl.ds(start, SUB)
-                pre = pre_ref[n, at, :]
+                pre = pre_ref[n, at, columns]
                 cdf, pdf = normal_parts(pre)
-                tokens = tokens_ref[n, at, :].astype(F32)
-                mixed_ref[n, line, within, :] = (tokens + pre * cdf).astype(BF16)
-                grad = grad_ref[n, line, within, :].astype(F32)
-                grad_pre_ref[n, at, :] = (grad * (cdf + pre * pdf)).astype(BF16)
-        stores[n].start()
-
-    def backward(n):
-        direct = grad_ref[n].reshape(rows, feature_dim).astype(F32)
-        grad_tokens = dot_nn(mix_t_ref[...], grad_pre_ref[n]) + direct
-        offset = n % samples * depth % LANE
-        share = dot_tn(pixels_of(n), grad_tokens.astype(BF16))[offset : offset + depth]
-        total_ref[...] = share if n == 0 else total_ref[...] + share
-
-    forward(0)
-    for n in range(chunk_count):
-        if n + 1 < chunk_count:
-            forward(n + 1)
-        pointwise(n)
-        backward(n)
+                tokens = tokens_ref[n, at, columns].astype(F32)
+                mixed_ref[n, line, within, columns] = (tokens + pre * cdf).astype(BF16)
+                grad = grad_ref[n, line, within, columns].astype(F32)
+                grad_pre_ref[n, at, columns] = (grad * (cdf + pre * pdf)).astype(BF16)
+
+        return [functools.partial(part, line) for line in range(WLAT)]
+
+    def backward(n, columns):
+        def spread():
+            direct = grad_ref[n, :, :, columns].reshape(rows, COLUMNS).astype(F32)
+            through = dot_nn(mix_t_ref[...], grad_pre_ref[n, :, columns])
+            grad_tokens_ref[n, :, columns] = (through + direct).astype(BF16)
+
+        def share():
+            s = n % samples
+            turned = turned_ref[n // samples, s * depth : (s + 1) * depth, :]
+            part = dot_nn(turned, grad_tokens_ref[n, :, columns])
+            total_ref[:, columns] = part if n == 0 else total_ref[:, columns] + part
+
+        return [spread, share]
+
+    units = [
+        (n, slice(start, start + COLUMNS))
+        for n in range(chunk_count)
+        for start in range(0, feature_dim, COLUMNS)
+    ]
+    for step in forward(*units[0]):
+        step()
+    for load in loads:
+        load.wait()
+    for i, unit in enumerate(units):
+        n, columns = unit
+        others = []
+        if i + 1 < len(units):
+            others += forward(*units[i + 1])
+        if columns.start == 0 and n % samples == 0:
+            others += turn(n)
+        if i > 0:
+            others += backward(*units[i - 1])
+        lines = pointwise(*unit)
+        for line, vector_step in enumerate(lines):
+            vector_step()
+            for step in others[line * len(others) // len(lines) : (line + 1) * len(others) // len(lines)]:
+                step()
+        if columns.stop == feature_dim:
+            stores[n].start()
+    for step in backward(*units[-1]):
+        step()
 
     level_load.wait()
     first, second = factor_shares(total_ref[...], up_ref, down_ref, level_ref)
@@ -376,6 +424,8 @@
             pltpu.VMEM((chunks, rows, feature_dim), F32),
             pltpu.VMEM((chunks, rows, feature_dim), BF16),
             pltpu.VMEM((chunks, rows, feature_dim), BF16),
+            pltpu.VMEM((chunks, rows, feature_dim), BF16),
+            pltpu.VMEM((chunks // samples, lanes, rows), BF16),
             pltpu.SemaphoreType.DMA((chunks,)),
             pltpu.SemaphoreType.DMA((chunks,)),
             pltpu.SemaphoreType.DMA,
@@ -446,13 +496,12 @@
             jnp.pad(adapter_down.T, ((0, 0), (0, pack_width - row_share))),
         ]
     )
-    factors = lax.all_gather(pack, "rep", axis=0, tiled=False)
 
     pixels = patches.reshape(features, col_count)
     direct = band_count <= MAX_PERMUTES and lat_rows == WLAT and half_padded == half_width
     if direct and features % LANE == 0 and col_count % LANE == 0:
         pieces = send_blocks(pixels, column_block_owner, band_count, block_width)
-        factors, arrived = exchange(pieces, factors)
+        arrived, factors = exchange(pieces, pack)
     else:
         block_ids = jnp.arange(band_count, dtype=jnp.int32)
         inverse = jnp.sum(
@@ -461,6 +510,7 @@
         outgoing = jnp.take(pixels.T.reshape(band_count, block_width, features), inverse, axis=0)
         outgoing = jnp.pad(outgoing, ((0, 0), (0, padded_width - block_width), (0, 0)))
         arrived = [lax.all_to_all(outgoing, "band", split_axis=0, concat_axis=0, tiled=True)]
+        factors = lax.all_gather(pack, "rep", axis=0, tiled=False)
 
     merged, up_through, down_t, mix, mix_t = prepare(
         variable_group_index,

time: 60.4 us -> 53.8 us (0.89)
  waiting for transfers between devices: 8.69 us -> 6.25 us
  starting transfers between devices: 12.8 us -> 10.7 us
  blocking collectives: 21.6 us -> 19.7 us
    ppermute x7, waiting for transfers between devices: 8.69 us -> 6.25 us  [swap(): lax.ppermute(values, axis, [(source, source ^ distance) for source in ran...]
    ppermute x7, starting transfers between devices: 12.8 us -> 10.7 us  [swap(): lax.ppermute(values, axis, [(source, source ^ distance) for source in ran...]
    all_gather x1, blocking collectives: 6.19 us -> 5.18 us  [exchange(): factors = lax.all_gather(pack, 'rep', axis=0, tiled=False)]
    all_to_all x1, blocking collectives: 15.4 us -> 14.5 us  [sum_shares(): lax.all_to_all(shares, ('band', 'rep'), split_axis=0, concat_axis=0, tile...]
  transfers between devices with their start and end apart: 7 -> 7, of which waited for: 3 -> 3; matrix products, arithmetic and copies ran while one was open for 0% -> 3% of each run, Pallas kernels for 5% -> 5%
where the time goes in v7:
time: 53.8 us; the launch traced here: 53.4 us
  blocking collectives  19.7 us (37%)
  Pallas kernels  14.1 us (26%)
  starting transfers between devices  10.7 us (20%)
  waiting for transfers between devices  6.25 us (12%)
  local copies, waits for them, and re-layouts  1.35 us (3%)
  other arithmetic  0.69 us (1%)
  between operations  0.69 us (1%)
    all_to_all x1, blocking collectives, sum_shares(): lax.all_to_all(shares, ('band', 'rep'), split_axis=0, concat_axis=0, tile...  14.5 us
    ppermute x7, starting transfers between devices, swap(): lax.ppermute(values, axis, [(source, source ^ distance) for source in ran...  10.7 us
    pallas_call x1, Pallas kernels, mix_blocks(): pl.pallas_call(lambda *refs: mix_kernel(refs[:len(arrived)], *refs[len(ar...  8.91 us
    ppermute x7, waiting for transfers between devices, swap(): lax.ppermute(values, axis, [(source, source ^ distance) for source in ran...  6.25 us
    all_gather x1, blocking collectives, exchange(): factors = lax.all_gather(pack, 'rep', axis=0, tiled=False)  5.18 us
    pallas_call x1, Pallas kernels, prepare(): pl.pallas_call(functools.partial(prep_kernel, row_share, half_width, half...  2.88 us
    pallas_call x1, Pallas kernels, send_blocks(): pl.pallas_call(send_kernel, out_shape=[jax.ShapeDtypeStruct((width, featu...  1.62 us
  transfers between devices with their start and end apart: 7, of which 3 were waited for; matrix products, arithmetic and copies ran while one was open for 3% of the time, Pallas kernels for 5%

profile of v7, /device:TPU:0, one launch (start us, length us, event | category | flops | bytes accessed | tf_op | source)
XLA Modules:
  0.0 53.4 jit_solution(4379083037287952034)
XLA Ops:
  0.6 1.6 %send_blocks.1 = (bf16[96,640]{1,0:T(8,128)(2,1)S(1)}, bf16[96,640]{1,0:T(8,128)(2,1)S(1)}, bf16[96,640]{1,0:T(8,128)(2,1)S(1)}, bf16[96,640]{1,0:T(8,128)(2,1)S...) custom-call(s32[8]{0:T(128)} %owner_hbm_ref.1, ...), custom_call_target="tpu_custom_call" | custom-call | tf_op jit(solution)/shard_map/send_blocks/pallas_call | solution.py:94
  2.3 3.0 %collective-permute-start = (bf16[96,640]{1,0:T(8,128)(2,1)S(1)}, bf16[96,640]{1,0:T(8,128)(2,1)S(1)}, u32[]{:S(2)}, u32[]{:S(2)}) collective-permute-start(bf16[96,640]{1,0:T(8,128)(2,1)S(1)} %get-tuple-element.26), channel_id=1, source_target_pairs={{0,4},{4,0},{8,12},{12,8},{16,20},{20,16},{24,28},{28,24},{1,5},{5... | collective-permute-start | bytes 368648 | tf_op jit(solution)/shard_map/ppermute | solution.py:58
  5.3 2.6 %collective-permute-start.1 = (bf16[96,640]{1,0:T(8,128)(2,1)S(1)}, bf16[96,640]{1,0:T(8,128)(2,1)S(1)}, u32[]{:S(2)}, u32[]{:S(2)}) collective-permute-start(bf16[96,640]{1,0:T(8,128)(2,1)S(1)} %get-tuple-element.28), channel_id=1, source_target_pairs={{0,16},{4,20},{8,24},{12,28},{16,0},{20,4},{24,8},{28,12},{1,17},{... | collective-permute-start | bytes 368648 | tf_op jit(solution)/shard_map/ppermute | solution.py:58
  7.8 0.0 collective-permute-start.2
  7.9 3.9 %collective-permute-start.3 = (bf16[96,640]{1,0:T(8,128)(2,1)S(1)}, bf16[96,640]{1,0:T(8,128)(2,1)S(1)}, u32[]{:S(2)}, u32[]{:S(2)}) collective-permute-start(bf16[96,640]{1,0:T(8,128)(2,1)S(1)} %get-tuple-element.30), channel_id=1, source_target_pairs={{0,24},{4,28},{8,16},{12,20},{16,8},{20,12},{24,0},{28,4},{1,25},{... | collective-permute-start | bytes 368648 | tf_op jit(solution)/shard_map/ppermute | solution.py:58
  11.8 1.1 %collective-permute-start.4 = (bf16[96,640]{1,0:T(8,128)(2,1)S(1)}, bf16[96,640]{1,0:T(8,128)(2,1)S(1)}, u32[]{:S(2)}, u32[]{:S(2)}) collective-permute-start(bf16[96,640]{1,0:T(8,128)(2,1)S(1)} %get-tuple-element.31), channel_id=1, source_target_pairs={{0,28},{4,24},{8,20},{12,16},{16,12},{20,8},{24,4},{28,0},{1,29},{... | collective-permute-start | bytes 368648 | tf_op jit(solution)/shard_map/ppermute | solution.py:58
  12.9 0.7 %pad_bitcast_fusion = bf16[1,16,128]{2,1,0:T(8,128)(2,1)S(1)} fusion(bf16[16,20]{1,0:T(8,128)(2,1)} %bitcast.13), kind=kLoop, calls=%fused_computation.1 | loop fusion | bytes 4736 | tf_op jit(solution)/shard_map/stack | solution.py:493
  13.6 0.7 %pad_maximum_fusion = bf16[2,16,128]{2,1,0:T(8,128)(2,1)S(1)} fusion(bf16[1,16,128]{2,1,0:T(8,128)(2,1)S(1)} %pad_bitcast_fusion, bf16[1,16,128]{2,1,0:T(8,128)(2,1)} %bitcast.14), kind=kLoop, calls=%fused_computation | loop fusion | flops 4096 | bytes 16384 | tf_op jit(solution)/shard_map/stack | solution.py:493
  14.3 0.0 collective-permute-done.refs_1_
  14.3 5.2 %all-gather = bf16[8,16,128]{2,1,0:T(8,128)(2,1)S(1)} all-gather(bf16[2,16,128]{2,1,0:T(8,128)(2,1)S(1)} %pad_maximum_fusion), channel_id=2, replica_groups=mesh['band'=8,'rep'=4] {'rep'}, dimensions={0}, use_global_device_ids=true | all-gather | bytes 40960 | tf_op jit(solution)/shard_map/all_gather | solution.py:115
  19.5 0.0 collective-permute-start.5
  19.5 3.2 %collective-permute-done.1.refs_2_ = bf16[96,640]{1,0:T(8,128)(2,1)S(1)} collective-permute-done((bf16[96,640]{1,0:T(8,128)(2,1)S(1)}, bf16[96,640]{1,0:T(8,128)(2,1)S(1)}, u32[]{:S(2)}, u32[]{:S(2)}) %collective-permute-start.1) | collective-permute-done | bytes 122912 | tf_op jit(solution)/shard_map/ppermute | solution.py:58
  22.7 0.0 collective-permute-start.6
  22.7 0.0 copy-start
  22.7 0.7 %copy-done = s32[5]{0:T(128)S(1)} copy-done((s32[5]{0:T(128)S(1)}, s32[5]{0:T(128)}, u32[]{:S(2)}) %copy-start) | copy-done | bytes 44
  23.3 2.9 %prepare.1 = (bf16[2,384,512]{2,1,0:T(8,128)(2,1)S(1)}, bf16[4,32,512]{2,1,0:T(8,128)(2,1)S(1)}, bf16[16,80]{1,0:T(8,128)(2,1)S(1)}, bf16[384,384]{1,0:T(8,128)(2,1)S(1)}, bf16[384,384]{1,0:T(8,128)(2,1)S(1)}) custom-call(s32[5]{0:T(128)S(1)} %copy-done, bf16[3,16,512]{2,1,0:T(8,128)(2,1)} %frozen_ref.1, bf16[4,2,16,128]{3,2,1,0:T(8,128)(2,1)S(1)} %bitcast.11, ...), custom_call_target="tpu_custom_call" | custom-call | flops 257949696 | bytes 4194304 | tf_op jit(solution)/shard_map/prepare/pallas_call | solution.py:188
  26.2 0.0 collective-permute-done.2.refs_3_
  26.2 0.0 collective-permute-done.3.refs_4_
  26.2 0.0 collective-permute-done.4.refs_5_
  26.2 0.6 %collective-permute-done.5.refs_6_ = bf16[96,640]{1,0:T(8,128)(2,1)S(1)} collective-permute-done((bf16[96,640]{1,0:T(8,128)(2,1)S(1)}, bf16[96,640]{1,0:T(8,128)(2,1)S(1)}, u32[]{:S(2)}, u32[]{:S(2)}) %collective-permute-start.5) | collective-permute-done | bytes 122912 | tf_op jit(solution)/shard_map/ppermute | solution.py:58
  26.8 2.5 %collective-permute-done.6.refs_7_ = bf16[96,640]{1,0:T(8,128)(2,1)S(1)} collective-permute-done((bf16[96,640]{1,0:T(8,128)(2,1)S(1)}, bf16[96,640]{1,0:T(8,128)(2,1)S(1)}, u32[]{:S(2)}, u32[]{:S(2)}) %collective-permute-start.6) | collective-permute-done | bytes 122912 | tf_op jit(solution)/shard_map/ppermute | solution.py:58
  29.3 8.9 %mix_blocks.1 = (bf16[2,8,96,512]{3,2,1,0:T(8,128)(2,1)}, bf16[32,24,128]{2,1,0:T(8,128)(2,1)S(1)}) custom-call(bf16[96,640]{1,0:T(8,128)(2,1)S(1)} %get-tuple-element.25.refs_0_, bf16[96,640]{1,0:T(8,128)(2,1)S(1)} %collective-permute-done.refs_1_, bf16[96,640]{1,0:T(8,128)(2,1)S(1)} %collective-permute-done.1.refs_2_, ...), custom_call_target="tpu_custom_call" | custom-call | flops 2415919104 | bytes 12582912 | tf_op jit(solution)/shard_map/mix_blocks/pallas_call | solution.py:410
  38.2 14.5 %all_to_all.5.parts_ref = bf16[32,24,128]{2,1,0:T(8,128)(2,1)S(1)} all-to-all(bf16[32,24,128]{2,1,0:T(8,128)(2,1)S(1)} %get-tuple-element.44), channel_id=1, replica_groups=mesh['band'=8,'rep'=4] {'band','rep'}, dimensions={0} | all-to-all | bytes 393216 | tf_op jit(solution)/shard_map/all_to_all | solution.py:456
  52.7 0.7 %sum_shares.1 = (f32[16,20]{1,0:T(8,128)}, f32[16,128]{1,0:T(8,128)}) custom-call(bf16[32,24,128]{2,1,0:T(8,128)(2,1)S(1)} %all_to_all.5.parts_ref), custom_call_target="tpu_custom_call" | custom-call | tf_op jit(solution)/shard_map/sum_shares/pallas_call | solution.py:457
Async XLA Ops:
  2.3 12.0 %collective-permute-start = (bf16[96,640]{1,0:T(8,128)(2,1)S(1)}, bf16[96,640]{1,0:T(8,128)(2,1)S(1)}, u32[]{:S(2)}, u32[]{:S(2)}) collective-permute-start(bf16[96,640]{1,0:T(8,128)(2,1)S(1)} %get-tuple-element.26), channel_id=1, source_target_pairs={{0,4},{4,0},{8,12},{12,8},{16,20},{20,16},{24,28},{28,24},{1,5},{5... | collective-permute-start | bytes 368648 | tf_op jit(solution)/shard_map/ppermute | solution.py:58
  5.3 17.4 %collective-permute-start.1 = (bf16[96,640]{1,0:T(8,128)(2,1)S(1)}, bf16[96,640]{1,0:T(8,128)(2,1)S(1)}, u32[]{:S(2)}, u32[]{:S(2)}) collective-permute-start(bf16[96,640]{1,0:T(8,128)(2,1)S(1)} %get-tuple-element.28), channel_id=1, source_target_pairs={{0,16},{4,20},{8,24},{12,28},{16,0},{20,4},{24,8},{28,12},{1,17},{... | collective-permute-start | bytes 368648 | tf_op jit(solution)/shard_map/ppermute | solution.py:58
  7.8 18.4 %collective-permute-start.2 = (bf16[96,640]{1,0:T(8,128)(2,1)S(1)}, bf16[96,640]{1,0:T(8,128)(2,1)S(1)}, u32[]{:S(2)}, u32[]{:S(2)}) collective-permute-start(bf16[96,640]{1,0:T(8,128)(2,1)S(1)} %get-tuple-element.29), channel_id=1, source_target_pairs={{0,20},{4,16},{8,28},{12,24},{16,4},{20,0},{24,12},{28,8},{1,21},{... | collective-permute-start | bytes 368648 | tf_op jit(solution)/shard_map/ppermute | solution.py:58
  7.9 18.4 %collective-permute-start.3 = (bf16[96,640]{1,0:T(8,128)(2,1)S(1)}, bf16[96,640]{1,0:T(8,128)(2,1)S(1)}, u32[]{:S(2)}, u32[]{:S(2)}) collective-permute-start(bf16[96,640]{1,0:T(8,128)(2,1)S(1)} %get-tuple-element.30), channel_id=1, source_target_pairs={{0,24},{4,28},{8,16},{12,20},{16,8},{20,12},{24,0},{28,4},{1,25},{... | collective-permute-start | bytes 368648 | tf_op jit(solution)/shard_map/ppermute | solution.py:58
  11.8 14.5 %collective-permute-start.4 = (bf16[96,640]{1,0:T(8,128)(2,1)S(1)}, bf16[96,640]{1,0:T(8,128)(2,1)S(1)}, u32[]{:S(2)}, u32[]{:S(2)}) collective-permute-start(bf16[96,640]{1,0:T(8,128)(2,1)S(1)} %get-tuple-element.31), channel_id=1, source_target_pairs={{0,28},{4,24},{8,20},{12,16},{16,12},{20,8},{24,4},{28,0},{1,29},{... | collective-permute-start | bytes 368648 | tf_op jit(solution)/shard_map/ppermute | solution.py:58
  19.5 7.3 %collective-permute-start.5 = (bf16[96,640]{1,0:T(8,128)(2,1)S(1)}, bf16[96,640]{1,0:T(8,128)(2,1)S(1)}, u32[]{:S(2)}, u32[]{:S(2)}) collective-permute-start(bf16[96,640]{1,0:T(8,128)(2,1)S(1)} %get-tuple-element.35), channel_id=1, source_target_pairs={{0,8},{4,12},{8,0},{12,4},{16,24},{20,28},{24,16},{28,20},{1,9},{5... | collective-permute-start | bytes 368648 | tf_op jit(solution)/shard_map/ppermute | solution.py:58
  22.7 6.6 %collective-permute-start.6 = (bf16[96,640]{1,0:T(8,128)(2,1)S(1)}, bf16[96,640]{1,0:T(8,128)(2,1)S(1)}, u32[]{:S(2)}, u32[]{:S(2)}) collective-permute-start(bf16[96,640]{1,0:T(8,128)(2,1)S(1)} %get-tuple-element.36), channel_id=1, source_target_pairs={{0,12},{4,8},{8,4},{12,0},{16,28},{20,24},{24,20},{28,16},{1,13},{... | collective-permute-start | bytes 368648 | tf_op jit(solution)/shard_map/ppermute | solution.py:58
  22.7 0.7 %copy-start = (s32[5]{0:T(128)S(1)}, s32[5]{0:T(128)}, u32[]{:S(2)}) copy-start(s32[5]{0:T(128)} %group_ref.1) | copy-start | bytes 64

commit v8 on v7

--- a/solution.py
+++ b/solution.py
@@ -12,7 +12,7 @@
 LANE = 128
 SUB = 16
 VMEM_LIMIT = 24 * 1024 * 1024
-MAX_PERMUTES = 8
+BANDS = 8
 FOLDS = 2
 COLUMNS = 256
 BF16 = jnp.bfloat16
@@ -58,66 +58,84 @@
     return lax.ppermute(values, axis, [(source, source ^ distance) for source in range(count)])
 
 
-def distances(band_count):
-    half = band_count // 2
-    return [0, 1] + list(range(half, band_count)) + list(range(2, half))
-
-
-def send_kernel(owner_hbm_ref, x_hbm_ref, *refs):
-    out_refs, (owner_ref, x_ref, turned_ref, owner_sem, x_sems) = refs[:-5], refs[-5:]
-    band_count, width = len(out_refs), out_refs[0].shape[0]
+def send_kernel(owner_hbm_ref, up_hbm_ref, down_hbm_ref, x_hbm_ref, own_ref, near_ref, beside_ref, *refs):
+    far_refs, pack_ref, scratch = refs[:-8], refs[-8], refs[-7:]
+    owner_ref, up_ref, down_ref, x_ref, turned_ref, small_sems, x_sems = scratch
+    width = own_ref.shape[0]
     features, columns = x_ref.shape
-    copies = [pltpu.make_async_copy(owner_hbm_ref, owner_ref, owner_sem)]
+    small = [
+        pltpu.make_async_copy(source, target, small_sems.at[n])
+        for n, (source, target) in enumerate(
+            [(owner_hbm_ref, owner_ref), (up_hbm_ref, up_ref), (down_hbm_ref, down_ref)]
+        )
+    ]
     parts = [slice(start, start + LANE) for start in range(0, features, LANE)]
-    for n, part in enumerate(parts):
-        copies.append(pltpu.make_async_copy(x_hbm_ref.at[part, :], x_ref.at[part, :], x_sems.at[n]))
-    for copy in copies:
+    large = [
+        pltpu.make_async_copy(x_hbm_ref.at[part, :], x_ref.at[part, :], x_sems.at[n])
+        for n, part in enumerate(parts)
+    ]
+    for copy in large + small:
         copy.start()
-    for n, part in enumerate(parts):
-        copies[n + 1].wait()
+    for copy, part in zip(large, parts):
+        copy.wait()
         for start in range(0, columns, LANE):
             at = slice(start, start + LANE)
             turned_ref[at, part] = x_ref[part, at].T
-    copies[0].wait()
+    for copy in small:
+        copy.wait()
+    pack_ref[...] = jnp.zeros_like(pack_ref)
+    pack_ref[0, :, : up_ref.shape[1]] = up_ref[...]
+    pack_ref[1, :, : down_ref.shape[1]] = down_ref[...]
     me = lax.axis_index("band")
-    for k, out_ref in zip(distances(band_count), out_refs):
-        target = jnp.bitwise_xor(me, k)
+
+    def block_of(distance):
+        target = jnp.bitwise_xor(me, distance)
         block = 0
-        for j in range(1, band_count):
+        for j in range(1, owner_ref.shape[0]):
             block = jnp.where(owner_ref[j] == target, j, block)
-        out_ref[...] = turned_ref[pl.ds(pl.multiple_of(block * width, SUB), width), :]
-
-
-def send_blocks(pixels, owner, band_count, width):
+        return turned_ref[pl.ds(pl.multiple_of(block * width, SUB), width), :]
+
+    own_ref[...] = block_of(0)
+    near_ref[0] = block_of(2)
+    near_ref[1] = block_of(3)
+    beside_ref[0] = block_of(1)
+    for n, far_ref in enumerate(far_refs):
+        far_ref[...] = block_of(BANDS // 2 + n)
+
+
+def send_blocks(pixels, owner, up, down_t, width, pack_shape):
     features, columns = pixels.shape
     any_space = pl.BlockSpec(memory_space=pl.ANY)
-    return pl.pallas_call(
+    vmem = pl.BlockSpec(memory_space=pltpu.VMEM)
+    blocks = [(width, features), (2, width, features), (1, width, features)]
+    blocks += [(width, features)] * (BANDS // 2)
+    own, near, beside, *far, pack = pl.pallas_call(
         send_kernel,
-        out_shape=[jax.ShapeDtypeStruct((width, features), BF16)] * band_count,
-        in_specs=[any_space, any_space],
-        out_specs=[pl.BlockSpec(memory_space=pltpu.VMEM)] * band_count,
+        out_shape=[jax.ShapeDtypeStruct(shape, BF16) for shape in [*blocks, pack_shape]],
+        in_specs=[any_space] * 4,
+        out_specs=[vmem] * (len(blocks) + 1),
         scratch_shapes=[
             pltpu.SMEM(owner.shape, jnp.int32),
+            pltpu.VMEM(up.shape, BF16),
+            pltpu.VMEM(down_t.shape, BF16),
             pltpu.VMEM((features, columns), BF16),
             pltpu.VMEM((columns, features), BF16),
-            pltpu.SemaphoreType.DMA,
+            pltpu.SemaphoreType.DMA((3,)),
             pltpu.SemaphoreType.DMA((features // LANE,)),
         ],
         compiler_params=params(),
         name="send_blocks",
-    )(in_hbm(owner), in_hbm(pixels))
-
-
-def exchange(pieces, pack):
-    order = distances(len(pieces))
-    near = swap(pieces[1], "band", order[1])
-    near, pack = lax.optimization_barrier((near, pack))
+    )(in_hbm(owner), in_hbm(up), in_hbm(down_t), in_hbm(pixels))
+    return own, near, beside, far, pack
+
+
+def exchange(own, near, beside, far, pack):
+    by_z = swap(near, "band", 2)
+    by_z, pack = lax.optimization_barrier((by_z, pack))
+    arrived_far = [swap(piece, "band", BANDS // 2 + n) for n, piece in enumerate(far)]
     factors = lax.all_gather(pack, "rep", axis=0, tiled=False)
-    first_late = 2 + len(pieces) // 2
-    far = [swap(piece, "band", k) for k, piece in zip(order[2:first_late], pieces[2:first_late])]
-    factors, *late = lax.optimization_barrier((factors, *pieces[first_late:]))
-    late = [swap(piece, "band", k) for k, piece in zip(order[first_late:], late)]
-    return [pieces[0], near, *far, *late], factors
+    joined, factors = lax.optimization_barrier((jnp.concatenate([beside, by_z[1:]], axis=0), factors))
+    return [own, by_z, swap(joined, "band", 1), *arrived_far], factors
 
 
 def expand_table(table, rows, half_width_padded, half_width, transpose):
@@ -136,7 +154,7 @@
     row_share,
     half_width,
     half_width_padded,
-    group_ref,
+    group_hbm_ref,
     frozen_ref,
     factors_ref,
     level_ref,
@@ -146,7 +164,11 @@
     down_ref,
     mix_ref,
     mix_t_ref,
+    group_ref,
+    group_sem,
 ):
+    load = pltpu.make_async_copy(group_hbm_ref, group_ref, group_sem)
+    load.start()
     reps, _, rank, share = factors_ref.shape
     levels = level_ref.shape[0]
     variables = group_ref.shape[0]
@@ -159,6 +181,7 @@
         down_t = down_t + dot_nn(factors_ref[r, 1], place.astype(BF16))
     down_t = down_t.astype(BF16)
     down_ref[...] = down_t
+    load.wait()
     base = jnp.concatenate([frozen_ref[group_ref[v]].astype(F32) for v in range(variables)], axis=0)
     merged = (base + dot_tn(down_t, up)).astype(BF16)
     stacked = jnp.concatenate([merged, up], axis=0)
@@ -194,12 +217,13 @@
             jax.ShapeDtypeStruct((rows, rows), BF16),
             jax.ShapeDtypeStruct((rows, rows), BF16),
         ],
-        in_specs=[pl.BlockSpec(memory_space=pltpu.SMEM)] + [vmem] * 4,
+        in_specs=[pl.BlockSpec(memory_space=pl.ANY)] + [vmem] * 4,
         out_specs=[vmem] * 5,
+        scratch_shapes=[pltpu.SMEM(groups.shape, jnp.int32), pltpu.SemaphoreType.DMA],
         compiler_params=params(),
         cost_estimate=pl.CostEstimate(flops=flops, bytes_accessed=4 * 2**20, transcendentals=0),
         name="prepare",
-    )(groups, in_hbm(frozen), factors, in_hbm(level_weight), in_hbm(mixer))
+    )(in_hbm(groups), in_hbm(frozen), factors, in_hbm(level_weight), in_hbm(mixer))
 
 
 def normal_parts(values):
@@ -259,6 +283,7 @@
     samples, reach, feature_dim = merged_ref.shape
     chunk_count, _, width, _ = grad_ref.shape
     halves = piece_refs[0].shape[-2] // width
+    arrived_directly = len(piece_refs) > 1
     depth = piece_refs[0].shape[-1] // samples
     rows = WLAT * width
 
@@ -279,16 +304,19 @@
     for load in loads:
         load.start()
     level_load.start()
-    if len(piece_refs) > 1:
+    if arrived_directly:
+        own_ref, by_z_ref, by_x_ref, *far_refs = piece_refs
+        sources = {0: own_ref, 1: by_x_ref.at[0], 2: by_z_ref.at[0], 3: by_x_ref.at[1]}
+        sources |= {BANDS // 2 + n: far_ref for n, far_ref in enumerate(far_refs)}
         me = lax.axis_index("band")
-        for k, piece_ref in zip(distances(len(piece_refs)), piece_refs):
+        for distance, piece_ref in sources.items():
             for half in range(halves):
                 within = slice(half * width, (half + 1) * width)
-                arrived_ref[half, jnp.bitwise_xor(me, k)] = piece_ref[within, :]
+                arrived_ref[half, jnp.bitwise_xor(me, distance)] = piece_ref[within, :]
 
     def pixels_of(n, lanes):
         window_row, half, _, _ = place(n)
-        if len(piece_refs) > 1:
+        if arrived_directly:
             block = arrived_ref[half, :, :, lanes]
         else:
             lines = slice(window_row * WLAT, (window_row + 1) * WLAT)
@@ -489,19 +517,14 @@
     padded_width = halves * half_padded
     features = samples * levels * channels
 
-    pack_width = round_up(max(row_share, col_share), LANE)
-    pack = jnp.stack(
-        [
-            jnp.pad(adapter_up, ((0, 0), (0, pack_width - col_share))),
-            jnp.pad(adapter_down.T, ((0, 0), (0, pack_width - row_share))),
-        ]
-    )
-
     pixels = patches.reshape(features, col_count)
-    direct = band_count <= MAX_PERMUTES and lat_rows == WLAT and half_padded == half_width
+    pack_shape = (2, rank, round_up(max(row_share, col_share), LANE))
+    direct = band_count == BANDS and lat_rows == WLAT and half_padded == half_width
     if direct and features % LANE == 0 and col_count % LANE == 0:
-        pieces = send_blocks(pixels, column_block_owner, band_count, block_width)
-        arrived, factors = exchange(pieces, pack)
+        pieces = send_blocks(
+            pixels, column_block_owner, adapter_up, adapter_down.T, block_width, pack_shape
+        )
+        arrived, factors = exchange(*pieces)
     else:
         block_ids = jnp.arange(band_count, dtype=jnp.int32)
         inverse = jnp.sum(
@@ -510,6 +533,12 @@
         outgoing = jnp.take(pixels.T.reshape(band_count, block_width, features), inverse, axis=0)
         outgoing = jnp.pad(outgoing, ((0, 0), (0, padded_width - block_width), (0, 0)))
         arrived = [lax.all_to_all(outgoing, "band", split_axis=0, concat_axis=0, tiled=True)]
+        pack = jnp.stack(
+            [
+                jnp.pad(array, ((0, 0), (0, pack_shape[2] - array.shape[1])))
+                for array in (adapter_up, adapter_down.T)
+            ]
+        )
         factors = lax.all_gather(pack, "rep", axis=0, tiled=False)
 
     merged, up_through, down_t, mix, mix_t = prepare(

time: 53.8 us -> 66.4 us (1.23)
  waiting for transfers between devices: 6.25 us -> 14.9 us
  blocking collectives: 19.7 us -> 23.2 us
  starting transfers between devices: 10.7 us -> 12.5 us
  local copies, waits for them, and re-layouts: 1.35 us -> 0.01 us
    ppermute x7 -> x6, waiting for transfers between devices: 6.25 us -> 14.9 us  [swap(): lax.ppermute(values, axis, [(source, source ^ distance) for source in ran...]
    all_to_all x1, blocking collectives: 14.5 us -> 18 us  [sum_shares(): lax.all_to_all(shares, ('band', 'rep'), split_axis=0, concat_axis=0, tile...]
    ppermute x7 -> x6, starting transfers between devices: 10.7 us -> 12.5 us  [swap(): lax.ppermute(values, axis, [(source, source ^ distance) for source in ran...]
    another operation x1 -> x0, local copies, waits for them, and re-layouts: 0.69 us -> none  [on_device(): jnp.stack([jnp.pad(adapter_up, ((0, 0), (0, pack_width - col_share))), jn...]
    another operation x1 -> x0, other arithmetic: 0.69 us -> none  [on_device(): jnp.stack([jnp.pad(adapter_up, ((0, 0), (0, pack_width - col_share))), jn...]
  transfers between devices with their start and end apart: 7 -> 6, of which waited for: 3 -> 3; matrix products, arithmetic and copies ran while one was open for 3% -> 0% of each run, Pallas kernels for 5% -> 5%
where the time goes in v8:
time: 66.4 us; the launch traced here: 66 us
  blocking collectives  23.2 us (35%)
  waiting for transfers between devices  14.9 us (22%)
  Pallas kernels  14.7 us (22%)
  starting transfers between devices  12.5 us (19%)
  between operations  0.68 us (1%)
    all_to_all x1, blocking collectives, sum_shares(): lax.all_to_all(shares, ('band', 'rep'), split_axis=0, concat_axis=0, tile...  18 us
    ppermute x6, waiting for transfers between devices, swap(): lax.ppermute(values, axis, [(source, source ^ distance) for source in ran...  14.9 us
    ppermute x6, starting transfers between devices, swap(): lax.ppermute(values, axis, [(source, source ^ distance) for source in ran...  12.5 us
    pallas_call x1, Pallas kernels, mix_blocks(): pl.pallas_call(lambda *refs: mix_kernel(refs[:len(arrived)], *refs[len(ar...  8.92 us
    all_gather x1, blocking collectives, exchange(): factors = lax.all_gather(pack, 'rep', axis=0, tiled=False)  5.18 us
    pallas_call x1, Pallas kernels, prepare(): pl.pallas_call(functools.partial(prep_kernel, row_share, half_width, half...  3.42 us
    pallas_call x1, Pallas kernels, send_blocks(): pl.pallas_call(send_kernel, out_shape=[jax.ShapeDtypeStruct(shape, BF16)...  1.64 us
  transfers between devices with their start and end apart: 6, of which 3 were waited for; matrix products, arithmetic and copies ran while one was open for 0% of the time, Pallas kernels for 5%

profile of v8, /device:TPU:0, one launch (start us, length us, event | category | flops | bytes accessed | tf_op | source)
XLA Modules:
  0.0 66.0 jit_solution(17493841571084589511)
XLA Ops:
  0.6 1.6 %send_blocks.1 = (bf16[96,640]{1,0:T(8,128)(2,1)S(1)}, bf16[2,96,640]{2,1,0:T(8,128)(2,1)S(1)}, bf16[1,96,640]{2,1,0:T(8,128)(2,1)S(1)}, bf16[96,640]{1,0:T(8,12...) custom-call(s32[8]{0:T(128)} %owner_hbm_ref.1, ...), custom_call_target="tpu_custom_call" | custom-call | tf_op jit(solution)/shard_map/send_blocks/pallas_call | solution.py:112
  2.3 3.1 %collective-permute-start = (bf16[2,96,640]{2,1,0:T(8,128)(2,1)S(1)}, bf16[2,96,640]{2,1,0:T(8,128)(2,1)S(1)}, u32[]{:S(2)}, u32[]{:S(2)}) collective-permute-start(bf16[2,96,640]{2,1,0:T(8,128)(2,1)S(1)} %get-tuple-element.25), channel_id=1, source_target_pairs={{0,8},{4,12},{8,0},{12,4},{16,24},{20,28},{24,16},{28,20},{1,9},{5... | collective-permute-start | bytes 737288 | tf_op jit(solution)/shard_map/ppermute | solution.py:58
  5.4 6.0 %collective-permute-done.refs_1_ = bf16[2,96,640]{2,1,0:T(8,128)(2,1)S(1)} collective-permute-done((bf16[2,96,640]{2,1,0:T(8,128)(2,1)S(1)}, bf16[2,96,640]{2,1,0:T(8,128)(2,1)S(1)}, u32[]{:S(2)}, u32[]{:S(2)}) %collective-permute-start) | collective-permute-done | bytes 245792 | tf_op jit(solution)/shard_map/ppermute | solution.py:58
  11.3 5.2 %all-gather = bf16[8,16,128]{2,1,0:T(8,128)(2,1)S(1)} all-gather(bf16[2,16,128]{2,1,0:T(8,128)(2,1)S(1)} %get-tuple-element.29), channel_id=2, replica_groups=mesh['band'=8,'rep'=4] {'rep'}, dimensions={0}, use_global_device_ids=true | all-gather | bytes 40960 | tf_op jit(solution)/shard_map/all_gather | solution.py:136
  16.6 1.7 %collective-permute-start.1 = (bf16[2,96,640]{2,1,0:T(8,128)(2,1)S(1)}, bf16[2,96,640]{2,1,0:T(8,128)(2,1)S(1)}, u32[]{:S(2)}, u32[]{:S(2)}) collective-permute-start(bf16[2,96,640]{2,1,0:T(8,128)(2,1)S(1)} %pad_maximum_fusion), channel_id=1, source_target_pairs={{0,4},{4,0},{8,12},{12,8},{16,20},{20,16},{24,28},{28,24},{1,5},{5... | collective-permute-start | bytes 737288 | tf_op jit(solution)/shard_map/ppermute | solution.py:58
  18.3 2.6 %collective-permute-start.2 = (bf16[96,640]{1,0:T(8,128)(2,1)S(1)}, bf16[96,640]{1,0:T(8,128)(2,1)S(1)}, u32[]{:S(2)}, u32[]{:S(2)}) collective-permute-start(bf16[96,640]{1,0:T(8,128)(2,1)S(1)} %get-tuple-element.31), channel_id=1, source_target_pairs={{0,16},{4,20},{8,24},{12,28},{16,0},{20,4},{24,8},{28,12},{1,17},{... | collective-permute-start | bytes 368648 | tf_op jit(solution)/shard_map/ppermute | solution.py:58
  20.9 0.1 collective-permute-start.3
  21.0 3.8 %collective-permute-start.4 = (bf16[96,640]{1,0:T(8,128)(2,1)S(1)}, bf16[96,640]{1,0:T(8,128)(2,1)S(1)}, u32[]{:S(2)}, u32[]{:S(2)}) collective-permute-start(bf16[96,640]{1,0:T(8,128)(2,1)S(1)} %get-tuple-element.33), channel_id=1, source_target_pairs={{0,24},{4,28},{8,16},{12,20},{16,8},{20,12},{24,0},{28,4},{1,25},{... | collective-permute-start | bytes 368648 | tf_op jit(solution)/shard_map/ppermute | solution.py:58
  24.8 1.1 %collective-permute-start.5 = (bf16[96,640]{1,0:T(8,128)(2,1)S(1)}, bf16[96,640]{1,0:T(8,128)(2,1)S(1)}, u32[]{:S(2)}, u32[]{:S(2)}) collective-permute-start(bf16[96,640]{1,0:T(8,128)(2,1)S(1)} %get-tuple-element.34), channel_id=1, source_target_pairs={{0,28},{4,24},{8,20},{12,16},{16,12},{20,8},{24,4},{28,0},{1,29},{... | collective-permute-start | bytes 368648 | tf_op jit(solution)/shard_map/ppermute | solution.py:58
  25.9 3.4 %prepare.1 = (bf16[2,384,512]{2,1,0:T(8,128)(2,1)S(1)}, bf16[4,32,512]{2,1,0:T(8,128)(2,1)S(1)}, bf16[16,80]{1,0:T(8,128)(2,1)S(1)}, bf16[384,384]{1,0:T(8,128)(2,1)S(1)}, bf16[384,384]{1,0:T(8,128)(2,1)S(1)}) custom-call(s32[5]{0:T(128)} %group_hbm_ref.1, bf16[3,16,512]{2,1,0:T(8,128)(2,1)} %frozen_ref.1, bf16[4,2,16,128]{3,2,1,0:T(8,128)(2,1)S(1)} %bitcast.8, ...), custom_call_target="tpu_custom_call" | custom-call | flops 257949696 | bytes 4194304 | tf_op jit(solution)/shard_map/prepare/pallas_call | solution.py:211
  29.3 6.5 %collective-permute-done.2.refs_3_ = bf16[96,640]{1,0:T(8,128)(2,1)S(1)} collective-permute-done((bf16[96,640]{1,0:T(8,128)(2,1)S(1)}, bf16[96,640]{1,0:T(8,128)(2,1)S(1)}, u32[]{:S(2)}, u32[]{:S(2)}) %collective-permute-start.2) | collective-permute-done | bytes 122912 | tf_op jit(solution)/shard_map/ppermute | solution.py:58
  35.9 2.4 %collective-permute-done.3.refs_4_ = bf16[96,640]{1,0:T(8,128)(2,1)S(1)} collective-permute-done((bf16[96,640]{1,0:T(8,128)(2,1)S(1)}, bf16[96,640]{1,0:T(8,128)(2,1)S(1)}, u32[]{:S(2)}, u32[]{:S(2)}) %collective-permute-start.3) | collective-permute-done | bytes 122912 | tf_op jit(solution)/shard_map/ppermute | solution.py:58
  38.3 0.0 collective-permute-done.4.refs_5_
  38.3 0.0 collective-permute-done.5.refs_6_
  38.3 0.0 collective-permute-done.1.refs_2_
  38.3 8.9 %mix_blocks.1 = (bf16[2,8,96,512]{3,2,1,0:T(8,128)(2,1)}, bf16[32,24,128]{2,1,0:T(8,128)(2,1)S(1)}) custom-call(bf16[96,640]{1,0:T(8,128)(2,1)S(1)} %get-tuple-element.24.refs_0_, bf16[2,96,640]{2,1,0:T(8,128)(2,1)S(1)} %collective-permute-done.refs_1_, bf16[2,96,640]{2,1,0:T(8,128)(2,1)S(1)} %collective-permute-done.1.refs_2_, ...), custom_call_target="tpu_custom_call" | custom-call | flops 2415919104 | bytes 12582912 | tf_op jit(solution)/shard_map/mix_blocks/pallas_call | solution.py:438
  47.3 18.0 %all_to_all.5.parts_ref = bf16[32,24,128]{2,1,0:T(8,128)(2,1)S(1)} all-to-all(bf16[32,24,128]{2,1,0:T(8,128)(2,1)S(1)} %get-tuple-element.42), channel_id=1, replica_groups=mesh['band'=8,'rep'=4] {'band','rep'}, dimensions={0} | all-to-all | bytes 393216 | tf_op jit(solution)/shard_map/all_to_all | solution.py:484
  65.3 0.7 %sum_shares.1 = (f32[16,20]{1,0:T(8,128)}, f32[16,128]{1,0:T(8,128)}) custom-call(bf16[32,24,128]{2,1,0:T(8,128)(2,1)S(1)} %all_to_all.5.parts_ref), custom_call_target="tpu_custom_call" | custom-call | tf_op jit(solution)/shard_map/sum_shares/pallas_call | solution.py:485
  (2 shorter events, 0.0 us)
Async XLA Ops:
  2.3 9.0 %collective-permute-start = (bf16[2,96,640]{2,1,0:T(8,128)(2,1)S(1)}, bf16[2,96,640]{2,1,0:T(8,128)(2,1)S(1)}, u32[]{:S(2)}, u32[]{:S(2)}) collective-permute-start(bf16[2,96,640]{2,1,0:T(8,128)(2,1)S(1)} %get-tuple-element.25), channel_id=1, source_target_pairs={{0,8},{4,12},{8,0},{12,4},{16,24},{20,28},{24,16},{28,20},{1,9},{5... | collective-permute-start | bytes 737288 | tf_op jit(solution)/shard_map/ppermute | solution.py:58
  16.6 21.8 %collective-permute-start.1 = (bf16[2,96,640]{2,1,0:T(8,128)(2,1)S(1)}, bf16[2,96,640]{2,1,0:T(8,128)(2,1)S(1)}, u32[]{:S(2)}, u32[]{:S(2)}) collective-permute-start(bf16[2,96,640]{2,1,0:T(8,128)(2,1)S(1)} %pad_maximum_fusion), channel_id=1, source_target_pairs={{0,4},{4,0},{8,12},{12,8},{16,20},{20,16},{24,28},{28,24},{1,5},{5... | collective-permute-start | bytes 737288 | tf_op jit(solution)/shard_map/ppermute | solution.py:58
  18.3 17.6 %collective-permute-start.2 = (bf16[96,640]{1,0:T(8,128)(2,1)S(1)}, bf16[96,640]{1,0:T(8,128)(2,1)S(1)}, u32[]{:S(2)}, u32[]{:S(2)}) collective-permute-start(bf16[96,640]{1,0:T(8,128)(2,1)S(1)} %get-tuple-element.31), channel_id=1, source_target_pairs={{0,16},{4,20},{8,24},{12,28},{16,0},{20,4},{24,8},{28,12},{1,17},{... | collective-permute-start | bytes 368648 | tf_op jit(solution)/shard_map/ppermute | solution.py:58
  20.9 17.5 %collective-permute-start.3 = (bf16[96,640]{1,0:T(8,128)(2,1)S(1)}, bf16[96,640]{1,0:T(8,128)(2,1)S(1)}, u32[]{:S(2)}, u32[]{:S(2)}) collective-permute-start(bf16[96,640]{1,0:T(8,128)(2,1)S(1)} %get-tuple-element.32), channel_id=1, source_target_pairs={{0,20},{4,16},{8,28},{12,24},{16,4},{20,0},{24,12},{28,8},{1,21},{... | collective-permute-start | bytes 368648 | tf_op jit(solution)/shard_map/ppermute | solution.py:58
  21.0 17.3 %collective-permute-start.4 = (bf16[96,640]{1,0:T(8,128)(2,1)S(1)}, bf16[96,640]{1,0:T(8,128)(2,1)S(1)}, u32[]{:S(2)}, u32[]{:S(2)}) collective-permute-start(bf16[96,640]{1,0:T(8,128)(2,1)S(1)} %get-tuple-element.33), channel_id=1, source_target_pairs={{0,24},{4,28},{8,16},{12,20},{16,8},{20,12},{24,0},{28,4},{1,25},{... | collective-permute-start | bytes 368648 | tf_op jit(solution)/shard_map/ppermute | solution.py:58
  24.8 13.5 %collective-permute-start.5 = (bf16[96,640]{1,0:T(8,128)(2,1)S(1)}, bf16[96,640]{1,0:T(8,128)(2,1)S(1)}, u32[]{:S(2)}, u32[]{:S(2)}) collective-permute-start(bf16[96,640]{1,0:T(8,128)(2,1)S(1)} %get-tuple-element.34), channel_id=1, source_target_pairs={{0,28},{4,24},{8,20},{12,16},{16,12},{20,8},{24,4},{28,0},{1,29},{... | collective-permute-start | bytes 368648 | tf_op jit(solution)/shard_map/ppermute | solution.py:58

commit v9 on v8

--- a/solution.py
+++ b/solution.py
@@ -98,7 +98,7 @@
     own_ref[...] = block_of(0)
     near_ref[0] = block_of(2)
     near_ref[1] = block_of(3)
-    beside_ref[0] = block_of(1)
+    beside_ref[...] = block_of(1)
     for n, far_ref in enumerate(far_refs):
         far_ref[...] = block_of(BANDS // 2 + n)
 
@@ -107,7 +107,7 @@
     features, columns = pixels.shape
     any_space = pl.BlockSpec(memory_space=pl.ANY)
     vmem = pl.BlockSpec(memory_space=pltpu.VMEM)
-    blocks = [(width, features), (2, width, features), (1, width, features)]
+    blocks = [(width, features), (2, width, features), (width, features)]
     blocks += [(width, features)] * (BANDS // 2)
     own, near, beside, *far, pack = pl.pallas_call(
         send_kernel,
@@ -134,8 +134,8 @@
     by_z, pack = lax.optimization_barrier((by_z, pack))
     arrived_far = [swap(piece, "band", BANDS // 2 + n) for n, piece in enumerate(far)]
     factors = lax.all_gather(pack, "rep", axis=0, tiled=False)
-    joined, factors = lax.optimization_barrier((jnp.concatenate([beside, by_z[1:]], axis=0), factors))
-    return [own, by_z, swap(joined, "band", 1), *arrived_far], factors
+    factors, beside, onward = lax.optimization_barrier((factors, beside, by_z[1]))
+    return [own, by_z, *arrived_far, swap(beside, "band", 1), swap(onward, "band", 1)], factors
 
 
 def expand_table(table, rows, half_width_padded, half_width, transpose):
@@ -305,8 +305,8 @@
         load.start()
     level_load.start()
     if arrived_directly:
-        own_ref, by_z_ref, by_x_ref, *far_refs = piece_refs
-        sources = {0: own_ref, 1: by_x_ref.at[0], 2: by_z_ref.at[0], 3: by_x_ref.at[1]}
+        own_ref, by_z_ref, *far_refs, beside_ref, onward_ref = piece_refs
+        sources = {0: own_ref, 1: beside_ref, 2: by_z_ref.at[0], 3: onward_ref}
         sources |= {BANDS // 2 + n: far_ref for n, far_ref in enumerate(far_refs)}
         me = lax.axis_index("band")
         for distance, piece_ref in sources.items():

time: 66.4 us -> 54.1 us (0.81)
  waiting for transfers between devices: 14.9 us -> 7.33 us
  blocking collectives: 23.2 us -> 18.2 us
    ppermute x6 -> x7, waiting for transfers between devices: 14.9 us -> 7.33 us  [swap(): lax.ppermute(values, axis, [(source, source ^ distance) for source in ran...]
    all_to_all x1, blocking collectives: 18 us -> 13.1 us  [sum_shares(): lax.all_to_all(shares, ('band', 'rep'), split_axis=0, concat_axis=0, tile...]
    ppermute x6 -> x7, starting transfers between devices: 12.5 us -> 12.8 us  [swap(): lax.ppermute(values, axis, [(source, source ^ distance) for source in ran...]
  transfers between devices with their start and end apart: 6 -> 7, of which waited for: 3 -> 4; matrix products, arithmetic and copies ran while one was open for 0% -> 0% of each run, Pallas kernels for 5% -> 6%
where the time goes in v9:
time: 54.1 us; the launch traced here: 53.7 us
  blocking collectives  18.2 us (34%)
  Pallas kernels  14.7 us (27%)
  starting transfers between devices  12.8 us (24%)
  waiting for transfers between devices  7.33 us (14%)
  between operations  0.67 us (1%)
    all_to_all x1, blocking collectives, sum_shares(): lax.all_to_all(shares, ('band', 'rep'), split_axis=0, concat_axis=0, tile...  13.1 us
    ppermute x7, starting transfers between devices, swap(): lax.ppermute(values, axis, [(source, source ^ distance) for source in ran...  12.8 us
    pallas_call x1, Pallas kernels, mix_blocks(): pl.pallas_call(lambda *refs: mix_kernel(refs[:len(arrived)], *refs[len(ar...  8.92 us
    ppermute x7, waiting for transfers between devices, swap(): lax.ppermute(values, axis, [(source, source ^ distance) for source in ran...  7.33 us
    all_gather x1, blocking collectives, exchange(): factors = lax.all_gather(pack, 'rep', axis=0, tiled=False)  5.18 us
    pallas_call x1, Pallas kernels, prepare(): pl.pallas_call(functools.partial(prep_kernel, row_share, half_width, half...  3.42 us
    pallas_call x1, Pallas kernels, send_blocks(): pl.pallas_call(send_kernel, out_shape=[jax.ShapeDtypeStruct(shape, BF16)...  1.64 us
  transfers between devices with their start and end apart: 7, of which 4 were waited for; matrix products, arithmetic and copies ran while one was open for 0% of the time, Pallas kernels for 6%

profile of v9, /device:TPU:0, one launch (start us, length us, event | category | flops | bytes accessed | tf_op | source)
XLA Modules:
  0.0 53.7 jit_solution(15296709805808385253)
XLA Ops:
  0.6 1.6 %send_blocks.1 = (bf16[96,640]{1,0:T(8,128)(2,1)S(1)}, bf16[2,96,640]{2,1,0:T(8,128)(2,1)S(1)}, bf16[96,640]{1,0:T(8,128)(2,1)S(1)}, bf16[96,640]{1,0:T(8,128)(2...) custom-call(s32[8]{0:T(128)} %owner_hbm_ref.1, ...), custom_call_target="tpu_custom_call" | custom-call | tf_op jit(solution)/shard_map/send_blocks/pallas_call | solution.py:112
  2.3 3.1 %collective-permute-start = (bf16[2,96,640]{2,1,0:T(8,128)(2,1)S(1)}, bf16[2,96,640]{2,1,0:T(8,128)(2,1)S(1)}, u32[]{:S(2)}, u32[]{:S(2)}) collective-permute-start(bf16[2,96,640]{2,1,0:T(8,128)(2,1)S(1)} %get-tuple-element.26), channel_id=1, source_target_pairs={{0,8},{4,12},{8,0},{12,4},{16,24},{20,28},{24,16},{28,20},{1,9},{5... | collective-permute-start | bytes 737288 | tf_op jit(solution)/shard_map/ppermute | solution.py:58
  5.4 2.6 %collective-permute-start.1 = (bf16[96,640]{1,0:T(8,128)(2,1)S(1)}, bf16[96,640]{1,0:T(8,128)(2,1)S(1)}, u32[]{:S(2)}, u32[]{:S(2)}) collective-permute-start(bf16[96,640]{1,0:T(8,128)(2,1)S(1)} %get-tuple-element.29), channel_id=1, source_target_pairs={{0,16},{4,20},{8,24},{12,28},{16,0},{20,4},{24,8},{28,12},{1,17},{... | collective-permute-start | bytes 368648 | tf_op jit(solution)/shard_map/ppermute | solution.py:58
  8.0 1.3 %collective-permute-start.2 = (bf16[96,640]{1,0:T(8,128)(2,1)S(1)}, bf16[96,640]{1,0:T(8,128)(2,1)S(1)}, u32[]{:S(2)}, u32[]{:S(2)}) collective-permute-start(bf16[96,640]{1,0:T(8,128)(2,1)S(1)} %get-tuple-element.30), channel_id=1, source_target_pairs={{0,20},{4,16},{8,28},{12,24},{16,4},{20,0},{24,12},{28,8},{1,21},{... | collective-permute-start | bytes 368648 | tf_op jit(solution)/shard_map/ppermute | solution.py:58
  9.2 2.5 %collective-permute-start.3 = (bf16[96,640]{1,0:T(8,128)(2,1)S(1)}, bf16[96,640]{1,0:T(8,128)(2,1)S(1)}, u32[]{:S(2)}, u32[]{:S(2)}) collective-permute-start(bf16[96,640]{1,0:T(8,128)(2,1)S(1)} %get-tuple-element.31), channel_id=1, source_target_pairs={{0,24},{4,28},{8,16},{12,20},{16,8},{20,12},{24,0},{28,4},{1,25},{... | collective-permute-start | bytes 368648 | tf_op jit(solution)/shard_map/ppermute | solution.py:58
  11.7 1.3 %collective-permute-start.4 = (bf16[96,640]{1,0:T(8,128)(2,1)S(1)}, bf16[96,640]{1,0:T(8,128)(2,1)S(1)}, u32[]{:S(2)}, u32[]{:S(2)}) collective-permute-start(bf16[96,640]{1,0:T(8,128)(2,1)S(1)} %get-tuple-element.32), channel_id=1, source_target_pairs={{0,28},{4,24},{8,20},{12,16},{16,12},{20,8},{24,4},{28,0},{1,29},{... | collective-permute-start | bytes 368648 | tf_op jit(solution)/shard_map/ppermute | solution.py:58
  13.0 2.6 %collective-permute-done.refs_1_ = bf16[2,96,640]{2,1,0:T(8,128)(2,1)S(1)} collective-permute-done((bf16[2,96,640]{2,1,0:T(8,128)(2,1)S(1)}, bf16[2,96,640]{2,1,0:T(8,128)(2,1)S(1)}, u32[]{:S(2)}, u32[]{:S(2)}) %collective-permute-start) | collective-permute-done | bytes 245792 | tf_op jit(solution)/shard_map/ppermute | solution.py:58
  15.6 5.2 %all-gather = bf16[8,16,128]{2,1,0:T(8,128)(2,1)S(1)} all-gather(bf16[2,16,128]{2,1,0:T(8,128)(2,1)S(1)} %get-tuple-element.33), channel_id=2, replica_groups=mesh['band'=8,'rep'=4] {'rep'}, dimensions={0}, use_global_device_ids=true | all-gather | bytes 40960 | tf_op jit(solution)/shard_map/all_gather | solution.py:136
  20.8 2.0 %collective-permute-start.5 = (bf16[96,640]{1,0:T(8,128)(2,1)S(1)}, bf16[96,640]{1,0:T(8,128)(2,1)S(1)}, u32[]{:S(2)}, u32[]{:S(2)}) collective-permute-start(bf16[96,640]{1,0:T(8,128)(2,1)S(1)} %get-tuple-element.35), channel_id=1, source_target_pairs={{0,4},{4,0},{8,12},{12,8},{16,20},{20,16},{24,28},{28,24},{1,5},{5... | collective-permute-start | bytes 368648 | tf_op jit(solution)/shard_map/ppermute | solution.py:58
  22.8 0.0 collective-permute-done.1.refs_2_
  22.8 0.1 collective-permute-start.6
  22.9 3.4 %prepare.1 = (bf16[2,384,512]{2,1,0:T(8,128)(2,1)S(1)}, bf16[4,32,512]{2,1,0:T(8,128)(2,1)S(1)}, bf16[16,80]{1,0:T(8,128)(2,1)S(1)}, bf16[384,384]{1,0:T(8,128)(2,1)S(1)}, bf16[384,384]{1,0:T(8,128)(2,1)S(1)}) custom-call(s32[5]{0:T(128)} %group_hbm_ref.1, bf16[3,16,512]{2,1,0:T(8,128)(2,1)} %frozen_ref.1, bf16[4,2,16,128]{3,2,1,0:T(8,128)(2,1)S(1)} %bitcast.10, ...), custom_call_target="tpu_custom_call" | custom-call | flops 257949696 | bytes 4194304 | tf_op jit(solution)/shard_map/prepare/pallas_call | solution.py:211
  26.3 0.2 collective-permute-done.2.refs_3_
  26.5 0.0 collective-permute-done.3.refs_4_
  26.5 0.0 collective-permute-done.4.refs_5_
  26.5 1.9 %collective-permute-done.5.refs_6_ = bf16[96,640]{1,0:T(8,128)(2,1)S(1)} collective-permute-done((bf16[96,640]{1,0:T(8,128)(2,1)S(1)}, bf16[96,640]{1,0:T(8,128)(2,1)S(1)}, u32[]{:S(2)}, u32[]{:S(2)}) %collective-permute-start.5) | collective-permute-done | bytes 122912 | tf_op jit(solution)/shard_map/ppermute | solution.py:58
  28.5 2.6 %collective-permute-done.6.refs_7_ = bf16[96,640]{1,0:T(8,128)(2,1)S(1)} collective-permute-done((bf16[96,640]{1,0:T(8,128)(2,1)S(1)}, bf16[96,640]{1,0:T(8,128)(2,1)S(1)}, u32[]{:S(2)}, u32[]{:S(2)}) %collective-permute-start.6) | collective-permute-done | bytes 122912 | tf_op jit(solution)/shard_map/ppermute | solution.py:58
  31.1 8.9 %mix_blocks.1 = (bf16[2,8,96,512]{3,2,1,0:T(8,128)(2,1)}, bf16[32,24,128]{2,1,0:T(8,128)(2,1)S(1)}) custom-call(bf16[96,640]{1,0:T(8,128)(2,1)S(1)} %get-tuple-element.25.refs_0_, bf16[2,96,640]{2,1,0:T(8,128)(2,1)S(1)} %collective-permute-done.refs_1_, bf16[96,640]{1,0:T(8,128)(2,1)S(1)} %collective-permute-done.1.refs_2_, ...), custom_call_target="tpu_custom_call" | custom-call | flops 2415919104 | bytes 12582912 | tf_op jit(solution)/shard_map/mix_blocks/pallas_call | solution.py:438
  40.0 13.1 %all_to_all.5.parts_ref = bf16[32,24,128]{2,1,0:T(8,128)(2,1)S(1)} all-to-all(bf16[32,24,128]{2,1,0:T(8,128)(2,1)S(1)} %get-tuple-element.44), channel_id=1, replica_groups=mesh['band'=8,'rep'=4] {'band','rep'}, dimensions={0} | all-to-all | bytes 393216 | tf_op jit(solution)/shard_map/all_to_all | solution.py:484
  53.0 0.7 %sum_shares.1 = (f32[16,20]{1,0:T(8,128)}, f32[16,128]{1,0:T(8,128)}) custom-call(bf16[32,24,128]{2,1,0:T(8,128)(2,1)S(1)} %all_to_all.5.parts_ref), custom_call_target="tpu_custom_call" | custom-call | tf_op jit(solution)/shard_map/sum_shares/pallas_call | solution.py:485
  (1 shorter events, 0.0 us)
Async XLA Ops:
  2.3 13.3 %collective-permute-start = (bf16[2,96,640]{2,1,0:T(8,128)(2,1)S(1)}, bf16[2,96,640]{2,1,0:T(8,128)(2,1)S(1)}, u32[]{:S(2)}, u32[]{:S(2)}) collective-permute-start(bf16[2,96,640]{2,1,0:T(8,128)(2,1)S(1)} %get-tuple-element.26), channel_id=1, source_target_pairs={{0,8},{4,12},{8,0},{12,4},{16,24},{20,28},{24,16},{28,20},{1,9},{5... | collective-permute-start | bytes 737288 | tf_op jit(solution)/shard_map/ppermute | solution.py:58
  5.4 17.4 %collective-permute-start.1 = (bf16[96,640]{1,0:T(8,128)(2,1)S(1)}, bf16[96,640]{1,0:T(8,128)(2,1)S(1)}, u32[]{:S(2)}, u32[]{:S(2)}) collective-permute-start(bf16[96,640]{1,0:T(8,128)(2,1)S(1)} %get-tuple-element.29), channel_id=1, source_target_pairs={{0,16},{4,20},{8,24},{12,28},{16,0},{20,4},{24,8},{28,12},{1,17},{... | collective-permute-start | bytes 368648 | tf_op jit(solution)/shard_map/ppermute | solution.py:58
  8.0 18.6 %collective-permute-start.2 = (bf16[96,640]{1,0:T(8,128)(2,1)S(1)}, bf16[96,640]{1,0:T(8,128)(2,1)S(1)}, u32[]{:S(2)}, u32[]{:S(2)}) collective-permute-start(bf16[96,640]{1,0:T(8,128)(2,1)S(1)} %get-tuple-element.30), channel_id=1, source_target_pairs={{0,20},{4,16},{8,28},{12,24},{16,4},{20,0},{24,12},{28,8},{1,21},{... | collective-permute-start | bytes 368648 | tf_op jit(solution)/shard_map/ppermute | solution.py:58
  9.2 17.3 %collective-permute-start.3 = (bf16[96,640]{1,0:T(8,128)(2,1)S(1)}, bf16[96,640]{1,0:T(8,128)(2,1)S(1)}, u32[]{:S(2)}, u32[]{:S(2)}) collective-permute-start(bf16[96,640]{1,0:T(8,128)(2,1)S(1)} %get-tuple-element.31), channel_id=1, source_target_pairs={{0,24},{4,28},{8,16},{12,20},{16,8},{20,12},{24,0},{28,4},{1,25},{... | collective-permute-start | bytes 368648 | tf_op jit(solution)/shard_map/ppermute | solution.py:58
  11.7 14.8 %collective-permute-start.4 = (bf16[96,640]{1,0:T(8,128)(2,1)S(1)}, bf16[96,640]{1,0:T(8,128)(2,1)S(1)}, u32[]{:S(2)}, u32[]{:S(2)}) collective-permute-start(bf16[96,640]{1,0:T(8,128)(2,1)S(1)} %get-tuple-element.32), channel_id=1, source_target_pairs={{0,28},{4,24},{8,20},{12,16},{16,12},{20,8},{24,4},{28,0},{1,29},{... | collective-permute-start | bytes 368648 | tf_op jit(solution)/shard_map/ppermute | solution.py:58
  20.8 7.7 %collective-permute-start.5 = (bf16[96,640]{1,0:T(8,128)(2,1)S(1)}, bf16[96,640]{1,0:T(8,128)(2,1)S(1)}, u32[]{:S(2)}, u32[]{:S(2)}) collective-permute-start(bf16[96,640]{1,0:T(8,128)(2,1)S(1)} %get-tuple-element.35), channel_id=1, source_target_pairs={{0,4},{4,0},{8,12},{12,8},{16,20},{20,16},{24,28},{28,24},{1,5},{5... | collective-permute-start | bytes 368648 | tf_op jit(solution)/shard_map/ppermute | solution.py:58
  22.8 8.3 %collective-permute-start.6 = (bf16[96,640]{1,0:T(8,128)(2,1)S(1)}, bf16[96,640]{1,0:T(8,128)(2,1)S(1)}, u32[]{:S(2)}, u32[]{:S(2)}) collective-permute-start(bf16[96,640]{1,0:T(8,128)(2,1)S(1)} %slice_bitcast_fusion), channel_id=1, source_target_pairs={{0,4},{4,0},{8,12},{12,8},{16,20},{20,16},{24,28},{28,24},{1,5},{5... | collective-permute-start | bytes 368648 | tf_op jit(solution)/shard_map/ppermute | solution.py:58

commit v10 on v9

--- a/solution.py
+++ b/solution.py
@@ -13,8 +13,10 @@
 SUB = 16
 VMEM_LIMIT = 24 * 1024 * 1024
 BANDS = 8
+ORDER = (0, 4, 1, 5, 2, 6, 7, 3)
 FOLDS = 2
 COLUMNS = 256
+PAIR = 2
 BF16 = jnp.bfloat16
 F32 = jnp.float32
 
@@ -58,10 +60,10 @@
     return lax.ppermute(values, axis, [(source, source ^ distance) for source in range(count)])
 
 
-def send_kernel(owner_hbm_ref, up_hbm_ref, down_hbm_ref, x_hbm_ref, own_ref, near_ref, beside_ref, *refs):
-    far_refs, pack_ref, scratch = refs[:-8], refs[-8], refs[-7:]
+def send_kernel(owner_hbm_ref, up_hbm_ref, down_hbm_ref, x_hbm_ref, *refs):
+    block_refs, pack_ref, scratch = refs[:-8], refs[-8], refs[-7:]
     owner_ref, up_ref, down_ref, x_ref, turned_ref, small_sems, x_sems = scratch
-    width = own_ref.shape[0]
+    width = block_refs[0].shape[0]
     features, columns = x_ref.shape
     small = [
         pltpu.make_async_copy(source, target, small_sems.at[n])
@@ -87,29 +89,20 @@
     pack_ref[0, :, : up_ref.shape[1]] = up_ref[...]
     pack_ref[1, :, : down_ref.shape[1]] = down_ref[...]
     me = lax.axis_index("band")
-
-    def block_of(distance):
+    for distance, block_ref in zip(ORDER, block_refs):
         target = jnp.bitwise_xor(me, distance)
         block = 0
         for j in range(1, owner_ref.shape[0]):
             block = jnp.where(owner_ref[j] == target, j, block)
-        return turned_ref[pl.ds(pl.multiple_of(block * width, SUB), width), :]
-
-    own_ref[...] = block_of(0)
-    near_ref[0] = block_of(2)
-    near_ref[1] = block_of(3)
-    beside_ref[...] = block_of(1)
-    for n, far_ref in enumerate(far_refs):
-        far_ref[...] = block_of(BANDS // 2 + n)
+        block_ref[...] = turned_ref[pl.ds(pl.multiple_of(block * width, SUB), width), :]
 
 
 def send_blocks(pixels, owner, up, down_t, width, pack_shape):
     features, columns = pixels.shape
     any_space = pl.BlockSpec(memory_space=pl.ANY)
     vmem = pl.BlockSpec(memory_space=pltpu.VMEM)
-    blocks = [(width, features), (2, width, features), (width, features)]
-    blocks += [(width, features)] * (BANDS // 2)
-    own, near, beside, *far, pack = pl.pallas_call(
+    blocks = [(width, features)] * BANDS
+    *blocks, pack = pl.pallas_call(
         send_kernel,
         out_shape=[jax.ShapeDtypeStruct(shape, BF16) for shape in [*blocks, pack_shape]],
         in_specs=[any_space] * 4,
@@ -126,16 +119,17 @@
         compiler_params=params(),
         name="send_blocks",
     )(in_hbm(owner), in_hbm(up), in_hbm(down_t), in_hbm(pixels))
-    return own, near, beside, far, pack
-
-
-def exchange(own, near, beside, far, pack):
-    by_z = swap(near, "band", 2)
-    by_z, pack = lax.optimization_barrier((by_z, pack))
-    arrived_far = [swap(piece, "band", BANDS // 2 + n) for n, piece in enumerate(far)]
-    factors = lax.all_gather(pack, "rep", axis=0, tiled=False)
-    factors, beside, onward = lax.optimization_barrier((factors, beside, by_z[1]))
-    return [own, by_z, *arrived_far, swap(beside, "band", 1), swap(onward, "band", 1)], factors
+    return blocks, pack
+
+
+def exchange(blocks):
+    arrived = dict(zip(ORDER, blocks))
+    for distance in ORDER[1:-2]:
+        arrived[distance] = swap(arrived[distance], "band", distance)
+    for distance, before in zip(ORDER[-2:], (1, 2)):
+        block, arrived[before] = lax.optimization_barrier((arrived[distance], arrived[before]))
+        arrived[distance] = swap(block, "band", distance)
+    return [arrived[distance] for distance in ORDER]
 
 
 def expand_table(table, rows, half_width_padded, half_width, transpose):
@@ -286,6 +280,9 @@
     arrived_directly = len(piece_refs) > 1
     depth = piece_refs[0].shape[-1] // samples
     rows = WLAT * width
+    group_rows = mix_ref.shape[0]
+    group = group_rows // WLAT
+    groups = [(slice(start, start + group), slice(start * WLAT, start * WLAT + group_rows)) for start in range(0, width, group)]
 
     def place(n):
         window_row, half, s = n // (halves * samples), n // samples % halves, n % samples
@@ -305,11 +302,8 @@
         load.start()
     level_load.start()
     if arrived_directly:
-        own_ref, by_z_ref, *far_refs, beside_ref, onward_ref = piece_refs
-        sources = {0: own_ref, 1: beside_ref, 2: by_z_ref.at[0], 3: onward_ref}
-        sources |= {BANDS // 2 + n: far_ref for n, far_ref in enumerate(far_refs)}
         me = lax.axis_index("band")
-        for distance, piece_ref in sources.items():
+        for distance, piece_ref in zip(ORDER, piece_refs):
             for half in range(halves):
                 within = slice(half * width, (half + 1) * width)
                 arrived_ref[half, jnp.bitwise_xor(me, distance)] = piece_ref[within, :]
@@ -336,31 +330,46 @@
 
         def embed():
             pixels = pixels_of(n, slice(lane, lane + reach))
-            tokens_ref[n, :, columns] = dot_nn(pixels, merged_ref[s, :, columns]).astype(BF16)
+            tokens = dot_nn(pixels, merged_ref[s, :, columns]).reshape(WLAT, width, COLUMNS)
+            for within, at in groups:
+                tokens_ref[n, at, columns] = tokens[:, within].reshape(group_rows, COLUMNS).astype(BF16)
 
         def mixing():
-            pre_ref[n, :, columns] = dot_nn(mix_ref[...], tokens_ref[n, :, columns])
+            for _, at in groups:
+                pre_ref[n, at, columns] = dot_nn(mix_ref[...], tokens_ref[n, at, columns])
 
         return [embed, mixing]
 
     def pointwise(n, columns):
-        def part(line):
-            for start in range(0, width, SUB):
-                at, within = pl.ds(line * width + start, SUB), pl.ds(start, SUB)
-                pre = pre_ref[n, at, columns]
+        def part(line, lanes):
+            grads = [grad_ref[n, line + k, :, lanes].astype(F32) for k in range(PAIR)]
+            mixed = []
+            for within, at in groups:
+                at = pl.ds(at.start + line * group, PAIR * group)
+                pre = pre_ref[n, at, lanes]
                 cdf, pdf = normal_parts(pre)
-                tokens = tokens_ref[n, at, columns].astype(F32)
-                mixed_ref[n, line, within, columns] = (tokens + pre * cdf).astype(BF16)
-                grad = grad_ref[n, line, within, columns].astype(F32)
-                grad_pre_ref[n, at, columns] = (grad * (cdf + pre * pdf)).astype(BF16)
-
-        return [functools.partial(part, line) for line in range(WLAT)]
+                mixed.append(tokens_ref[n, at, lanes].astype(F32) + pre * cdf)
+                grad = jnp.concatenate([grad[within] for grad in grads], axis=0)
+                grad_pre_ref[n, at, lanes] = (grad * (cdf + pre * pdf)).astype(BF16)
+            for k in range(PAIR):
+                rows_of_line = [values[k * group : (k + 1) * group] for values in mixed]
+                mixed_ref[n, line + k, :, lanes] = jnp.concatenate(rows_of_line, axis=0).astype(BF16)
+
+        return [
+            functools.partial(part, line, slice(start, start + LANE))
+            for line in range(0, WLAT, PAIR)
+            for start in range(columns.start, columns.stop, LANE)
+        ]
 
     def backward(n, columns):
         def spread():
-            direct = grad_ref[n, :, :, columns].reshape(rows, COLUMNS).astype(F32)
-            through = dot_nn(mix_t_ref[...], grad_pre_ref[n, :, columns])
-            grad_tokens_ref[n, :, columns] = (through + direct).astype(BF16)
+            direct = grad_ref[n, :, :, columns].astype(F32)
+            through = [
+                dot_nn(mix_t_ref[...], grad_pre_ref[n, at, columns]).reshape(WLAT, group, COLUMNS)
+                for _, at in groups
+            ]
+            total = jnp.concatenate(through, axis=1) + direct
+            grad_tokens_ref[n, :, columns] = total.reshape(rows, COLUMNS).astype(BF16)
 
         def share():
             s = n % samples
@@ -377,8 +386,6 @@
     ]
     for step in forward(*units[0]):
         step()
-    for load in loads:
-        load.wait()
     for i, unit in enumerate(units):
         n, columns = unit
         others = []
@@ -388,6 +395,8 @@
             others += turn(n)
         if i > 0:
             others += backward(*units[i - 1])
+        if columns.start == 0:
+            loads[n].wait()
         lines = pointwise(*unit)
         for line, vector_step in enumerate(lines):
             vector_step()
@@ -406,12 +415,12 @@
     folds = rank // (share_ref.shape[1] - rank)
     depth_rows, fold_lanes, row_share = rank // folds, columns // folds, channels // reps
     packed = jnp.zeros((depth_rows, feature_dim), F32)
-    row, lane = iota2((channels, feature_dim), 0), iota2((channels, feature_dim), 1)
+    row, lane = iota2((channels, feature_dim), 0), iota2((1, feature_dim), 1)
     rep, lane = lane // columns, lane % columns
     for fold in range(folds):
         inside = lane - fold * fold_lanes
-        pick = (row == inside + rep * row_share) & (inside >= 0) & (inside < row_share)
-        pick = jnp.where(pick, 1.0, 0.0).astype(BF16)
+        target = jnp.where((inside >= 0) & (inside < row_share), inside + rep * row_share, -1)
+        pick = jnp.where(row == target, 1.0, 0.0).astype(BF16)
         part = first[fold * depth_rows : (fold + 1) * depth_rows].astype(BF16)
         packed = packed + dot_nn(part, pick)
     payload = jnp.concatenate([second, packed], axis=0).astype(BF16)
@@ -515,16 +524,17 @@
     half_width = block_width // halves
     half_padded = round_up(half_width, SUB)
     padded_width = halves * half_padded
+    group = 2 * WLON if half_width % (2 * WLON) == 0 else half_padded
     features = samples * levels * channels
 
     pixels = patches.reshape(features, col_count)
     pack_shape = (2, rank, round_up(max(row_share, col_share), LANE))
     direct = band_count == BANDS and lat_rows == WLAT and half_padded == half_width
     if direct and features % LANE == 0 and col_count % LANE == 0:
-        pieces = send_blocks(
+        blocks, pack = send_blocks(
             pixels, column_block_owner, adapter_up, adapter_down.T, block_width, pack_shape
         )
-        arrived, factors = exchange(*pieces)
+        arrived = exchange(blocks)
     else:
         block_ids = jnp.arange(band_count, dtype=jnp.int32)
         inverse = jnp.sum(
@@ -539,7 +549,7 @@
                 for array in (adapter_up, adapter_down.T)
             ]
         )
-        factors = lax.all_gather(pack, "rep", axis=0, tiled=False)
+    factors = lax.all_gather(pack, "rep", axis=0, tiled=False)
 
     merged, up_through, down_t, mix, mix_t = prepare(
         variable_group_index,
@@ -549,8 +559,8 @@
         window_patch_mixer,
         samples,
         row_share,
-        half_width,
-        half_padded,
+        min(half_width, group),
+        group,
     )
     grad = mixed_token_gradient.reshape(samples, lat_rows, block_width, feature_dim)
     if padded_width != block_width:

time: 54.1 us -> 54.2 us (level)
  blocking collectives: 18.2 us -> 21.7 us
  waiting for transfers between devices: 7.33 us -> 3.96 us
  Pallas kernels: 14.7 us -> 15.3 us
  starting transfers between devices: 12.8 us -> 12.2 us
    all_to_all x1, blocking collectives: 13.1 us -> 16.5 us  [sum_shares(): lax.all_to_all(shares, ('band', 'rep'), split_axis=0, concat_axis=0, tile...]
    ppermute x7, waiting for transfers between devices: 7.33 us -> 3.96 us  [swap(): lax.ppermute(values, axis, [(source, source ^ distance) for source in ran...]
    pallas_call x1, Pallas kernels: 8.92 us -> 9.88 us  [mix_blocks(): pl.pallas_call(lambda *refs: mix_kernel(refs[:len(arrived)], *refs[len(ar...]
    ppermute x7, starting transfers between devices: 12.8 us -> 12.2 us  [swap(): lax.ppermute(values, axis, [(source, source ^ distance) for source in ran...]
  transfers between devices with their start and end apart: 7 -> 7, of which waited for: 4 -> 3; matrix products, arithmetic and copies ran while one was open for 0% -> 0% of each run, Pallas kernels for 6% -> 6%
where the time goes in v10:
time: 54.2 us; the launch traced here: 53.9 us
  blocking collectives  21.7 us (40%)
  Pallas kernels  15.3 us (28%)
  starting transfers between devices  12.2 us (23%)
  waiting for transfers between devices  3.96 us (7%)
  between operations  0.66 us (1%)
    all_to_all x1, blocking collectives, sum_shares(): lax.all_to_all(shares, ('band', 'rep'), split_axis=0, concat_axis=0, tile...  16.5 us
    ppermute x7, starting transfers between devices, swap(): lax.ppermute(values, axis, [(source, source ^ distance) for source in ran...  12.2 us
    pallas_call x1, Pallas kernels, mix_blocks(): pl.pallas_call(lambda *refs: mix_kernel(refs[:len(arrived)], *refs[len(ar...  9.88 us
    all_gather x1, blocking collectives, on_device(): factors = lax.all_gather(pack, 'rep', axis=0, tiled=False)  5.18 us
    ppermute x7, waiting for transfers between devices, swap(): lax.ppermute(values, axis, [(source, source ^ distance) for source in ran...  3.96 us
    pallas_call x1, Pallas kernels, prepare(): pl.pallas_call(functools.partial(prep_kernel, row_share, half_width, half...  3.1 us
    pallas_call x1, Pallas kernels, send_blocks(): pl.pallas_call(send_kernel, out_shape=[jax.ShapeDtypeStruct(shape, BF16)...  1.64 us
  transfers between devices with their start and end apart: 7, of which 3 were waited for; matrix products, arithmetic and copies ran while one was open for 0% of the time, Pallas kernels for 6%

profile of v10, /device:TPU:0, one launch (start us, length us, event | category | flops | bytes accessed | tf_op | source)
XLA Modules:
  0.0 53.9 jit_solution(15456846586362101650)
XLA Ops:
  0.6 1.6 %send_blocks.1 = (bf16[96,640]{1,0:T(8,128)(2,1)S(1)}, bf16[96,640]{1,0:T(8,128)(2,1)S(1)}, bf16[96,640]{1,0:T(8,128)(2,1)S(1)}, bf16[96,640]{1,0:T(8,128)(2,1)S...) custom-call(s32[8]{0:T(128)} %owner_hbm_ref.1, ...), custom_call_target="tpu_custom_call" | custom-call | tf_op jit(solution)/shard_map/send_blocks/pallas_call | solution.py:105
  2.3 3.0 %collective-permute-start.1 = (bf16[96,640]{1,0:T(8,128)(2,1)S(1)}, bf16[96,640]{1,0:T(8,128)(2,1)S(1)}, u32[]{:S(2)}, u32[]{:S(2)}) collective-permute-start(bf16[96,640]{1,0:T(8,128)(2,1)S(1)} %get-tuple-element.28), channel_id=1, source_target_pairs={{0,4},{4,0},{8,12},{12,8},{16,20},{20,16},{24,28},{28,24},{1,5},{5... | collective-permute-start | bytes 368648 | tf_op jit(solution)/shard_map/ppermute | solution.py:60
  5.3 1.6 %collective-permute-start.3 = (bf16[96,640]{1,0:T(8,128)(2,1)S(1)}, bf16[96,640]{1,0:T(8,128)(2,1)S(1)}, u32[]{:S(2)}, u32[]{:S(2)}) collective-permute-start(bf16[96,640]{1,0:T(8,128)(2,1)S(1)} %get-tuple-element.32), channel_id=1, source_target_pairs={{0,8},{4,12},{8,0},{12,4},{16,24},{20,28},{24,16},{28,20},{1,9},{5... | collective-permute-start | bytes 368648 | tf_op jit(solution)/shard_map/ppermute | solution.py:60
  6.9 2.6 %collective-permute-start = (bf16[96,640]{1,0:T(8,128)(2,1)S(1)}, bf16[96,640]{1,0:T(8,128)(2,1)S(1)}, u32[]{:S(2)}, u32[]{:S(2)}) collective-permute-start(bf16[96,640]{1,0:T(8,128)(2,1)S(1)} %get-tuple-element.26), channel_id=1, source_target_pairs={{0,16},{4,20},{8,24},{12,28},{16,0},{20,4},{24,8},{28,12},{1,17},{... | collective-permute-start | bytes 368648 | tf_op jit(solution)/shard_map/ppermute | solution.py:60
  9.4 0.3 collective-permute-start.2
  9.8 2.5 %collective-permute-start.4 = (bf16[96,640]{1,0:T(8,128)(2,1)S(1)}, bf16[96,640]{1,0:T(8,128)(2,1)S(1)}, u32[]{:S(2)}, u32[]{:S(2)}) collective-permute-start(bf16[96,640]{1,0:T(8,128)(2,1)S(1)} %get-tuple-element.34), channel_id=1, source_target_pairs={{0,24},{4,28},{8,16},{12,20},{16,8},{20,12},{24,0},{28,4},{1,25},{... | collective-permute-start | bytes 368648 | tf_op jit(solution)/shard_map/ppermute | solution.py:60
  12.2 0.0 collective-permute-done.1.refs_2_
  12.2 2.3 %collective-permute-start.5 = (bf16[96,640]{1,0:T(8,128)(2,1)S(1)}, bf16[96,640]{1,0:T(8,128)(2,1)S(1)}, u32[]{:S(2)}, u32[]{:S(2)}) collective-permute-start(bf16[96,640]{1,0:T(8,128)(2,1)S(1)} %get-tuple-element.35), channel_id=1, source_target_pairs={{0,28},{4,24},{8,20},{12,16},{16,12},{20,8},{24,4},{28,0},{1,29},{... | collective-permute-start | bytes 368648 | tf_op jit(solution)/shard_map/ppermute | solution.py:60
  14.5 0.0 collective-permute-done.3.refs_4_
  14.5 0.0 collective-permute-start.6
  14.5 5.2 %all-gather = bf16[8,16,128]{2,1,0:T(8,128)(2,1)S(1)} all-gather(bf16[2,16,128]{2,1,0:T(8,128)(2,1)S(1)} %get-tuple-element.37), channel_id=2, replica_groups=mesh['band'=8,'rep'=4] {'rep'}, dimensions={0}, use_global_device_ids=true | all-gather | bytes 40960 | tf_op jit(solution)/shard_map/all_gather | solution.py:552
  19.7 3.1 %prepare.1 = (bf16[2,384,512]{2,1,0:T(8,128)(2,1)S(1)}, bf16[4,32,512]{2,1,0:T(8,128)(2,1)S(1)}, bf16[16,80]{1,0:T(8,128)(2,1)S(1)}, bf16[192,192]{1,0:T(8,128)(2,1)S(1)}, bf16[192,192]{1,0:T(8,128)(2,1)S(1)}) custom-call(s32[5]{0:T(128)} %group_hbm_ref.1, bf16[3,16,512]{2,1,0:T(8,128)(2,1)} %frozen_ref.1, bf16[4,2,16,128]{3,2,1,0:T(8,128)(2,1)S(1)} %bitcast.8, ...), custom_call_target="tpu_custom_call" | custom-call | flops 215482368 | bytes 4194304 | tf_op jit(solution)/shard_map/prepare/pallas_call | solution.py:205
  22.8 1.0 %collective-permute-done.refs_1_ = bf16[96,640]{1,0:T(8,128)(2,1)S(1)} collective-permute-done((bf16[96,640]{1,0:T(8,128)(2,1)S(1)}, bf16[96,640]{1,0:T(8,128)(2,1)S(1)}, u32[]{:S(2)}, u32[]{:S(2)}) %collective-permute-start) | collective-permute-done | bytes 122912 | tf_op jit(solution)/shard_map/ppermute | solution.py:60
  23.8 2.2 %collective-permute-done.2.refs_3_ = bf16[96,640]{1,0:T(8,128)(2,1)S(1)} collective-permute-done((bf16[96,640]{1,0:T(8,128)(2,1)S(1)}, bf16[96,640]{1,0:T(8,128)(2,1)S(1)}, u32[]{:S(2)}, u32[]{:S(2)}) %collective-permute-start.2) | collective-permute-done | bytes 122912 | tf_op jit(solution)/shard_map/ppermute | solution.py:60
  26.0 0.0 collective-permute-done.4.refs_5_
  26.0 0.0 collective-permute-done.5.refs_6_
  26.0 0.8 %collective-permute-done.6.refs_7_ = bf16[96,640]{1,0:T(8,128)(2,1)S(1)} collective-permute-done((bf16[96,640]{1,0:T(8,128)(2,1)S(1)}, bf16[96,640]{1,0:T(8,128)(2,1)S(1)}, u32[]{:S(2)}, u32[]{:S(2)}) %collective-permute-start.6) | collective-permute-done | bytes 122912 | tf_op jit(solution)/shard_map/ppermute | solution.py:60
  26.8 9.9 %mix_blocks.1 = (bf16[2,8,96,512]{3,2,1,0:T(8,128)(2,1)}, bf16[32,24,128]{2,1,0:T(8,128)(2,1)S(1)}) custom-call(bf16[96,640]{1,0:T(8,128)(2,1)S(1)} %get-tuple-element.25.refs_0_, bf16[96,640]{1,0:T(8,128)(2,1)S(1)} %collective-permute-done.refs_1_, bf16[96,640]{1,0:T(8,128)(2,1)S(1)} %collective-permute-done.1.refs_2_, ...), custom_call_target="tpu_custom_call" | custom-call | flops 2415919104 | bytes 12582912 | tf_op jit(solution)/shard_map/mix_blocks/pallas_call | solution.py:447
  36.6 16.5 %all_to_all.5.parts_ref = bf16[32,24,128]{2,1,0:T(8,128)(2,1)S(1)} all-to-all(bf16[32,24,128]{2,1,0:T(8,128)(2,1)S(1)} %get-tuple-element.44), channel_id=1, replica_groups=mesh['band'=8,'rep'=4] {'band','rep'}, dimensions={0} | all-to-all | bytes 393216 | tf_op jit(solution)/shard_map/all_to_all | solution.py:493
  53.2 0.7 %sum_shares.1 = (f32[16,20]{1,0:T(8,128)}, f32[16,128]{1,0:T(8,128)}) custom-call(bf16[32,24,128]{2,1,0:T(8,128)(2,1)S(1)} %all_to_all.5.parts_ref), custom_call_target="tpu_custom_call" | custom-call | tf_op jit(solution)/shard_map/sum_shares/pallas_call | solution.py:494
Async XLA Ops:
  2.3 10.0 %collective-permute-start.1 = (bf16[96,640]{1,0:T(8,128)(2,1)S(1)}, bf16[96,640]{1,0:T(8,128)(2,1)S(1)}, u32[]{:S(2)}, u32[]{:S(2)}) collective-permute-start(bf16[96,640]{1,0:T(8,128)(2,1)S(1)} %get-tuple-element.28), channel_id=1, source_target_pairs={{0,4},{4,0},{8,12},{12,8},{16,20},{20,16},{24,28},{28,24},{1,5},{5... | collective-permute-start | bytes 368648 | tf_op jit(solution)/shard_map/ppermute | solution.py:60
  5.3 9.2 %collective-permute-start.3 = (bf16[96,640]{1,0:T(8,128)(2,1)S(1)}, bf16[96,640]{1,0:T(8,128)(2,1)S(1)}, u32[]{:S(2)}, u32[]{:S(2)}) collective-permute-start(bf16[96,640]{1,0:T(8,128)(2,1)S(1)} %get-tuple-element.32), channel_id=1, source_target_pairs={{0,8},{4,12},{8,0},{12,4},{16,24},{20,28},{24,16},{28,20},{1,9},{5... | collective-permute-start | bytes 368648 | tf_op jit(solution)/shard_map/ppermute | solution.py:60
  6.9 16.9 %collective-permute-start = (bf16[96,640]{1,0:T(8,128)(2,1)S(1)}, bf16[96,640]{1,0:T(8,128)(2,1)S(1)}, u32[]{:S(2)}, u32[]{:S(2)}) collective-permute-start(bf16[96,640]{1,0:T(8,128)(2,1)S(1)} %get-tuple-element.26), channel_id=1, source_target_pairs={{0,16},{4,20},{8,24},{12,28},{16,0},{20,4},{24,8},{28,12},{1,17},{... | collective-permute-start | bytes 368648 | tf_op jit(solution)/shard_map/ppermute | solution.py:60
  9.4 16.5 %collective-permute-start.2 = (bf16[96,640]{1,0:T(8,128)(2,1)S(1)}, bf16[96,640]{1,0:T(8,128)(2,1)S(1)}, u32[]{:S(2)}, u32[]{:S(2)}) collective-permute-start(bf16[96,640]{1,0:T(8,128)(2,1)S(1)} %get-tuple-element.30), channel_id=1, source_target_pairs={{0,20},{4,16},{8,28},{12,24},{16,4},{20,0},{24,12},{28,8},{1,21},{... | collective-permute-start | bytes 368648 | tf_op jit(solution)/shard_map/ppermute | solution.py:60
  9.8 16.2 %collective-permute-start.4 = (bf16[96,640]{1,0:T(8,128)(2,1)S(1)}, bf16[96,640]{1,0:T(8,128)(2,1)S(1)}, u32[]{:S(2)}, u32[]{:S(2)}) collective-permute-start(bf16[96,640]{1,0:T(8,128)(2,1)S(1)} %get-tuple-element.34), channel_id=1, source_target_pairs={{0,24},{4,28},{8,16},{12,20},{16,8},{20,12},{24,0},{28,4},{1,25},{... | collective-permute-start | bytes 368648 | tf_op jit(solution)/shard_map/ppermute | solution.py:60
  12.2 13.8 %collective-permute-start.5 = (bf16[96,640]{1,0:T(8,128)(2,1)S(1)}, bf16[96,640]{1,0:T(8,128)(2,1)S(1)}, u32[]{:S(2)}, u32[]{:S(2)}) collective-permute-start(bf16[96,640]{1,0:T(8,128)(2,1)S(1)} %get-tuple-element.35), channel_id=1, source_target_pairs={{0,28},{4,24},{8,20},{12,16},{16,12},{20,8},{24,4},{28,0},{1,29},{... | collective-permute-start | bytes 368648 | tf_op jit(solution)/shard_map/ppermute | solution.py:60
  14.5 12.2 %collective-permute-start.6 = (bf16[96,640]{1,0:T(8,128)(2,1)S(1)}, bf16[96,640]{1,0:T(8,128)(2,1)S(1)}, u32[]{:S(2)}, u32[]{:S(2)}) collective-permute-start(bf16[96,640]{1,0:T(8,128)(2,1)S(1)} %get-tuple-element.36), channel_id=1, source_target_pairs={{0,12},{4,8},{8,4},{12,0},{16,28},{20,24},{24,20},{28,16},{1,13},{... | collective-permute-start | bytes 368648 | tf_op jit(solution)/shard_map/ppermute | solution.py:60

commit v11 on v10

--- a/solution.py
+++ b/solution.py
@@ -16,7 +16,6 @@
 ORDER = (0, 4, 1, 5, 2, 6, 7, 3)
 FOLDS = 2
 COLUMNS = 256
-PAIR = 2
 BF16 = jnp.bfloat16
 F32 = jnp.float32
 
@@ -260,22 +259,22 @@
     level_hbm_ref,
     mixed_hbm_ref,
     share_ref,
-    arrived_ref,
-    grad_ref,
-    mixed_ref,
+    arrived_refs,
+    turned_refs,
+    grad_refs,
+    mixed_refs,
+    pre_refs,
+    tokens_refs,
+    grad_pre_refs,
+    grad_tokens_refs,
     level_ref,
     total_ref,
-    pre_ref,
-    tokens_ref,
-    grad_pre_ref,
-    grad_tokens_ref,
-    turned_ref,
     grad_sems,
     mixed_sems,
     level_sem,
 ):
     samples, reach, feature_dim = merged_ref.shape
-    chunk_count, _, width, _ = grad_ref.shape
+    chunk_count, (_, width, _) = len(grad_refs), grad_refs[0].shape
     halves = piece_refs[0].shape[-2] // width
     arrived_directly = len(piece_refs) > 1
     depth = piece_refs[0].shape[-1] // samples
@@ -290,11 +289,11 @@
         return window_row, half, s, (s, lines, columns)
 
     loads = [
-        pltpu.make_async_copy(grad_hbm_ref.at[place(n)[3]], grad_ref.at[n], grad_sems.at[n])
+        pltpu.make_async_copy(grad_hbm_ref.at[place(n)[3]], grad_refs[n], grad_sems.at[n])
         for n in range(chunk_count)
     ]
     stores = [
-        pltpu.make_async_copy(mixed_ref.at[n], mixed_hbm_ref.at[place(n)[3]], mixed_sems.at[n])
+        pltpu.make_async_copy(mixed_refs[n], mixed_hbm_ref.at[place(n)[3]], mixed_sems.at[n])
         for n in range(chunk_count)
     ]
     level_load = pltpu.make_async_copy(level_hbm_ref, level_ref, level_sem)
@@ -306,12 +305,12 @@
         for distance, piece_ref in zip(ORDER, piece_refs):
             for half in range(halves):
                 within = slice(half * width, (half + 1) * width)
-                arrived_ref[half, jnp.bitwise_xor(me, distance)] = piece_ref[within, :]
+                arrived_refs[half][jnp.bitwise_xor(me, distance)] = piece_ref[within, :]
 
     def pixels_of(n, lanes):
         window_row, half, _, _ = place(n)
         if arrived_directly:
-            block = arrived_ref[half, :, :, lanes]
+            block = arrived_refs[half][:, :, lanes]
         else:
             lines = slice(window_row * WLAT, (window_row + 1) * WLAT)
             block = piece_refs[0][lines, half * width : (half + 1) * width, lanes]
@@ -319,7 +318,7 @@
 
     def turn(n):
         def part(lanes):
-            turned_ref[n // samples, lanes, :] = pixels_of(n, lanes).T
+            turned_refs[n // samples][lanes, :] = pixels_of(n, lanes).T
 
         starts = range(0, samples * depth, LANE)
         return [functools.partial(part, slice(start, start + LANE)) for start in starts]
@@ -332,49 +331,51 @@
             pixels = pixels_of(n, slice(lane, lane + reach))
             tokens = dot_nn(pixels, merged_ref[s, :, columns]).reshape(WLAT, width, COLUMNS)
             for within, at in groups:
-                tokens_ref[n, at, columns] = tokens[:, within].reshape(group_rows, COLUMNS).astype(BF16)
+                tokens_refs[n][at, columns] = tokens[:, within].reshape(group_rows, COLUMNS).astype(BF16)
 
         def mixing():
             for _, at in groups:
-                pre_ref[n, at, columns] = dot_nn(mix_ref[...], tokens_ref[n, at, columns])
+                pre_refs[n][at, columns] = dot_nn(mix_ref[...], tokens_refs[n][at, columns])
 
         return [embed, mixing]
+
+    pair = 1 if group % SUB == 0 else 2
 
     def pointwise(n, columns):
         def part(line, lanes):
-            grads = [grad_ref[n, line + k, :, lanes].astype(F32) for k in range(PAIR)]
+            grads = [grad_refs[n][line + k, :, lanes].astype(F32) for k in range(pair)]
             mixed = []
             for within, at in groups:
-                at = pl.ds(at.start + line * group, PAIR * group)
-                pre = pre_ref[n, at, lanes]
+                at = pl.ds(at.start + line * group, pair * group)
+                pre = pre_refs[n][at, lanes]
                 cdf, pdf = normal_parts(pre)
-                mixed.append(tokens_ref[n, at, lanes].astype(F32) + pre * cdf)
+                mixed.append(tokens_refs[n][at, lanes].astype(F32) + pre * cdf)
                 grad = jnp.concatenate([grad[within] for grad in grads], axis=0)
-                grad_pre_ref[n, at, lanes] = (grad * (cdf + pre * pdf)).astype(BF16)
-            for k in range(PAIR):
+                grad_pre_refs[n][at, lanes] = (grad * (cdf + pre * pdf)).astype(BF16)
+            for k in range(pair):
                 rows_of_line = [values[k * group : (k + 1) * group] for values in mixed]
-                mixed_ref[n, line + k, :, lanes] = jnp.concatenate(rows_of_line, axis=0).astype(BF16)
+                mixed_refs[n][line + k, :, lanes] = jnp.concatenate(rows_of_line, axis=0).astype(BF16)
 
         return [
             functools.partial(part, line, slice(start, start + LANE))
-            for line in range(0, WLAT, PAIR)
+            for line in range(0, WLAT, pair)
             for start in range(columns.start, columns.stop, LANE)
         ]
 
     def backward(n, columns):
         def spread():
-            direct = grad_ref[n, :, :, columns].astype(F32)
+            direct = grad_refs[n][:, :, columns].astype(F32)
             through = [
-                dot_nn(mix_t_ref[...], grad_pre_ref[n, at, columns]).reshape(WLAT, group, COLUMNS)
+                dot_nn(mix_t_ref[...], grad_pre_refs[n][at, columns]).reshape(WLAT, group, COLUMNS)
                 for _, at in groups
             ]
             total = jnp.concatenate(through, axis=1) + direct
-            grad_tokens_ref[n, :, columns] = total.reshape(rows, COLUMNS).astype(BF16)
+            grad_tokens_refs[n][:, columns] = total.reshape(rows, COLUMNS).astype(BF16)
 
         def share():
             s = n % samples
-            turned = turned_ref[n // samples, s * depth : (s + 1) * depth, :]
-            part = dot_nn(turned, grad_tokens_ref[n, :, columns])
+            turned = turned_refs[n // samples][s * depth : (s + 1) * depth, :]
+            part = dot_nn(turned, grad_tokens_refs[n][:, columns])
             total_ref[:, columns] = part if n == 0 else total_ref[:, columns] + part
 
         return [spread, share]
@@ -386,6 +387,8 @@
     ]
     for step in forward(*units[0]):
         step()
+    for load in loads:
+        load.wait()
     for i, unit in enumerate(units):
         n, columns = unit
         others = []
@@ -395,15 +398,13 @@
             others += turn(n)
         if i > 0:
             others += backward(*units[i - 1])
-        if columns.start == 0:
-            loads[n].wait()
         lines = pointwise(*unit)
         for line, vector_step in enumerate(lines):
             vector_step()
             for step in others[line * len(others) // len(lines) : (line + 1) * len(others) // len(lines)]:
                 step()
-        if columns.stop == feature_dim:
-            stores[n].start()
+    for store in stores:
+        store.start()
     for step in backward(*units[-1]):
         step()
 
@@ -453,16 +454,16 @@
         in_specs=[vmem] * len(local) + [any_space, any_space],
         out_specs=[any_space, vmem],
         scratch_shapes=[
-            pltpu.VMEM((halves, WLAT, width, lanes), BF16),
-            pltpu.VMEM((chunks, WLAT, width, feature_dim), BF16),
-            pltpu.VMEM((chunks, WLAT, width, feature_dim), BF16),
+            [pltpu.VMEM((WLAT, width, lanes), BF16)] * halves,
+            [pltpu.VMEM((lanes, rows), BF16)] * (chunks // samples),
+            [pltpu.VMEM((WLAT, width, feature_dim), BF16)] * chunks,
+            [pltpu.VMEM((WLAT, width, feature_dim), BF16)] * chunks,
+            [pltpu.VMEM((rows, feature_dim), F32)] * chunks,
+            [pltpu.VMEM((rows, feature_dim), BF16)] * chunks,
+            [pltpu.VMEM((rows, feature_dim), BF16)] * chunks,
+            [pltpu.VMEM((rows, feature_dim), BF16)] * chunks,
             pltpu.VMEM(level_weight.shape, BF16),
             pltpu.VMEM((lanes // samples, feature_dim), F32),
-            pltpu.VMEM((chunks, rows, feature_dim), F32),
-            pltpu.VMEM((chunks, rows, feature_dim), BF16),
-            pltpu.VMEM((chunks, rows, feature_dim), BF16),
-            pltpu.VMEM((chunks, rows, feature_dim), BF16),
-            pltpu.VMEM((chunks // samples, lanes, rows), BF16),
             pltpu.SemaphoreType.DMA((chunks,)),
             pltpu.SemaphoreType.DMA((chunks,)),
             pltpu.SemaphoreType.DMA,
@@ -524,7 +525,6 @@
     half_width = block_width // halves
     half_padded = round_up(half_width, SUB)
     padded_width = halves * half_padded
-    group = 2 * WLON if half_width % (2 * WLON) == 0 else half_padded
     features = samples * levels * channels
 
     pixels = patches.reshape(features, col_count)
@@ -559,8 +559,8 @@
         window_patch_mixer,
         samples,
         row_share,
-        min(half_width, group),
-        group,
+        half_width,
+        half_padded,
     )
     grad = mixed_token_gradient.reshape(samples, lat_rows, block_width, feature_dim)
     if padded_width != block_width:

time: 54.2 us -> 54.3 us (level)
  no operation moved by 1% of the time
where the time goes in v11:
time: 54.3 us; the launch traced here: 54 us
  blocking collectives  21.7 us (40%)
  Pallas kernels  15.8 us (29%)
  starting transfers between devices  12.2 us (22%)
  waiting for transfers between devices  3.63 us (7%)
  between operations  0.66 us (1%)
    all_to_all x1, blocking collectives, sum_shares(): lax.all_to_all(shares, ('band', 'rep'), split_axis=0, concat_axis=0, tile...  16.5 us
    ppermute x7, starting transfers between devices, swap(): lax.ppermute(values, axis, [(source, source ^ distance) for source in ran...  12.2 us
    pallas_call x1, Pallas kernels, mix_blocks(): pl.pallas_call(lambda *refs: mix_kernel(refs[:len(arrived)], *refs[len(ar...  10 us
    all_gather x1, blocking collectives, on_device(): factors = lax.all_gather(pack, 'rep', axis=0, tiled=False)  5.18 us
    ppermute x7, waiting for transfers between devices, swap(): lax.ppermute(values, axis, [(source, source ^ distance) for source in ran...  3.63 us
    pallas_call x1, Pallas kernels, prepare(): pl.pallas_call(functools.partial(prep_kernel, row_share, half_width, half...  3.42 us
    pallas_call x1, Pallas kernels, send_blocks(): pl.pallas_call(send_kernel, out_shape=[jax.ShapeDtypeStruct(shape, BF16)...  1.64 us
  transfers between devices with their start and end apart: 7, of which 3 were waited for; matrix products, arithmetic and copies ran while one was open for 0% of the time, Pallas kernels for 6%

profile of v11, /device:TPU:0, one launch (start us, length us, event | category | flops | bytes accessed | tf_op | source)
XLA Modules:
  0.0 54.0 jit_solution(6284233670466702628)
XLA Ops:
  0.6 1.6 %send_blocks.1 = (bf16[96,640]{1,0:T(8,128)(2,1)S(1)}, bf16[96,640]{1,0:T(8,128)(2,1)S(1)}, bf16[96,640]{1,0:T(8,128)(2,1)S(1)}, bf16[96,640]{1,0:T(8,128)(2,1)S...) custom-call(s32[8]{0:T(128)} %owner_hbm_ref.1, ...), custom_call_target="tpu_custom_call" | custom-call | tf_op jit(solution)/shard_map/send_blocks/pallas_call | solution.py:104
  2.3 3.0 %collective-permute-start.1 = (bf16[96,640]{1,0:T(8,128)(2,1)S(1)}, bf16[96,640]{1,0:T(8,128)(2,1)S(1)}, u32[]{:S(2)}, u32[]{:S(2)}) collective-permute-start(bf16[96,640]{1,0:T(8,128)(2,1)S(1)} %get-tuple-element.28), channel_id=1, source_target_pairs={{0,4},{4,0},{8,12},{12,8},{16,20},{20,16},{24,28},{28,24},{1,5},{5... | collective-permute-start | bytes 368648 | tf_op jit(solution)/shard_map/ppermute | solution.py:59
  5.3 1.6 %collective-permute-start.3 = (bf16[96,640]{1,0:T(8,128)(2,1)S(1)}, bf16[96,640]{1,0:T(8,128)(2,1)S(1)}, u32[]{:S(2)}, u32[]{:S(2)}) collective-permute-start(bf16[96,640]{1,0:T(8,128)(2,1)S(1)} %get-tuple-element.32), channel_id=1, source_target_pairs={{0,8},{4,12},{8,0},{12,4},{16,24},{20,28},{24,16},{28,20},{1,9},{5... | collective-permute-start | bytes 368648 | tf_op jit(solution)/shard_map/ppermute | solution.py:59
  6.9 2.6 %collective-permute-start = (bf16[96,640]{1,0:T(8,128)(2,1)S(1)}, bf16[96,640]{1,0:T(8,128)(2,1)S(1)}, u32[]{:S(2)}, u32[]{:S(2)}) collective-permute-start(bf16[96,640]{1,0:T(8,128)(2,1)S(1)} %get-tuple-element.26), channel_id=1, source_target_pairs={{0,16},{4,20},{8,24},{12,28},{16,0},{20,4},{24,8},{28,12},{1,17},{... | collective-permute-start | bytes 368648 | tf_op jit(solution)/shard_map/ppermute | solution.py:59
  9.4 0.3 collective-permute-start.2
  9.8 2.5 %collective-permute-start.4 = (bf16[96,640]{1,0:T(8,128)(2,1)S(1)}, bf16[96,640]{1,0:T(8,128)(2,1)S(1)}, u32[]{:S(2)}, u32[]{:S(2)}) collective-permute-start(bf16[96,640]{1,0:T(8,128)(2,1)S(1)} %get-tuple-element.34), channel_id=1, source_target_pairs={{0,24},{4,28},{8,16},{12,20},{16,8},{20,12},{24,0},{28,4},{1,25},{... | collective-permute-start | bytes 368648 | tf_op jit(solution)/shard_map/ppermute | solution.py:59
  12.2 0.0 collective-permute-done.1.refs_2_
  12.2 2.3 %collective-permute-start.5 = (bf16[96,640]{1,0:T(8,128)(2,1)S(1)}, bf16[96,640]{1,0:T(8,128)(2,1)S(1)}, u32[]{:S(2)}, u32[]{:S(2)}) collective-permute-start(bf16[96,640]{1,0:T(8,128)(2,1)S(1)} %get-tuple-element.35), channel_id=1, source_target_pairs={{0,28},{4,24},{8,20},{12,16},{16,12},{20,8},{24,4},{28,0},{1,29},{... | collective-permute-start | bytes 368648 | tf_op jit(solution)/shard_map/ppermute | solution.py:59
  14.5 0.0 collective-permute-done.3.refs_4_
  14.5 0.0 collective-permute-start.6
  14.5 5.2 %all-gather = bf16[8,16,128]{2,1,0:T(8,128)(2,1)S(1)} all-gather(bf16[2,16,128]{2,1,0:T(8,128)(2,1)S(1)} %get-tuple-element.37), channel_id=2, replica_groups=mesh['band'=8,'rep'=4] {'rep'}, dimensions={0}, use_global_device_ids=true | all-gather | bytes 40960 | tf_op jit(solution)/shard_map/all_gather | solution.py:552
  19.7 3.4 %prepare.1 = (bf16[2,384,512]{2,1,0:T(8,128)(2,1)S(1)}, bf16[4,32,512]{2,1,0:T(8,128)(2,1)S(1)}, bf16[16,80]{1,0:T(8,128)(2,1)S(1)}, bf16[384,384]{1,0:T(8,128)(2,1)S(1)}, bf16[384,384]{1,0:T(8,128)(2,1)S(1)}) custom-call(s32[5]{0:T(128)} %group_hbm_ref.1, bf16[3,16,512]{2,1,0:T(8,128)(2,1)} %frozen_ref.1, bf16[4,2,16,128]{3,2,1,0:T(8,128)(2,1)S(1)} %bitcast.8, ...), custom_call_target="tpu_custom_call" | custom-call | flops 257949696 | bytes 4194304 | tf_op jit(solution)/shard_map/prepare/pallas_call | solution.py:204
  23.1 0.7 %collective-permute-done.refs_1_ = bf16[96,640]{1,0:T(8,128)(2,1)S(1)} collective-permute-done((bf16[96,640]{1,0:T(8,128)(2,1)S(1)}, bf16[96,640]{1,0:T(8,128)(2,1)S(1)}, u32[]{:S(2)}, u32[]{:S(2)}) %collective-permute-start) | collective-permute-done | bytes 122912 | tf_op jit(solution)/shard_map/ppermute | solution.py:59
  23.8 2.2 %collective-permute-done.2.refs_3_ = bf16[96,640]{1,0:T(8,128)(2,1)S(1)} collective-permute-done((bf16[96,640]{1,0:T(8,128)(2,1)S(1)}, bf16[96,640]{1,0:T(8,128)(2,1)S(1)}, u32[]{:S(2)}, u32[]{:S(2)}) %collective-permute-start.2) | collective-permute-done | bytes 122912 | tf_op jit(solution)/shard_map/ppermute | solution.py:59
  26.0 0.0 collective-permute-done.4.refs_5_
  26.0 0.0 collective-permute-done.5.refs_6_
  26.0 0.8 %collective-permute-done.6.refs_7_ = bf16[96,640]{1,0:T(8,128)(2,1)S(1)} collective-permute-done((bf16[96,640]{1,0:T(8,128)(2,1)S(1)}, bf16[96,640]{1,0:T(8,128)(2,1)S(1)}, u32[]{:S(2)}, u32[]{:S(2)}) %collective-permute-start.6) | collective-permute-done | bytes 122912 | tf_op jit(solution)/shard_map/ppermute | solution.py:59
  26.8 10.0 %mix_blocks.1 = (bf16[2,8,96,512]{3,2,1,0:T(8,128)(2,1)}, bf16[32,24,128]{2,1,0:T(8,128)(2,1)S(1)}) custom-call(bf16[96,640]{1,0:T(8,128)(2,1)S(1)} %get-tuple-element.25.refs_0_, bf16[96,640]{1,0:T(8,128)(2,1)S(1)} %collective-permute-done.refs_1_, bf16[96,640]{1,0:T(8,128)(2,1)S(1)} %collective-permute-done.1.refs_2_, ...), custom_call_target="tpu_custom_call" | custom-call | flops 2415919104 | bytes 12582912 | tf_op jit(solution)/shard_map/mix_blocks/pallas_call | solution.py:448
  36.8 16.5 %all_to_all.5.parts_ref = bf16[32,24,128]{2,1,0:T(8,128)(2,1)S(1)} all-to-all(bf16[32,24,128]{2,1,0:T(8,128)(2,1)S(1)} %get-tuple-element.44), channel_id=1, replica_groups=mesh['band'=8,'rep'=4] {'band','rep'}, dimensions={0} | all-to-all | bytes 393216 | tf_op jit(solution)/shard_map/all_to_all | solution.py:494
  53.3 0.7 %sum_shares.1 = (f32[16,20]{1,0:T(8,128)}, f32[16,128]{1,0:T(8,128)}) custom-call(bf16[32,24,128]{2,1,0:T(8,128)(2,1)S(1)} %all_to_all.5.parts_ref), custom_call_target="tpu_custom_call" | custom-call | tf_op jit(solution)/shard_map/sum_shares/pallas_call | solution.py:495
Async XLA Ops:
  2.3 10.0 %collective-permute-start.1 = (bf16[96,640]{1,0:T(8,128)(2,1)S(1)}, bf16[96,640]{1,0:T(8,128)(2,1)S(1)}, u32[]{:S(2)}, u32[]{:S(2)}) collective-permute-start(bf16[96,640]{1,0:T(8,128)(2,1)S(1)} %get-tuple-element.28), channel_id=1, source_target_pairs={{0,4},{4,0},{8,12},{12,8},{16,20},{20,16},{24,28},{28,24},{1,5},{5... | collective-permute-start | bytes 368648 | tf_op jit(solution)/shard_map/ppermute | solution.py:59
  5.3 9.2 %collective-permute-start.3 = (bf16[96,640]{1,0:T(8,128)(2,1)S(1)}, bf16[96,640]{1,0:T(8,128)(2,1)S(1)}, u32[]{:S(2)}, u32[]{:S(2)}) collective-permute-start(bf16[96,640]{1,0:T(8,128)(2,1)S(1)} %get-tuple-element.32), channel_id=1, source_target_pairs={{0,8},{4,12},{8,0},{12,4},{16,24},{20,28},{24,16},{28,20},{1,9},{5... | collective-permute-start | bytes 368648 | tf_op jit(solution)/shard_map/ppermute | solution.py:59
  6.9 16.9 %collective-permute-start = (bf16[96,640]{1,0:T(8,128)(2,1)S(1)}, bf16[96,640]{1,0:T(8,128)(2,1)S(1)}, u32[]{:S(2)}, u32[]{:S(2)}) collective-permute-start(bf16[96,640]{1,0:T(8,128)(2,1)S(1)} %get-tuple-element.26), channel_id=1, source_target_pairs={{0,16},{4,20},{8,24},{12,28},{16,0},{20,4},{24,8},{28,12},{1,17},{... | collective-permute-start | bytes 368648 | tf_op jit(solution)/shard_map/ppermute | solution.py:59
  9.4 16.5 %collective-permute-start.2 = (bf16[96,640]{1,0:T(8,128)(2,1)S(1)}, bf16[96,640]{1,0:T(8,128)(2,1)S(1)}, u32[]{:S(2)}, u32[]{:S(2)}) collective-permute-start(bf16[96,640]{1,0:T(8,128)(2,1)S(1)} %get-tuple-element.30), channel_id=1, source_target_pairs={{0,20},{4,16},{8,28},{12,24},{16,4},{20,0},{24,12},{28,8},{1,21},{... | collective-permute-start | bytes 368648 | tf_op jit(solution)/shard_map/ppermute | solution.py:59
  9.8 16.2 %collective-permute-start.4 = (bf16[96,640]{1,0:T(8,128)(2,1)S(1)}, bf16[96,640]{1,0:T(8,128)(2,1)S(1)}, u32[]{:S(2)}, u32[]{:S(2)}) collective-permute-start(bf16[96,640]{1,0:T(8,128)(2,1)S(1)} %get-tuple-element.34), channel_id=1, source_target_pairs={{0,24},{4,28},{8,16},{12,20},{16,8},{20,12},{24,0},{28,4},{1,25},{... | collective-permute-start | bytes 368648 | tf_op jit(solution)/shard_map/ppermute | solution.py:59
  12.2 13.8 %collective-permute-start.5 = (bf16[96,640]{1,0:T(8,128)(2,1)S(1)}, bf16[96,640]{1,0:T(8,128)(2,1)S(1)}, u32[]{:S(2)}, u32[]{:S(2)}) collective-permute-start(bf16[96,640]{1,0:T(8,128)(2,1)S(1)} %get-tuple-element.35), channel_id=1, source_target_pairs={{0,28},{4,24},{8,20},{12,16},{16,12},{20,8},{24,4},{28,0},{1,29},{... | collective-permute-start | bytes 368648 | tf_op jit(solution)/shard_map/ppermute | solution.py:59
  14.5 12.2 %collective-permute-start.6 = (bf16[96,640]{1,0:T(8,128)(2,1)S(1)}, bf16[96,640]{1,0:T(8,128)(2,1)S(1)}, u32[]{:S(2)}, u32[]{:S(2)}) collective-permute-start(bf16[96,640]{1,0:T(8,128)(2,1)S(1)} %get-tuple-element.36), channel_id=1, source_target_pairs={{0,12},{4,8},{8,4},{12,0},{16,28},{20,24},{24,20},{28,16},{1,13},{... | collective-permute-start | bytes 368648 | tf_op jit(solution)/shard_map/ppermute | solution.py:59

commit v12 on v11

--- a/solution.py
+++ b/solution.py
@@ -220,15 +220,8 @@
 
 
 def normal_parts(values):
-    bell = jnp.exp2(values * values * -0.7213475204444817)
-    scaled = 1.0 + 0.23164189 * jnp.abs(values)
-    t = pl.reciprocal(scaled, approx=True)
-    t = t * (2.0 - scaled * t)
-    tail = t * (
-        0.127414796 + t * (-0.142248368 + t * (0.7107068705 + t * (-0.7265760135 + t * 0.5307027145)))
-    )
-    tail = tail * bell
-    return jnp.where(values < 0.0, tail, 1.0 - tail), 0.3989422804014327 * bell
+    cdf = 0.5 + 0.5 * lax.erf(values * 0.7071067811865476)
+    return cdf, 0.3989422804014327 * jnp.exp2(values * values * -0.7213475204444817)
 
 
 def factor_shares(total, up_ref, down_ref, level_ref):
@@ -279,9 +272,6 @@
     arrived_directly = len(piece_refs) > 1
     depth = piece_refs[0].shape[-1] // samples
     rows = WLAT * width
-    group_rows = mix_ref.shape[0]
-    group = group_rows // WLAT
-    groups = [(slice(start, start + group), slice(start * WLAT, start * WLAT + group_rows)) for start in range(0, width, group)]
 
     def place(n):
         window_row, half, s = n // (halves * samples), n // samples % halves, n % samples
@@ -329,48 +319,31 @@
 
         def embed():
             pixels = pixels_of(n, slice(lane, lane + reach))
-            tokens = dot_nn(pixels, merged_ref[s, :, columns]).reshape(WLAT, width, COLUMNS)
-            for within, at in groups:
-                tokens_refs[n][at, columns] = tokens[:, within].reshape(group_rows, COLUMNS).astype(BF16)
+            tokens_refs[n][:, columns] = dot_nn(pixels, merged_ref[s, :, columns]).astype(BF16)
 
         def mixing():
-            for _, at in groups:
-                pre_refs[n][at, columns] = dot_nn(mix_ref[...], tokens_refs[n][at, columns])
+            pre_refs[n][:, columns] = dot_nn(mix_ref[...], tokens_refs[n][:, columns])
 
         return [embed, mixing]
 
-    pair = 1 if group % SUB == 0 else 2
-
     def pointwise(n, columns):
-        def part(line, lanes):
-            grads = [grad_refs[n][line + k, :, lanes].astype(F32) for k in range(pair)]
-            mixed = []
-            for within, at in groups:
-                at = pl.ds(at.start + line * group, pair * group)
-                pre = pre_refs[n][at, lanes]
+        def part(line):
+            for start in range(0, width, SUB):
+                at, within = pl.ds(line * width + start, SUB), pl.ds(start, SUB)
+                pre = pre_refs[n][at, columns]
                 cdf, pdf = normal_parts(pre)
-                mixed.append(tokens_refs[n][at, lanes].astype(F32) + pre * cdf)
-                grad = jnp.concatenate([grad[within] for grad in grads], axis=0)
-                grad_pre_refs[n][at, lanes] = (grad * (cdf + pre * pdf)).astype(BF16)
-            for k in range(pair):
-                rows_of_line = [values[k * group : (k + 1) * group] for values in mixed]
-                mixed_refs[n][line + k, :, lanes] = jnp.concatenate(rows_of_line, axis=0).astype(BF16)
-
-        return [
-            functools.partial(part, line, slice(start, start + LANE))
-            for line in range(0, WLAT, pair)
-            for start in range(columns.start, columns.stop, LANE)
-        ]
+                tokens = tokens_refs[n][at, columns].astype(F32)
+                mixed_refs[n][line, within, columns] = (tokens + pre * cdf).astype(BF16)
+                grad = grad_refs[n][line, within, columns].astype(F32)
+                grad_pre_refs[n][at, columns] = (grad * (cdf + pre * pdf)).astype(BF16)
+
+        return [functools.partial(part, line) for line in range(WLAT)]
 
     def backward(n, columns):
         def spread():
-            direct = grad_refs[n][:, :, columns].astype(F32)
-            through = [
-                dot_nn(mix_t_ref[...], grad_pre_refs[n][at, columns]).reshape(WLAT, group, COLUMNS)
-                for _, at in groups
-            ]
-            total = jnp.concatenate(through, axis=1) + direct
-            grad_tokens_refs[n][:, columns] = total.reshape(rows, COLUMNS).astype(BF16)
+            direct = grad_refs[n][:, :, columns].reshape(rows, COLUMNS).astype(F32)
+            through = dot_nn(mix_t_ref[...], grad_pre_refs[n][:, columns])
+            grad_tokens_refs[n][:, columns] = (through + direct).astype(BF16)
 
         def share():
             s = n % samples
@@ -403,8 +376,8 @@
             vector_step()
             for step in others[line * len(others) // len(lines) : (line + 1) * len(others) // len(lines)]:
                 step()
-    for store in stores:
-        store.start()
+        if columns.stop == feature_dim:
+            stores[n].start()
     for step in backward(*units[-1]):
         step()
 

time: 54.3 us -> 52.3 us (0.963)
  Pallas kernels: 15.8 us -> 13.7 us
    pallas_call x1, Pallas kernels: 10 us -> 7.92 us  [mix_blocks(): pl.pallas_call(lambda *refs: mix_kernel(refs[:len(arrived)], *refs[len(ar...]
  transfers between devices with their start and end apart: 7 -> 7, of which waited for: 3 -> 3; matrix products, arithmetic and copies ran while one was open for 0% -> 0% of each run, Pallas kernels for 6% -> 7%
where the time goes in v12:
time: 52.3 us; the launch traced here: 51.9 us
  blocking collectives  21.7 us (41%)
  Pallas kernels  13.7 us (26%)
  starting transfers between devices  12.2 us (23%)
  waiting for transfers between devices  3.63 us (7%)
  between operations  0.66 us (1%)
    all_to_all x1, blocking collectives, sum_shares(): lax.all_to_all(shares, ('band', 'rep'), split_axis=0, concat_axis=0, tile...  16.5 us
    ppermute x7, starting transfers between devices, swap(): lax.ppermute(values, axis, [(source, source ^ distance) for source in ran...  12.2 us
    pallas_call x1, Pallas kernels, mix_blocks(): pl.pallas_call(lambda *refs: mix_kernel(refs[:len(arrived)], *refs[len(ar...  7.92 us
    all_gather x1, blocking collectives, on_device(): factors = lax.all_gather(pack, 'rep', axis=0, tiled=False)  5.18 us
    ppermute x7, waiting for transfers between devices, swap(): lax.ppermute(values, axis, [(source, source ^ distance) for source in ran...  3.63 us
    pallas_call x1, Pallas kernels, prepare(): pl.pallas_call(functools.partial(prep_kernel, row_share, half_width, half...  3.42 us
    pallas_call x1, Pallas kernels, send_blocks(): pl.pallas_call(send_kernel, out_shape=[jax.ShapeDtypeStruct(shape, BF16)...  1.64 us
  transfers between devices with their start and end apart: 7, of which 3 were waited for; matrix products, arithmetic and copies ran while one was open for 0% of the time, Pallas kernels for 7%

profile of v12, /device:TPU:0, one launch (start us, length us, event | category | flops | bytes accessed | tf_op | source)
XLA Modules:
  0.0 51.9 jit_solution(13885765796509773260)
XLA Ops:
  0.6 1.6 %send_blocks.1 = (bf16[96,640]{1,0:T(8,128)(2,1)S(1)}, bf16[96,640]{1,0:T(8,128)(2,1)S(1)}, bf16[96,640]{1,0:T(8,128)(2,1)S(1)}, bf16[96,640]{1,0:T(8,128)(2,1)S...) custom-call(s32[8]{0:T(128)} %owner_hbm_ref.1, ...), custom_call_target="tpu_custom_call" | custom-call | tf_op jit(solution)/shard_map/send_blocks/pallas_call | solution.py:104
  2.3 3.0 %collective-permute-start.1 = (bf16[96,640]{1,0:T(8,128)(2,1)S(1)}, bf16[96,640]{1,0:T(8,128)(2,1)S(1)}, u32[]{:S(2)}, u32[]{:S(2)}) collective-permute-start(bf16[96,640]{1,0:T(8,128)(2,1)S(1)} %get-tuple-element.28), channel_id=1, source_target_pairs={{0,4},{4,0},{8,12},{12,8},{16,20},{20,16},{24,28},{28,24},{1,5},{5... | collective-permute-start | bytes 368648 | tf_op jit(solution)/shard_map/ppermute | solution.py:59
  5.3 1.6 %collective-permute-start.3 = (bf16[96,640]{1,0:T(8,128)(2,1)S(1)}, bf16[96,640]{1,0:T(8,128)(2,1)S(1)}, u32[]{:S(2)}, u32[]{:S(2)}) collective-permute-start(bf16[96,640]{1,0:T(8,128)(2,1)S(1)} %get-tuple-element.32), channel_id=1, source_target_pairs={{0,8},{4,12},{8,0},{12,4},{16,24},{20,28},{24,16},{28,20},{1,9},{5... | collective-permute-start | bytes 368648 | tf_op jit(solution)/shard_map/ppermute | solution.py:59
  6.9 2.6 %collective-permute-start = (bf16[96,640]{1,0:T(8,128)(2,1)S(1)}, bf16[96,640]{1,0:T(8,128)(2,1)S(1)}, u32[]{:S(2)}, u32[]{:S(2)}) collective-permute-start(bf16[96,640]{1,0:T(8,128)(2,1)S(1)} %get-tuple-element.26), channel_id=1, source_target_pairs={{0,16},{4,20},{8,24},{12,28},{16,0},{20,4},{24,8},{28,12},{1,17},{... | collective-permute-start | bytes 368648 | tf_op jit(solution)/shard_map/ppermute | solution.py:59
  9.4 0.3 collective-permute-start.2
  9.8 2.5 %collective-permute-start.4 = (bf16[96,640]{1,0:T(8,128)(2,1)S(1)}, bf16[96,640]{1,0:T(8,128)(2,1)S(1)}, u32[]{:S(2)}, u32[]{:S(2)}) collective-permute-start(bf16[96,640]{1,0:T(8,128)(2,1)S(1)} %get-tuple-element.34), channel_id=1, source_target_pairs={{0,24},{4,28},{8,16},{12,20},{16,8},{20,12},{24,0},{28,4},{1,25},{... | collective-permute-start | bytes 368648 | tf_op jit(solution)/shard_map/ppermute | solution.py:59
  12.2 0.0 collective-permute-done.1.refs_2_
  12.2 2.3 %collective-permute-start.5 = (bf16[96,640]{1,0:T(8,128)(2,1)S(1)}, bf16[96,640]{1,0:T(8,128)(2,1)S(1)}, u32[]{:S(2)}, u32[]{:S(2)}) collective-permute-start(bf16[96,640]{1,0:T(8,128)(2,1)S(1)} %get-tuple-element.35), channel_id=1, source_target_pairs={{0,28},{4,24},{8,20},{12,16},{16,12},{20,8},{24,4},{28,0},{1,29},{... | collective-permute-start | bytes 368648 | tf_op jit(solution)/shard_map/ppermute | solution.py:59
  14.5 0.0 collective-permute-done.3.refs_4_
  14.5 0.0 collective-permute-start.6
  14.5 5.2 %all-gather = bf16[8,16,128]{2,1,0:T(8,128)(2,1)S(1)} all-gather(bf16[2,16,128]{2,1,0:T(8,128)(2,1)S(1)} %get-tuple-element.37), channel_id=2, replica_groups=mesh['band'=8,'rep'=4] {'rep'}, dimensions={0}, use_global_device_ids=true | all-gather | bytes 40960 | tf_op jit(solution)/shard_map/all_gather | solution.py:525
  19.7 3.4 %prepare.1 = (bf16[2,384,512]{2,1,0:T(8,128)(2,1)S(1)}, bf16[4,32,512]{2,1,0:T(8,128)(2,1)S(1)}, bf16[16,80]{1,0:T(8,128)(2,1)S(1)}, bf16[384,384]{1,0:T(8,128)(2,1)S(1)}, bf16[384,384]{1,0:T(8,128)(2,1)S(1)}) custom-call(s32[5]{0:T(128)} %group_hbm_ref.1, bf16[3,16,512]{2,1,0:T(8,128)(2,1)} %frozen_ref.1, bf16[4,2,16,128]{3,2,1,0:T(8,128)(2,1)S(1)} %bitcast.8, ...), custom_call_target="tpu_custom_call" | custom-call | flops 257949696 | bytes 4194304 | tf_op jit(solution)/shard_map/prepare/pallas_call | solution.py:204
  23.1 0.7 %collective-permute-done.refs_1_ = bf16[96,640]{1,0:T(8,128)(2,1)S(1)} collective-permute-done((bf16[96,640]{1,0:T(8,128)(2,1)S(1)}, bf16[96,640]{1,0:T(8,128)(2,1)S(1)}, u32[]{:S(2)}, u32[]{:S(2)}) %collective-permute-start) | collective-permute-done | bytes 122912 | tf_op jit(solution)/shard_map/ppermute | solution.py:59
  23.8 2.2 %collective-permute-done.2.refs_3_ = bf16[96,640]{1,0:T(8,128)(2,1)S(1)} collective-permute-done((bf16[96,640]{1,0:T(8,128)(2,1)S(1)}, bf16[96,640]{1,0:T(8,128)(2,1)S(1)}, u32[]{:S(2)}, u32[]{:S(2)}) %collective-permute-start.2) | collective-permute-done | bytes 122912 | tf_op jit(solution)/shard_map/ppermute | solution.py:59
  26.0 0.0 collective-permute-done.4.refs_5_
  26.0 0.0 collective-permute-done.5.refs_6_
  26.0 0.8 %collective-permute-done.6.refs_7_ = bf16[96,640]{1,0:T(8,128)(2,1)S(1)} collective-permute-done((bf16[96,640]{1,0:T(8,128)(2,1)S(1)}, bf16[96,640]{1,0:T(8,128)(2,1)S(1)}, u32[]{:S(2)}, u32[]{:S(2)}) %collective-permute-start.6) | collective-permute-done | bytes 122912 | tf_op jit(solution)/shard_map/ppermute | solution.py:59
  26.8 7.9 %mix_blocks.1 = (bf16[2,8,96,512]{3,2,1,0:T(8,128)(2,1)}, bf16[32,24,128]{2,1,0:T(8,128)(2,1)S(1)}) custom-call(bf16[96,640]{1,0:T(8,128)(2,1)S(1)} %get-tuple-element.25.refs_0_, bf16[96,640]{1,0:T(8,128)(2,1)S(1)} %collective-permute-done.refs_1_, bf16[96,640]{1,0:T(8,128)(2,1)S(1)} %collective-permute-done.1.refs_2_, ...), custom_call_target="tpu_custom_call" | custom-call | flops 2415919104 | bytes 12582912 | tf_op jit(solution)/shard_map/mix_blocks/pallas_call | solution.py:421
  34.7 16.5 %all_to_all.5.parts_ref = bf16[32,24,128]{2,1,0:T(8,128)(2,1)S(1)} all-to-all(bf16[32,24,128]{2,1,0:T(8,128)(2,1)S(1)} %get-tuple-element.44), channel_id=1, replica_groups=mesh['band'=8,'rep'=4] {'band','rep'}, dimensions={0} | all-to-all | bytes 393216 | tf_op jit(solution)/shard_map/all_to_all | solution.py:467
  51.2 0.7 %sum_shares.1 = (f32[16,20]{1,0:T(8,128)}, f32[16,128]{1,0:T(8,128)}) custom-call(bf16[32,24,128]{2,1,0:T(8,128)(2,1)S(1)} %all_to_all.5.parts_ref), custom_call_target="tpu_custom_call" | custom-call | tf_op jit(solution)/shard_map/sum_shares/pallas_call | solution.py:468
Async XLA Ops:
  2.3 10.0 %collective-permute-start.1 = (bf16[96,640]{1,0:T(8,128)(2,1)S(1)}, bf16[96,640]{1,0:T(8,128)(2,1)S(1)}, u32[]{:S(2)}, u32[]{:S(2)}) collective-permute-start(bf16[96,640]{1,0:T(8,128)(2,1)S(1)} %get-tuple-element.28), channel_id=1, source_target_pairs={{0,4},{4,0},{8,12},{12,8},{16,20},{20,16},{24,28},{28,24},{1,5},{5... | collective-permute-start | bytes 368648 | tf_op jit(solution)/shard_map/ppermute | solution.py:59
  5.3 9.2 %collective-permute-start.3 = (bf16[96,640]{1,0:T(8,128)(2,1)S(1)}, bf16[96,640]{1,0:T(8,128)(2,1)S(1)}, u32[]{:S(2)}, u32[]{:S(2)}) collective-permute-start(bf16[96,640]{1,0:T(8,128)(2,1)S(1)} %get-tuple-element.32), channel_id=1, source_target_pairs={{0,8},{4,12},{8,0},{12,4},{16,24},{20,28},{24,16},{28,20},{1,9},{5... | collective-permute-start | bytes 368648 | tf_op jit(solution)/shard_map/ppermute | solution.py:59
  6.9 16.9 %collective-permute-start = (bf16[96,640]{1,0:T(8,128)(2,1)S(1)}, bf16[96,640]{1,0:T(8,128)(2,1)S(1)}, u32[]{:S(2)}, u32[]{:S(2)}) collective-permute-start(bf16[96,640]{1,0:T(8,128)(2,1)S(1)} %get-tuple-element.26), channel_id=1, source_target_pairs={{0,16},{4,20},{8,24},{12,28},{16,0},{20,4},{24,8},{28,12},{1,17},{... | collective-permute-start | bytes 368648 | tf_op jit(solution)/shard_map/ppermute | solution.py:59
  9.4 16.5 %collective-permute-start.2 = (bf16[96,640]{1,0:T(8,128)(2,1)S(1)}, bf16[96,640]{1,0:T(8,128)(2,1)S(1)}, u32[]{:S(2)}, u32[]{:S(2)}) collective-permute-start(bf16[96,640]{1,0:T(8,128)(2,1)S(1)} %get-tuple-element.30), channel_id=1, source_target_pairs={{0,20},{4,16},{8,28},{12,24},{16,4},{20,0},{24,12},{28,8},{1,21},{... | collective-permute-start | bytes 368648 | tf_op jit(solution)/shard_map/ppermute | solution.py:59
  9.8 16.2 %collective-permute-start.4 = (bf16[96,640]{1,0:T(8,128)(2,1)S(1)}, bf16[96,640]{1,0:T(8,128)(2,1)S(1)}, u32[]{:S(2)}, u32[]{:S(2)}) collective-permute-start(bf16[96,640]{1,0:T(8,128)(2,1)S(1)} %get-tuple-element.34), channel_id=1, source_target_pairs={{0,24},{4,28},{8,16},{12,20},{16,8},{20,12},{24,0},{28,4},{1,25},{... | collective-permute-start | bytes 368648 | tf_op jit(solution)/shard_map/ppermute | solution.py:59
  12.2 13.8 %collective-permute-start.5 = (bf16[96,640]{1,0:T(8,128)(2,1)S(1)}, bf16[96,640]{1,0:T(8,128)(2,1)S(1)}, u32[]{:S(2)}, u32[]{:S(2)}) collective-permute-start(bf16[96,640]{1,0:T(8,128)(2,1)S(1)} %get-tuple-element.35), channel_id=1, source_target_pairs={{0,28},{4,24},{8,20},{12,16},{16,12},{20,8},{24,4},{28,0},{1,29},{... | collective-permute-start | bytes 368648 | tf_op jit(solution)/shard_map/ppermute | solution.py:59
  14.5 12.2 %collective-permute-start.6 = (bf16[96,640]{1,0:T(8,128)(2,1)S(1)}, bf16[96,640]{1,0:T(8,128)(2,1)S(1)}, u32[]{:S(2)}, u32[]{:S(2)}) collective-permute-start(bf16[96,640]{1,0:T(8,128)(2,1)S(1)} %get-tuple-element.36), channel_id=1, source_target_pairs={{0,12},{4,8},{8,4},{12,0},{16,28},{20,24},{24,20},{28,16},{1,13},{... | collective-permute-start | bytes 368648 | tf_op jit(solution)/shard_map/ppermute | solution.py:59

commit v13 on v12

--- a/solution.py
+++ b/solution.py
@@ -148,20 +148,31 @@
     half_width,
     half_width_padded,
     group_hbm_ref,
+    level_hbm_ref,
+    grad_hbm_ref,
     frozen_ref,
     factors_ref,
-    level_ref,
     mixer_ref,
     merged_ref,
     up_ref,
     down_ref,
     mix_ref,
     mix_t_ref,
+    level_ref,
+    grad_ref,
     group_ref,
-    group_sem,
+    sems,
 ):
-    load = pltpu.make_async_copy(group_hbm_ref, group_ref, group_sem)
-    load.start()
+    sources = [group_hbm_ref, level_hbm_ref, grad_hbm_ref]
+    loads = [
+        pltpu.make_async_copy(source, target, sems.at[n])
+        for n, (source, target) in enumerate(zip(sources, [group_ref, level_ref, grad_ref]))
+    ]
+    for load in loads:
+        load.start()
+    rows = mix_ref.shape[0]
+    mix_ref[...] = expand_table(mixer_ref[...], rows, half_width_padded, half_width, False)
+    mix_t_ref[...] = expand_table(mixer_ref[...], rows, half_width_padded, half_width, True)
     reps, _, rank, share = factors_ref.shape
     levels = level_ref.shape[0]
     variables = group_ref.shape[0]
@@ -174,11 +185,12 @@
         down_t = down_t + dot_nn(factors_ref[r, 1], place.astype(BF16))
     down_t = down_t.astype(BF16)
     down_ref[...] = down_t
-    load.wait()
+    loads[0].wait()
     base = jnp.concatenate([frozen_ref[group_ref[v]].astype(F32) for v in range(variables)], axis=0)
     merged = (base + dot_tn(down_t, up)).astype(BF16)
     stacked = jnp.concatenate([merged, up], axis=0)
     merged_ref[...] = jnp.zeros_like(merged_ref)
+    loads[1].wait()
     for level in range(levels):
         through = dot_nn(stacked, level_ref[level])
         weights = through[:channels].astype(BF16)
@@ -188,12 +200,10 @@
         up_high, up_low = split_hi_lo(through[channels:])
         up_ref[level, :rank, :] = up_high
         up_ref[level, rank:, :] = up_low
-    rows = mix_ref.shape[0]
-    mix_ref[...] = expand_table(mixer_ref[...], rows, half_width_padded, half_width, False)
-    mix_t_ref[...] = expand_table(mixer_ref[...], rows, half_width_padded, half_width, True)
-
-
-def prepare(groups, frozen, factors, level_weight, mixer, samples, row_share, half_width, half_width_padded):
+    loads[2].wait()
+
+
+def prepare(groups, frozen, factors, level_weight, mixer, grad, row_share, half_width, half_width_padded):
     reps, _, rank, _ = factors.shape
     levels, feature_dim, _ = level_weight.shape
     channels = groups.shape[0] * frozen.shape[1]
@@ -201,22 +211,25 @@
     rows = WLAT * half_width_padded
     vmem = pl.BlockSpec(memory_space=pltpu.VMEM)
     flops = 2 * levels * (channels + rank) * feature_dim * feature_dim + 4 * rows * rows * WLAT * WLON
+    shapes = [
+        (grad.shape[0], reach, feature_dim),
+        (levels, 2 * rank, feature_dim),
+        (rank, channels),
+        (rows, rows),
+        (rows, rows),
+        level_weight.shape,
+        grad.shape,
+    ]
     return pl.pallas_call(
         functools.partial(prep_kernel, row_share, half_width, half_width_padded),
-        out_shape=[
-            jax.ShapeDtypeStruct((samples, reach, feature_dim), BF16),
-            jax.ShapeDtypeStruct((levels, 2 * rank, feature_dim), BF16),
-            jax.ShapeDtypeStruct((rank, channels), BF16),
-            jax.ShapeDtypeStruct((rows, rows), BF16),
-            jax.ShapeDtypeStruct((rows, rows), BF16),
-        ],
-        in_specs=[pl.BlockSpec(memory_space=pl.ANY)] + [vmem] * 4,
-        out_specs=[vmem] * 5,
-        scratch_shapes=[pltpu.SMEM(groups.shape, jnp.int32), pltpu.SemaphoreType.DMA],
+        out_shape=[jax.ShapeDtypeStruct(shape, BF16) for shape in shapes],
+        in_specs=[pl.BlockSpec(memory_space=pl.ANY)] * 3 + [vmem] * 3,
+        out_specs=[vmem] * len(shapes),
+        scratch_shapes=[pltpu.SMEM(groups.shape, jnp.int32), pltpu.SemaphoreType.DMA((3,))],
         compiler_params=params(),
-        cost_estimate=pl.CostEstimate(flops=flops, bytes_accessed=4 * 2**20, transcendentals=0),
+        cost_estimate=pl.CostEstimate(flops=flops, bytes_accessed=6 * 2**20, transcendentals=0),
         name="prepare",
-    )(in_hbm(groups), in_hbm(frozen), factors, in_hbm(level_weight), in_hbm(mixer))
+    )(in_hbm(groups), in_hbm(level_weight), in_hbm(grad), in_hbm(frozen), factors, in_hbm(mixer))
 
 
 def normal_parts(values):
@@ -248,26 +261,22 @@
     mix_t_ref,
     up_ref,
     down_ref,
-    grad_hbm_ref,
-    level_hbm_ref,
+    grad_ref,
+    level_ref,
     mixed_hbm_ref,
     share_ref,
     arrived_refs,
     turned_refs,
-    grad_refs,
     mixed_refs,
     pre_refs,
     tokens_refs,
     grad_pre_refs,
     grad_tokens_refs,
-    level_ref,
     total_ref,
-    grad_sems,
     mixed_sems,
-    level_sem,
 ):
     samples, reach, feature_dim = merged_ref.shape
-    chunk_count, (_, width, _) = len(grad_refs), grad_refs[0].shape
+    chunk_count, (_, width, _) = len(mixed_refs), mixed_refs[0].shape
     halves = piece_refs[0].shape[-2] // width
     arrived_directly = len(piece_refs) > 1
     depth = piece_refs[0].shape[-1] // samples
@@ -278,24 +287,15 @@
         lines, columns = pl.ds(window_row * WLAT, WLAT), pl.ds(half * width, width)
         return window_row, half, s, (s, lines, columns)
 
-    loads = [
-        pltpu.make_async_copy(grad_hbm_ref.at[place(n)[3]], grad_refs[n], grad_sems.at[n])
-        for n in range(chunk_count)
-    ]
     stores = [
         pltpu.make_async_copy(mixed_refs[n], mixed_hbm_ref.at[place(n)[3]], mixed_sems.at[n])
         for n in range(chunk_count)
     ]
-    level_load = pltpu.make_async_copy(level_hbm_ref, level_ref, level_sem)
-    for load in loads:
-        load.start()
-    level_load.start()
-    if arrived_directly:
+    def arrange(half):
         me = lax.axis_index("band")
         for distance, piece_ref in zip(ORDER, piece_refs):
-            for half in range(halves):
-                within = slice(half * width, (half + 1) * width)
-                arrived_refs[half][jnp.bitwise_xor(me, distance)] = piece_ref[within, :]
+            within = slice(half * width, (half + 1) * width)
+            arrived_refs[half][jnp.bitwise_xor(me, distance)] = piece_ref[within, :]
 
     def pixels_of(n, lanes):
         window_row, half, _, _ = place(n)
@@ -326,6 +326,10 @@
 
         return [embed, mixing]
 
+    def grad_line(n, line, within, columns):
+        _, _, s, (_, lines, first) = place(n)
+        return grad_ref[s, lines.start + line, pl.ds(first.start + within.start, within.size), columns]
+
     def pointwise(n, columns):
         def part(line):
             for start in range(0, width, SUB):
@@ -334,14 +338,15 @@
                 cdf, pdf = normal_parts(pre)
                 tokens = tokens_refs[n][at, columns].astype(F32)
                 mixed_refs[n][line, within, columns] = (tokens + pre * cdf).astype(BF16)
-                grad = grad_refs[n][line, within, columns].astype(F32)
+                grad = grad_line(n, line, within, columns).astype(F32)
                 grad_pre_refs[n][at, columns] = (grad * (cdf + pre * pdf)).astype(BF16)
 
         return [functools.partial(part, line) for line in range(WLAT)]
 
     def backward(n, columns):
         def spread():
-            direct = grad_refs[n][:, :, columns].reshape(rows, COLUMNS).astype(F32)
+            _, _, s, (_, lines, within) = place(n)
+            direct = grad_ref[s, lines, within, columns].reshape(rows, COLUMNS).astype(F32)
             through = dot_nn(mix_t_ref[...], grad_pre_refs[n][:, columns])
             grad_tokens_refs[n][:, columns] = (through + direct).astype(BF16)
 
@@ -358,10 +363,10 @@
         for n in range(chunk_count)
         for start in range(0, feature_dim, COLUMNS)
     ]
+    if arrived_directly:
+        arrange(0)
     for step in forward(*units[0]):
         step()
-    for load in loads:
-        load.wait()
     for i, unit in enumerate(units):
         n, columns = unit
         others = []
@@ -369,6 +374,8 @@
             others += forward(*units[i + 1])
         if columns.start == 0 and n % samples == 0:
             others += turn(n)
+            if arrived_directly and n // samples + 1 < halves:
+                others.append(functools.partial(arrange, n // samples + 1))
         if i > 0:
             others += backward(*units[i - 1])
         lines = pointwise(*unit)
@@ -381,7 +388,6 @@
     for step in backward(*units[-1]):
         step()
 
-    level_load.wait()
     first, second = factor_shares(total_ref[...], up_ref, down_ref, level_ref)
     rank, channels = down_ref.shape
     columns = share_ref.shape[2]
@@ -424,22 +430,18 @@
             jax.ShapeDtypeStruct(grad.shape, BF16),
             jax.ShapeDtypeStruct(share_shape, BF16),
         ],
-        in_specs=[vmem] * len(local) + [any_space, any_space],
+        in_specs=[vmem] * (len(local) + 2),
         out_specs=[any_space, vmem],
         scratch_shapes=[
             [pltpu.VMEM((WLAT, width, lanes), BF16)] * halves,
             [pltpu.VMEM((lanes, rows), BF16)] * (chunks // samples),
             [pltpu.VMEM((WLAT, width, feature_dim), BF16)] * chunks,
-            [pltpu.VMEM((WLAT, width, feature_dim), BF16)] * chunks,
             [pltpu.VMEM((rows, feature_dim), F32)] * chunks,
             [pltpu.VMEM((rows, feature_dim), BF16)] * chunks,
             [pltpu.VMEM((rows, feature_dim), BF16)] * chunks,
             [pltpu.VMEM((rows, feature_dim), BF16)] * chunks,
-            pltpu.VMEM(level_weight.shape, BF16),
             pltpu.VMEM((lanes // samples, feature_dim), F32),
             pltpu.SemaphoreType.DMA((chunks,)),
-            pltpu.SemaphoreType.DMA((chunks,)),
-            pltpu.SemaphoreType.DMA,
         ],
         compiler_params=params(),
         cost_estimate=pl.CostEstimate(
@@ -448,7 +450,7 @@
             transcendentals=samples * lat_rows * block_width * feature_dim,
         ),
         name="mix_blocks",
-    )(*local, in_hbm(grad), in_hbm(level_weight))
+    )(*local, grad, level_weight)
 
 
 def sum_kernel(parts_ref, first_ref, second_ref):
@@ -524,22 +526,22 @@
         )
     factors = lax.all_gather(pack, "rep", axis=0, tiled=False)
 
-    merged, up_through, down_t, mix, mix_t = prepare(
+    grad = mixed_token_gradient.reshape(samples, lat_rows, block_width, feature_dim)
+    if padded_width != block_width:
+        grad = jnp.pad(grad, ((0, 0), (0, 0), (0, padded_width - block_width), (0, 0)))
+    merged, up_through, down_t, mix, mix_t, level_copy, grad_copy = prepare(
         variable_group_index,
         frozen_patch_weight,
         factors,
         level_merge_weight,
         window_patch_mixer,
-        samples,
+        grad,
         row_share,
         half_width,
         half_padded,
     )
-    grad = mixed_token_gradient.reshape(samples, lat_rows, block_width, feature_dim)
-    if padded_width != block_width:
-        grad = jnp.pad(grad, ((0, 0), (0, 0), (0, padded_width - block_width), (0, 0)))
     mixed, shares = mix_blocks(
-        halves, arrived, merged, mix, mix_t, grad, up_through, down_t, level_merge_weight, band_count, reps
+        halves, arrived, merged, mix, mix_t, grad_copy, up_through, down_t, level_copy, band_count, reps
     )
     if padded_width != block_width:
         mixed = mixed[:, :, :block_width]

time: 52.3 us -> 52 us (level)
  no operation moved by 1% of the time
where the time goes in v13:
time: 52 us; the launch traced here: 51.6 us
  blocking collectives  21.7 us (42%)
  Pallas kernels  13.4 us (26%)
  starting transfers between devices  12.2 us (23%)
  waiting for transfers between devices  3.6 us (7%)
  between operations  0.66 us (1%)
    all_to_all x1, blocking collectives, sum_shares(): lax.all_to_all(shares, ('band', 'rep'), split_axis=0, concat_axis=0, tile...  16.5 us
    ppermute x7, starting transfers between devices, swap(): lax.ppermute(values, axis, [(source, source ^ distance) for source in ran...  12.2 us
    pallas_call x1, Pallas kernels, mix_blocks(): pl.pallas_call(lambda *refs: mix_kernel(refs[:len(arrived)], *refs[len(ar...  7.63 us
    all_gather x1, blocking collectives, on_device(): factors = lax.all_gather(pack, 'rep', axis=0, tiled=False)  5.18 us
    ppermute x7, waiting for transfers between devices, swap(): lax.ppermute(values, axis, [(source, source ^ distance) for source in ran...  3.6 us
    pallas_call x1, Pallas kernels, prepare(): pl.pallas_call(functools.partial(prep_kernel, row_share, half_width, half...  3.45 us
    pallas_call x1, Pallas kernels, send_blocks(): pl.pallas_call(send_kernel, out_shape=[jax.ShapeDtypeStruct(shape, BF16)...  1.64 us
  transfers between devices with their start and end apart: 7, of which 3 were waited for; matrix products, arithmetic and copies ran while one was open for 0% of the time, Pallas kernels for 7%

profile of v13, /device:TPU:0, one launch (start us, length us, event | category | flops | bytes accessed | tf_op | source)
XLA Modules:
  0.0 51.6 jit_solution(3234848386835664598)
XLA Ops:
  0.6 1.6 %send_blocks.1 = (bf16[96,640]{1,0:T(8,128)(2,1)S(1)}, bf16[96,640]{1,0:T(8,128)(2,1)S(1)}, bf16[96,640]{1,0:T(8,128)(2,1)S(1)}, bf16[96,640]{1,0:T(8,128)(2,1)S...) custom-call(s32[8]{0:T(128)} %owner_hbm_ref.1, ...), custom_call_target="tpu_custom_call" | custom-call | tf_op jit(solution)/shard_map/send_blocks/pallas_call | solution.py:104
  2.3 3.0 %collective-permute-start.1 = (bf16[96,640]{1,0:T(8,128)(2,1)S(1)}, bf16[96,640]{1,0:T(8,128)(2,1)S(1)}, u32[]{:S(2)}, u32[]{:S(2)}) collective-permute-start(bf16[96,640]{1,0:T(8,128)(2,1)S(1)} %get-tuple-element.30), channel_id=1, source_target_pairs={{0,4},{4,0},{8,12},{12,8},{16,20},{20,16},{24,28},{28,24},{1,5},{5... | collective-permute-start | bytes 368648 | tf_op jit(solution)/shard_map/ppermute | solution.py:59
  5.3 1.6 %collective-permute-start.3 = (bf16[96,640]{1,0:T(8,128)(2,1)S(1)}, bf16[96,640]{1,0:T(8,128)(2,1)S(1)}, u32[]{:S(2)}, u32[]{:S(2)}) collective-permute-start(bf16[96,640]{1,0:T(8,128)(2,1)S(1)} %get-tuple-element.34), channel_id=1, source_target_pairs={{0,8},{4,12},{8,0},{12,4},{16,24},{20,28},{24,16},{28,20},{1,9},{5... | collective-permute-start | bytes 368648 | tf_op jit(solution)/shard_map/ppermute | solution.py:59
  6.9 2.6 %collective-permute-start = (bf16[96,640]{1,0:T(8,128)(2,1)S(1)}, bf16[96,640]{1,0:T(8,128)(2,1)S(1)}, u32[]{:S(2)}, u32[]{:S(2)}) collective-permute-start(bf16[96,640]{1,0:T(8,128)(2,1)S(1)} %get-tuple-element.28), channel_id=1, source_target_pairs={{0,16},{4,20},{8,24},{12,28},{16,0},{20,4},{24,8},{28,12},{1,17},{... | collective-permute-start | bytes 368648 | tf_op jit(solution)/shard_map/ppermute | solution.py:59
  9.4 0.3 collective-permute-start.2
  9.8 2.5 %collective-permute-start.4 = (bf16[96,640]{1,0:T(8,128)(2,1)S(1)}, bf16[96,640]{1,0:T(8,128)(2,1)S(1)}, u32[]{:S(2)}, u32[]{:S(2)}) collective-permute-start(bf16[96,640]{1,0:T(8,128)(2,1)S(1)} %get-tuple-element.36), channel_id=1, source_target_pairs={{0,24},{4,28},{8,16},{12,20},{16,8},{20,12},{24,0},{28,4},{1,25},{... | collective-permute-start | bytes 368648 | tf_op jit(solution)/shard_map/ppermute | solution.py:59
  12.2 0.0 collective-permute-done.1.refs_2_
  12.2 2.3 %collective-permute-start.5 = (bf16[96,640]{1,0:T(8,128)(2,1)S(1)}, bf16[96,640]{1,0:T(8,128)(2,1)S(1)}, u32[]{:S(2)}, u32[]{:S(2)}) collective-permute-start(bf16[96,640]{1,0:T(8,128)(2,1)S(1)} %get-tuple-element.37), channel_id=1, source_target_pairs={{0,28},{4,24},{8,20},{12,16},{16,12},{20,8},{24,4},{28,0},{1,29},{... | collective-permute-start | bytes 368648 | tf_op jit(solution)/shard_map/ppermute | solution.py:59
  14.5 0.0 collective-permute-done.3.refs_4_
  14.5 0.0 collective-permute-start.6
  14.5 5.2 %all-gather = bf16[8,16,128]{2,1,0:T(8,128)(2,1)S(1)} all-gather(bf16[2,16,128]{2,1,0:T(8,128)(2,1)S(1)} %get-tuple-element.39), channel_id=2, replica_groups=mesh['band'=8,'rep'=4] {'rep'}, dimensions={0}, use_global_device_ids=true | all-gather | bytes 40960 | tf_op jit(solution)/shard_map/all_gather | solution.py:527
  19.7 3.5 %prepare.1 = (bf16[2,384,512]{2,1,0:T(8,128)(2,1)S(1)}, bf16[4,32,512]{2,1,0:T(8,128)(2,1)S(1)}, bf16[16,80]{1,0:T(8,128)(2,1)S(1)}, bf16[384,384]{1,0:T(8,128)(...) custom-call(s32[5]{0:T(128)} %group_hbm_ref.1, ...), custom_call_target="tpu_custom_call" | custom-call | flops 257949696 | bytes 6291456 | tf_op jit(solution)/shard_map/prepare/pallas_call | solution.py:223
  23.2 0.6 %collective-permute-done.refs_1_ = bf16[96,640]{1,0:T(8,128)(2,1)S(1)} collective-permute-done((bf16[96,640]{1,0:T(8,128)(2,1)S(1)}, bf16[96,640]{1,0:T(8,128)(2,1)S(1)}, u32[]{:S(2)}, u32[]{:S(2)}) %collective-permute-start) | collective-permute-done | bytes 122912 | tf_op jit(solution)/shard_map/ppermute | solution.py:59
  23.8 2.2 %collective-permute-done.2.refs_3_ = bf16[96,640]{1,0:T(8,128)(2,1)S(1)} collective-permute-done((bf16[96,640]{1,0:T(8,128)(2,1)S(1)}, bf16[96,640]{1,0:T(8,128)(2,1)S(1)}, u32[]{:S(2)}, u32[]{:S(2)}) %collective-permute-start.2) | collective-permute-done | bytes 122912 | tf_op jit(solution)/shard_map/ppermute | solution.py:59
  26.0 0.0 collective-permute-done.4.refs_5_
  26.0 0.0 collective-permute-done.5.refs_6_
  26.0 0.8 %collective-permute-done.6.refs_7_ = bf16[96,640]{1,0:T(8,128)(2,1)S(1)} collective-permute-done((bf16[96,640]{1,0:T(8,128)(2,1)S(1)}, bf16[96,640]{1,0:T(8,128)(2,1)S(1)}, u32[]{:S(2)}, u32[]{:S(2)}) %collective-permute-start.6) | collective-permute-done | bytes 122912 | tf_op jit(solution)/shard_map/ppermute | solution.py:59
  26.8 7.6 %mix_blocks.1 = (bf16[2,8,96,512]{3,2,1,0:T(8,128)(2,1)}, bf16[32,24,128]{2,1,0:T(8,128)(2,1)S(1)}) custom-call(bf16[96,640]{1,0:T(8,128)(2,1)S(1)} %get-tuple-element.27.refs_0_, bf16[96,640]{1,0:T(8,128)(2,1)S(1)} %collective-permute-done.refs_1_, bf16[96,640]{1,0:T(8,128)(2,1)S(1)} %collective-permute-done.1.refs_2_, ...), custom_call_target="tpu_custom_call" | custom-call | flops 2415919104 | bytes 12582912 | tf_op jit(solution)/shard_map/mix_blocks/pallas_call | solution.py:427
  34.4 16.5 %all_to_all.5.parts_ref = bf16[32,24,128]{2,1,0:T(8,128)(2,1)S(1)} all-to-all(bf16[32,24,128]{2,1,0:T(8,128)(2,1)S(1)} %get-tuple-element.48), channel_id=1, replica_groups=mesh['band'=8,'rep'=4] {'band','rep'}, dimensions={0} | all-to-all | bytes 393216 | tf_op jit(solution)/shard_map/all_to_all | solution.py:469
  50.9 0.7 %sum_shares.1 = (f32[16,20]{1,0:T(8,128)}, f32[16,128]{1,0:T(8,128)}) custom-call(bf16[32,24,128]{2,1,0:T(8,128)(2,1)S(1)} %all_to_all.5.parts_ref), custom_call_target="tpu_custom_call" | custom-call | tf_op jit(solution)/shard_map/sum_shares/pallas_call | solution.py:470
Async XLA Ops:
  2.3 10.0 %collective-permute-start.1 = (bf16[96,640]{1,0:T(8,128)(2,1)S(1)}, bf16[96,640]{1,0:T(8,128)(2,1)S(1)}, u32[]{:S(2)}, u32[]{:S(2)}) collective-permute-start(bf16[96,640]{1,0:T(8,128)(2,1)S(1)} %get-tuple-element.30), channel_id=1, source_target_pairs={{0,4},{4,0},{8,12},{12,8},{16,20},{20,16},{24,28},{28,24},{1,5},{5... | collective-permute-start | bytes 368648 | tf_op jit(solution)/shard_map/ppermute | solution.py:59
  5.3 9.2 %collective-permute-start.3 = (bf16[96,640]{1,0:T(8,128)(2,1)S(1)}, bf16[96,640]{1,0:T(8,128)(2,1)S(1)}, u32[]{:S(2)}, u32[]{:S(2)}) collective-permute-start(bf16[96,640]{1,0:T(8,128)(2,1)S(1)} %get-tuple-element.34), channel_id=1, source_target_pairs={{0,8},{4,12},{8,0},{12,4},{16,24},{20,28},{24,16},{28,20},{1,9},{5... | collective-permute-start | bytes 368648 | tf_op jit(solution)/shard_map/ppermute | solution.py:59
  6.9 16.9 %collective-permute-start = (bf16[96,640]{1,0:T(8,128)(2,1)S(1)}, bf16[96,640]{1,0:T(8,128)(2,1)S(1)}, u32[]{:S(2)}, u32[]{:S(2)}) collective-permute-start(bf16[96,640]{1,0:T(8,128)(2,1)S(1)} %get-tuple-element.28), channel_id=1, source_target_pairs={{0,16},{4,20},{8,24},{12,28},{16,0},{20,4},{24,8},{28,12},{1,17},{... | collective-permute-start | bytes 368648 | tf_op jit(solution)/shard_map/ppermute | solution.py:59
  9.4 16.5 %collective-permute-start.2 = (bf16[96,640]{1,0:T(8,128)(2,1)S(1)}, bf16[96,640]{1,0:T(8,128)(2,1)S(1)}, u32[]{:S(2)}, u32[]{:S(2)}) collective-permute-start(bf16[96,640]{1,0:T(8,128)(2,1)S(1)} %get-tuple-element.32), channel_id=1, source_target_pairs={{0,20},{4,16},{8,28},{12,24},{16,4},{20,0},{24,12},{28,8},{1,21},{... | collective-permute-start | bytes 368648 | tf_op jit(solution)/shard_map/ppermute | solution.py:59
  9.8 16.2 %collective-permute-start.4 = (bf16[96,640]{1,0:T(8,128)(2,1)S(1)}, bf16[96,640]{1,0:T(8,128)(2,1)S(1)}, u32[]{:S(2)}, u32[]{:S(2)}) collective-permute-start(bf16[96,640]{1,0:T(8,128)(2,1)S(1)} %get-tuple-element.36), channel_id=1, source_target_pairs={{0,24},{4,28},{8,16},{12,20},{16,8},{20,12},{24,0},{28,4},{1,25},{... | collective-permute-start | bytes 368648 | tf_op jit(solution)/shard_map/ppermute | solution.py:59
  12.2 13.8 %collective-permute-start.5 = (bf16[96,640]{1,0:T(8,128)(2,1)S(1)}, bf16[96,640]{1,0:T(8,128)(2,1)S(1)}, u32[]{:S(2)}, u32[]{:S(2)}) collective-permute-start(bf16[96,640]{1,0:T(8,128)(2,1)S(1)} %get-tuple-element.37), channel_id=1, source_target_pairs={{0,28},{4,24},{8,20},{12,16},{16,12},{20,8},{24,4},{28,0},{1,29},{... | collective-permute-start | bytes 368648 | tf_op jit(solution)/shard_map/ppermute | solution.py:59
  14.5 12.2 %collective-permute-start.6 = (bf16[96,640]{1,0:T(8,128)(2,1)S(1)}, bf16[96,640]{1,0:T(8,128)(2,1)S(1)}, u32[]{:S(2)}, u32[]{:S(2)}) collective-permute-start(bf16[96,640]{1,0:T(8,128)(2,1)S(1)} %get-tuple-element.38), channel_id=1, source_target_pairs={{0,12},{4,8},{8,4},{12,0},{16,28},{20,24},{24,20},{28,16},{1,13},{... | collective-permute-start | bytes 368648 | tf_op jit(solution)/shard_map/ppermute | solution.py:59

commit v14 on v13

--- a/solution.py
+++ b/solution.py
@@ -282,6 +282,14 @@
     depth = piece_refs[0].shape[-1] // samples
     rows = WLAT * width
 
+    group_rows = mix_ref.shape[0]
+    group = group_rows // WLAT
+    groups = [
+        (slice(start, start + group), slice(start * WLAT, start * WLAT + group_rows))
+        for start in range(0, width, group)
+    ]
+    pair = 1 if group % SUB == 0 else 2
+
     def place(n):
         window_row, half, s = n // (halves * samples), n // samples % halves, n % samples
         lines, columns = pl.ds(window_row * WLAT, WLAT), pl.ds(half * width, width)
@@ -319,36 +327,48 @@
 
         def embed():
             pixels = pixels_of(n, slice(lane, lane + reach))
-            tokens_refs[n][:, columns] = dot_nn(pixels, merged_ref[s, :, columns]).astype(BF16)
+            tokens = dot_nn(pixels, merged_ref[s, :, columns]).reshape(WLAT, width, COLUMNS)
+            for within, at in groups:
+                tokens_refs[n][at, columns] = tokens[:, within].reshape(group_rows, COLUMNS).astype(BF16)
 
         def mixing():
-            pre_refs[n][:, columns] = dot_nn(mix_ref[...], tokens_refs[n][:, columns])
+            for _, at in groups:
+                pre_refs[n][at, columns] = dot_nn(mix_ref[...], tokens_refs[n][at, columns])
 
         return [embed, mixing]
 
-    def grad_line(n, line, within, columns):
-        _, _, s, (_, lines, first) = place(n)
-        return grad_ref[s, lines.start + line, pl.ds(first.start + within.start, within.size), columns]
-
     def pointwise(n, columns):
-        def part(line):
-            for start in range(0, width, SUB):
-                at, within = pl.ds(line * width + start, SUB), pl.ds(start, SUB)
-                pre = pre_refs[n][at, columns]
+        _, _, s, (_, lines, across) = place(n)
+
+        def part(line, lanes):
+            grads = [grad_ref[s, lines.start + line + k, across, lanes].astype(F32) for k in range(pair)]
+            mixed = []
+            for within, at in groups:
+                at = pl.ds(at.start + line * group, pair * group)
+                pre = pre_refs[n][at, lanes]
                 cdf, pdf = normal_parts(pre)
-                tokens = tokens_refs[n][at, columns].astype(F32)
-                mixed_refs[n][line, within, columns] = (tokens + pre * cdf).astype(BF16)
-                grad = grad_line(n, line, within, columns).astype(F32)
-                grad_pre_refs[n][at, columns] = (grad * (cdf + pre * pdf)).astype(BF16)
-
-        return [functools.partial(part, line) for line in range(WLAT)]
+                mixed.append(tokens_refs[n][at, lanes].astype(F32) + pre * cdf)
+                grad = jnp.concatenate([values[within] for values in grads], axis=0)
+                grad_pre_refs[n][at, lanes] = (grad * (cdf + pre * pdf)).astype(BF16)
+            for k in range(pair):
+                parts = [values[k * group : (k + 1) * group] for values in mixed]
+                mixed_refs[n][line + k, :, lanes] = jnp.concatenate(parts, axis=0).astype(BF16)
+
+        return [
+            functools.partial(part, line, slice(start, start + LANE))
+            for line in range(0, WLAT, pair)
+            for start in range(columns.start, columns.stop, LANE)
+        ]
 
     def backward(n, columns):
         def spread():
             _, _, s, (_, lines, within) = place(n)
-            direct = grad_ref[s, lines, within, columns].reshape(rows, COLUMNS).astype(F32)
-            through = dot_nn(mix_t_ref[...], grad_pre_refs[n][:, columns])
-            grad_tokens_refs[n][:, columns] = (through + direct).astype(BF16)
+            through = [
+                dot_nn(mix_t_ref[...], grad_pre_refs[n][at, columns]).reshape(WLAT, group, COLUMNS)
+                for _, at in groups
+            ]
+            total = jnp.concatenate(through, axis=1) + grad_ref[s, lines, within, columns].astype(F32)
+            grad_tokens_refs[n][:, columns] = total.reshape(rows, COLUMNS).astype(BF16)
 
         def share():
             s = n % samples
@@ -500,6 +520,7 @@
     half_width = block_width // halves
     half_padded = round_up(half_width, SUB)
     padded_width = halves * half_padded
+    group = 2 * WLON if half_width % (2 * WLON) == 0 else half_padded
     features = samples * levels * channels
 
     pixels = patches.reshape(features, col_count)
@@ -537,8 +558,8 @@
         window_patch_mixer,
         grad,
         row_share,
-        half_width,
-        half_padded,
+        min(half_width, group),
+        group,
     )
     mixed, shares = mix_blocks(
         halves, arrived, merged, mix, mix_t, grad_copy, up_through, down_t, level_copy, band_count, reps

time: 52 us -> 51.3 us (0.987)
  Pallas kernels: 13.4 us -> 12.2 us
  waiting for transfers between devices: 3.6 us -> 4.16 us
    pallas_call x1, Pallas kernels: 7.63 us -> 6.98 us  [mix_blocks(): pl.pallas_call(lambda *refs: mix_kernel(refs[:len(arrived)], *refs[len(ar...]
    pallas_call x1, Pallas kernels: 3.45 us -> 2.9 us  [prepare(): pl.pallas_call(functools.partial(prep_kernel, row_share, half_width, half...]
    ppermute x7, waiting for transfers between devices: 3.6 us -> 4.16 us  [swap(): lax.ppermute(values, axis, [(source, source ^ distance) for source in ran...]
  transfers between devices with their start and end apart: 7 -> 7, of which waited for: 3 -> 3; matrix products, arithmetic and copies ran while one was open for 0% -> 0% of each run, Pallas kernels for 7% -> 6%
where the time goes in v14:
time: 51.3 us; the launch traced here: 51 us
  blocking collectives  21.7 us (42%)
  Pallas kernels  12.2 us (24%)
  starting transfers between devices  12.2 us (24%)
  waiting for transfers between devices  4.16 us (8%)
  between operations  0.66 us (1%)
    all_to_all x1, blocking collectives, sum_shares(): lax.all_to_all(shares, ('band', 'rep'), split_axis=0, concat_axis=0, tile...  16.5 us
    ppermute x7, starting transfers between devices, swap(): lax.ppermute(values, axis, [(source, source ^ distance) for source in ran...  12.2 us
    pallas_call x1, Pallas kernels, mix_blocks(): pl.pallas_call(lambda *refs: mix_kernel(refs[:len(arrived)], *refs[len(ar...  6.98 us
    all_gather x1, blocking collectives, on_device(): factors = lax.all_gather(pack, 'rep', axis=0, tiled=False)  5.18 us
    ppermute x7, waiting for transfers between devices, swap(): lax.ppermute(values, axis, [(source, source ^ distance) for source in ran...  4.16 us
    pallas_call x1, Pallas kernels, prepare(): pl.pallas_call(functools.partial(prep_kernel, row_share, half_width, half...  2.9 us
    pallas_call x1, Pallas kernels, send_blocks(): pl.pallas_call(send_kernel, out_shape=[jax.ShapeDtypeStruct(shape, BF16)...  1.64 us
  transfers between devices with their start and end apart: 7, of which 3 were waited for; matrix products, arithmetic and copies ran while one was open for 0% of the time, Pallas kernels for 6%

profile of v14, /device:TPU:0, one launch (start us, length us, event | category | flops | bytes accessed | tf_op | source)
XLA Modules:
  0.0 51.0 jit_solution(10168525157923786152)
XLA Ops:
  0.6 1.6 %send_blocks.1 = (bf16[96,640]{1,0:T(8,128)(2,1)S(1)}, bf16[96,640]{1,0:T(8,128)(2,1)S(1)}, bf16[96,640]{1,0:T(8,128)(2,1)S(1)}, bf16[96,640]{1,0:T(8,128)(2,1)S...) custom-call(s32[8]{0:T(128)} %owner_hbm_ref.1, ...), custom_call_target="tpu_custom_call" | custom-call | tf_op jit(solution)/shard_map/send_blocks/pallas_call | solution.py:104
  2.3 3.0 %collective-permute-start.1 = (bf16[96,640]{1,0:T(8,128)(2,1)S(1)}, bf16[96,640]{1,0:T(8,128)(2,1)S(1)}, u32[]{:S(2)}, u32[]{:S(2)}) collective-permute-start(bf16[96,640]{1,0:T(8,128)(2,1)S(1)} %get-tuple-element.30), channel_id=1, source_target_pairs={{0,4},{4,0},{8,12},{12,8},{16,20},{20,16},{24,28},{28,24},{1,5},{5... | collective-permute-start | bytes 368648 | tf_op jit(solution)/shard_map/ppermute | solution.py:59
  5.3 1.6 %collective-permute-start.3 = (bf16[96,640]{1,0:T(8,128)(2,1)S(1)}, bf16[96,640]{1,0:T(8,128)(2,1)S(1)}, u32[]{:S(2)}, u32[]{:S(2)}) collective-permute-start(bf16[96,640]{1,0:T(8,128)(2,1)S(1)} %get-tuple-element.34), channel_id=1, source_target_pairs={{0,8},{4,12},{8,0},{12,4},{16,24},{20,28},{24,16},{28,20},{1,9},{5... | collective-permute-start | bytes 368648 | tf_op jit(solution)/shard_map/ppermute | solution.py:59
  6.9 2.6 %collective-permute-start = (bf16[96,640]{1,0:T(8,128)(2,1)S(1)}, bf16[96,640]{1,0:T(8,128)(2,1)S(1)}, u32[]{:S(2)}, u32[]{:S(2)}) collective-permute-start(bf16[96,640]{1,0:T(8,128)(2,1)S(1)} %get-tuple-element.28), channel_id=1, source_target_pairs={{0,16},{4,20},{8,24},{12,28},{16,0},{20,4},{24,8},{28,12},{1,17},{... | collective-permute-start | bytes 368648 | tf_op jit(solution)/shard_map/ppermute | solution.py:59
  9.4 0.3 collective-permute-start.2
  9.8 2.5 %collective-permute-start.4 = (bf16[96,640]{1,0:T(8,128)(2,1)S(1)}, bf16[96,640]{1,0:T(8,128)(2,1)S(1)}, u32[]{:S(2)}, u32[]{:S(2)}) collective-permute-start(bf16[96,640]{1,0:T(8,128)(2,1)S(1)} %get-tuple-element.36), channel_id=1, source_target_pairs={{0,24},{4,28},{8,16},{12,20},{16,8},{20,12},{24,0},{28,4},{1,25},{... | collective-permute-start | bytes 368648 | tf_op jit(solution)/shard_map/ppermute | solution.py:59
  12.2 0.0 collective-permute-done.1.refs_2_
  12.2 2.3 %collective-permute-start.5 = (bf16[96,640]{1,0:T(8,128)(2,1)S(1)}, bf16[96,640]{1,0:T(8,128)(2,1)S(1)}, u32[]{:S(2)}, u32[]{:S(2)}) collective-permute-start(bf16[96,640]{1,0:T(8,128)(2,1)S(1)} %get-tuple-element.37), channel_id=1, source_target_pairs={{0,28},{4,24},{8,20},{12,16},{16,12},{20,8},{24,4},{28,0},{1,29},{... | collective-permute-start | bytes 368648 | tf_op jit(solution)/shard_map/ppermute | solution.py:59
  14.5 0.0 collective-permute-done.3.refs_4_
  14.5 0.0 collective-permute-start.6
  14.5 5.2 %all-gather = bf16[8,16,128]{2,1,0:T(8,128)(2,1)S(1)} all-gather(bf16[2,16,128]{2,1,0:T(8,128)(2,1)S(1)} %get-tuple-element.39), channel_id=2, replica_groups=mesh['band'=8,'rep'=4] {'rep'}, dimensions={0}, use_global_device_ids=true | all-gather | bytes 40960 | tf_op jit(solution)/shard_map/all_gather | solution.py:548
  19.7 2.9 %prepare.1 = (bf16[2,384,512]{2,1,0:T(8,128)(2,1)S(1)}, bf16[4,32,512]{2,1,0:T(8,128)(2,1)S(1)}, bf16[16,80]{1,0:T(8,128)(2,1)S(1)}, bf16[192,192]{1,0:T(8,128)(...) custom-call(s32[5]{0:T(128)} %group_hbm_ref.1, ...), custom_call_target="tpu_custom_call" | custom-call | flops 215482368 | bytes 6291456 | tf_op jit(solution)/shard_map/prepare/pallas_call | solution.py:223
  22.6 1.2 %collective-permute-done.refs_1_ = bf16[96,640]{1,0:T(8,128)(2,1)S(1)} collective-permute-done((bf16[96,640]{1,0:T(8,128)(2,1)S(1)}, bf16[96,640]{1,0:T(8,128)(2,1)S(1)}, u32[]{:S(2)}, u32[]{:S(2)}) %collective-permute-start) | collective-permute-done | bytes 122912 | tf_op jit(solution)/shard_map/ppermute | solution.py:59
  23.8 2.2 %collective-permute-done.2.refs_3_ = bf16[96,640]{1,0:T(8,128)(2,1)S(1)} collective-permute-done((bf16[96,640]{1,0:T(8,128)(2,1)S(1)}, bf16[96,640]{1,0:T(8,128)(2,1)S(1)}, u32[]{:S(2)}, u32[]{:S(2)}) %collective-permute-start.2) | collective-permute-done | bytes 122912 | tf_op jit(solution)/shard_map/ppermute | solution.py:59
  26.0 0.0 collective-permute-done.4.refs_5_
  26.0 0.0 collective-permute-done.5.refs_6_
  26.0 0.8 %collective-permute-done.6.refs_7_ = bf16[96,640]{1,0:T(8,128)(2,1)S(1)} collective-permute-done((bf16[96,640]{1,0:T(8,128)(2,1)S(1)}, bf16[96,640]{1,0:T(8,128)(2,1)S(1)}, u32[]{:S(2)}, u32[]{:S(2)}) %collective-permute-start.6) | collective-permute-done | bytes 122912 | tf_op jit(solution)/shard_map/ppermute | solution.py:59
  26.8 7.0 %mix_blocks.1 = (bf16[2,8,96,512]{3,2,1,0:T(8,128)(2,1)}, bf16[32,24,128]{2,1,0:T(8,128)(2,1)S(1)}) custom-call(bf16[96,640]{1,0:T(8,128)(2,1)S(1)} %get-tuple-element.27.refs_0_, bf16[96,640]{1,0:T(8,128)(2,1)S(1)} %collective-permute-done.refs_1_, bf16[96,640]{1,0:T(8,128)(2,1)S(1)} %collective-permute-done.1.refs_2_, ...), custom_call_target="tpu_custom_call" | custom-call | flops 2415919104 | bytes 12582912 | tf_op jit(solution)/shard_map/mix_blocks/pallas_call | solution.py:447
  33.7 16.5 %all_to_all.5.parts_ref = bf16[32,24,128]{2,1,0:T(8,128)(2,1)S(1)} all-to-all(bf16[32,24,128]{2,1,0:T(8,128)(2,1)S(1)} %get-tuple-element.48), channel_id=1, replica_groups=mesh['band'=8,'rep'=4] {'band','rep'}, dimensions={0} | all-to-all | bytes 393216 | tf_op jit(solution)/shard_map/all_to_all | solution.py:489
  50.3 0.7 %sum_shares.1 = (f32[16,20]{1,0:T(8,128)}, f32[16,128]{1,0:T(8,128)}) custom-call(bf16[32,24,128]{2,1,0:T(8,128)(2,1)S(1)} %all_to_all.5.parts_ref), custom_call_target="tpu_custom_call" | custom-call | tf_op jit(solution)/shard_map/sum_shares/pallas_call | solution.py:490
Async XLA Ops:
  2.3 10.0 %collective-permute-start.1 = (bf16[96,640]{1,0:T(8,128)(2,1)S(1)}, bf16[96,640]{1,0:T(8,128)(2,1)S(1)}, u32[]{:S(2)}, u32[]{:S(2)}) collective-permute-start(bf16[96,640]{1,0:T(8,128)(2,1)S(1)} %get-tuple-element.30), channel_id=1, source_target_pairs={{0,4},{4,0},{8,12},{12,8},{16,20},{20,16},{24,28},{28,24},{1,5},{5... | collective-permute-start | bytes 368648 | tf_op jit(solution)/shard_map/ppermute | solution.py:59
  5.3 9.2 %collective-permute-start.3 = (bf16[96,640]{1,0:T(8,128)(2,1)S(1)}, bf16[96,640]{1,0:T(8,128)(2,1)S(1)}, u32[]{:S(2)}, u32[]{:S(2)}) collective-permute-start(bf16[96,640]{1,0:T(8,128)(2,1)S(1)} %get-tuple-element.34), channel_id=1, source_target_pairs={{0,8},{4,12},{8,0},{12,4},{16,24},{20,28},{24,16},{28,20},{1,9},{5... | collective-permute-start | bytes 368648 | tf_op jit(solution)/shard_map/ppermute | solution.py:59
  6.9 16.9 %collective-permute-start = (bf16[96,640]{1,0:T(8,128)(2,1)S(1)}, bf16[96,640]{1,0:T(8,128)(2,1)S(1)}, u32[]{:S(2)}, u32[]{:S(2)}) collective-permute-start(bf16[96,640]{1,0:T(8,128)(2,1)S(1)} %get-tuple-element.28), channel_id=1, source_target_pairs={{0,16},{4,20},{8,24},{12,28},{16,0},{20,4},{24,8},{28,12},{1,17},{... | collective-permute-start | bytes 368648 | tf_op jit(solution)/shard_map/ppermute | solution.py:59
  9.4 16.5 %collective-permute-start.2 = (bf16[96,640]{1,0:T(8,128)(2,1)S(1)}, bf16[96,640]{1,0:T(8,128)(2,1)S(1)}, u32[]{:S(2)}, u32[]{:S(2)}) collective-permute-start(bf16[96,640]{1,0:T(8,128)(2,1)S(1)} %get-tuple-element.32), channel_id=1, source_target_pairs={{0,20},{4,16},{8,28},{12,24},{16,4},{20,0},{24,12},{28,8},{1,21},{... | collective-permute-start | bytes 368648 | tf_op jit(solution)/shard_map/ppermute | solution.py:59
  9.8 16.2 %collective-permute-start.4 = (bf16[96,640]{1,0:T(8,128)(2,1)S(1)}, bf16[96,640]{1,0:T(8,128)(2,1)S(1)}, u32[]{:S(2)}, u32[]{:S(2)}) collective-permute-start(bf16[96,640]{1,0:T(8,128)(2,1)S(1)} %get-tuple-element.36), channel_id=1, source_target_pairs={{0,24},{4,28},{8,16},{12,20},{16,8},{20,12},{24,0},{28,4},{1,25},{... | collective-permute-start | bytes 368648 | tf_op jit(solution)/shard_map/ppermute | solution.py:59
  12.2 13.8 %collective-permute-start.5 = (bf16[96,640]{1,0:T(8,128)(2,1)S(1)}, bf16[96,640]{1,0:T(8,128)(2,1)S(1)}, u32[]{:S(2)}, u32[]{:S(2)}) collective-permute-start(bf16[96,640]{1,0:T(8,128)(2,1)S(1)} %get-tuple-element.37), channel_id=1, source_target_pairs={{0,28},{4,24},{8,20},{12,16},{16,12},{20,8},{24,4},{28,0},{1,29},{... | collective-permute-start | bytes 368648 | tf_op jit(solution)/shard_map/ppermute | solution.py:59
  14.5 12.2 %collective-permute-start.6 = (bf16[96,640]{1,0:T(8,128)(2,1)S(1)}, bf16[96,640]{1,0:T(8,128)(2,1)S(1)}, u32[]{:S(2)}, u32[]{:S(2)}) collective-permute-start(bf16[96,640]{1,0:T(8,128)(2,1)S(1)} %get-tuple-element.38), channel_id=1, source_target_pairs={{0,12},{4,8},{8,4},{12,0},{16,28},{20,24},{24,20},{28,16},{1,13},{... | collective-permute-start | bytes 368648 | tf_op jit(solution)/shard_map/ppermute | solution.py:59

commit v15 on v14

--- a/solution.py
+++ b/solution.py
@@ -131,9 +131,9 @@
     return [arrived[distance] for distance in ORDER]
 
 
-def expand_table(table, rows, half_width_padded, half_width, transpose):
+def expand_table(table, rows, half_width_padded, half_width, flip, transpose):
     position = iota2((rows, WLAT * WLON), 0)
-    line, col = position // half_width_padded, position % half_width_padded
+    line, col = jnp.bitwise_xor(position // half_width_padded, flip), position % half_width_padded
     target = iota2((rows, WLAT * WLON), 1)
     pick = jnp.where((target == line * WLON + col % WLON) & (col < half_width), 1.0, 0.0).astype(BF16)
     left = (dot_nt if transpose else dot_nn)(pick, table).astype(BF16)
@@ -144,6 +144,7 @@
 
 
 def prep_kernel(
+    direct,
     row_share,
     half_width,
     half_width_padded,
@@ -163,16 +164,22 @@
     group_ref,
     sems,
 ):
-    sources = [group_hbm_ref, level_hbm_ref, grad_hbm_ref]
+    pairs = [(group_hbm_ref, group_ref), (level_hbm_ref, level_ref)]
+    flip = lax.axis_index("band") if direct else 0
+    if direct:
+        pairs += [
+            (grad_hbm_ref.at[:, jnp.bitwise_xor(flip, line)], grad_ref.at[:, line]) for line in range(WLAT)
+        ]
+    else:
+        pairs.append((grad_hbm_ref, grad_ref))
     loads = [
-        pltpu.make_async_copy(source, target, sems.at[n])
-        for n, (source, target) in enumerate(zip(sources, [group_ref, level_ref, grad_ref]))
+        pltpu.make_async_copy(source, target, sems.at[n]) for n, (source, target) in enumerate(pairs)
     ]
     for load in loads:
         load.start()
     rows = mix_ref.shape[0]
-    mix_ref[...] = expand_table(mixer_ref[...], rows, half_width_padded, half_width, False)
-    mix_t_ref[...] = expand_table(mixer_ref[...], rows, half_width_padded, half_width, True)
+    mix_ref[...] = expand_table(mixer_ref[...], rows, half_width_padded, half_width, flip, False)
+    mix_t_ref[...] = expand_table(mixer_ref[...], rows, half_width_padded, half_width, flip, True)
     reps, _, rank, share = factors_ref.shape
     levels = level_ref.shape[0]
     variables = group_ref.shape[0]
@@ -200,10 +207,11 @@
         up_high, up_low = split_hi_lo(through[channels:])
         up_ref[level, :rank, :] = up_high
         up_ref[level, rank:, :] = up_low
-    loads[2].wait()
-
-
-def prepare(groups, frozen, factors, level_weight, mixer, grad, row_share, half_width, half_width_padded):
+    for load in loads[2:]:
+        load.wait()
+
+
+def prepare(direct, groups, frozen, factors, level_weight, mixer, grad, row_share, half_width, half_width_padded):
     reps, _, rank, _ = factors.shape
     levels, feature_dim, _ = level_weight.shape
     channels = groups.shape[0] * frozen.shape[1]
@@ -221,11 +229,11 @@
         grad.shape,
     ]
     return pl.pallas_call(
-        functools.partial(prep_kernel, row_share, half_width, half_width_padded),
+        functools.partial(prep_kernel, direct, row_share, half_width, half_width_padded),
         out_shape=[jax.ShapeDtypeStruct(shape, BF16) for shape in shapes],
         in_specs=[pl.BlockSpec(memory_space=pl.ANY)] * 3 + [vmem] * 3,
         out_specs=[vmem] * len(shapes),
-        scratch_shapes=[pltpu.SMEM(groups.shape, jnp.int32), pltpu.SemaphoreType.DMA((3,))],
+        scratch_shapes=[pltpu.SMEM(groups.shape, jnp.int32), pltpu.SemaphoreType.DMA((2 + WLAT,))],
         compiler_params=params(),
         cost_estimate=pl.CostEstimate(flops=flops, bytes_accessed=6 * 2**20, transcendentals=0),
         name="prepare",
@@ -255,6 +263,7 @@
 
 
 def mix_kernel(
+    direct,
     piece_refs,
     merged_ref,
     mix_ref,
@@ -265,7 +274,6 @@
     level_ref,
     mixed_hbm_ref,
     share_ref,
-    arrived_refs,
     turned_refs,
     mixed_refs,
     pre_refs,
@@ -277,8 +285,6 @@
 ):
     samples, reach, feature_dim = merged_ref.shape
     chunk_count, (_, width, _) = len(mixed_refs), mixed_refs[0].shape
-    halves = piece_refs[0].shape[-2] // width
-    arrived_directly = len(piece_refs) > 1
     depth = piece_refs[0].shape[-1] // samples
     rows = WLAT * width
 
@@ -290,29 +296,29 @@
     ]
     pair = 1 if group % SUB == 0 else 2
 
-    def place(n):
-        window_row, half, s = n // (halves * samples), n // samples % halves, n % samples
-        lines, columns = pl.ds(window_row * WLAT, WLAT), pl.ds(half * width, width)
-        return window_row, half, s, (s, lines, columns)
-
+    def lines_of(n):
+        return pl.ds(n // samples * WLAT, WLAT)
+
+    if direct:
+        me = lax.axis_index("band")
+        targets = [
+            (mixed_refs[n].at[line], mixed_hbm_ref.at[n, jnp.bitwise_xor(me, line)])
+            for n in range(chunk_count)
+            for line in range(WLAT)
+        ]
+    else:
+        targets = [
+            (mixed_refs[n], mixed_hbm_ref.at[n % samples, lines_of(n)]) for n in range(chunk_count)
+        ]
     stores = [
-        pltpu.make_async_copy(mixed_refs[n], mixed_hbm_ref.at[place(n)[3]], mixed_sems.at[n])
-        for n in range(chunk_count)
-    ]
-    def arrange(half):
-        me = lax.axis_index("band")
-        for distance, piece_ref in zip(ORDER, piece_refs):
-            within = slice(half * width, (half + 1) * width)
-            arrived_refs[half][jnp.bitwise_xor(me, distance)] = piece_ref[within, :]
+        pltpu.make_async_copy(source, target, mixed_sems.at[n]) for n, (source, target) in enumerate(targets)
+    ]
 
     def pixels_of(n, lanes):
-        window_row, half, _, _ = place(n)
-        if arrived_directly:
-            block = arrived_refs[half][:, :, lanes]
-        else:
-            lines = slice(window_row * WLAT, (window_row + 1) * WLAT)
-            block = piece_refs[0][lines, half * width : (half + 1) * width, lanes]
-        return block.reshape(rows, lanes.stop - lanes.start)
+        if direct:
+            by_distance = dict(zip(ORDER, piece_refs))
+            return jnp.concatenate([by_distance[line][:, lanes] for line in range(WLAT)], axis=0)
+        return piece_refs[0][lines_of(n), :, lanes].reshape(rows, lanes.stop - lanes.start)
 
     def turn(n):
         def part(lanes):
@@ -338,36 +344,40 @@
         return [embed, mixing]
 
     def pointwise(n, columns):
-        _, _, s, (_, lines, across) = place(n)
-
-        def part(line, lanes):
-            grads = [grad_ref[s, lines.start + line + k, across, lanes].astype(F32) for k in range(pair)]
+        s, first_line = n % samples, n // samples * WLAT
+
+        def part(line, across, lanes):
+            grads = [grad_ref[s, first_line + line + k, across, lanes].astype(F32) for k in range(pair)]
             mixed = []
             for within, at in groups:
+                if within.start < across.start or within.stop > across.stop:
+                    continue
                 at = pl.ds(at.start + line * group, pair * group)
                 pre = pre_refs[n][at, lanes]
                 cdf, pdf = normal_parts(pre)
                 mixed.append(tokens_refs[n][at, lanes].astype(F32) + pre * cdf)
-                grad = jnp.concatenate([values[within] for values in grads], axis=0)
+                first = within.start - across.start
+                grad = jnp.concatenate([values[first : first + group] for values in grads], axis=0)
                 grad_pre_refs[n][at, lanes] = (grad * (cdf + pre * pdf)).astype(BF16)
             for k in range(pair):
                 parts = [values[k * group : (k + 1) * group] for values in mixed]
-                mixed_refs[n][line + k, :, lanes] = jnp.concatenate(parts, axis=0).astype(BF16)
+                mixed_refs[n][line + k, across, lanes] = jnp.concatenate(parts, axis=0).astype(BF16)
 
         return [
-            functools.partial(part, line, slice(start, start + LANE))
+            functools.partial(part, line, slice(across, across + pair * group), slice(start, start + LANE))
             for line in range(0, WLAT, pair)
+            for across in range(0, width, pair * group)
             for start in range(columns.start, columns.stop, LANE)
         ]
 
     def backward(n, columns):
         def spread():
-            _, _, s, (_, lines, within) = place(n)
+            direct_part = grad_ref[n % samples, lines_of(n), :, columns].astype(F32)
             through = [
                 dot_nn(mix_t_ref[...], grad_pre_refs[n][at, columns]).reshape(WLAT, group, COLUMNS)
                 for _, at in groups
             ]
-            total = jnp.concatenate(through, axis=1) + grad_ref[s, lines, within, columns].astype(F32)
+            total = jnp.concatenate(through, axis=1) + direct_part
             grad_tokens_refs[n][:, columns] = total.reshape(rows, COLUMNS).astype(BF16)
 
         def share():
@@ -383,8 +393,6 @@
         for n in range(chunk_count)
         for start in range(0, feature_dim, COLUMNS)
     ]
-    if arrived_directly:
-        arrange(0)
     for step in forward(*units[0]):
         step()
     for i, unit in enumerate(units):
@@ -394,8 +402,6 @@
             others += forward(*units[i + 1])
         if columns.start == 0 and n % samples == 0:
             others += turn(n)
-            if arrived_directly and n // samples + 1 < halves:
-                others.append(functools.partial(arrange, n // samples + 1))
         if i > 0:
             others += backward(*units[i - 1])
         lines = pointwise(*unit)
@@ -404,7 +410,9 @@
             for step in others[line * len(others) // len(lines) : (line + 1) * len(others) // len(lines)]:
                 step()
         if columns.stop == feature_dim:
-            stores[n].start()
+            each = len(stores) // chunk_count
+            for store in stores[n * each : (n + 1) * each]:
+                store.start()
     for step in backward(*units[-1]):
         step()
 
@@ -431,21 +439,21 @@
         store.wait()
 
 
-def mix_blocks(halves, arrived, merged, mix, mix_t, grad, up_through, down_t, level_weight, band_count, reps):
+def mix_blocks(direct, arrived, merged, mix, mix_t, grad, up_through, down_t, level_weight, band_count, reps):
     samples, lat_rows, block_width, feature_dim = grad.shape
-    width = block_width // halves
+    width = block_width
     lanes = arrived[0].shape[-1]
     reach = merged.shape[1]
     rows = WLAT * width
     rank = down_t.shape[0]
-    chunks = lat_rows // WLAT * halves * samples
+    chunks = lat_rows // WLAT * samples
     share_shape = (band_count * reps, rank + rank // FOLDS, feature_dim // reps)
     flops = 2 * samples * lat_rows * block_width * feature_dim * (2 * reach + 2 * rows)
     vmem = pl.BlockSpec(memory_space=pltpu.VMEM)
     any_space = pl.BlockSpec(memory_space=pl.ANY)
     local = [*arrived, merged, mix, mix_t, up_through, down_t]
     return pl.pallas_call(
-        lambda *refs: mix_kernel(refs[: len(arrived)], *refs[len(arrived) :]),
+        lambda *refs: mix_kernel(direct, refs[: len(arrived)], *refs[len(arrived) :]),
         out_shape=[
             jax.ShapeDtypeStruct(grad.shape, BF16),
             jax.ShapeDtypeStruct(share_shape, BF16),
@@ -453,7 +461,6 @@
         in_specs=[vmem] * (len(local) + 2),
         out_specs=[any_space, vmem],
         scratch_shapes=[
-            [pltpu.VMEM((WLAT, width, lanes), BF16)] * halves,
             [pltpu.VMEM((lanes, rows), BF16)] * (chunks // samples),
             [pltpu.VMEM((WLAT, width, feature_dim), BF16)] * chunks,
             [pltpu.VMEM((rows, feature_dim), F32)] * chunks,
@@ -461,7 +468,7 @@
             [pltpu.VMEM((rows, feature_dim), BF16)] * chunks,
             [pltpu.VMEM((rows, feature_dim), BF16)] * chunks,
             pltpu.VMEM((lanes // samples, feature_dim), F32),
-            pltpu.SemaphoreType.DMA((chunks,)),
+            pltpu.SemaphoreType.DMA((chunks * WLAT,)),
         ],
         compiler_params=params(),
         cost_estimate=pl.CostEstimate(
@@ -516,17 +523,15 @@
     row_share = adapter_down.shape[0]
     lat_rows = band_count * row_count
     block_width = col_count // band_count
-    halves = 2 if block_width % (2 * SUB * WLON // 4) == 0 else 1
-    half_width = block_width // halves
-    half_padded = round_up(half_width, SUB)
-    padded_width = halves * half_padded
-    group = 2 * WLON if half_width % (2 * WLON) == 0 else half_padded
+    padded_width = round_up(block_width, SUB)
+    group = 2 * WLON if block_width % (2 * WLON) == 0 else padded_width
     features = samples * levels * channels
 
     pixels = patches.reshape(features, col_count)
     pack_shape = (2, rank, round_up(max(row_share, col_share), LANE))
-    direct = band_count == BANDS and lat_rows == WLAT and half_padded == half_width
-    if direct and features % LANE == 0 and col_count % LANE == 0:
+    direct = band_count == BANDS and lat_rows == WLAT and padded_width == block_width
+    direct = direct and features % LANE == 0 and col_count % LANE == 0
+    if direct:
         blocks, pack = send_blocks(
             pixels, column_block_owner, adapter_up, adapter_down.T, block_width, pack_shape
         )
@@ -551,6 +556,7 @@
     if padded_width != block_width:
         grad = jnp.pad(grad, ((0, 0), (0, 0), (0, padded_width - block_width), (0, 0)))
     merged, up_through, down_t, mix, mix_t, level_copy, grad_copy = prepare(
+        direct,
         variable_group_index,
         frozen_patch_weight,
         factors,
@@ -558,11 +564,11 @@
         window_patch_mixer,
         grad,
         row_share,
-        min(half_width, group),
+        min(block_width, group),
         group,
     )
     mixed, shares = mix_blocks(
-        halves, arrived, merged, mix, mix_t, grad_copy, up_through, down_t, level_copy, band_count, reps
+        direct, arrived, merged, mix, mix_t, grad_copy, up_through, down_t, level_copy, band_count, reps
     )
     if padded_width != block_width:
         mixed = mixed[:, :, :block_width]

time: 51.3 us -> 51.3 us (level)
  no operation moved by 1% of the time
where the time goes in v15:
time: 51.3 us; the launch traced here: 50.9 us
  blocking collectives  21.7 us (42%)
  Pallas kernels  12.3 us (24%)
  starting transfers between devices  12.2 us (24%)
  waiting for transfers between devices  4.08 us (8%)
  between operations  0.66 us (1%)
    all_to_all x1, blocking collectives, sum_shares(): lax.all_to_all(shares, ('band', 'rep'), split_axis=0, concat_axis=0, tile...  16.5 us
    ppermute x7, starting transfers between devices, swap(): lax.ppermute(values, axis, [(source, source ^ distance) for source in ran...  12.2 us
    pallas_call x1, Pallas kernels, mix_blocks(): pl.pallas_call(lambda *refs: mix_kernel(direct, refs[:len(arrived)], *ref...  6.94 us
    all_gather x1, blocking collectives, on_device(): factors = lax.all_gather(pack, 'rep', axis=0, tiled=False)  5.18 us
    ppermute x7, waiting for transfers between devices, swap(): lax.ppermute(values, axis, [(source, source ^ distance) for source in ran...  4.08 us
    pallas_call x1, Pallas kernels, prepare(): pl.pallas_call(functools.partial(prep_kernel, direct, row_share, half_wid...  2.98 us
    pallas_call x1, Pallas kernels, send_blocks(): pl.pallas_call(send_kernel, out_shape=[jax.ShapeDtypeStruct(shape, BF16)...  1.64 us
  transfers between devices with their start and end apart: 7, of which 3 were waited for; matrix products, arithmetic and copies ran while one was open for 0% of the time, Pallas kernels for 6%

profile of v15, /device:TPU:0, one launch (start us, length us, event | category | flops | bytes accessed | tf_op | source)
XLA Modules:
  0.0 50.9 jit_solution(8942256241929801991)
XLA Ops:
  0.6 1.6 %send_blocks.1 = (bf16[96,640]{1,0:T(8,128)(2,1)S(1)}, bf16[96,640]{1,0:T(8,128)(2,1)S(1)}, bf16[96,640]{1,0:T(8,128)(2,1)S(1)}, bf16[96,640]{1,0:T(8,128)(2,1)S...) custom-call(s32[8]{0:T(128)} %owner_hbm_ref.1, ...), custom_call_target="tpu_custom_call" | custom-call | tf_op jit(solution)/shard_map/send_blocks/pallas_call | solution.py:104
  2.3 3.0 %collective-permute-start.1 = (bf16[96,640]{1,0:T(8,128)(2,1)S(1)}, bf16[96,640]{1,0:T(8,128)(2,1)S(1)}, u32[]{:S(2)}, u32[]{:S(2)}) collective-permute-start(bf16[96,640]{1,0:T(8,128)(2,1)S(1)} %get-tuple-element.30), channel_id=1, source_target_pairs={{0,4},{4,0},{8,12},{12,8},{16,20},{20,16},{24,28},{28,24},{1,5},{5... | collective-permute-start | bytes 368648 | tf_op jit(solution)/shard_map/ppermute | solution.py:59
  5.3 1.6 %collective-permute-start.3 = (bf16[96,640]{1,0:T(8,128)(2,1)S(1)}, bf16[96,640]{1,0:T(8,128)(2,1)S(1)}, u32[]{:S(2)}, u32[]{:S(2)}) collective-permute-start(bf16[96,640]{1,0:T(8,128)(2,1)S(1)} %get-tuple-element.34), channel_id=1, source_target_pairs={{0,8},{4,12},{8,0},{12,4},{16,24},{20,28},{24,16},{28,20},{1,9},{5... | collective-permute-start | bytes 368648 | tf_op jit(solution)/shard_map/ppermute | solution.py:59
  6.9 2.6 %collective-permute-start = (bf16[96,640]{1,0:T(8,128)(2,1)S(1)}, bf16[96,640]{1,0:T(8,128)(2,1)S(1)}, u32[]{:S(2)}, u32[]{:S(2)}) collective-permute-start(bf16[96,640]{1,0:T(8,128)(2,1)S(1)} %get-tuple-element.28), channel_id=1, source_target_pairs={{0,16},{4,20},{8,24},{12,28},{16,0},{20,4},{24,8},{28,12},{1,17},{... | collective-permute-start | bytes 368648 | tf_op jit(solution)/shard_map/ppermute | solution.py:59
  9.4 0.3 collective-permute-start.2
  9.8 2.5 %collective-permute-start.4 = (bf16[96,640]{1,0:T(8,128)(2,1)S(1)}, bf16[96,640]{1,0:T(8,128)(2,1)S(1)}, u32[]{:S(2)}, u32[]{:S(2)}) collective-permute-start(bf16[96,640]{1,0:T(8,128)(2,1)S(1)} %get-tuple-element.36), channel_id=1, source_target_pairs={{0,24},{4,28},{8,16},{12,20},{16,8},{20,12},{24,0},{28,4},{1,25},{... | collective-permute-start | bytes 368648 | tf_op jit(solution)/shard_map/ppermute | solution.py:59
  12.2 0.0 collective-permute-done.1.refs_2_
  12.2 2.3 %collective-permute-start.5 = (bf16[96,640]{1,0:T(8,128)(2,1)S(1)}, bf16[96,640]{1,0:T(8,128)(2,1)S(1)}, u32[]{:S(2)}, u32[]{:S(2)}) collective-permute-start(bf16[96,640]{1,0:T(8,128)(2,1)S(1)} %get-tuple-element.37), channel_id=1, source_target_pairs={{0,28},{4,24},{8,20},{12,16},{16,12},{20,8},{24,4},{28,0},{1,29},{... | collective-permute-start | bytes 368648 | tf_op jit(solution)/shard_map/ppermute | solution.py:59
  14.5 0.0 collective-permute-done.3.refs_4_
  14.5 0.0 collective-permute-start.6
  14.5 5.2 %all-gather = bf16[8,16,128]{2,1,0:T(8,128)(2,1)S(1)} all-gather(bf16[2,16,128]{2,1,0:T(8,128)(2,1)S(1)} %get-tuple-element.39), channel_id=2, replica_groups=mesh['band'=8,'rep'=4] {'rep'}, dimensions={0}, use_global_device_ids=true | all-gather | bytes 40960 | tf_op jit(solution)/shard_map/all_gather | solution.py:553
  19.7 3.0 %prepare.1 = (bf16[2,384,512]{2,1,0:T(8,128)(2,1)S(1)}, bf16[4,32,512]{2,1,0:T(8,128)(2,1)S(1)}, bf16[16,80]{1,0:T(8,128)(2,1)S(1)}, bf16[192,192]{1,0:T(8,128)(...) custom-call(s32[5]{0:T(128)} %group_hbm_ref.1, ...), custom_call_target="tpu_custom_call" | custom-call | flops 215482368 | bytes 6291456 | tf_op jit(solution)/shard_map/prepare/pallas_call | solution.py:231
  22.7 1.1 %collective-permute-done.refs_1_ = bf16[96,640]{1,0:T(8,128)(2,1)S(1)} collective-permute-done((bf16[96,640]{1,0:T(8,128)(2,1)S(1)}, bf16[96,640]{1,0:T(8,128)(2,1)S(1)}, u32[]{:S(2)}, u32[]{:S(2)}) %collective-permute-start) | collective-permute-done | bytes 122912 | tf_op jit(solution)/shard_map/ppermute | solution.py:59
  23.8 2.2 %collective-permute-done.2.refs_3_ = bf16[96,640]{1,0:T(8,128)(2,1)S(1)} collective-permute-done((bf16[96,640]{1,0:T(8,128)(2,1)S(1)}, bf16[96,640]{1,0:T(8,128)(2,1)S(1)}, u32[]{:S(2)}, u32[]{:S(2)}) %collective-permute-start.2) | collective-permute-done | bytes 122912 | tf_op jit(solution)/shard_map/ppermute | solution.py:59
  26.0 0.0 collective-permute-done.4.refs_5_
  26.0 0.0 collective-permute-done.5.refs_6_
  26.0 0.8 %collective-permute-done.6.refs_7_ = bf16[96,640]{1,0:T(8,128)(2,1)S(1)} collective-permute-done((bf16[96,640]{1,0:T(8,128)(2,1)S(1)}, bf16[96,640]{1,0:T(8,128)(2,1)S(1)}, u32[]{:S(2)}, u32[]{:S(2)}) %collective-permute-start.6) | collective-permute-done | bytes 122912 | tf_op jit(solution)/shard_map/ppermute | solution.py:59
  26.8 6.9 %mix_blocks.1 = (bf16[2,8,96,512]{3,2,1,0:T(8,128)(2,1)}, bf16[32,24,128]{2,1,0:T(8,128)(2,1)S(1)}) custom-call(bf16[96,640]{1,0:T(8,128)(2,1)S(1)} %get-tuple-element.27.refs_0_, bf16[96,640]{1,0:T(8,128)(2,1)S(1)} %collective-permute-done.refs_1_, bf16[96,640]{1,0:T(8,128)(2,1)S(1)} %collective-permute-done.1.refs_2_, ...), custom_call_target="tpu_custom_call" | custom-call | flops 3623878656 | bytes 12582912 | tf_op jit(solution)/shard_map/mix_blocks/pallas_call | solution.py:455
  33.7 16.5 %all_to_all.5.parts_ref = bf16[32,24,128]{2,1,0:T(8,128)(2,1)S(1)} all-to-all(bf16[32,24,128]{2,1,0:T(8,128)(2,1)S(1)} %get-tuple-element.48), channel_id=1, replica_groups=mesh['band'=8,'rep'=4] {'band','rep'}, dimensions={0} | all-to-all | bytes 393216 | tf_op jit(solution)/shard_map/all_to_all | solution.py:496
  50.2 0.7 %sum_shares.1 = (f32[16,20]{1,0:T(8,128)}, f32[16,128]{1,0:T(8,128)}) custom-call(bf16[32,24,128]{2,1,0:T(8,128)(2,1)S(1)} %all_to_all.5.parts_ref), custom_call_target="tpu_custom_call" | custom-call | tf_op jit(solution)/shard_map/sum_shares/pallas_call | solution.py:497
Async XLA Ops:
  2.3 10.0 %collective-permute-start.1 = (bf16[96,640]{1,0:T(8,128)(2,1)S(1)}, bf16[96,640]{1,0:T(8,128)(2,1)S(1)}, u32[]{:S(2)}, u32[]{:S(2)}) collective-permute-start(bf16[96,640]{1,0:T(8,128)(2,1)S(1)} %get-tuple-element.30), channel_id=1, source_target_pairs={{0,4},{4,0},{8,12},{12,8},{16,20},{20,16},{24,28},{28,24},{1,5},{5... | collective-permute-start | bytes 368648 | tf_op jit(solution)/shard_map/ppermute | solution.py:59
  5.3 9.2 %collective-permute-start.3 = (bf16[96,640]{1,0:T(8,128)(2,1)S(1)}, bf16[96,640]{1,0:T(8,128)(2,1)S(1)}, u32[]{:S(2)}, u32[]{:S(2)}) collective-permute-start(bf16[96,640]{1,0:T(8,128)(2,1)S(1)} %get-tuple-element.34), channel_id=1, source_target_pairs={{0,8},{4,12},{8,0},{12,4},{16,24},{20,28},{24,16},{28,20},{1,9},{5... | collective-permute-start | bytes 368648 | tf_op jit(solution)/shard_map/ppermute | solution.py:59
  6.9 16.9 %collective-permute-start = (bf16[96,640]{1,0:T(8,128)(2,1)S(1)}, bf16[96,640]{1,0:T(8,128)(2,1)S(1)}, u32[]{:S(2)}, u32[]{:S(2)}) collective-permute-start(bf16[96,640]{1,0:T(8,128)(2,1)S(1)} %get-tuple-element.28), channel_id=1, source_target_pairs={{0,16},{4,20},{8,24},{12,28},{16,0},{20,4},{24,8},{28,12},{1,17},{... | collective-permute-start | bytes 368648 | tf_op jit(solution)/shard_map/ppermute | solution.py:59
  9.4 16.5 %collective-permute-start.2 = (bf16[96,640]{1,0:T(8,128)(2,1)S(1)}, bf16[96,640]{1,0:T(8,128)(2,1)S(1)}, u32[]{:S(2)}, u32[]{:S(2)}) collective-permute-start(bf16[96,640]{1,0:T(8,128)(2,1)S(1)} %get-tuple-element.32), channel_id=1, source_target_pairs={{0,20},{4,16},{8,28},{12,24},{16,4},{20,0},{24,12},{28,8},{1,21},{... | collective-permute-start | bytes 368648 | tf_op jit(solution)/shard_map/ppermute | solution.py:59
  9.8 16.2 %collective-permute-start.4 = (bf16[96,640]{1,0:T(8,128)(2,1)S(1)}, bf16[96,640]{1,0:T(8,128)(2,1)S(1)}, u32[]{:S(2)}, u32[]{:S(2)}) collective-permute-start(bf16[96,640]{1,0:T(8,128)(2,1)S(1)} %get-tuple-element.36), channel_id=1, source_target_pairs={{0,24},{4,28},{8,16},{12,20},{16,8},{20,12},{24,0},{28,4},{1,25},{... | collective-permute-start | bytes 368648 | tf_op jit(solution)/shard_map/ppermute | solution.py:59
  12.2 13.8 %collective-permute-start.5 = (bf16[96,640]{1,0:T(8,128)(2,1)S(1)}, bf16[96,640]{1,0:T(8,128)(2,1)S(1)}, u32[]{:S(2)}, u32[]{:S(2)}) collective-permute-start(bf16[96,640]{1,0:T(8,128)(2,1)S(1)} %get-tuple-element.37), channel_id=1, source_target_pairs={{0,28},{4,24},{8,20},{12,16},{16,12},{20,8},{24,4},{28,0},{1,29},{... | collective-permute-start | bytes 368648 | tf_op jit(solution)/shard_map/ppermute | solution.py:59
  14.5 12.2 %collective-permute-start.6 = (bf16[96,640]{1,0:T(8,128)(2,1)S(1)}, bf16[96,640]{1,0:T(8,128)(2,1)S(1)}, u32[]{:S(2)}, u32[]{:S(2)}) collective-permute-start(bf16[96,640]{1,0:T(8,128)(2,1)S(1)} %get-tuple-element.38), channel_id=1, source_target_pairs={{0,12},{4,8},{8,4},{12,0},{16,28},{20,24},{24,20},{28,16},{1,13},{... | collective-permute-start | bytes 368648 | tf_op jit(solution)/shard_map/ppermute | solution.py:59

commit v16 on v15

--- a/solution.py
+++ b/solution.py
@@ -14,6 +14,7 @@
 VMEM_LIMIT = 24 * 1024 * 1024
 BANDS = 8
 ORDER = (0, 4, 1, 5, 2, 6, 7, 3)
+EARLY = 6
 FOLDS = 2
 COLUMNS = 256
 BF16 = jnp.bfloat16
@@ -128,7 +129,7 @@
     for distance, before in zip(ORDER[-2:], (1, 2)):
         block, arrived[before] = lax.optimization_barrier((arrived[distance], arrived[before]))
         arrived[distance] = swap(block, "band", distance)
-    return [arrived[distance] for distance in ORDER]
+    return [arrived[distance] for distance in range(BANDS)]
 
 
 def expand_table(table, rows, half_width_padded, half_width, flip, transpose):
@@ -262,6 +263,53 @@
     return first, second[:rank] + second[rank:]
 
 
+def turned_whole(lines, width):
+    return lines * width // LANE * LANE
+
+
+def embed_kernel(*refs):
+    piece_refs, (merged_ref, tokens_ref, turned_ref) = refs[:-3], refs[-3:]
+    samples, reach, feature_dim = merged_ref.shape
+    width, features = piece_refs[0].shape
+    depth = features // samples
+    group = 2 * WLON
+    rows = len(piece_refs) * group
+    positions = turned_ref.shape[1]
+    for s in range(samples):
+        lane = s * depth // LANE * LANE
+        pixels = jnp.concatenate([piece_ref[:, lane : lane + reach] for piece_ref in piece_refs], axis=0)
+        for start in range(0, feature_dim, COLUMNS):
+            columns = slice(start, start + COLUMNS)
+            tokens = dot_nn(pixels, merged_ref[s, :, columns]).reshape(len(piece_refs), width, COLUMNS)
+            for n in range(width // group):
+                part = tokens[:, n * group : (n + 1) * group].reshape(rows, COLUMNS)
+                tokens_ref[s, n * rows : (n + 1) * rows, columns] = part.astype(BF16)
+    for start in range(0, features, LANE):
+        lanes = slice(start, start + LANE)
+        pixels = jnp.concatenate([piece_ref[:, lanes] for piece_ref in piece_refs], axis=0)
+        turned_ref[lanes, :] = pixels[:positions].T
+
+
+def embed_early(pieces, merged):
+    samples, _, feature_dim = merged.shape
+    width, features = pieces[0].shape
+    count = len(pieces) * width
+    return pl.pallas_call(
+        embed_kernel,
+        out_shape=[
+            jax.ShapeDtypeStruct((samples, count, feature_dim), BF16),
+            jax.ShapeDtypeStruct((features, turned_whole(len(pieces), width)), BF16),
+        ],
+        in_specs=[pl.BlockSpec(memory_space=pltpu.VMEM)] * (len(pieces) + 1),
+        out_specs=[pl.BlockSpec(memory_space=pltpu.VMEM)] * 2,
+        compiler_params=params(),
+        cost_estimate=pl.CostEstimate(
+            flops=2 * count * features * feature_dim, bytes_accessed=4 * 2**20, transcendentals=0
+        ),
+        name="embed_early",
+    )(*pieces, merged)
+
+
 def mix_kernel(
     direct,
     piece_refs,
@@ -296,6 +344,12 @@
     ]
     pair = 1 if group % SUB == 0 else 2
 
+    early = EARLY if direct else 0
+    early_rows, late_rows = early * group, (WLAT - early) * group
+    if direct:
+        *line_refs, early_tokens_ref, early_turned_ref = piece_refs
+        early_positions = early_turned_ref.shape[1]
+
     def lines_of(n):
         return pl.ds(n // samples * WLAT, WLAT)
 
@@ -316,16 +370,25 @@
 
     def pixels_of(n, lanes):
         if direct:
-            by_distance = dict(zip(ORDER, piece_refs))
-            return jnp.concatenate([by_distance[line][:, lanes] for line in range(WLAT)], axis=0)
+            return jnp.concatenate([line_ref[:, lanes] for line_ref in line_refs], axis=0)
         return piece_refs[0][lines_of(n), :, lanes].reshape(rows, lanes.stop - lanes.start)
 
     def turn(n):
         def part(lanes):
-            turned_refs[n // samples][lanes, :] = pixels_of(n, lanes).T
+            pixels = pixels_of(n, lanes)
+            if direct:
+                before = early_positions - (early - 1) * width
+                pixels = pixels[before:]
+            turned_refs[n // samples][lanes, :] = pixels.T
 
         starts = range(0, samples * depth, LANE)
         return [functools.partial(part, slice(start, start + LANE)) for start in starts]
+
+    def tokens_at(n, block, line, count, columns):
+        if line < early:
+            at = pl.ds(block * early_rows + line * group, count * group)
+            return early_tokens_ref[n % samples, at, columns]
+        return tokens_refs[n][pl.ds(block * late_rows + (line - early) * group, count * group), columns]
 
     def forward(n, columns):
         s = n % samples
@@ -333,13 +396,19 @@
 
         def embed():
             pixels = pixels_of(n, slice(lane, lane + reach))
-            tokens = dot_nn(pixels, merged_ref[s, :, columns]).reshape(WLAT, width, COLUMNS)
-            for within, at in groups:
-                tokens_refs[n][at, columns] = tokens[:, within].reshape(group_rows, COLUMNS).astype(BF16)
+            if direct:
+                pixels = pixels[width:]
+            tokens = dot_nn(pixels, merged_ref[s, :, columns]).reshape(WLAT - early, width, COLUMNS)
+            for block, (within, _) in enumerate(groups):
+                part = tokens[:, within].reshape(late_rows, COLUMNS).astype(BF16)
+                tokens_refs[n][block * late_rows : (block + 1) * late_rows, columns] = part
 
         def mixing():
-            for _, at in groups:
-                pre_refs[n][at, columns] = dot_nn(mix_ref[...], tokens_refs[n][at, columns])
+            for block, (_, at) in enumerate(groups):
+                tokens = tokens_at(n, block, early, WLAT - early, columns)
+                if direct:
+                    tokens = jnp.concatenate([tokens_at(n, block, 0, early, columns), tokens], axis=0)
+                pre_refs[n][at, columns] = dot_nn(mix_ref[...], tokens)
 
         return [embed, mixing]
 
@@ -349,13 +418,13 @@
         def part(line, across, lanes):
             grads = [grad_ref[s, first_line + line + k, across, lanes].astype(F32) for k in range(pair)]
             mixed = []
-            for within, at in groups:
+            for block, (within, at) in enumerate(groups):
                 if within.start < across.start or within.stop > across.stop:
                     continue
                 at = pl.ds(at.start + line * group, pair * group)
                 pre = pre_refs[n][at, lanes]
                 cdf, pdf = normal_parts(pre)
-                mixed.append(tokens_refs[n][at, lanes].astype(F32) + pre * cdf)
+                mixed.append(tokens_at(n, block, line, pair, lanes).astype(F32) + pre * cdf)
                 first = within.start - across.start
                 grad = jnp.concatenate([values[first : first + group] for values in grads], axis=0)
                 grad_pre_refs[n][at, lanes] = (grad * (cdf + pre * pdf)).astype(BF16)
@@ -382,8 +451,11 @@
 
         def share():
             s = n % samples
-            turned = turned_refs[n // samples][s * depth : (s + 1) * depth, :]
-            part = dot_nn(turned, grad_tokens_refs[n][:, columns])
+            features = slice(s * depth, (s + 1) * depth)
+            late = rows - turned_refs[0].shape[1]
+            part = dot_nn(turned_refs[n // samples][features, :], grad_tokens_refs[n][late:, columns])
+            if direct:
+                part = part + dot_nn(early_turned_ref[features, :], grad_tokens_refs[n][:late, columns])
             total_ref[:, columns] = part if n == 0 else total_ref[:, columns] + part
 
         return [spread, share]
@@ -443,6 +515,8 @@
     samples, lat_rows, block_width, feature_dim = grad.shape
     width = block_width
     lanes = arrived[0].shape[-1]
+    early = EARLY if direct else 0
+    turned_early = turned_whole(early, width)
     reach = merged.shape[1]
     rows = WLAT * width
     rank = down_t.shape[0]
@@ -461,10 +535,10 @@
         in_specs=[vmem] * (len(local) + 2),
         out_specs=[any_space, vmem],
         scratch_shapes=[
-            [pltpu.VMEM((lanes, rows), BF16)] * (chunks // samples),
+            [pltpu.VMEM((lanes, rows - turned_early), BF16)] * (chunks // samples),
             [pltpu.VMEM((WLAT, width, feature_dim), BF16)] * chunks,
             [pltpu.VMEM((rows, feature_dim), F32)] * chunks,
-            [pltpu.VMEM((rows, feature_dim), BF16)] * chunks,
+            [pltpu.VMEM((rows - early * width, feature_dim), BF16)] * chunks,
             [pltpu.VMEM((rows, feature_dim), BF16)] * chunks,
             [pltpu.VMEM((rows, feature_dim), BF16)] * chunks,
             pltpu.VMEM((lanes // samples, feature_dim), F32),
@@ -567,6 +641,8 @@
         min(block_width, group),
         group,
     )
+    if direct:
+        arrived = [*arrived[EARLY - 1 :], *embed_early(arrived[:EARLY], merged)]
     mixed, shares = mix_blocks(
         direct, arrived, merged, mix, mix_t, grad_copy, up_through, down_t, level_copy, band_count, reps
     )

time: 51.3 us -> 50.3 us (0.981)
  waiting for transfers between devices: 4.08 us -> 3.06 us
  starting transfers between devices: 12.2 us -> 12.9 us
    ppermute x7, waiting for transfers between devices: 4.08 us -> 3.06 us  [swap(): lax.ppermute(values, axis, [(source, source ^ distance) for source in ran...]
    pallas_call x1, Pallas kernels: 6.94 us -> 5.99 us  [mix_blocks(): pl.pallas_call(lambda *refs: mix_kernel(direct, refs[:len(arrived)], *ref...]
    pallas_call x0 -> x1, Pallas kernels: none -> 0.78 us  [embed_early(): pl.pallas_call(embed_kernel, out_shape=[jax.ShapeDtypeStruct((samples, co...]
    ppermute x7, starting transfers between devices: 12.2 us -> 12.9 us  [swap(): lax.ppermute(values, axis, [(source, source ^ distance) for source in ran...]
  transfers between devices with their start and end apart: 7 -> 7, of which waited for: 3 -> 1; matrix products, arithmetic and copies ran while one was open for 0% -> 0% of each run, Pallas kernels for 6% -> 8%
where the time goes in v16:
time: 50.3 us; the launch traced here: 50 us
  blocking collectives  21.2 us (42%)
  starting transfers between devices  12.9 us (26%)
  Pallas kernels  12.1 us (24%)
  waiting for transfers between devices  3.06 us (6%)
  between operations  0.69 us (1%)
    all_to_all x1, blocking collectives, sum_shares(): lax.all_to_all(shares, ('band', 'rep'), split_axis=0, concat_axis=0, tile...  16.1 us
    ppermute x7, starting transfers between devices, swap(): lax.ppermute(values, axis, [(source, source ^ distance) for source in ran...  12.9 us
    pallas_call x1, Pallas kernels, mix_blocks(): pl.pallas_call(lambda *refs: mix_kernel(direct, refs[:len(arrived)], *ref...  5.99 us
    all_gather x1, blocking collectives, on_device(): factors = lax.all_gather(pack, 'rep', axis=0, tiled=False)  5.18 us
    ppermute x7, waiting for transfers between devices, swap(): lax.ppermute(values, axis, [(source, source ^ distance) for source in ran...  3.06 us
    pallas_call x1, Pallas kernels, prepare(): pl.pallas_call(functools.partial(prep_kernel, direct, row_share, half_wid...  2.98 us
    pallas_call x1, Pallas kernels, send_blocks(): pl.pallas_call(send_kernel, out_shape=[jax.ShapeDtypeStruct(shape, BF16)...  1.64 us
  transfers between devices with their start and end apart: 7, of which 1 were waited for; matrix products, arithmetic and copies ran while one was open for 0% of the time, Pallas kernels for 8%

profile of v16, /device:TPU:0, one launch (start us, length us, event | category | flops | bytes accessed | tf_op | source)
XLA Modules:
  0.0 50.0 jit_solution(10182619558497044926)
XLA Ops:
  0.6 1.6 %send_blocks.1 = (bf16[96,640]{1,0:T(8,128)(2,1)S(1)}, bf16[96,640]{1,0:T(8,128)(2,1)S(1)}, bf16[96,640]{1,0:T(8,128)(2,1)S(1)}, bf16[96,640]{1,0:T(8,128)(2,1)S...) custom-call(s32[8]{0:T(128)} %owner_hbm_ref.1, ...), custom_call_target="tpu_custom_call" | custom-call | tf_op jit(solution)/shard_map/send_blocks/pallas_call | solution.py:105
  2.3 3.1 %collective-permute-start.4 = (bf16[96,640]{1,0:T(8,128)(2,1)S(1)}, bf16[96,640]{1,0:T(8,128)(2,1)S(1)}, u32[]{:S(2)}, u32[]{:S(2)}) collective-permute-start(bf16[96,640]{1,0:T(8,128)(2,1)S(1)} %get-tuple-element.37), channel_id=1, source_target_pairs={{0,8},{4,12},{8,0},{12,4},{16,24},{20,28},{24,16},{28,20},{1,9},{5... | collective-permute-start | bytes 368648 | tf_op jit(solution)/shard_map/ppermute | solution.py:60
  5.4 1.5 %collective-permute-start.2 = (bf16[96,640]{1,0:T(8,128)(2,1)S(1)}, bf16[96,640]{1,0:T(8,128)(2,1)S(1)}, u32[]{:S(2)}, u32[]{:S(2)}) collective-permute-start(bf16[96,640]{1,0:T(8,128)(2,1)S(1)} %get-tuple-element.32), channel_id=1, source_target_pairs={{0,4},{4,0},{8,12},{12,8},{16,20},{20,16},{24,28},{28,24},{1,5},{5... | collective-permute-start | bytes 368648 | tf_op jit(solution)/shard_map/ppermute | solution.py:60
  6.9 2.6 %collective-permute-start = (bf16[96,640]{1,0:T(8,128)(2,1)S(1)}, bf16[96,640]{1,0:T(8,128)(2,1)S(1)}, u32[]{:S(2)}, u32[]{:S(2)}) collective-permute-start(bf16[96,640]{1,0:T(8,128)(2,1)S(1)} %get-tuple-element.29), channel_id=1, source_target_pairs={{0,20},{4,16},{8,28},{12,24},{16,4},{20,0},{24,12},{28,8},{1,21},{... | collective-permute-start | bytes 368648 | tf_op jit(solution)/shard_map/ppermute | solution.py:60
  9.4 0.3 collective-permute-start.6
  9.8 0.0 collective-permute-done.4.refs_2_
  9.8 1.6 %collective-permute-start.5 = (bf16[96,640]{1,0:T(8,128)(2,1)S(1)}, bf16[96,640]{1,0:T(8,128)(2,1)S(1)}, u32[]{:S(2)}, u32[]{:S(2)}) collective-permute-start(bf16[96,640]{1,0:T(8,128)(2,1)S(1)} %get-tuple-element.39), channel_id=1, source_target_pairs={{0,12},{4,8},{8,4},{12,0},{16,28},{20,24},{24,20},{28,16},{1,13},{... | collective-permute-start | bytes 368648 | tf_op jit(solution)/shard_map/ppermute | solution.py:60
  11.4 3.6 %collective-permute-start.1 = (bf16[96,640]{1,0:T(8,128)(2,1)S(1)}, bf16[96,640]{1,0:T(8,128)(2,1)S(1)}, u32[]{:S(2)}, u32[]{:S(2)}) collective-permute-start(bf16[96,640]{1,0:T(8,128)(2,1)S(1)} %get-tuple-element.30), channel_id=1, source_target_pairs={{0,24},{4,28},{8,16},{12,20},{16,8},{20,12},{24,0},{28,4},{1,25},{... | collective-permute-start | bytes 368648 | tf_op jit(solution)/shard_map/ppermute | solution.py:60
  15.0 0.0 collective-permute-done.2.refs_1_
  15.0 0.2 collective-permute-start.3
  15.2 5.2 %all-gather = bf16[8,16,128]{2,1,0:T(8,128)(2,1)S(1)} all-gather(bf16[2,16,128]{2,1,0:T(8,128)(2,1)S(1)} %get-tuple-element.41), channel_id=2, replica_groups=mesh['band'=8,'rep'=4] {'rep'}, dimensions={0}, use_global_device_ids=true | all-gather | bytes 40960 | tf_op jit(solution)/shard_map/all_gather | solution.py:627
  20.3 3.0 %prepare.1 = (bf16[2,384,512]{2,1,0:T(8,128)(2,1)S(1)}, bf16[4,32,512]{2,1,0:T(8,128)(2,1)S(1)}, bf16[16,80]{1,0:T(8,128)(2,1)S(1)}, bf16[192,192]{1,0:T(8,128)(...) custom-call(s32[5]{0:T(128)} %group_hbm_ref.1, ...), custom_call_target="tpu_custom_call" | custom-call | flops 215482368 | bytes 6291456 | tf_op jit(solution)/shard_map/prepare/pallas_call | solution.py:232
  23.3 0.0 collective-permute-done.refs_5_.refs_0_
  23.3 3.0 %collective-permute-done.6.refs_4_ = bf16[96,640]{1,0:T(8,128)(2,1)S(1)} collective-permute-done((bf16[96,640]{1,0:T(8,128)(2,1)S(1)}, bf16[96,640]{1,0:T(8,128)(2,1)S(1)}, u32[]{:S(2)}, u32[]{:S(2)}) %collective-permute-start.6) | collective-permute-done | bytes 122912 | tf_op jit(solution)/shard_map/ppermute | solution.py:60
  26.4 0.0 collective-permute-done.5.refs_3_
  26.4 0.8 %embed_early.1 = (bf16[2,576,512]{2,1,0:T(8,128)(2,1)S(1)}, bf16[640,512]{1,0:T(8,128)(2,1)S(1)}) custom-call(bf16[96,640]{1,0:T(8,128)(2,1)S(1)} %get-tuple-element.34.refs_0_, bf16[96,640]{1,0:T(8,128)(2,1)S(1)} %collective-permute-done.2.refs_1_, bf16[96,640]{1,0:T(8,128)(2,1)S(1)} %collective-permute-done.4.refs_2_, ...), custom_call_target="tpu_custom_call" | custom-call | flops 377487360 | bytes 4194304 | tf_op jit(solution)/shard_map/embed_early/pallas_call | solution.py:297
  27.2 0.0 collective-permute-done.1.refs_1_
  27.2 0.0 collective-permute-done.3.refs_2_
  27.2 6.0 %mix_blocks.1 = (bf16[2,8,96,512]{3,2,1,0:T(8,128)(2,1)}, bf16[32,24,128]{2,1,0:T(8,128)(2,1)S(1)}) custom-call(bf16[96,640]{1,0:T(8,128)(2,1)S(1)} %collective-permute-done.refs_5_.refs_0_, bf16[96,640]{1,0:T(8,128)(2,1)S(1)} %collective-permute-done.1.refs_1_, bf16[96,640]{1,0:T(8,128)(2,1)S(1)} %collective-permute-done.3.refs_2_, ...), custom_call_target="tpu_custom_call" | custom-call | flops 3623878656 | bytes 12582912 | tf_op jit(solution)/shard_map/mix_blocks/pallas_call | solution.py:529
  33.2 16.1 %all_to_all.5.parts_ref = bf16[32,24,128]{2,1,0:T(8,128)(2,1)S(1)} all-to-all(bf16[32,24,128]{2,1,0:T(8,128)(2,1)S(1)} %get-tuple-element.52), channel_id=1, replica_groups=mesh['band'=8,'rep'=4] {'band','rep'}, dimensions={0} | all-to-all | bytes 393216 | tf_op jit(solution)/shard_map/all_to_all | solution.py:570
  49.2 0.7 %sum_shares.1 = (f32[16,20]{1,0:T(8,128)}, f32[16,128]{1,0:T(8,128)}) custom-call(bf16[32,24,128]{2,1,0:T(8,128)(2,1)S(1)} %all_to_all.5.parts_ref), custom_call_target="tpu_custom_call" | custom-call | tf_op jit(solution)/shard_map/sum_shares/pallas_call | solution.py:571
Async XLA Ops:
  2.3 7.5 %collective-permute-start.4 = (bf16[96,640]{1,0:T(8,128)(2,1)S(1)}, bf16[96,640]{1,0:T(8,128)(2,1)S(1)}, u32[]{:S(2)}, u32[]{:S(2)}) collective-permute-start(bf16[96,640]{1,0:T(8,128)(2,1)S(1)} %get-tuple-element.37), channel_id=1, source_target_pairs={{0,8},{4,12},{8,0},{12,4},{16,24},{20,28},{24,16},{28,20},{1,9},{5... | collective-permute-start | bytes 368648 | tf_op jit(solution)/shard_map/ppermute | solution.py:60
  5.4 9.6 %collective-permute-start.2 = (bf16[96,640]{1,0:T(8,128)(2,1)S(1)}, bf16[96,640]{1,0:T(8,128)(2,1)S(1)}, u32[]{:S(2)}, u32[]{:S(2)}) collective-permute-start(bf16[96,640]{1,0:T(8,128)(2,1)S(1)} %get-tuple-element.32), channel_id=1, source_target_pairs={{0,4},{4,0},{8,12},{12,8},{16,20},{20,16},{24,28},{28,24},{1,5},{5... | collective-permute-start | bytes 368648 | tf_op jit(solution)/shard_map/ppermute | solution.py:60
  6.9 16.5 %collective-permute-start = (bf16[96,640]{1,0:T(8,128)(2,1)S(1)}, bf16[96,640]{1,0:T(8,128)(2,1)S(1)}, u32[]{:S(2)}, u32[]{:S(2)}) collective-permute-start(bf16[96,640]{1,0:T(8,128)(2,1)S(1)} %get-tuple-element.29), channel_id=1, source_target_pairs={{0,20},{4,16},{8,28},{12,24},{16,4},{20,0},{24,12},{28,8},{1,21},{... | collective-permute-start | bytes 368648 | tf_op jit(solution)/shard_map/ppermute | solution.py:60
  9.4 17.0 %collective-permute-start.6 = (bf16[96,640]{1,0:T(8,128)(2,1)S(1)}, bf16[96,640]{1,0:T(8,128)(2,1)S(1)}, u32[]{:S(2)}, u32[]{:S(2)}) collective-permute-start(bf16[96,640]{1,0:T(8,128)(2,1)S(1)} %get-tuple-element.40), channel_id=1, source_target_pairs={{0,16},{4,20},{8,24},{12,28},{16,0},{20,4},{24,8},{28,12},{1,17},{... | collective-permute-start | bytes 368648 | tf_op jit(solution)/shard_map/ppermute | solution.py:60
  9.8 16.6 %collective-permute-start.5 = (bf16[96,640]{1,0:T(8,128)(2,1)S(1)}, bf16[96,640]{1,0:T(8,128)(2,1)S(1)}, u32[]{:S(2)}, u32[]{:S(2)}) collective-permute-start(bf16[96,640]{1,0:T(8,128)(2,1)S(1)} %get-tuple-element.39), channel_id=1, source_target_pairs={{0,12},{4,8},{8,4},{12,0},{16,28},{20,24},{24,20},{28,16},{1,13},{... | collective-permute-start | bytes 368648 | tf_op jit(solution)/shard_map/ppermute | solution.py:60
  11.4 15.8 %collective-permute-start.1 = (bf16[96,640]{1,0:T(8,128)(2,1)S(1)}, bf16[96,640]{1,0:T(8,128)(2,1)S(1)}, u32[]{:S(2)}, u32[]{:S(2)}) collective-permute-start(bf16[96,640]{1,0:T(8,128)(2,1)S(1)} %get-tuple-element.30), channel_id=1, source_target_pairs={{0,24},{4,28},{8,16},{12,20},{16,8},{20,12},{24,0},{28,4},{1,25},{... | collective-permute-start | bytes 368648 | tf_op jit(solution)/shard_map/ppermute | solution.py:60
  15.0 12.2 %collective-permute-start.3 = (bf16[96,640]{1,0:T(8,128)(2,1)S(1)}, bf16[96,640]{1,0:T(8,128)(2,1)S(1)}, u32[]{:S(2)}, u32[]{:S(2)}) collective-permute-start(bf16[96,640]{1,0:T(8,128)(2,1)S(1)} %get-tuple-element.33), channel_id=1, source_target_pairs={{0,28},{4,24},{8,20},{12,16},{16,12},{20,8},{24,4},{28,0},{1,29},{... | collective-permute-start | bytes 368648 | tf_op jit(solution)/shard_map/ppermute | solution.py:60

commit v17 on v16

--- a/solution.py
+++ b/solution.py
@@ -15,6 +15,7 @@
 BANDS = 8
 ORDER = (0, 4, 1, 5, 2, 6, 7, 3)
 EARLY = 6
+SLOTS = (0, 1, 4, 5, 6, 2, 3, 7)
 FOLDS = 2
 COLUMNS = 256
 BF16 = jnp.bfloat16
@@ -122,19 +123,25 @@
     return blocks, pack
 
 
-def exchange(blocks):
+def exchange(blocks, pack):
     arrived = dict(zip(ORDER, blocks))
-    for distance in ORDER[1:-2]:
+    for distance in (1, 4, 5, 6, 2):
         arrived[distance] = swap(arrived[distance], "band", distance)
-    for distance, before in zip(ORDER[-2:], (1, 2)):
-        block, arrived[before] = lax.optimization_barrier((arrived[distance], arrived[before]))
-        arrived[distance] = swap(block, "band", distance)
-    return [arrived[distance] for distance in range(BANDS)]
+    arrived[1], pack = lax.optimization_barrier((arrived[1], pack))
+    factors = lax.all_gather(pack, "rep", axis=0, tiled=False)
+    arrived[7], factors = lax.optimization_barrier((arrived[7], factors))
+    arrived[7] = swap(arrived[7], "band", 7)
+    arrived[3], factors = lax.optimization_barrier((arrived[3], factors))
+    arrived[3] = swap(arrived[3], "band", 3)
+    return [arrived[distance] for distance in SLOTS], factors
 
 
 def expand_table(table, rows, half_width_padded, half_width, flip, transpose):
     position = iota2((rows, WLAT * WLON), 0)
-    line, col = jnp.bitwise_xor(position // half_width_padded, flip), position % half_width_padded
+    line, col = position // half_width_padded, position % half_width_padded
+    if flip is not None:
+        distance = sum(jnp.where(line == slot, far, 0) for slot, far in enumerate(SLOTS))
+        line = jnp.bitwise_xor(distance, flip)
     target = iota2((rows, WLAT * WLON), 1)
     pick = jnp.where((target == line * WLON + col % WLON) & (col < half_width), 1.0, 0.0).astype(BF16)
     left = (dot_nt if transpose else dot_nn)(pick, table).astype(BF16)
@@ -166,10 +173,11 @@
     sems,
 ):
     pairs = [(group_hbm_ref, group_ref), (level_hbm_ref, level_ref)]
-    flip = lax.axis_index("band") if direct else 0
+    flip = lax.axis_index("band") if direct else None
     if direct:
         pairs += [
-            (grad_hbm_ref.at[:, jnp.bitwise_xor(flip, line)], grad_ref.at[:, line]) for line in range(WLAT)
+            (grad_hbm_ref.at[:, jnp.bitwise_xor(flip, far)], grad_ref.at[:, slot])
+            for slot, far in enumerate(SLOTS)
         ]
     else:
         pairs.append((grad_hbm_ref, grad_ref))
@@ -333,7 +341,7 @@
 ):
     samples, reach, feature_dim = merged_ref.shape
     chunk_count, (_, width, _) = len(mixed_refs), mixed_refs[0].shape
-    depth = piece_refs[0].shape[-1] // samples
+    depth = piece_refs[-1].shape[-1] // samples
     rows = WLAT * width
 
     group_rows = mix_ref.shape[0]
@@ -347,7 +355,7 @@
     early = EARLY if direct else 0
     early_rows, late_rows = early * group, (WLAT - early) * group
     if direct:
-        *line_refs, early_tokens_ref, early_turned_ref = piece_refs
+        early_tokens_ref, early_turned_ref, *line_refs = piece_refs
         early_positions = early_turned_ref.shape[1]
 
     def lines_of(n):
@@ -356,9 +364,9 @@
     if direct:
         me = lax.axis_index("band")
         targets = [
-            (mixed_refs[n].at[line], mixed_hbm_ref.at[n, jnp.bitwise_xor(me, line)])
+            (mixed_refs[n].at[slot], mixed_hbm_ref.at[n, jnp.bitwise_xor(me, far)])
             for n in range(chunk_count)
-            for line in range(WLAT)
+            for slot, far in enumerate(SLOTS)
         ]
     else:
         targets = [
@@ -514,7 +522,7 @@
 def mix_blocks(direct, arrived, merged, mix, mix_t, grad, up_through, down_t, level_weight, band_count, reps):
     samples, lat_rows, block_width, feature_dim = grad.shape
     width = block_width
-    lanes = arrived[0].shape[-1]
+    lanes = arrived[-1].shape[-1]
     early = EARLY if direct else 0
     turned_early = turned_whole(early, width)
     reach = merged.shape[1]
@@ -609,7 +617,7 @@
         blocks, pack = send_blocks(
             pixels, column_block_owner, adapter_up, adapter_down.T, block_width, pack_shape
         )
-        arrived = exchange(blocks)
+        arrived, factors = exchange(blocks, pack)
     else:
         block_ids = jnp.arange(band_count, dtype=jnp.int32)
         inverse = jnp.sum(
@@ -624,7 +632,7 @@
                 for array in (adapter_up, adapter_down.T)
             ]
         )
-    factors = lax.all_gather(pack, "rep", axis=0, tiled=False)
+        factors = lax.all_gather(pack, "rep", axis=0, tiled=False)
 
     grad = mixed_token_gradient.reshape(samples, lat_rows, block_width, feature_dim)
     if padded_width != block_width:
@@ -642,7 +650,7 @@
         group,
     )
     if direct:
-        arrived = [*arrived[EARLY - 1 :], *embed_early(arrived[:EARLY], merged)]
+        arrived = [*embed_early(arrived[:EARLY], merged), *arrived[EARLY - 1 :]]
     mixed, shares = mix_blocks(
         direct, arrived, merged, mix, mix_t, grad_copy, up_through, down_t, level_copy, band_count, reps
     )

time: 50.3 us -> 50 us (level)
  starting transfers between devices: 12.9 us -> 14.8 us
  waiting for transfers between devices: 3.06 us -> 1.88 us
  blocking collectives: 21.2 us -> 20.1 us
    ppermute x7, starting transfers between devices: 12.9 us -> 14.8 us  [swap(): lax.ppermute(values, axis, [(source, source ^ distance) for source in ran...]
    ppermute x7, waiting for transfers between devices: 3.06 us -> 1.88 us  [swap(): lax.ppermute(values, axis, [(source, source ^ distance) for source in ran...]
    all_to_all x1, blocking collectives: 16.1 us -> 14.9 us  [sum_shares(): lax.all_to_all(shares, ('band', 'rep'), split_axis=0, concat_axis=0, tile...]
  transfers between devices with their start and end apart: 7 -> 7, of which waited for: 1 -> 2; matrix products, arithmetic and copies ran while one was open for 0% -> 0% of each run, Pallas kernels for 8% -> 8%
where the time goes in v17:
time: 50 us; the launch traced here: 49.6 us
  blocking collectives  20.1 us (40%)
  starting transfers between devices  14.8 us (30%)
  Pallas kernels  12.1 us (24%)
  waiting for transfers between devices  1.88 us (4%)
  between operations  0.69 us (1%)
    all_to_all x1, blocking collectives, sum_shares(): lax.all_to_all(shares, ('band', 'rep'), split_axis=0, concat_axis=0, tile...  14.9 us
    ppermute x7, starting transfers between devices, swap(): lax.ppermute(values, axis, [(source, source ^ distance) for source in ran...  14.8 us
    pallas_call x1, Pallas kernels, mix_blocks(): pl.pallas_call(lambda *refs: mix_kernel(direct, refs[:len(arrived)], *ref...  5.99 us
    all_gather x1, blocking collectives, exchange(): factors = lax.all_gather(pack, 'rep', axis=0, tiled=False)  5.18 us
    pallas_call x1, Pallas kernels, prepare(): pl.pallas_call(functools.partial(prep_kernel, direct, row_share, half_wid...  2.98 us
    ppermute x7, waiting for transfers between devices, swap(): lax.ppermute(values, axis, [(source, source ^ distance) for source in ran...  1.88 us
    pallas_call x1, Pallas kernels, send_blocks(): pl.pallas_call(send_kernel, out_shape=[jax.ShapeDtypeStruct(shape, BF16)...  1.64 us
  transfers between devices with their start and end apart: 7, of which 2 were waited for; matrix products, arithmetic and copies ran while one was open for 0% of the time, Pallas kernels for 8%

profile of v17, /device:TPU:0, one launch (start us, length us, event | category | flops | bytes accessed | tf_op | source)
XLA Modules:
  0.0 49.6 jit_solution(7317564720499801957)
XLA Ops:
  0.6 1.6 %send_blocks.1 = (bf16[96,640]{1,0:T(8,128)(2,1)S(1)}, bf16[96,640]{1,0:T(8,128)(2,1)S(1)}, bf16[96,640]{1,0:T(8,128)(2,1)S(1)}, bf16[96,640]{1,0:T(8,128)(2,1)S...) custom-call(s32[8]{0:T(128)} %owner_hbm_ref.1, ...), custom_call_target="tpu_custom_call" | custom-call | tf_op jit(solution)/shard_map/send_blocks/pallas_call | solution.py:106
  2.3 3.0 %collective-permute-start = (bf16[96,640]{1,0:T(8,128)(2,1)S(1)}, bf16[96,640]{1,0:T(8,128)(2,1)S(1)}, u32[]{:S(2)}, u32[]{:S(2)}) collective-permute-start(bf16[96,640]{1,0:T(8,128)(2,1)S(1)} %get-tuple-element.32), channel_id=1, source_target_pairs={{0,4},{4,0},{8,12},{12,8},{16,20},{20,16},{24,28},{28,24},{1,5},{5... | collective-permute-start | bytes 368648 | tf_op jit(solution)/shard_map/ppermute | solution.py:61
  5.3 2.6 %collective-permute-start.1 = (bf16[96,640]{1,0:T(8,128)(2,1)S(1)}, bf16[96,640]{1,0:T(8,128)(2,1)S(1)}, u32[]{:S(2)}, u32[]{:S(2)}) collective-permute-start(bf16[96,640]{1,0:T(8,128)(2,1)S(1)} %get-tuple-element.35), channel_id=1, source_target_pairs={{0,16},{4,20},{8,24},{12,28},{16,0},{20,4},{24,8},{28,12},{1,17},{... | collective-permute-start | bytes 368648 | tf_op jit(solution)/shard_map/ppermute | solution.py:61
  7.9 0.0 collective-permute-start.2
  7.9 3.9 %collective-permute-start.3 = (bf16[96,640]{1,0:T(8,128)(2,1)S(1)}, bf16[96,640]{1,0:T(8,128)(2,1)S(1)}, u32[]{:S(2)}, u32[]{:S(2)}) collective-permute-start(bf16[96,640]{1,0:T(8,128)(2,1)S(1)} %get-tuple-element.37), channel_id=1, source_target_pairs={{0,24},{4,28},{8,16},{12,20},{16,8},{20,12},{24,0},{28,4},{1,25},{... | collective-permute-start | bytes 368648 | tf_op jit(solution)/shard_map/ppermute | solution.py:61
  11.8 0.0 collective-permute-start.4
  11.8 0.0 collective-permute-done.refs_1_
  11.8 5.2 %all-gather = bf16[8,16,128]{2,1,0:T(8,128)(2,1)S(1)} all-gather(bf16[2,16,128]{2,1,0:T(8,128)(2,1)S(1)} %get-tuple-element.41), channel_id=2, replica_groups=mesh['band'=8,'rep'=4] {'rep'}, dimensions={0}, use_global_device_ids=true | all-gather | bytes 40960 | tf_op jit(solution)/shard_map/all_gather | solution.py:131
  17.0 3.0 %collective-permute-start.5 = (bf16[96,640]{1,0:T(8,128)(2,1)S(1)}, bf16[96,640]{1,0:T(8,128)(2,1)S(1)}, u32[]{:S(2)}, u32[]{:S(2)}) collective-permute-start(bf16[96,640]{1,0:T(8,128)(2,1)S(1)} %get-tuple-element.47), channel_id=1, source_target_pairs={{0,12},{4,8},{8,4},{12,0},{16,28},{20,24},{24,20},{28,16},{1,13},{... | collective-permute-start | bytes 368648 | tf_op jit(solution)/shard_map/ppermute | solution.py:61
  19.9 0.2 collective-permute-done.1.refs_2_
  20.1 2.4 %collective-permute-start.6 = (bf16[96,640]{1,0:T(8,128)(2,1)S(1)}, bf16[96,640]{1,0:T(8,128)(2,1)S(1)}, u32[]{:S(2)}, u32[]{:S(2)}) collective-permute-start(bf16[96,640]{1,0:T(8,128)(2,1)S(1)} %get-tuple-element.48), channel_id=1, source_target_pairs={{0,28},{4,24},{8,20},{12,16},{16,12},{20,8},{24,4},{28,0},{1,29},{... | collective-permute-start | bytes 368648 | tf_op jit(solution)/shard_map/ppermute | solution.py:61
  22.5 3.0 %prepare.1 = (bf16[2,384,512]{2,1,0:T(8,128)(2,1)S(1)}, bf16[4,32,512]{2,1,0:T(8,128)(2,1)S(1)}, bf16[16,80]{1,0:T(8,128)(2,1)S(1)}, bf16[192,192]{1,0:T(8,128)(...) custom-call(s32[5]{0:T(128)} %group_hbm_ref.1, ...), custom_call_target="tpu_custom_call" | custom-call | flops 215482368 | bytes 6291456 | tf_op jit(solution)/shard_map/prepare/pallas_call | solution.py:240
  25.5 0.0 collective-permute-done.2.refs_3_
  25.5 0.0 collective-permute-done.3.refs_4_
  25.5 0.0 collective-permute-done.4.refs_5_.refs_2_
  25.5 0.8 %embed_early.1 = (bf16[2,576,512]{2,1,0:T(8,128)(2,1)S(1)}, bf16[640,512]{1,0:T(8,128)(2,1)S(1)}) custom-call(bf16[96,640]{1,0:T(8,128)(2,1)S(1)} %get-tuple-element.31.refs_0_, bf16[96,640]{1,0:T(8,128)(2,1)S(1)} %collective-permute-done.refs_1_, bf16[96,640]{1,0:T(8,128)(2,1)S(1)} %collective-permute-done.1.refs_2_, ...), custom_call_target="tpu_custom_call" | custom-call | flops 377487360 | bytes 4194304 | tf_op jit(solution)/shard_map/embed_early/pallas_call | solution.py:305
  26.3 1.7 %collective-permute-done.5.refs_3_ = bf16[96,640]{1,0:T(8,128)(2,1)S(1)} collective-permute-done((bf16[96,640]{1,0:T(8,128)(2,1)S(1)}, bf16[96,640]{1,0:T(8,128)(2,1)S(1)}, u32[]{:S(2)}, u32[]{:S(2)}) %collective-permute-start.5) | collective-permute-done | bytes 122912 | tf_op jit(solution)/shard_map/ppermute | solution.py:61
  28.0 0.0 collective-permute-done.6.refs_4_
  28.0 6.0 %mix_blocks.1 = (bf16[2,8,96,512]{3,2,1,0:T(8,128)(2,1)}, bf16[32,24,128]{2,1,0:T(8,128)(2,1)S(1)}) custom-call(bf16[2,576,512]{2,1,0:T(8,128)(2,1)S(1)} %get-tuple-element.45.refs_0_, bf16[640,512]{1,0:T(8,128)(2,1)S(1)} %get-tuple-element.46.refs_1_, bf16[96,640]{1,0:T(8,128)(2,1)S(1)} %collective-permute-done.4.refs_5_.refs_2_, ...), custom_call_target="tpu_custom_call" | custom-call | flops 3623878656 | bytes 12582912 | tf_op jit(solution)/shard_map/mix_blocks/pallas_call | solution.py:537
  34.0 14.9 %all_to_all.5.parts_ref = bf16[32,24,128]{2,1,0:T(8,128)(2,1)S(1)} all-to-all(bf16[32,24,128]{2,1,0:T(8,128)(2,1)S(1)} %get-tuple-element.56), channel_id=1, replica_groups=mesh['band'=8,'rep'=4] {'band','rep'}, dimensions={0} | all-to-all | bytes 393216 | tf_op jit(solution)/shard_map/all_to_all | solution.py:578
  48.9 0.7 %sum_shares.1 = (f32[16,20]{1,0:T(8,128)}, f32[16,128]{1,0:T(8,128)}) custom-call(bf16[32,24,128]{2,1,0:T(8,128)(2,1)S(1)} %all_to_all.5.parts_ref), custom_call_target="tpu_custom_call" | custom-call | tf_op jit(solution)/shard_map/sum_shares/pallas_call | solution.py:579
Async XLA Ops:
  2.3 9.5 %collective-permute-start = (bf16[96,640]{1,0:T(8,128)(2,1)S(1)}, bf16[96,640]{1,0:T(8,128)(2,1)S(1)}, u32[]{:S(2)}, u32[]{:S(2)}) collective-permute-start(bf16[96,640]{1,0:T(8,128)(2,1)S(1)} %get-tuple-element.32), channel_id=1, source_target_pairs={{0,4},{4,0},{8,12},{12,8},{16,20},{20,16},{24,28},{28,24},{1,5},{5... | collective-permute-start | bytes 368648 | tf_op jit(solution)/shard_map/ppermute | solution.py:61
  5.3 14.8 %collective-permute-start.1 = (bf16[96,640]{1,0:T(8,128)(2,1)S(1)}, bf16[96,640]{1,0:T(8,128)(2,1)S(1)}, u32[]{:S(2)}, u32[]{:S(2)}) collective-permute-start(bf16[96,640]{1,0:T(8,128)(2,1)S(1)} %get-tuple-element.35), channel_id=1, source_target_pairs={{0,16},{4,20},{8,24},{12,28},{16,0},{20,4},{24,8},{28,12},{1,17},{... | collective-permute-start | bytes 368648 | tf_op jit(solution)/shard_map/ppermute | solution.py:61
  7.9 17.6 %collective-permute-start.2 = (bf16[96,640]{1,0:T(8,128)(2,1)S(1)}, bf16[96,640]{1,0:T(8,128)(2,1)S(1)}, u32[]{:S(2)}, u32[]{:S(2)}) collective-permute-start(bf16[96,640]{1,0:T(8,128)(2,1)S(1)} %get-tuple-element.36), channel_id=1, source_target_pairs={{0,20},{4,16},{8,28},{12,24},{16,4},{20,0},{24,12},{28,8},{1,21},{... | collective-permute-start | bytes 368648 | tf_op jit(solution)/shard_map/ppermute | solution.py:61
  7.9 17.6 %collective-permute-start.3 = (bf16[96,640]{1,0:T(8,128)(2,1)S(1)}, bf16[96,640]{1,0:T(8,128)(2,1)S(1)}, u32[]{:S(2)}, u32[]{:S(2)}) collective-permute-start(bf16[96,640]{1,0:T(8,128)(2,1)S(1)} %get-tuple-element.37), channel_id=1, source_target_pairs={{0,24},{4,28},{8,16},{12,20},{16,8},{20,12},{24,0},{28,4},{1,25},{... | collective-permute-start | bytes 368648 | tf_op jit(solution)/shard_map/ppermute | solution.py:61
  11.8 13.8 %collective-permute-start.4 = (bf16[96,640]{1,0:T(8,128)(2,1)S(1)}, bf16[96,640]{1,0:T(8,128)(2,1)S(1)}, u32[]{:S(2)}, u32[]{:S(2)}) collective-permute-start(bf16[96,640]{1,0:T(8,128)(2,1)S(1)} %get-tuple-element.38), channel_id=1, source_target_pairs={{0,8},{4,12},{8,0},{12,4},{16,24},{20,28},{24,16},{28,20},{1,9},{5... | collective-permute-start | bytes 368648 | tf_op jit(solution)/shard_map/ppermute | solution.py:61
  17.0 11.0 %collective-permute-start.5 = (bf16[96,640]{1,0:T(8,128)(2,1)S(1)}, bf16[96,640]{1,0:T(8,128)(2,1)S(1)}, u32[]{:S(2)}, u32[]{:S(2)}) collective-permute-start(bf16[96,640]{1,0:T(8,128)(2,1)S(1)} %get-tuple-element.47), channel_id=1, source_target_pairs={{0,12},{4,8},{8,4},{12,0},{16,28},{20,24},{24,20},{28,16},{1,13},{... | collective-permute-start | bytes 368648 | tf_op jit(solution)/shard_map/ppermute | solution.py:61
  20.1 7.9 %collective-permute-start.6 = (bf16[96,640]{1,0:T(8,128)(2,1)S(1)}, bf16[96,640]{1,0:T(8,128)(2,1)S(1)}, u32[]{:S(2)}, u32[]{:S(2)}) collective-permute-start(bf16[96,640]{1,0:T(8,128)(2,1)S(1)} %get-tuple-element.48), channel_id=1, source_target_pairs={{0,28},{4,24},{8,20},{12,16},{16,12},{20,8},{24,4},{28,0},{1,29},{... | collective-permute-start | bytes 368648 | tf_op jit(solution)/shard_map/ppermute | solution.py:61

commit v18 on v17

--- a/solution.py
+++ b/solution.py
@@ -257,17 +257,15 @@
 def factor_shares(total, up_ref, down_ref, level_ref):
     levels, two_rank, feature_dim = up_ref.shape
     rank, channels = down_ref.shape
-    high, low = split_hi_lo(total)
-    down = down_ref[...]
-    first = jnp.zeros((rank, channels), F32)
+    total = total.astype(BF16)
+    first = jnp.zeros((two_rank, channels), F32)
     second = jnp.zeros((two_rank, feature_dim), F32)
     for level in range(levels):
-        at = slice(level * channels, (level + 1) * channels)
-        both = dot_nt(up_ref[level], high[at])
-        first = first + both[:rank] + both[rank:] + dot_nt(up_ref[level, :rank, :], low[at])
-        through = dot_nn(down, high[at]) + dot_nn(down, low[at])
-        through = jnp.concatenate(split_hi_lo(through), axis=0)
+        part = total[level * channels : (level + 1) * channels]
+        first = first + dot_nt(up_ref[level], part)
+        through = jnp.concatenate(split_hi_lo(dot_nn(down_ref[...], part)), axis=0)
         second = second + dot_nt(through, level_ref[level])
+    first = first[:rank] + first[rank:]
     return first, second[:rank] + second[rank:]
 
 

time: 50 us -> 49.9 us (level)
  no operation moved by 1% of the time
where the time goes in v18:
time: 49.9 us; the launch traced here: 49.5 us
  blocking collectives  20.1 us (40%)
  starting transfers between devices  14.8 us (30%)
  Pallas kernels  12 us (24%)
  waiting for transfers between devices  1.88 us (4%)
  between operations  0.69 us (1%)
    all_to_all x1, blocking collectives, sum_shares(): lax.all_to_all(shares, ('band', 'rep'), split_axis=0, concat_axis=0, tile...  14.9 us
    ppermute x7, starting transfers between devices, swap(): lax.ppermute(values, axis, [(source, source ^ distance) for source in ran...  14.8 us
    pallas_call x1, Pallas kernels, mix_blocks(): pl.pallas_call(lambda *refs: mix_kernel(direct, refs[:len(arrived)], *ref...  5.89 us
    all_gather x1, blocking collectives, exchange(): factors = lax.all_gather(pack, 'rep', axis=0, tiled=False)  5.18 us
    pallas_call x1, Pallas kernels, prepare(): pl.pallas_call(functools.partial(prep_kernel, direct, row_share, half_wid...  2.98 us
    ppermute x7, waiting for transfers between devices, swap(): lax.ppermute(values, axis, [(source, source ^ distance) for source in ran...  1.88 us
    pallas_call x1, Pallas kernels, send_blocks(): pl.pallas_call(send_kernel, out_shape=[jax.ShapeDtypeStruct(shape, BF16)...  1.64 us
  transfers between devices with their start and end apart: 7, of which 2 were waited for; matrix products, arithmetic and copies ran while one was open for 0% of the time, Pallas kernels for 8%

profile of v18, /device:TPU:0, one launch (start us, length us, event | category | flops | bytes accessed | tf_op | source)
XLA Modules:
  0.0 49.5 jit_solution(17647136778924247062)
XLA Ops:
  0.6 1.6 %send_blocks.1 = (bf16[96,640]{1,0:T(8,128)(2,1)S(1)}, bf16[96,640]{1,0:T(8,128)(2,1)S(1)}, bf16[96,640]{1,0:T(8,128)(2,1)S(1)}, bf16[96,640]{1,0:T(8,128)(2,1)S...) custom-call(s32[8]{0:T(128)} %owner_hbm_ref.1, ...), custom_call_target="tpu_custom_call" | custom-call | tf_op jit(solution)/shard_map/send_blocks/pallas_call | solution.py:106
  2.3 3.0 %collective-permute-start = (bf16[96,640]{1,0:T(8,128)(2,1)S(1)}, bf16[96,640]{1,0:T(8,128)(2,1)S(1)}, u32[]{:S(2)}, u32[]{:S(2)}) collective-permute-start(bf16[96,640]{1,0:T(8,128)(2,1)S(1)} %get-tuple-element.32), channel_id=1, source_target_pairs={{0,4},{4,0},{8,12},{12,8},{16,20},{20,16},{24,28},{28,24},{1,5},{5... | collective-permute-start | bytes 368648 | tf_op jit(solution)/shard_map/ppermute | solution.py:61
  5.3 2.6 %collective-permute-start.1 = (bf16[96,640]{1,0:T(8,128)(2,1)S(1)}, bf16[96,640]{1,0:T(8,128)(2,1)S(1)}, u32[]{:S(2)}, u32[]{:S(2)}) collective-permute-start(bf16[96,640]{1,0:T(8,128)(2,1)S(1)} %get-tuple-element.35), channel_id=1, source_target_pairs={{0,16},{4,20},{8,24},{12,28},{16,0},{20,4},{24,8},{28,12},{1,17},{... | collective-permute-start | bytes 368648 | tf_op jit(solution)/shard_map/ppermute | solution.py:61
  7.9 0.0 collective-permute-start.2
  7.9 3.9 %collective-permute-start.3 = (bf16[96,640]{1,0:T(8,128)(2,1)S(1)}, bf16[96,640]{1,0:T(8,128)(2,1)S(1)}, u32[]{:S(2)}, u32[]{:S(2)}) collective-permute-start(bf16[96,640]{1,0:T(8,128)(2,1)S(1)} %get-tuple-element.37), channel_id=1, source_target_pairs={{0,24},{4,28},{8,16},{12,20},{16,8},{20,12},{24,0},{28,4},{1,25},{... | collective-permute-start | bytes 368648 | tf_op jit(solution)/shard_map/ppermute | solution.py:61
  11.8 0.0 collective-permute-start.4
  11.8 0.0 collective-permute-done.refs_1_
  11.8 5.2 %all-gather = bf16[8,16,128]{2,1,0:T(8,128)(2,1)S(1)} all-gather(bf16[2,16,128]{2,1,0:T(8,128)(2,1)S(1)} %get-tuple-element.41), channel_id=2, replica_groups=mesh['band'=8,'rep'=4] {'rep'}, dimensions={0}, use_global_device_ids=true | all-gather | bytes 40960 | tf_op jit(solution)/shard_map/all_gather | solution.py:131
  17.0 3.0 %collective-permute-start.5 = (bf16[96,640]{1,0:T(8,128)(2,1)S(1)}, bf16[96,640]{1,0:T(8,128)(2,1)S(1)}, u32[]{:S(2)}, u32[]{:S(2)}) collective-permute-start(bf16[96,640]{1,0:T(8,128)(2,1)S(1)} %get-tuple-element.47), channel_id=1, source_target_pairs={{0,12},{4,8},{8,4},{12,0},{16,28},{20,24},{24,20},{28,16},{1,13},{... | collective-permute-start | bytes 368648 | tf_op jit(solution)/shard_map/ppermute | solution.py:61
  19.9 0.2 collective-permute-done.1.refs_2_
  20.1 2.4 %collective-permute-start.6 = (bf16[96,640]{1,0:T(8,128)(2,1)S(1)}, bf16[96,640]{1,0:T(8,128)(2,1)S(1)}, u32[]{:S(2)}, u32[]{:S(2)}) collective-permute-start(bf16[96,640]{1,0:T(8,128)(2,1)S(1)} %get-tuple-element.48), channel_id=1, source_target_pairs={{0,28},{4,24},{8,20},{12,16},{16,12},{20,8},{24,4},{28,0},{1,29},{... | collective-permute-start | bytes 368648 | tf_op jit(solution)/shard_map/ppermute | solution.py:61
  22.5 3.0 %prepare.1 = (bf16[2,384,512]{2,1,0:T(8,128)(2,1)S(1)}, bf16[4,32,512]{2,1,0:T(8,128)(2,1)S(1)}, bf16[16,80]{1,0:T(8,128)(2,1)S(1)}, bf16[192,192]{1,0:T(8,128)(...) custom-call(s32[5]{0:T(128)} %group_hbm_ref.1, ...), custom_call_target="tpu_custom_call" | custom-call | flops 215482368 | bytes 6291456 | tf_op jit(solution)/shard_map/prepare/pallas_call | solution.py:240
  25.5 0.0 collective-permute-done.2.refs_3_
  25.5 0.0 collective-permute-done.3.refs_4_
  25.5 0.0 collective-permute-done.4.refs_5_.refs_2_
  25.5 0.8 %embed_early.1 = (bf16[2,576,512]{2,1,0:T(8,128)(2,1)S(1)}, bf16[640,512]{1,0:T(8,128)(2,1)S(1)}) custom-call(bf16[96,640]{1,0:T(8,128)(2,1)S(1)} %get-tuple-element.31.refs_0_, bf16[96,640]{1,0:T(8,128)(2,1)S(1)} %collective-permute-done.refs_1_, bf16[96,640]{1,0:T(8,128)(2,1)S(1)} %collective-permute-done.1.refs_2_, ...), custom_call_target="tpu_custom_call" | custom-call | flops 377487360 | bytes 4194304 | tf_op jit(solution)/shard_map/embed_early/pallas_call | solution.py:303
  26.3 1.7 %collective-permute-done.5.refs_3_ = bf16[96,640]{1,0:T(8,128)(2,1)S(1)} collective-permute-done((bf16[96,640]{1,0:T(8,128)(2,1)S(1)}, bf16[96,640]{1,0:T(8,128)(2,1)S(1)}, u32[]{:S(2)}, u32[]{:S(2)}) %collective-permute-start.5) | collective-permute-done | bytes 122912 | tf_op jit(solution)/shard_map/ppermute | solution.py:61
  28.0 0.0 collective-permute-done.6.refs_4_
  28.0 5.9 %mix_blocks.1 = (bf16[2,8,96,512]{3,2,1,0:T(8,128)(2,1)}, bf16[32,24,128]{2,1,0:T(8,128)(2,1)S(1)}) custom-call(bf16[2,576,512]{2,1,0:T(8,128)(2,1)S(1)} %get-tuple-element.45.refs_0_, bf16[640,512]{1,0:T(8,128)(2,1)S(1)} %get-tuple-element.46.refs_1_, bf16[96,640]{1,0:T(8,128)(2,1)S(1)} %collective-permute-done.4.refs_5_.refs_2_, ...), custom_call_target="tpu_custom_call" | custom-call | flops 3623878656 | bytes 12582912 | tf_op jit(solution)/shard_map/mix_blocks/pallas_call | solution.py:535
  33.9 14.9 %all_to_all.5.parts_ref = bf16[32,24,128]{2,1,0:T(8,128)(2,1)S(1)} all-to-all(bf16[32,24,128]{2,1,0:T(8,128)(2,1)S(1)} %get-tuple-element.56), channel_id=1, replica_groups=mesh['band'=8,'rep'=4] {'band','rep'}, dimensions={0} | all-to-all | bytes 393216 | tf_op jit(solution)/shard_map/all_to_all | solution.py:576
  48.8 0.7 %sum_shares.1 = (f32[16,20]{1,0:T(8,128)}, f32[16,128]{1,0:T(8,128)}) custom-call(bf16[32,24,128]{2,1,0:T(8,128)(2,1)S(1)} %all_to_all.5.parts_ref), custom_call_target="tpu_custom_call" | custom-call | tf_op jit(solution)/shard_map/sum_shares/pallas_call | solution.py:577
Async XLA Ops:
  2.3 9.5 %collective-permute-start = (bf16[96,640]{1,0:T(8,128)(2,1)S(1)}, bf16[96,640]{1,0:T(8,128)(2,1)S(1)}, u32[]{:S(2)}, u32[]{:S(2)}) collective-permute-start(bf16[96,640]{1,0:T(8,128)(2,1)S(1)} %get-tuple-element.32), channel_id=1, source_target_pairs={{0,4},{4,0},{8,12},{12,8},{16,20},{20,16},{24,28},{28,24},{1,5},{5... | collective-permute-start | bytes 368648 | tf_op jit(solution)/shard_map/ppermute | solution.py:61
  5.3 14.8 %collective-permute-start.1 = (bf16[96,640]{1,0:T(8,128)(2,1)S(1)}, bf16[96,640]{1,0:T(8,128)(2,1)S(1)}, u32[]{:S(2)}, u32[]{:S(2)}) collective-permute-start(bf16[96,640]{1,0:T(8,128)(2,1)S(1)} %get-tuple-element.35), channel_id=1, source_target_pairs={{0,16},{4,20},{8,24},{12,28},{16,0},{20,4},{24,8},{28,12},{1,17},{... | collective-permute-start | bytes 368648 | tf_op jit(solution)/shard_map/ppermute | solution.py:61
  7.9 17.6 %collective-permute-start.2 = (bf16[96,640]{1,0:T(8,128)(2,1)S(1)}, bf16[96,640]{1,0:T(8,128)(2,1)S(1)}, u32[]{:S(2)}, u32[]{:S(2)}) collective-permute-start(bf16[96,640]{1,0:T(8,128)(2,1)S(1)} %get-tuple-element.36), channel_id=1, source_target_pairs={{0,20},{4,16},{8,28},{12,24},{16,4},{20,0},{24,12},{28,8},{1,21},{... | collective-permute-start | bytes 368648 | tf_op jit(solution)/shard_map/ppermute | solution.py:61
  7.9 17.6 %collective-permute-start.3 = (bf16[96,640]{1,0:T(8,128)(2,1)S(1)}, bf16[96,640]{1,0:T(8,128)(2,1)S(1)}, u32[]{:S(2)}, u32[]{:S(2)}) collective-permute-start(bf16[96,640]{1,0:T(8,128)(2,1)S(1)} %get-tuple-element.37), channel_id=1, source_target_pairs={{0,24},{4,28},{8,16},{12,20},{16,8},{20,12},{24,0},{28,4},{1,25},{... | collective-permute-start | bytes 368648 | tf_op jit(solution)/shard_map/ppermute | solution.py:61
  11.8 13.8 %collective-permute-start.4 = (bf16[96,640]{1,0:T(8,128)(2,1)S(1)}, bf16[96,640]{1,0:T(8,128)(2,1)S(1)}, u32[]{:S(2)}, u32[]{:S(2)}) collective-permute-start(bf16[96,640]{1,0:T(8,128)(2,1)S(1)} %get-tuple-element.38), channel_id=1, source_target_pairs={{0,8},{4,12},{8,0},{12,4},{16,24},{20,28},{24,16},{28,20},{1,9},{5... | collective-permute-start | bytes 368648 | tf_op jit(solution)/shard_map/ppermute | solution.py:61
  17.0 11.0 %collective-permute-start.5 = (bf16[96,640]{1,0:T(8,128)(2,1)S(1)}, bf16[96,640]{1,0:T(8,128)(2,1)S(1)}, u32[]{:S(2)}, u32[]{:S(2)}) collective-permute-start(bf16[96,640]{1,0:T(8,128)(2,1)S(1)} %get-tuple-element.47), channel_id=1, source_target_pairs={{0,12},{4,8},{8,4},{12,0},{16,28},{20,24},{24,20},{28,16},{1,13},{... | collective-permute-start | bytes 368648 | tf_op jit(solution)/shard_map/ppermute | solution.py:61
  20.1 7.9 %collective-permute-start.6 = (bf16[96,640]{1,0:T(8,128)(2,1)S(1)}, bf16[96,640]{1,0:T(8,128)(2,1)S(1)}, u32[]{:S(2)}, u32[]{:S(2)}) collective-permute-start(bf16[96,640]{1,0:T(8,128)(2,1)S(1)} %get-tuple-element.48), channel_id=1, source_target_pairs={{0,28},{4,24},{8,20},{12,16},{16,12},{20,8},{24,4},{28,0},{1,29},{... | collective-permute-start | bytes 368648 | tf_op jit(solution)/shard_map/ppermute | solution.py:61

commit v19 on v17

--- a/solution.py
+++ b/solution.py
@@ -17,7 +17,7 @@
 EARLY = 6
 SLOTS = (0, 1, 4, 5, 6, 2, 3, 7)
 FOLDS = 2
-COLUMNS = 256
+COLUMNS = 512
 BF16 = jnp.bfloat16
 F32 = jnp.float32
 
@@ -411,14 +411,13 @@
                 part = tokens[:, within].reshape(late_rows, COLUMNS).astype(BF16)
                 tokens_refs[n][block * late_rows : (block + 1) * late_rows, columns] = part
 
-        def mixing():
-            for block, (_, at) in enumerate(groups):
-                tokens = tokens_at(n, block, early, WLAT - early, columns)
-                if direct:
-                    tokens = jnp.concatenate([tokens_at(n, block, 0, early, columns), tokens], axis=0)
-                pre_refs[n][at, columns] = dot_nn(mix_ref[...], tokens)
-
-        return [embed, mixing]
+        def mixing(block, at):
+            tokens = tokens_at(n, block, early, WLAT - early, columns)
+            if direct:
+                tokens = jnp.concatenate([tokens_at(n, block, 0, early, columns), tokens], axis=0)
+            pre_refs[n][at, columns] = dot_nn(mix_ref[...], tokens)
+
+        return [embed] + [functools.partial(mixing, block, at) for block, (_, at) in enumerate(groups)]
 
     def pointwise(n, columns):
         s, first_line = n % samples, n // samples * WLAT

time: 50 us -> 49.5 us (0.990)
  Pallas kernels: 12.1 us -> 11.6 us
    pallas_call x1, Pallas kernels: 5.99 us -> 5.48 us  [mix_blocks(): pl.pallas_call(lambda *refs: mix_kernel(direct, refs[:len(arrived)], *ref...]
where the time goes in v19:
time: 49.5 us; the launch traced here: 49.1 us
  blocking collectives  20.1 us (41%)
  starting transfers between devices  14.8 us (30%)
  Pallas kernels  11.6 us (23%)
  waiting for transfers between devices  1.88 us (4%)
  between operations  0.69 us (1%)
    all_to_all x1, blocking collectives, sum_shares(): lax.all_to_all(shares, ('band', 'rep'), split_axis=0, concat_axis=0, tile...  14.9 us
    ppermute x7, starting transfers between devices, swap(): lax.ppermute(values, axis, [(source, source ^ distance) for source in ran...  14.8 us
    pallas_call x1, Pallas kernels, mix_blocks(): pl.pallas_call(lambda *refs: mix_kernel(direct, refs[:len(arrived)], *ref...  5.48 us
    all_gather x1, blocking collectives, exchange(): factors = lax.all_gather(pack, 'rep', axis=0, tiled=False)  5.18 us
    pallas_call x1, Pallas kernels, prepare(): pl.pallas_call(functools.partial(prep_kernel, direct, row_share, half_wid...  2.98 us
    ppermute x7, waiting for transfers between devices, swap(): lax.ppermute(values, axis, [(source, source ^ distance) for source in ran...  1.88 us
    pallas_call x1, Pallas kernels, send_blocks(): pl.pallas_call(send_kernel, out_shape=[jax.ShapeDtypeStruct(shape, BF16)...  1.64 us
  transfers between devices with their start and end apart: 7, of which 2 were waited for; matrix products, arithmetic and copies ran while one was open for 0% of the time, Pallas kernels for 8%

profile of v19, /device:TPU:0, one launch (start us, length us, event | category | flops | bytes accessed | tf_op | source)
XLA Modules:
  0.0 49.1 jit_solution(6323234558927799885)
XLA Ops:
  0.6 1.6 %send_blocks.1 = (bf16[96,640]{1,0:T(8,128)(2,1)S(1)}, bf16[96,640]{1,0:T(8,128)(2,1)S(1)}, bf16[96,640]{1,0:T(8,128)(2,1)S(1)}, bf16[96,640]{1,0:T(8,128)(2,1)S...) custom-call(s32[8]{0:T(128)} %owner_hbm_ref.1, ...), custom_call_target="tpu_custom_call" | custom-call | tf_op jit(solution)/shard_map/send_blocks/pallas_call | solution.py:106
  2.3 3.0 %collective-permute-start = (bf16[96,640]{1,0:T(8,128)(2,1)S(1)}, bf16[96,640]{1,0:T(8,128)(2,1)S(1)}, u32[]{:S(2)}, u32[]{:S(2)}) collective-permute-start(bf16[96,640]{1,0:T(8,128)(2,1)S(1)} %get-tuple-element.32), channel_id=1, source_target_pairs={{0,4},{4,0},{8,12},{12,8},{16,20},{20,16},{24,28},{28,24},{1,5},{5... | collective-permute-start | bytes 368648 | tf_op jit(solution)/shard_map/ppermute | solution.py:61
  5.3 2.6 %collective-permute-start.1 = (bf16[96,640]{1,0:T(8,128)(2,1)S(1)}, bf16[96,640]{1,0:T(8,128)(2,1)S(1)}, u32[]{:S(2)}, u32[]{:S(2)}) collective-permute-start(bf16[96,640]{1,0:T(8,128)(2,1)S(1)} %get-tuple-element.35), channel_id=1, source_target_pairs={{0,16},{4,20},{8,24},{12,28},{16,0},{20,4},{24,8},{28,12},{1,17},{... | collective-permute-start | bytes 368648 | tf_op jit(solution)/shard_map/ppermute | solution.py:61
  7.9 0.0 collective-permute-start.2
  7.9 3.9 %collective-permute-start.3 = (bf16[96,640]{1,0:T(8,128)(2,1)S(1)}, bf16[96,640]{1,0:T(8,128)(2,1)S(1)}, u32[]{:S(2)}, u32[]{:S(2)}) collective-permute-start(bf16[96,640]{1,0:T(8,128)(2,1)S(1)} %get-tuple-element.37), channel_id=1, source_target_pairs={{0,24},{4,28},{8,16},{12,20},{16,8},{20,12},{24,0},{28,4},{1,25},{... | collective-permute-start | bytes 368648 | tf_op jit(solution)/shard_map/ppermute | solution.py:61
  11.8 0.0 collective-permute-start.4
  11.8 0.0 collective-permute-done.refs_1_
  11.8 5.2 %all-gather = bf16[8,16,128]{2,1,0:T(8,128)(2,1)S(1)} all-gather(bf16[2,16,128]{2,1,0:T(8,128)(2,1)S(1)} %get-tuple-element.41), channel_id=2, replica_groups=mesh['band'=8,'rep'=4] {'rep'}, dimensions={0}, use_global_device_ids=true | all-gather | bytes 40960 | tf_op jit(solution)/shard_map/all_gather | solution.py:131
  17.0 3.0 %collective-permute-start.5 = (bf16[96,640]{1,0:T(8,128)(2,1)S(1)}, bf16[96,640]{1,0:T(8,128)(2,1)S(1)}, u32[]{:S(2)}, u32[]{:S(2)}) collective-permute-start(bf16[96,640]{1,0:T(8,128)(2,1)S(1)} %get-tuple-element.47), channel_id=1, source_target_pairs={{0,12},{4,8},{8,4},{12,0},{16,28},{20,24},{24,20},{28,16},{1,13},{... | collective-permute-start | bytes 368648 | tf_op jit(solution)/shard_map/ppermute | solution.py:61
  19.9 0.2 collective-permute-done.1.refs_2_
  20.1 2.4 %collective-permute-start.6 = (bf16[96,640]{1,0:T(8,128)(2,1)S(1)}, bf16[96,640]{1,0:T(8,128)(2,1)S(1)}, u32[]{:S(2)}, u32[]{:S(2)}) collective-permute-start(bf16[96,640]{1,0:T(8,128)(2,1)S(1)} %get-tuple-element.48), channel_id=1, source_target_pairs={{0,28},{4,24},{8,20},{12,16},{16,12},{20,8},{24,4},{28,0},{1,29},{... | collective-permute-start | bytes 368648 | tf_op jit(solution)/shard_map/ppermute | solution.py:61
  22.5 3.0 %prepare.1 = (bf16[2,384,512]{2,1,0:T(8,128)(2,1)S(1)}, bf16[4,32,512]{2,1,0:T(8,128)(2,1)S(1)}, bf16[16,80]{1,0:T(8,128)(2,1)S(1)}, bf16[192,192]{1,0:T(8,128)(...) custom-call(s32[5]{0:T(128)} %group_hbm_ref.1, ...), custom_call_target="tpu_custom_call" | custom-call | flops 215482368 | bytes 6291456 | tf_op jit(solution)/shard_map/prepare/pallas_call | solution.py:240
  25.5 0.0 collective-permute-done.2.refs_3_
  25.5 0.0 collective-permute-done.3.refs_4_
  25.5 0.0 collective-permute-done.4.refs_5_.refs_2_
  25.5 0.8 %embed_early.1 = (bf16[2,576,512]{2,1,0:T(8,128)(2,1)S(1)}, bf16[640,512]{1,0:T(8,128)(2,1)S(1)}) custom-call(bf16[96,640]{1,0:T(8,128)(2,1)S(1)} %get-tuple-element.31.refs_0_, bf16[96,640]{1,0:T(8,128)(2,1)S(1)} %collective-permute-done.refs_1_, bf16[96,640]{1,0:T(8,128)(2,1)S(1)} %collective-permute-done.1.refs_2_, ...), custom_call_target="tpu_custom_call" | custom-call | flops 377487360 | bytes 4194304 | tf_op jit(solution)/shard_map/embed_early/pallas_call | solution.py:305
  26.3 1.7 %collective-permute-done.5.refs_3_ = bf16[96,640]{1,0:T(8,128)(2,1)S(1)} collective-permute-done((bf16[96,640]{1,0:T(8,128)(2,1)S(1)}, bf16[96,640]{1,0:T(8,128)(2,1)S(1)}, u32[]{:S(2)}, u32[]{:S(2)}) %collective-permute-start.5) | collective-permute-done | bytes 122912 | tf_op jit(solution)/shard_map/ppermute | solution.py:61
  28.0 0.0 collective-permute-done.6.refs_4_
  28.0 5.5 %mix_blocks.1 = (bf16[2,8,96,512]{3,2,1,0:T(8,128)(2,1)}, bf16[32,24,128]{2,1,0:T(8,128)(2,1)S(1)}) custom-call(bf16[2,576,512]{2,1,0:T(8,128)(2,1)S(1)} %get-tuple-element.45.refs_0_, bf16[640,512]{1,0:T(8,128)(2,1)S(1)} %get-tuple-element.46.refs_1_, bf16[96,640]{1,0:T(8,128)(2,1)S(1)} %collective-permute-done.4.refs_5_.refs_2_, ...), custom_call_target="tpu_custom_call" | custom-call | flops 3623878656 | bytes 12582912 | tf_op jit(solution)/shard_map/mix_blocks/pallas_call | solution.py:536
  33.5 14.9 %all_to_all.5.parts_ref = bf16[32,24,128]{2,1,0:T(8,128)(2,1)S(1)} all-to-all(bf16[32,24,128]{2,1,0:T(8,128)(2,1)S(1)} %get-tuple-element.56), channel_id=1, replica_groups=mesh['band'=8,'rep'=4] {'band','rep'}, dimensions={0} | all-to-all | bytes 393216 | tf_op jit(solution)/shard_map/all_to_all | solution.py:577
  48.4 0.7 %sum_shares.1 = (f32[16,20]{1,0:T(8,128)}, f32[16,128]{1,0:T(8,128)}) custom-call(bf16[32,24,128]{2,1,0:T(8,128)(2,1)S(1)} %all_to_all.5.parts_ref), custom_call_target="tpu_custom_call" | custom-call | tf_op jit(solution)/shard_map/sum_shares/pallas_call | solution.py:578
Async XLA Ops:
  2.3 9.5 %collective-permute-start = (bf16[96,640]{1,0:T(8,128)(2,1)S(1)}, bf16[96,640]{1,0:T(8,128)(2,1)S(1)}, u32[]{:S(2)}, u32[]{:S(2)}) collective-permute-start(bf16[96,640]{1,0:T(8,128)(2,1)S(1)} %get-tuple-element.32), channel_id=1, source_target_pairs={{0,4},{4,0},{8,12},{12,8},{16,20},{20,16},{24,28},{28,24},{1,5},{5... | collective-permute-start | bytes 368648 | tf_op jit(solution)/shard_map/ppermute | solution.py:61
  5.3 14.8 %collective-permute-start.1 = (bf16[96,640]{1,0:T(8,128)(2,1)S(1)}, bf16[96,640]{1,0:T(8,128)(2,1)S(1)}, u32[]{:S(2)}, u32[]{:S(2)}) collective-permute-start(bf16[96,640]{1,0:T(8,128)(2,1)S(1)} %get-tuple-element.35), channel_id=1, source_target_pairs={{0,16},{4,20},{8,24},{12,28},{16,0},{20,4},{24,8},{28,12},{1,17},{... | collective-permute-start | bytes 368648 | tf_op jit(solution)/shard_map/ppermute | solution.py:61
  7.9 17.6 %collective-permute-start.2 = (bf16[96,640]{1,0:T(8,128)(2,1)S(1)}, bf16[96,640]{1,0:T(8,128)(2,1)S(1)}, u32[]{:S(2)}, u32[]{:S(2)}) collective-permute-start(bf16[96,640]{1,0:T(8,128)(2,1)S(1)} %get-tuple-element.36), channel_id=1, source_target_pairs={{0,20},{4,16},{8,28},{12,24},{16,4},{20,0},{24,12},{28,8},{1,21},{... | collective-permute-start | bytes 368648 | tf_op jit(solution)/shard_map/ppermute | solution.py:61
  7.9 17.6 %collective-permute-start.3 = (bf16[96,640]{1,0:T(8,128)(2,1)S(1)}, bf16[96,640]{1,0:T(8,128)(2,1)S(1)}, u32[]{:S(2)}, u32[]{:S(2)}) collective-permute-start(bf16[96,640]{1,0:T(8,128)(2,1)S(1)} %get-tuple-element.37), channel_id=1, source_target_pairs={{0,24},{4,28},{8,16},{12,20},{16,8},{20,12},{24,0},{28,4},{1,25},{... | collective-permute-start | bytes 368648 | tf_op jit(solution)/shard_map/ppermute | solution.py:61
  11.8 13.8 %collective-permute-start.4 = (bf16[96,640]{1,0:T(8,128)(2,1)S(1)}, bf16[96,640]{1,0:T(8,128)(2,1)S(1)}, u32[]{:S(2)}, u32[]{:S(2)}) collective-permute-start(bf16[96,640]{1,0:T(8,128)(2,1)S(1)} %get-tuple-element.38), channel_id=1, source_target_pairs={{0,8},{4,12},{8,0},{12,4},{16,24},{20,28},{24,16},{28,20},{1,9},{5... | collective-permute-start | bytes 368648 | tf_op jit(solution)/shard_map/ppermute | solution.py:61
  17.0 11.0 %collective-permute-start.5 = (bf16[96,640]{1,0:T(8,128)(2,1)S(1)}, bf16[96,640]{1,0:T(8,128)(2,1)S(1)}, u32[]{:S(2)}, u32[]{:S(2)}) collective-permute-start(bf16[96,640]{1,0:T(8,128)(2,1)S(1)} %get-tuple-element.47), channel_id=1, source_target_pairs={{0,12},{4,8},{8,4},{12,0},{16,28},{20,24},{24,20},{28,16},{1,13},{... | collective-permute-start | bytes 368648 | tf_op jit(solution)/shard_map/ppermute | solution.py:61
  20.1 7.9 %collective-permute-start.6 = (bf16[96,640]{1,0:T(8,128)(2,1)S(1)}, bf16[96,640]{1,0:T(8,128)(2,1)S(1)}, u32[]{:S(2)}, u32[]{:S(2)}) collective-permute-start(bf16[96,640]{1,0:T(8,128)(2,1)S(1)} %get-tuple-element.48), channel_id=1, source_target_pairs={{0,28},{4,24},{8,20},{12,16},{16,12},{20,8},{24,4},{28,0},{1,29},{... | collective-permute-start | bytes 368648 | tf_op jit(solution)/shard_map/ppermute | solution.py:61

commit v20 on v19

--- a/solution.py
+++ b/solution.py
@@ -17,7 +17,7 @@
 EARLY = 6
 SLOTS = (0, 1, 4, 5, 6, 2, 3, 7)
 FOLDS = 2
-COLUMNS = 512
+COLUMNS = 256
 BF16 = jnp.bfloat16
 F32 = jnp.float32
 
@@ -286,12 +286,10 @@
     for s in range(samples):
         lane = s * depth // LANE * LANE
         pixels = jnp.concatenate([piece_ref[:, lane : lane + reach] for piece_ref in piece_refs], axis=0)
-        for start in range(0, feature_dim, COLUMNS):
-            columns = slice(start, start + COLUMNS)
-            tokens = dot_nn(pixels, merged_ref[s, :, columns]).reshape(len(piece_refs), width, COLUMNS)
-            for n in range(width // group):
-                part = tokens[:, n * group : (n + 1) * group].reshape(rows, COLUMNS)
-                tokens_ref[s, n * rows : (n + 1) * rows, columns] = part.astype(BF16)
+        tokens = dot_nn(pixels, merged_ref[s]).reshape(len(piece_refs), width, feature_dim)
+        for n in range(width // group):
+            part = tokens[:, n * group : (n + 1) * group].reshape(rows, feature_dim)
+            tokens_ref[s, n * rows : (n + 1) * rows, :] = part.astype(BF16)
     for start in range(0, features, LANE):
         lanes = slice(start, start + LANE)
         pixels = jnp.concatenate([piece_ref[:, lanes] for piece_ref in piece_refs], axis=0)
@@ -406,9 +404,9 @@
             pixels = pixels_of(n, slice(lane, lane + reach))
             if direct:
                 pixels = pixels[width:]
-            tokens = dot_nn(pixels, merged_ref[s, :, columns]).reshape(WLAT - early, width, COLUMNS)
+            tokens = dot_nn(pixels, merged_ref[s, :, columns]).reshape(WLAT - early, width, -1)
             for block, (within, _) in enumerate(groups):
-                part = tokens[:, within].reshape(late_rows, COLUMNS).astype(BF16)
+                part = tokens[:, within].reshape(late_rows, -1).astype(BF16)
                 tokens_refs[n][block * late_rows : (block + 1) * late_rows, columns] = part
 
         def mixing(block, at):
@@ -450,11 +448,11 @@
         def spread():
             direct_part = grad_ref[n % samples, lines_of(n), :, columns].astype(F32)
             through = [
-                dot_nn(mix_t_ref[...], grad_pre_refs[n][at, columns]).reshape(WLAT, group, COLUMNS)
+                dot_nn(mix_t_ref[...], grad_pre_refs[n][at, columns]).reshape(WLAT, group, -1)
                 for _, at in groups
             ]
             total = jnp.concatenate(through, axis=1) + direct_part
-            grad_tokens_refs[n][:, columns] = total.reshape(rows, COLUMNS).astype(BF16)
+            grad_tokens_refs[n][:, columns] = total.reshape(rows, -1).astype(BF16)
 
         def share():
             s = n % samples
@@ -467,10 +465,9 @@
 
         return [spread, share]
 
-    units = [
-        (n, slice(start, start + COLUMNS))
-        for n in range(chunk_count)
-        for start in range(0, feature_dim, COLUMNS)
+    units = [(n, slice(0, feature_dim)) for n in range(chunk_count - 1)]
+    units += [
+        (chunk_count - 1, slice(start, start + COLUMNS)) for start in range(0, feature_dim, COLUMNS)
     ]
     for step in forward(*units[0]):
         step()

time: 49.5 us -> 49.9 us (level)
  no operation moved by 1% of the time
where the time goes in v20:
time: 49.9 us; the launch traced here: 49.5 us
  blocking collectives  20.1 us (40%)
  starting transfers between devices  14.8 us (30%)
  Pallas kernels  12 us (24%)
  waiting for transfers between devices  1.88 us (4%)
  between operations  0.69 us (1%)
    all_to_all x1, blocking collectives, sum_shares(): lax.all_to_all(shares, ('band', 'rep'), split_axis=0, concat_axis=0, tile...  14.9 us
    ppermute x7, starting transfers between devices, swap(): lax.ppermute(values, axis, [(source, source ^ distance) for source in ran...  14.8 us
    pallas_call x1, Pallas kernels, mix_blocks(): pl.pallas_call(lambda *refs: mix_kernel(direct, refs[:len(arrived)], *ref...  5.89 us
    all_gather x1, blocking collectives, exchange(): factors = lax.all_gather(pack, 'rep', axis=0, tiled=False)  5.18 us
    pallas_call x1, Pallas kernels, prepare(): pl.pallas_call(functools.partial(prep_kernel, direct, row_share, half_wid...  2.98 us
    ppermute x7, waiting for transfers between devices, swap(): lax.ppermute(values, axis, [(source, source ^ distance) for source in ran...  1.88 us
    pallas_call x1, Pallas kernels, send_blocks(): pl.pallas_call(send_kernel, out_shape=[jax.ShapeDtypeStruct(shape, BF16)...  1.64 us
  transfers between devices with their start and end apart: 7, of which 2 were waited for; matrix products, arithmetic and copies ran while one was open for 0% of the time, Pallas kernels for 8%

profile of v20, /device:TPU:0, one launch (start us, length us, event | category | flops | bytes accessed | tf_op | source)
XLA Modules:
  0.0 49.5 jit_solution(16077568858484172139)
XLA Ops:
  0.6 1.6 %send_blocks.1 = (bf16[96,640]{1,0:T(8,128)(2,1)S(1)}, bf16[96,640]{1,0:T(8,128)(2,1)S(1)}, bf16[96,640]{1,0:T(8,128)(2,1)S(1)}, bf16[96,640]{1,0:T(8,128)(2,1)S...) custom-call(s32[8]{0:T(128)} %owner_hbm_ref.1, ...), custom_call_target="tpu_custom_call" | custom-call | tf_op jit(solution)/shard_map/send_blocks/pallas_call | solution.py:106
  2.3 3.0 %collective-permute-start = (bf16[96,640]{1,0:T(8,128)(2,1)S(1)}, bf16[96,640]{1,0:T(8,128)(2,1)S(1)}, u32[]{:S(2)}, u32[]{:S(2)}) collective-permute-start(bf16[96,640]{1,0:T(8,128)(2,1)S(1)} %get-tuple-element.32), channel_id=1, source_target_pairs={{0,4},{4,0},{8,12},{12,8},{16,20},{20,16},{24,28},{28,24},{1,5},{5... | collective-permute-start | bytes 368648 | tf_op jit(solution)/shard_map/ppermute | solution.py:61
  5.3 2.6 %collective-permute-start.1 = (bf16[96,640]{1,0:T(8,128)(2,1)S(1)}, bf16[96,640]{1,0:T(8,128)(2,1)S(1)}, u32[]{:S(2)}, u32[]{:S(2)}) collective-permute-start(bf16[96,640]{1,0:T(8,128)(2,1)S(1)} %get-tuple-element.35), channel_id=1, source_target_pairs={{0,16},{4,20},{8,24},{12,28},{16,0},{20,4},{24,8},{28,12},{1,17},{... | collective-permute-start | bytes 368648 | tf_op jit(solution)/shard_map/ppermute | solution.py:61
  7.9 0.0 collective-permute-start.2
  7.9 3.9 %collective-permute-start.3 = (bf16[96,640]{1,0:T(8,128)(2,1)S(1)}, bf16[96,640]{1,0:T(8,128)(2,1)S(1)}, u32[]{:S(2)}, u32[]{:S(2)}) collective-permute-start(bf16[96,640]{1,0:T(8,128)(2,1)S(1)} %get-tuple-element.37), channel_id=1, source_target_pairs={{0,24},{4,28},{8,16},{12,20},{16,8},{20,12},{24,0},{28,4},{1,25},{... | collective-permute-start | bytes 368648 | tf_op jit(solution)/shard_map/ppermute | solution.py:61
  11.8 0.0 collective-permute-start.4
  11.8 0.0 collective-permute-done.refs_1_
  11.8 5.2 %all-gather = bf16[8,16,128]{2,1,0:T(8,128)(2,1)S(1)} all-gather(bf16[2,16,128]{2,1,0:T(8,128)(2,1)S(1)} %get-tuple-element.41), channel_id=2, replica_groups=mesh['band'=8,'rep'=4] {'rep'}, dimensions={0}, use_global_device_ids=true | all-gather | bytes 40960 | tf_op jit(solution)/shard_map/all_gather | solution.py:131
  17.0 3.0 %collective-permute-start.5 = (bf16[96,640]{1,0:T(8,128)(2,1)S(1)}, bf16[96,640]{1,0:T(8,128)(2,1)S(1)}, u32[]{:S(2)}, u32[]{:S(2)}) collective-permute-start(bf16[96,640]{1,0:T(8,128)(2,1)S(1)} %get-tuple-element.47), channel_id=1, source_target_pairs={{0,12},{4,8},{8,4},{12,0},{16,28},{20,24},{24,20},{28,16},{1,13},{... | collective-permute-start | bytes 368648 | tf_op jit(solution)/shard_map/ppermute | solution.py:61
  19.9 0.2 collective-permute-done.1.refs_2_
  20.1 2.4 %collective-permute-start.6 = (bf16[96,640]{1,0:T(8,128)(2,1)S(1)}, bf16[96,640]{1,0:T(8,128)(2,1)S(1)}, u32[]{:S(2)}, u32[]{:S(2)}) collective-permute-start(bf16[96,640]{1,0:T(8,128)(2,1)S(1)} %get-tuple-element.48), channel_id=1, source_target_pairs={{0,28},{4,24},{8,20},{12,16},{16,12},{20,8},{24,4},{28,0},{1,29},{... | collective-permute-start | bytes 368648 | tf_op jit(solution)/shard_map/ppermute | solution.py:61
  22.5 3.0 %prepare.1 = (bf16[2,384,512]{2,1,0:T(8,128)(2,1)S(1)}, bf16[4,32,512]{2,1,0:T(8,128)(2,1)S(1)}, bf16[16,80]{1,0:T(8,128)(2,1)S(1)}, bf16[192,192]{1,0:T(8,128)(...) custom-call(s32[5]{0:T(128)} %group_hbm_ref.1, ...), custom_call_target="tpu_custom_call" | custom-call | flops 215482368 | bytes 6291456 | tf_op jit(solution)/shard_map/prepare/pallas_call | solution.py:240
  25.5 0.0 collective-permute-done.2.refs_3_
  25.5 0.0 collective-permute-done.3.refs_4_
  25.5 0.0 collective-permute-done.4.refs_5_.refs_2_
  25.5 0.8 %embed_early.1 = (bf16[2,576,512]{2,1,0:T(8,128)(2,1)S(1)}, bf16[640,512]{1,0:T(8,128)(2,1)S(1)}) custom-call(bf16[96,640]{1,0:T(8,128)(2,1)S(1)} %get-tuple-element.31.refs_0_, bf16[96,640]{1,0:T(8,128)(2,1)S(1)} %collective-permute-done.refs_1_, bf16[96,640]{1,0:T(8,128)(2,1)S(1)} %collective-permute-done.1.refs_2_, ...), custom_call_target="tpu_custom_call" | custom-call | flops 377487360 | bytes 4194304 | tf_op jit(solution)/shard_map/embed_early/pallas_call | solution.py:303
  26.3 1.7 %collective-permute-done.5.refs_3_ = bf16[96,640]{1,0:T(8,128)(2,1)S(1)} collective-permute-done((bf16[96,640]{1,0:T(8,128)(2,1)S(1)}, bf16[96,640]{1,0:T(8,128)(2,1)S(1)}, u32[]{:S(2)}, u32[]{:S(2)}) %collective-permute-start.5) | collective-permute-done | bytes 122912 | tf_op jit(solution)/shard_map/ppermute | solution.py:61
  28.0 0.0 collective-permute-done.6.refs_4_
  28.0 5.9 %mix_blocks.1 = (bf16[2,8,96,512]{3,2,1,0:T(8,128)(2,1)}, bf16[32,24,128]{2,1,0:T(8,128)(2,1)S(1)}) custom-call(bf16[2,576,512]{2,1,0:T(8,128)(2,1)S(1)} %get-tuple-element.45.refs_0_, bf16[640,512]{1,0:T(8,128)(2,1)S(1)} %get-tuple-element.46.refs_1_, bf16[96,640]{1,0:T(8,128)(2,1)S(1)} %collective-permute-done.4.refs_5_.refs_2_, ...), custom_call_target="tpu_custom_call" | custom-call | flops 3623878656 | bytes 12582912 | tf_op jit(solution)/shard_map/mix_blocks/pallas_call | solution.py:533
  33.9 14.9 %all_to_all.5.parts_ref = bf16[32,24,128]{2,1,0:T(8,128)(2,1)S(1)} all-to-all(bf16[32,24,128]{2,1,0:T(8,128)(2,1)S(1)} %get-tuple-element.56), channel_id=1, replica_groups=mesh['band'=8,'rep'=4] {'band','rep'}, dimensions={0} | all-to-all | bytes 393216 | tf_op jit(solution)/shard_map/all_to_all | solution.py:574
  48.8 0.7 %sum_shares.1 = (f32[16,20]{1,0:T(8,128)}, f32[16,128]{1,0:T(8,128)}) custom-call(bf16[32,24,128]{2,1,0:T(8,128)(2,1)S(1)} %all_to_all.5.parts_ref), custom_call_target="tpu_custom_call" | custom-call | tf_op jit(solution)/shard_map/sum_shares/pallas_call | solution.py:575
Async XLA Ops:
  2.3 9.5 %collective-permute-start = (bf16[96,640]{1,0:T(8,128)(2,1)S(1)}, bf16[96,640]{1,0:T(8,128)(2,1)S(1)}, u32[]{:S(2)}, u32[]{:S(2)}) collective-permute-start(bf16[96,640]{1,0:T(8,128)(2,1)S(1)} %get-tuple-element.32), channel_id=1, source_target_pairs={{0,4},{4,0},{8,12},{12,8},{16,20},{20,16},{24,28},{28,24},{1,5},{5... | collective-permute-start | bytes 368648 | tf_op jit(solution)/shard_map/ppermute | solution.py:61
  5.3 14.8 %collective-permute-start.1 = (bf16[96,640]{1,0:T(8,128)(2,1)S(1)}, bf16[96,640]{1,0:T(8,128)(2,1)S(1)}, u32[]{:S(2)}, u32[]{:S(2)}) collective-permute-start(bf16[96,640]{1,0:T(8,128)(2,1)S(1)} %get-tuple-element.35), channel_id=1, source_target_pairs={{0,16},{4,20},{8,24},{12,28},{16,0},{20,4},{24,8},{28,12},{1,17},{... | collective-permute-start | bytes 368648 | tf_op jit(solution)/shard_map/ppermute | solution.py:61
  7.9 17.6 %collective-permute-start.2 = (bf16[96,640]{1,0:T(8,128)(2,1)S(1)}, bf16[96,640]{1,0:T(8,128)(2,1)S(1)}, u32[]{:S(2)}, u32[]{:S(2)}) collective-permute-start(bf16[96,640]{1,0:T(8,128)(2,1)S(1)} %get-tuple-element.36), channel_id=1, source_target_pairs={{0,20},{4,16},{8,28},{12,24},{16,4},{20,0},{24,12},{28,8},{1,21},{... | collective-permute-start | bytes 368648 | tf_op jit(solution)/shard_map/ppermute | solution.py:61
  7.9 17.6 %collective-permute-start.3 = (bf16[96,640]{1,0:T(8,128)(2,1)S(1)}, bf16[96,640]{1,0:T(8,128)(2,1)S(1)}, u32[]{:S(2)}, u32[]{:S(2)}) collective-permute-start(bf16[96,640]{1,0:T(8,128)(2,1)S(1)} %get-tuple-element.37), channel_id=1, source_target_pairs={{0,24},{4,28},{8,16},{12,20},{16,8},{20,12},{24,0},{28,4},{1,25},{... | collective-permute-start | bytes 368648 | tf_op jit(solution)/shard_map/ppermute | solution.py:61
  11.8 13.8 %collective-permute-start.4 = (bf16[96,640]{1,0:T(8,128)(2,1)S(1)}, bf16[96,640]{1,0:T(8,128)(2,1)S(1)}, u32[]{:S(2)}, u32[]{:S(2)}) collective-permute-start(bf16[96,640]{1,0:T(8,128)(2,1)S(1)} %get-tuple-element.38), channel_id=1, source_target_pairs={{0,8},{4,12},{8,0},{12,4},{16,24},{20,28},{24,16},{28,20},{1,9},{5... | collective-permute-start | bytes 368648 | tf_op jit(solution)/shard_map/ppermute | solution.py:61
  17.0 11.0 %collective-permute-start.5 = (bf16[96,640]{1,0:T(8,128)(2,1)S(1)}, bf16[96,640]{1,0:T(8,128)(2,1)S(1)}, u32[]{:S(2)}, u32[]{:S(2)}) collective-permute-start(bf16[96,640]{1,0:T(8,128)(2,1)S(1)} %get-tuple-element.47), channel_id=1, source_target_pairs={{0,12},{4,8},{8,4},{12,0},{16,28},{20,24},{24,20},{28,16},{1,13},{... | collective-permute-start | bytes 368648 | tf_op jit(solution)/shard_map/ppermute | solution.py:61
  20.1 7.9 %collective-permute-start.6 = (bf16[96,640]{1,0:T(8,128)(2,1)S(1)}, bf16[96,640]{1,0:T(8,128)(2,1)S(1)}, u32[]{:S(2)}, u32[]{:S(2)}) collective-permute-start(bf16[96,640]{1,0:T(8,128)(2,1)S(1)} %get-tuple-element.48), channel_id=1, source_target_pairs={{0,28},{4,24},{8,20},{12,16},{16,12},{20,8},{24,4},{28,0},{1,29},{... | collective-permute-start | bytes 368648 | tf_op jit(solution)/shard_map/ppermute | solution.py:61

commit v21 on v19

--- a/solution.py
+++ b/solution.py
@@ -483,11 +483,8 @@
             others += turn(n)
         if i > 0:
             others += backward(*units[i - 1])
-        lines = pointwise(*unit)
-        for line, vector_step in enumerate(lines):
-            vector_step()
-            for step in others[line * len(others) // len(lines) : (line + 1) * len(others) // len(lines)]:
-                step()
+        for step in others + pointwise(*unit):
+            step()
         if columns.stop == feature_dim:
             each = len(stores) // chunk_count
             for store in stores[n * each : (n + 1) * each]:

time: 49.5 us -> 49.5 us (level)
  no operation moved by 1% of the time
where the time goes in v21:
time: 49.5 us; the launch traced here: 49.1 us
  blocking collectives  20.1 us (41%)
  starting transfers between devices  14.8 us (30%)
  Pallas kernels  11.6 us (23%)
  waiting for transfers between devices  1.88 us (4%)
  between operations  0.69 us (1%)
    all_to_all x1, blocking collectives, sum_shares(): lax.all_to_all(shares, ('band', 'rep'), split_axis=0, concat_axis=0, tile...  14.9 us
    ppermute x7, starting transfers between devices, swap(): lax.ppermute(values, axis, [(source, source ^ distance) for source in ran...  14.8 us
    pallas_call x1, Pallas kernels, mix_blocks(): pl.pallas_call(lambda *refs: mix_kernel(direct, refs[:len(arrived)], *ref...  5.48 us
    all_gather x1, blocking collectives, exchange(): factors = lax.all_gather(pack, 'rep', axis=0, tiled=False)  5.18 us
    pallas_call x1, Pallas kernels, prepare(): pl.pallas_call(functools.partial(prep_kernel, direct, row_share, half_wid...  2.98 us
    ppermute x7, waiting for transfers between devices, swap(): lax.ppermute(values, axis, [(source, source ^ distance) for source in ran...  1.88 us
    pallas_call x1, Pallas kernels, send_blocks(): pl.pallas_call(send_kernel, out_shape=[jax.ShapeDtypeStruct(shape, BF16)...  1.64 us
  transfers between devices with their start and end apart: 7, of which 2 were waited for; matrix products, arithmetic and copies ran while one was open for 0% of the time, Pallas kernels for 8%

profile of v21, /device:TPU:0, one launch (start us, length us, event | category | flops | bytes accessed | tf_op | source)
XLA Modules:
  0.0 49.1 jit_solution(6323234558927799885)
XLA Ops:
  0.6 1.6 %send_blocks.1 = (bf16[96,640]{1,0:T(8,128)(2,1)S(1)}, bf16[96,640]{1,0:T(8,128)(2,1)S(1)}, bf16[96,640]{1,0:T(8,128)(2,1)S(1)}, bf16[96,640]{1,0:T(8,128)(2,1)S...) custom-call(s32[8]{0:T(128)} %owner_hbm_ref.1, ...), custom_call_target="tpu_custom_call" | custom-call | tf_op jit(solution)/shard_map/send_blocks/pallas_call | solution.py:106
  2.3 3.0 %collective-permute-start = (bf16[96,640]{1,0:T(8,128)(2,1)S(1)}, bf16[96,640]{1,0:T(8,128)(2,1)S(1)}, u32[]{:S(2)}, u32[]{:S(2)}) collective-permute-start(bf16[96,640]{1,0:T(8,128)(2,1)S(1)} %get-tuple-element.32), channel_id=1, source_target_pairs={{0,4},{4,0},{8,12},{12,8},{16,20},{20,16},{24,28},{28,24},{1,5},{5... | collective-permute-start | bytes 368648 | tf_op jit(solution)/shard_map/ppermute | solution.py:61
  5.3 2.6 %collective-permute-start.1 = (bf16[96,640]{1,0:T(8,128)(2,1)S(1)}, bf16[96,640]{1,0:T(8,128)(2,1)S(1)}, u32[]{:S(2)}, u32[]{:S(2)}) collective-permute-start(bf16[96,640]{1,0:T(8,128)(2,1)S(1)} %get-tuple-element.35), channel_id=1, source_target_pairs={{0,16},{4,20},{8,24},{12,28},{16,0},{20,4},{24,8},{28,12},{1,17},{... | collective-permute-start | bytes 368648 | tf_op jit(solution)/shard_map/ppermute | solution.py:61
  7.9 0.0 collective-permute-start.2
  7.9 3.9 %collective-permute-start.3 = (bf16[96,640]{1,0:T(8,128)(2,1)S(1)}, bf16[96,640]{1,0:T(8,128)(2,1)S(1)}, u32[]{:S(2)}, u32[]{:S(2)}) collective-permute-start(bf16[96,640]{1,0:T(8,128)(2,1)S(1)} %get-tuple-element.37), channel_id=1, source_target_pairs={{0,24},{4,28},{8,16},{12,20},{16,8},{20,12},{24,0},{28,4},{1,25},{... | collective-permute-start | bytes 368648 | tf_op jit(solution)/shard_map/ppermute | solution.py:61
  11.8 0.0 collective-permute-start.4
  11.8 0.0 collective-permute-done.refs_1_
  11.8 5.2 %all-gather = bf16[8,16,128]{2,1,0:T(8,128)(2,1)S(1)} all-gather(bf16[2,16,128]{2,1,0:T(8,128)(2,1)S(1)} %get-tuple-element.41), channel_id=2, replica_groups=mesh['band'=8,'rep'=4] {'rep'}, dimensions={0}, use_global_device_ids=true | all-gather | bytes 40960 | tf_op jit(solution)/shard_map/all_gather | solution.py:131
  17.0 3.0 %collective-permute-start.5 = (bf16[96,640]{1,0:T(8,128)(2,1)S(1)}, bf16[96,640]{1,0:T(8,128)(2,1)S(1)}, u32[]{:S(2)}, u32[]{:S(2)}) collective-permute-start(bf16[96,640]{1,0:T(8,128)(2,1)S(1)} %get-tuple-element.47), channel_id=1, source_target_pairs={{0,12},{4,8},{8,4},{12,0},{16,28},{20,24},{24,20},{28,16},{1,13},{... | collective-permute-start | bytes 368648 | tf_op jit(solution)/shard_map/ppermute | solution.py:61
  19.9 0.2 collective-permute-done.1.refs_2_
  20.1 2.4 %collective-permute-start.6 = (bf16[96,640]{1,0:T(8,128)(2,1)S(1)}, bf16[96,640]{1,0:T(8,128)(2,1)S(1)}, u32[]{:S(2)}, u32[]{:S(2)}) collective-permute-start(bf16[96,640]{1,0:T(8,128)(2,1)S(1)} %get-tuple-element.48), channel_id=1, source_target_pairs={{0,28},{4,24},{8,20},{12,16},{16,12},{20,8},{24,4},{28,0},{1,29},{... | collective-permute-start | bytes 368648 | tf_op jit(solution)/shard_map/ppermute | solution.py:61
  22.5 3.0 %prepare.1 = (bf16[2,384,512]{2,1,0:T(8,128)(2,1)S(1)}, bf16[4,32,512]{2,1,0:T(8,128)(2,1)S(1)}, bf16[16,80]{1,0:T(8,128)(2,1)S(1)}, bf16[192,192]{1,0:T(8,128)(...) custom-call(s32[5]{0:T(128)} %group_hbm_ref.1, ...), custom_call_target="tpu_custom_call" | custom-call | flops 215482368 | bytes 6291456 | tf_op jit(solution)/shard_map/prepare/pallas_call | solution.py:240
  25.5 0.0 collective-permute-done.2.refs_3_
  25.5 0.0 collective-permute-done.3.refs_4_
  25.5 0.0 collective-permute-done.4.refs_5_.refs_2_
  25.5 0.8 %embed_early.1 = (bf16[2,576,512]{2,1,0:T(8,128)(2,1)S(1)}, bf16[640,512]{1,0:T(8,128)(2,1)S(1)}) custom-call(bf16[96,640]{1,0:T(8,128)(2,1)S(1)} %get-tuple-element.31.refs_0_, bf16[96,640]{1,0:T(8,128)(2,1)S(1)} %collective-permute-done.refs_1_, bf16[96,640]{1,0:T(8,128)(2,1)S(1)} %collective-permute-done.1.refs_2_, ...), custom_call_target="tpu_custom_call" | custom-call | flops 377487360 | bytes 4194304 | tf_op jit(solution)/shard_map/embed_early/pallas_call | solution.py:305
  26.3 1.7 %collective-permute-done.5.refs_3_ = bf16[96,640]{1,0:T(8,128)(2,1)S(1)} collective-permute-done((bf16[96,640]{1,0:T(8,128)(2,1)S(1)}, bf16[96,640]{1,0:T(8,128)(2,1)S(1)}, u32[]{:S(2)}, u32[]{:S(2)}) %collective-permute-start.5) | collective-permute-done | bytes 122912 | tf_op jit(solution)/shard_map/ppermute | solution.py:61
  28.0 0.0 collective-permute-done.6.refs_4_
  28.0 5.5 %mix_blocks.1 = (bf16[2,8,96,512]{3,2,1,0:T(8,128)(2,1)}, bf16[32,24,128]{2,1,0:T(8,128)(2,1)S(1)}) custom-call(bf16[2,576,512]{2,1,0:T(8,128)(2,1)S(1)} %get-tuple-element.45.refs_0_, bf16[640,512]{1,0:T(8,128)(2,1)S(1)} %get-tuple-element.46.refs_1_, bf16[96,640]{1,0:T(8,128)(2,1)S(1)} %collective-permute-done.4.refs_5_.refs_2_, ...), custom_call_target="tpu_custom_call" | custom-call | flops 3623878656 | bytes 12582912 | tf_op jit(solution)/shard_map/mix_blocks/pallas_call | solution.py:533
  33.5 14.9 %all_to_all.5.parts_ref = bf16[32,24,128]{2,1,0:T(8,128)(2,1)S(1)} all-to-all(bf16[32,24,128]{2,1,0:T(8,128)(2,1)S(1)} %get-tuple-element.56), channel_id=1, replica_groups=mesh['band'=8,'rep'=4] {'band','rep'}, dimensions={0} | all-to-all | bytes 393216 | tf_op jit(solution)/shard_map/all_to_all | solution.py:574
  48.4 0.7 %sum_shares.1 = (f32[16,20]{1,0:T(8,128)}, f32[16,128]{1,0:T(8,128)}) custom-call(bf16[32,24,128]{2,1,0:T(8,128)(2,1)S(1)} %all_to_all.5.parts_ref), custom_call_target="tpu_custom_call" | custom-call | tf_op jit(solution)/shard_map/sum_shares/pallas_call | solution.py:575
Async XLA Ops:
  2.3 9.5 %collective-permute-start = (bf16[96,640]{1,0:T(8,128)(2,1)S(1)}, bf16[96,640]{1,0:T(8,128)(2,1)S(1)}, u32[]{:S(2)}, u32[]{:S(2)}) collective-permute-start(bf16[96,640]{1,0:T(8,128)(2,1)S(1)} %get-tuple-element.32), channel_id=1, source_target_pairs={{0,4},{4,0},{8,12},{12,8},{16,20},{20,16},{24,28},{28,24},{1,5},{5... | collective-permute-start | bytes 368648 | tf_op jit(solution)/shard_map/ppermute | solution.py:61
  5.3 14.8 %collective-permute-start.1 = (bf16[96,640]{1,0:T(8,128)(2,1)S(1)}, bf16[96,640]{1,0:T(8,128)(2,1)S(1)}, u32[]{:S(2)}, u32[]{:S(2)}) collective-permute-start(bf16[96,640]{1,0:T(8,128)(2,1)S(1)} %get-tuple-element.35), channel_id=1, source_target_pairs={{0,16},{4,20},{8,24},{12,28},{16,0},{20,4},{24,8},{28,12},{1,17},{... | collective-permute-start | bytes 368648 | tf_op jit(solution)/shard_map/ppermute | solution.py:61
  7.9 17.6 %collective-permute-start.2 = (bf16[96,640]{1,0:T(8,128)(2,1)S(1)}, bf16[96,640]{1,0:T(8,128)(2,1)S(1)}, u32[]{:S(2)}, u32[]{:S(2)}) collective-permute-start(bf16[96,640]{1,0:T(8,128)(2,1)S(1)} %get-tuple-element.36), channel_id=1, source_target_pairs={{0,20},{4,16},{8,28},{12,24},{16,4},{20,0},{24,12},{28,8},{1,21},{... | collective-permute-start | bytes 368648 | tf_op jit(solution)/shard_map/ppermute | solution.py:61
  7.9 17.6 %collective-permute-start.3 = (bf16[96,640]{1,0:T(8,128)(2,1)S(1)}, bf16[96,640]{1,0:T(8,128)(2,1)S(1)}, u32[]{:S(2)}, u32[]{:S(2)}) collective-permute-start(bf16[96,640]{1,0:T(8,128)(2,1)S(1)} %get-tuple-element.37), channel_id=1, source_target_pairs={{0,24},{4,28},{8,16},{12,20},{16,8},{20,12},{24,0},{28,4},{1,25},{... | collective-permute-start | bytes 368648 | tf_op jit(solution)/shard_map/ppermute | solution.py:61
  11.8 13.8 %collective-permute-start.4 = (bf16[96,640]{1,0:T(8,128)(2,1)S(1)}, bf16[96,640]{1,0:T(8,128)(2,1)S(1)}, u32[]{:S(2)}, u32[]{:S(2)}) collective-permute-start(bf16[96,640]{1,0:T(8,128)(2,1)S(1)} %get-tuple-element.38), channel_id=1, source_target_pairs={{0,8},{4,12},{8,0},{12,4},{16,24},{20,28},{24,16},{28,20},{1,9},{5... | collective-permute-start | bytes 368648 | tf_op jit(solution)/shard_map/ppermute | solution.py:61
  17.0 11.0 %collective-permute-start.5 = (bf16[96,640]{1,0:T(8,128)(2,1)S(1)}, bf16[96,640]{1,0:T(8,128)(2,1)S(1)}, u32[]{:S(2)}, u32[]{:S(2)}) collective-permute-start(bf16[96,640]{1,0:T(8,128)(2,1)S(1)} %get-tuple-element.47), channel_id=1, source_target_pairs={{0,12},{4,8},{8,4},{12,0},{16,28},{20,24},{24,20},{28,16},{1,13},{... | collective-permute-start | bytes 368648 | tf_op jit(solution)/shard_map/ppermute | solution.py:61
  20.1 7.9 %collective-permute-start.6 = (bf16[96,640]{1,0:T(8,128)(2,1)S(1)}, bf16[96,640]{1,0:T(8,128)(2,1)S(1)}, u32[]{:S(2)}, u32[]{:S(2)}) collective-permute-start(bf16[96,640]{1,0:T(8,128)(2,1)S(1)} %get-tuple-element.48), channel_id=1, source_target_pairs={{0,28},{4,24},{8,20},{12,16},{16,12},{20,8},{24,4},{28,0},{1,29},{... | collective-permute-start | bytes 368648 | tf_op jit(solution)/shard_map/ppermute | solution.py:61

commit v22 on v19

--- a/solution.py
+++ b/solution.py
@@ -257,17 +257,15 @@
 def factor_shares(total, up_ref, down_ref, level_ref):
     levels, two_rank, feature_dim = up_ref.shape
     rank, channels = down_ref.shape
-    high, low = split_hi_lo(total)
-    down = down_ref[...]
-    first = jnp.zeros((rank, channels), F32)
+    total = total.astype(BF16)
+    first = jnp.zeros((two_rank, channels), F32)
     second = jnp.zeros((two_rank, feature_dim), F32)
     for level in range(levels):
-        at = slice(level * channels, (level + 1) * channels)
-        both = dot_nt(up_ref[level], high[at])
-        first = first + both[:rank] + both[rank:] + dot_nt(up_ref[level, :rank, :], low[at])
-        through = dot_nn(down, high[at]) + dot_nn(down, low[at])
-        through = jnp.concatenate(split_hi_lo(through), axis=0)
+        part = total[level * channels : (level + 1) * channels]
+        first = first + dot_nt(up_ref[level], part)
+        through = jnp.concatenate(split_hi_lo(dot_nn(down_ref[...], part)), axis=0)
         second = second + dot_nt(through, level_ref[level])
+    first = first[:rank] + first[rank:]
     return first, second[:rank] + second[rank:]
 
 

time: 49.5 us -> 49.5 us (level)
  no operation moved by 1% of the time
where the time goes in v22:
time: 49.5 us; the launch traced here: 49.1 us
  blocking collectives  20.1 us (41%)
  starting transfers between devices  14.8 us (30%)
  Pallas kernels  11.6 us (23%)
  waiting for transfers between devices  1.88 us (4%)
  between operations  0.69 us (1%)
    all_to_all x1, blocking collectives, sum_shares(): lax.all_to_all(shares, ('band', 'rep'), split_axis=0, concat_axis=0, tile...  14.9 us
    ppermute x7, starting transfers between devices, swap(): lax.ppermute(values, axis, [(source, source ^ distance) for source in ran...  14.8 us
    pallas_call x1, Pallas kernels, mix_blocks(): pl.pallas_call(lambda *refs: mix_kernel(direct, refs[:len(arrived)], *ref...  5.46 us
    all_gather x1, blocking collectives, exchange(): factors = lax.all_gather(pack, 'rep', axis=0, tiled=False)  5.18 us
    pallas_call x1, Pallas kernels, prepare(): pl.pallas_call(functools.partial(prep_kernel, direct, row_share, half_wid...  2.98 us
    ppermute x7, waiting for transfers between devices, swap(): lax.ppermute(values, axis, [(source, source ^ distance) for source in ran...  1.88 us
    pallas_call x1, Pallas kernels, send_blocks(): pl.pallas_call(send_kernel, out_shape=[jax.ShapeDtypeStruct(shape, BF16)...  1.64 us
  transfers between devices with their start and end apart: 7, of which 2 were waited for; matrix products, arithmetic and copies ran while one was open for 0% of the time, Pallas kernels for 8%

profile of v22, /device:TPU:0, one launch (start us, length us, event | category | flops | bytes accessed | tf_op | source)
XLA Modules:
  0.0 49.1 jit_solution(12906916910498462105)
XLA Ops:
  0.6 1.6 %send_blocks.1 = (bf16[96,640]{1,0:T(8,128)(2,1)S(1)}, bf16[96,640]{1,0:T(8,128)(2,1)S(1)}, bf16[96,640]{1,0:T(8,128)(2,1)S(1)}, bf16[96,640]{1,0:T(8,128)(2,1)S...) custom-call(s32[8]{0:T(128)} %owner_hbm_ref.1, ...), custom_call_target="tpu_custom_call" | custom-call | tf_op jit(solution)/shard_map/send_blocks/pallas_call | solution.py:106
  2.3 3.0 %collective-permute-start = (bf16[96,640]{1,0:T(8,128)(2,1)S(1)}, bf16[96,640]{1,0:T(8,128)(2,1)S(1)}, u32[]{:S(2)}, u32[]{:S(2)}) collective-permute-start(bf16[96,640]{1,0:T(8,128)(2,1)S(1)} %get-tuple-element.32), channel_id=1, source_target_pairs={{0,4},{4,0},{8,12},{12,8},{16,20},{20,16},{24,28},{28,24},{1,5},{5... | collective-permute-start | bytes 368648 | tf_op jit(solution)/shard_map/ppermute | solution.py:61
  5.3 2.6 %collective-permute-start.1 = (bf16[96,640]{1,0:T(8,128)(2,1)S(1)}, bf16[96,640]{1,0:T(8,128)(2,1)S(1)}, u32[]{:S(2)}, u32[]{:S(2)}) collective-permute-start(bf16[96,640]{1,0:T(8,128)(2,1)S(1)} %get-tuple-element.35), channel_id=1, source_target_pairs={{0,16},{4,20},{8,24},{12,28},{16,0},{20,4},{24,8},{28,12},{1,17},{... | collective-permute-start | bytes 368648 | tf_op jit(solution)/shard_map/ppermute | solution.py:61
  7.9 0.0 collective-permute-start.2
  7.9 3.9 %collective-permute-start.3 = (bf16[96,640]{1,0:T(8,128)(2,1)S(1)}, bf16[96,640]{1,0:T(8,128)(2,1)S(1)}, u32[]{:S(2)}, u32[]{:S(2)}) collective-permute-start(bf16[96,640]{1,0:T(8,128)(2,1)S(1)} %get-tuple-element.37), channel_id=1, source_target_pairs={{0,24},{4,28},{8,16},{12,20},{16,8},{20,12},{24,0},{28,4},{1,25},{... | collective-permute-start | bytes 368648 | tf_op jit(solution)/shard_map/ppermute | solution.py:61
  11.8 0.0 collective-permute-start.4
  11.8 0.0 collective-permute-done.refs_1_
  11.8 5.2 %all-gather = bf16[8,16,128]{2,1,0:T(8,128)(2,1)S(1)} all-gather(bf16[2,16,128]{2,1,0:T(8,128)(2,1)S(1)} %get-tuple-element.41), channel_id=2, replica_groups=mesh['band'=8,'rep'=4] {'rep'}, dimensions={0}, use_global_device_ids=true | all-gather | bytes 40960 | tf_op jit(solution)/shard_map/all_gather | solution.py:131
  17.0 3.0 %collective-permute-start.5 = (bf16[96,640]{1,0:T(8,128)(2,1)S(1)}, bf16[96,640]{1,0:T(8,128)(2,1)S(1)}, u32[]{:S(2)}, u32[]{:S(2)}) collective-permute-start(bf16[96,640]{1,0:T(8,128)(2,1)S(1)} %get-tuple-element.47), channel_id=1, source_target_pairs={{0,12},{4,8},{8,4},{12,0},{16,28},{20,24},{24,20},{28,16},{1,13},{... | collective-permute-start | bytes 368648 | tf_op jit(solution)/shard_map/ppermute | solution.py:61
  19.9 0.2 collective-permute-done.1.refs_2_
  20.1 2.4 %collective-permute-start.6 = (bf16[96,640]{1,0:T(8,128)(2,1)S(1)}, bf16[96,640]{1,0:T(8,128)(2,1)S(1)}, u32[]{:S(2)}, u32[]{:S(2)}) collective-permute-start(bf16[96,640]{1,0:T(8,128)(2,1)S(1)} %get-tuple-element.48), channel_id=1, source_target_pairs={{0,28},{4,24},{8,20},{12,16},{16,12},{20,8},{24,4},{28,0},{1,29},{... | collective-permute-start | bytes 368648 | tf_op jit(solution)/shard_map/ppermute | solution.py:61
  22.5 3.0 %prepare.1 = (bf16[2,384,512]{2,1,0:T(8,128)(2,1)S(1)}, bf16[4,32,512]{2,1,0:T(8,128)(2,1)S(1)}, bf16[16,80]{1,0:T(8,128)(2,1)S(1)}, bf16[192,192]{1,0:T(8,128)(...) custom-call(s32[5]{0:T(128)} %group_hbm_ref.1, ...), custom_call_target="tpu_custom_call" | custom-call | flops 215482368 | bytes 6291456 | tf_op jit(solution)/shard_map/prepare/pallas_call | solution.py:240
  25.5 0.0 collective-permute-done.2.refs_3_
  25.5 0.0 collective-permute-done.3.refs_4_
  25.5 0.0 collective-permute-done.4.refs_5_.refs_2_
  25.5 0.8 %embed_early.1 = (bf16[2,576,512]{2,1,0:T(8,128)(2,1)S(1)}, bf16[640,512]{1,0:T(8,128)(2,1)S(1)}) custom-call(bf16[96,640]{1,0:T(8,128)(2,1)S(1)} %get-tuple-element.31.refs_0_, bf16[96,640]{1,0:T(8,128)(2,1)S(1)} %collective-permute-done.refs_1_, bf16[96,640]{1,0:T(8,128)(2,1)S(1)} %collective-permute-done.1.refs_2_, ...), custom_call_target="tpu_custom_call" | custom-call | flops 377487360 | bytes 4194304 | tf_op jit(solution)/shard_map/embed_early/pallas_call | solution.py:303
  26.3 1.7 %collective-permute-done.5.refs_3_ = bf16[96,640]{1,0:T(8,128)(2,1)S(1)} collective-permute-done((bf16[96,640]{1,0:T(8,128)(2,1)S(1)}, bf16[96,640]{1,0:T(8,128)(2,1)S(1)}, u32[]{:S(2)}, u32[]{:S(2)}) %collective-permute-start.5) | collective-permute-done | bytes 122912 | tf_op jit(solution)/shard_map/ppermute | solution.py:61
  28.0 0.0 collective-permute-done.6.refs_4_
  28.0 5.5 %mix_blocks.1 = (bf16[2,8,96,512]{3,2,1,0:T(8,128)(2,1)}, bf16[32,24,128]{2,1,0:T(8,128)(2,1)S(1)}) custom-call(bf16[2,576,512]{2,1,0:T(8,128)(2,1)S(1)} %get-tuple-element.45.refs_0_, bf16[640,512]{1,0:T(8,128)(2,1)S(1)} %get-tuple-element.46.refs_1_, bf16[96,640]{1,0:T(8,128)(2,1)S(1)} %collective-permute-done.4.refs_5_.refs_2_, ...), custom_call_target="tpu_custom_call" | custom-call | flops 3623878656 | bytes 12582912 | tf_op jit(solution)/shard_map/mix_blocks/pallas_call | solution.py:534
  33.5 14.9 %all_to_all.5.parts_ref = bf16[32,24,128]{2,1,0:T(8,128)(2,1)S(1)} all-to-all(bf16[32,24,128]{2,1,0:T(8,128)(2,1)S(1)} %get-tuple-element.56), channel_id=1, replica_groups=mesh['band'=8,'rep'=4] {'band','rep'}, dimensions={0} | all-to-all | bytes 393216 | tf_op jit(solution)/shard_map/all_to_all | solution.py:575
  48.4 0.7 %sum_shares.1 = (f32[16,20]{1,0:T(8,128)}, f32[16,128]{1,0:T(8,128)}) custom-call(bf16[32,24,128]{2,1,0:T(8,128)(2,1)S(1)} %all_to_all.5.parts_ref), custom_call_target="tpu_custom_call" | custom-call | tf_op jit(solution)/shard_map/sum_shares/pallas_call | solution.py:576
Async XLA Ops:
  2.3 9.5 %collective-permute-start = (bf16[96,640]{1,0:T(8,128)(2,1)S(1)}, bf16[96,640]{1,0:T(8,128)(2,1)S(1)}, u32[]{:S(2)}, u32[]{:S(2)}) collective-permute-start(bf16[96,640]{1,0:T(8,128)(2,1)S(1)} %get-tuple-element.32), channel_id=1, source_target_pairs={{0,4},{4,0},{8,12},{12,8},{16,20},{20,16},{24,28},{28,24},{1,5},{5... | collective-permute-start | bytes 368648 | tf_op jit(solution)/shard_map/ppermute | solution.py:61
  5.3 14.8 %collective-permute-start.1 = (bf16[96,640]{1,0:T(8,128)(2,1)S(1)}, bf16[96,640]{1,0:T(8,128)(2,1)S(1)}, u32[]{:S(2)}, u32[]{:S(2)}) collective-permute-start(bf16[96,640]{1,0:T(8,128)(2,1)S(1)} %get-tuple-element.35), channel_id=1, source_target_pairs={{0,16},{4,20},{8,24},{12,28},{16,0},{20,4},{24,8},{28,12},{1,17},{... | collective-permute-start | bytes 368648 | tf_op jit(solution)/shard_map/ppermute | solution.py:61
  7.9 17.6 %collective-permute-start.2 = (bf16[96,640]{1,0:T(8,128)(2,1)S(1)}, bf16[96,640]{1,0:T(8,128)(2,1)S(1)}, u32[]{:S(2)}, u32[]{:S(2)}) collective-permute-start(bf16[96,640]{1,0:T(8,128)(2,1)S(1)} %get-tuple-element.36), channel_id=1, source_target_pairs={{0,20},{4,16},{8,28},{12,24},{16,4},{20,0},{24,12},{28,8},{1,21},{... | collective-permute-start | bytes 368648 | tf_op jit(solution)/shard_map/ppermute | solution.py:61
  7.9 17.6 %collective-permute-start.3 = (bf16[96,640]{1,0:T(8,128)(2,1)S(1)}, bf16[96,640]{1,0:T(8,128)(2,1)S(1)}, u32[]{:S(2)}, u32[]{:S(2)}) collective-permute-start(bf16[96,640]{1,0:T(8,128)(2,1)S(1)} %get-tuple-element.37), channel_id=1, source_target_pairs={{0,24},{4,28},{8,16},{12,20},{16,8},{20,12},{24,0},{28,4},{1,25},{... | collective-permute-start | bytes 368648 | tf_op jit(solution)/shard_map/ppermute | solution.py:61
  11.8 13.8 %collective-permute-start.4 = (bf16[96,640]{1,0:T(8,128)(2,1)S(1)}, bf16[96,640]{1,0:T(8,128)(2,1)S(1)}, u32[]{:S(2)}, u32[]{:S(2)}) collective-permute-start(bf16[96,640]{1,0:T(8,128)(2,1)S(1)} %get-tuple-element.38), channel_id=1, source_target_pairs={{0,8},{4,12},{8,0},{12,4},{16,24},{20,28},{24,16},{28,20},{1,9},{5... | collective-permute-start | bytes 368648 | tf_op jit(solution)/shard_map/ppermute | solution.py:61
  17.0 11.0 %collective-permute-start.5 = (bf16[96,640]{1,0:T(8,128)(2,1)S(1)}, bf16[96,640]{1,0:T(8,128)(2,1)S(1)}, u32[]{:S(2)}, u32[]{:S(2)}) collective-permute-start(bf16[96,640]{1,0:T(8,128)(2,1)S(1)} %get-tuple-element.47), channel_id=1, source_target_pairs={{0,12},{4,8},{8,4},{12,0},{16,28},{20,24},{24,20},{28,16},{1,13},{... | collective-permute-start | bytes 368648 | tf_op jit(solution)/shard_map/ppermute | solution.py:61
  20.1 7.9 %collective-permute-start.6 = (bf16[96,640]{1,0:T(8,128)(2,1)S(1)}, bf16[96,640]{1,0:T(8,128)(2,1)S(1)}, u32[]{:S(2)}, u32[]{:S(2)}) collective-permute-start(bf16[96,640]{1,0:T(8,128)(2,1)S(1)} %get-tuple-element.48), channel_id=1, source_target_pairs={{0,28},{4,24},{8,20},{12,16},{16,12},{20,8},{24,4},{28,0},{1,29},{... | collective-permute-start | bytes 368648 | tf_op jit(solution)/shard_map/ppermute | solution.py:61
